TPU v7x, 32 devices: a whole 2x2x4 slice. The times are simulated.
32 devices in a mesh: dp: 2 (over core), expert: 16 (over z, y, x).
Axes of the slice: x: 2, y: 2, z: 4, core: 2. Of those that a mesh axis runs over, the one named last changes fastest.
Arguments:
- tokens: bfloat16 [4096, 2048], P(('dp', 'expert')), may hold values from -6 to 6
- attn_gain: bfloat16 [2048], P(('dp', 'expert')), may hold values from 0.5 to 1.5
- kv_gain: bfloat16 [512], P(('dp', 'expert')), may hold values from 0.5 to 1.5
- ffn_gain: bfloat16 [2048], P(('dp', 'expert')), may hold values from 0.5 to 1.5
- q_weight: bfloat16 [2048, 3072], P(('dp', 'expert')), may hold values from -0.125 to 0.125
- kv_down_weight: bfloat16 [2048, 576], P(('dp', 'expert')), may hold values from -0.125 to 0.125
- kv_up_weight: bfloat16 [512, 4096], P(('dp', 'expert')), may hold values from -0.25 to 0.25
- out_weight: bfloat16 [2048, 2048], P(('dp', 'expert')), may hold values from -0.5 to 0.5
- shared_gate_up: bfloat16 [2048, 2, 2816], P(('dp', 'expert')), may hold values from -0.125 to 0.125
- shared_down: bfloat16 [2816, 2048], P(('dp', 'expert')), may hold values from -0.109375 to 0.109375
- expert_gate_up: bfloat16 [16, 2048, 2, 1408], P('expert', 'dp'), may hold values from -0.125 to 0.125
- expert_down: bfloat16 [16, 1408, 2048], P('expert', 'dp'), may hold values from -0.15625 to 0.15625
- routes: int32 [4096, 6], P(('dp', 'expert')), may hold values from 0 to 15, all different within a row; in each aligned block of 128 rows (0 to 127, 128 to 255, ...) at most 72 rows name the same one
- gates: float32 [4096, 6], P(('dp', 'expert')), may hold values from 0.2 to 0.5
- lengths: int32 [32, 2], P(('dp', 'expert')), may hold values from 1 to 96, 128 in all within a row
- out_grad: bfloat16 [4096, 2048], P(('dp', 'expert')), may hold values from -6 to 6
Outputs:
- output: bfloat16 [4096, 2048], P(('dp', 'expert'))
- grad_tokens: bfloat16 [4096, 2048], P(('dp', 'expert'))
- grad_attn_gain: float32 [2048], P(('dp', 'expert'))
- grad_kv_gain: float32 [512], P(('dp', 'expert'))
- grad_ffn_gain: float32 [2048], P(('dp', 'expert'))
- grad_q_weight: float32 [2048, 3072], P(('dp', 'expert'))
- grad_kv_down: float32 [2048, 576], P(('dp', 'expert'))
- grad_kv_up: float32 [512, 4096], P(('dp', 'expert'))
- grad_out_weight: float32 [2048, 2048], P(('dp', 'expert'))
- grad_shared_gate_up: float32 [2048, 2, 2816], P(('dp', 'expert'))
- grad_shared_down: float32 [2816, 2048], P(('dp', 'expert'))
- grad_expert_gate_up: float32 [16, 2048, 2, 1408], P('expert', 'dp')
- grad_expert_down: float32 [16, 1408, 2048], P('expert', 'dp')
Inputs may be any that keep to these rules, and one draw needn't show every extreme that they name: `routes`: A token's 6 experts are distinct. Among the 128 rows of one device, each expert is named by at most 72 rows, a bound that some block reaches. `lengths`: each row sums to 128; no entry exceeds 96.
All inputs are finite; a program needn't handle non-finite values.
Results may differ from a plain program's by a relative error of at most 0.019.
Values may be sent and summed in bfloat16 or wider, within the bound.
No kernel may reach another device: no remote copies, remote signals or barrier semaphores. Data moves between devices by JAX's collectives and lax.ppermute only.
A program may use at most 320 MiB of HBM per device.

v0:
```python
import jax
import jax.numpy as jnp
from jax import lax
from jax.sharding import PartitionSpec as P

H = 16
DH = 128
DR = 64
DV = 128
KVR = 512
TOP = 6


norm_eps = 1e-06
rope_base = 50000.0
masked_score = -1e30


def norm_apply(values, scales):
    return values * lax.rsqrt(jnp.mean(values * values, axis=-1, keepdims=True) + norm_eps) * scales


def norm_back(values, scales, upstream):
    unused, pullback = jax.vjp(norm_apply, values, scales.astype(jnp.float32))
    return pullback(upstream)


def rotate(values, cosine_table, sine_table):
    half_width = values.shape[-1] // 2
    front_half = values[..., :half_width]
    back_half = values[..., half_width:]
    return jnp.concatenate(
        [
            front_half * cosine_table - back_half * sine_table,
            front_half * sine_table + back_half * cosine_table,
        ],
        axis=-1,
    )


def swish_gate(gate_up):
    gate_part = gate_up[..., 0, :]
    return gate_part * jax.nn.sigmoid(gate_part) * gate_up[..., 1, :]


def swish_back(gate_up, upstream):
    unused, pullback = jax.vjp(swish_gate, gate_up)
    return pullback(upstream)[0]


def layout(lengths_row, row_count):
    doc_ends = jnp.cumsum(lengths_row)
    places = jnp.arange(row_count, dtype=jnp.int32)
    passed_end = (places[:, None] >= doc_ends[None, :]).astype(jnp.int32)
    doc_ids = jnp.sum(passed_end, axis=1)
    starts = jnp.sum(passed_end * lengths_row[None, :], axis=1)
    return (doc_ids, places - starts)


def angles(offsets, rope_width):
    frequency = rope_base ** (-2.0 * jnp.arange(rope_width // 2, dtype=jnp.float32) / rope_width)
    turned = offsets.astype(jnp.float32)[:, None] * frequency[None, :]
    return (jnp.cos(turned), jnp.sin(turned))


def shards(
    tokens,
    attn_gain,
    kv_gain,
    ffn_gain,
    q_weight,
    kv_down_weight,
    kv_up_weight,
    out_weight,
    shared_gate_up,
    shared_down,
    expert_gate_up,
    expert_down,
    routes,
    gates,
    lengths,
    out_grad,
):
    f32 = jnp.float32
    bf16 = jnp.bfloat16
    row_count = tokens.shape[0]
    model_width = tokens.shape[1]
    scale_factor = (DH + DR) ** (-0.5)
    dense_full = (
        lax.all_gather(attn_gain, ("dp", "expert"), axis=0, tiled=True),
        lax.all_gather(kv_gain, ("dp", "expert"), axis=0, tiled=True),
        lax.all_gather(ffn_gain, ("dp", "expert"), axis=0, tiled=True),
        lax.all_gather(q_weight, ("dp", "expert"), axis=0, tiled=True),
        lax.all_gather(kv_down_weight, ("dp", "expert"), axis=0, tiled=True),
        lax.all_gather(kv_up_weight, ("dp", "expert"), axis=0, tiled=True),
        lax.all_gather(out_weight, ("dp", "expert"), axis=0, tiled=True),
        lax.all_gather(shared_gate_up, ("dp", "expert"), axis=0, tiled=True),
        lax.all_gather(shared_down, ("dp", "expert"), axis=0, tiled=True),
    )
    (
        attn_scale,
        kv_scale,
        ffn_scale,
        q_full,
        kv_down,
        kv_up,
        out_full,
        shared_pair_w,
        shared_out_w,
    ) = dense_full
    pair_local, down_local = (
        lax.all_gather(expert_gate_up, "dp", axis=1, tiled=True),
        lax.all_gather(expert_down, "dp", axis=1, tiled=True),
    )
    expert_pair_w = pair_local[0]
    expert_down_w = down_local[0]
    resid_in = tokens.astype(f32)
    normed = norm_apply(resid_in, attn_scale).astype(bf16)
    q_heads = jnp.dot(normed, q_full, preferred_element_type=f32).reshape(row_count, H, DH + DR)
    kv_joint = jnp.dot(normed, kv_down, preferred_element_type=f32)
    latent = kv_joint[:, :KVR]
    kv_normed = norm_apply(latent, kv_scale).astype(bf16)
    kv_heads = jnp.dot(kv_normed, kv_up, preferred_element_type=f32).reshape(row_count, H, DH + DV)
    doc_ids, offsets = layout(lengths[0], row_count)
    cosine_table, sine_table = angles(offsets, DR)
    queries = jnp.concatenate(
        [q_heads[..., :DH], rotate(q_heads[..., DH:], cosine_table[:, None], sine_table[:, None])],
        axis=-1,
    ).astype(bf16)
    rope_key = rotate(kv_joint[:, KVR:], cosine_table, sine_table)
    key_heads = jnp.concatenate(
        [kv_heads[..., :DH], jnp.broadcast_to(rope_key[:, None, :], (row_count, H, DR))], axis=-1
    ).astype(bf16)
    values = kv_heads[..., DH:].astype(bf16)
    places = jnp.arange(row_count, dtype=jnp.int32)
    allowed = (doc_ids[:, None] == doc_ids[None, :]) & (places[:, None] >= places[None, :])
    scores = (
        jnp.einsum("thd,shd->hts", queries, key_heads, preferred_element_type=f32) * scale_factor
    )
    scores = jnp.where(allowed[None], scores, masked_score)
    highest = jnp.max(scores, axis=-1, keepdims=True)
    weights = jnp.exp(scores - highest)
    denominator = jnp.sum(weights, axis=-1, keepdims=True)
    log_total = highest + jnp.log(denominator)
    weights_low = (weights / denominator).astype(bf16)
    attended = (
        jnp.einsum("hts,shd->thd", weights_low, values, preferred_element_type=f32)
        .reshape(row_count, H * DV)
        .astype(bf16)
    )
    resid = resid_in + jnp.dot(attended, out_full, preferred_element_type=f32)
    ffn_in = norm_apply(resid, ffn_scale).astype(bf16)
    shared_pair = jnp.einsum("td,dcf->tcf", ffn_in, shared_pair_w, preferred_element_type=f32)
    shared_hidden = swish_gate(shared_pair).astype(bf16)
    shared_term = jnp.dot(shared_hidden, shared_out_w, preferred_element_type=f32)
    expert_count = lax.axis_size("expert")
    capacity = min(row_count, 3 * row_count * TOP // (2 * expert_count))
    flat_routes = routes.reshape(-1)
    onehot = (flat_routes[:, None] == jnp.arange(expert_count, dtype=jnp.int32)[None, :]).astype(
        jnp.int32
    )
    before = jnp.cumsum(onehot, axis=0) - onehot
    slot_in = jnp.sum(before * onehot, axis=1)
    destination = flat_routes * capacity + slot_in
    slot_match = (
        jnp.arange(expert_count * capacity, dtype=jnp.int32)[:, None] == destination[None, :]
    )
    pair_token = jnp.arange(row_count * TOP, dtype=jnp.int32) // TOP
    slot_token = jnp.sum(jnp.where(slot_match, pair_token[None, :], 0), axis=1)
    slot_gate = jnp.sum(jnp.where(slot_match, gates.reshape(-1)[None, :], 0.0), axis=1)
    slot_live = jnp.any(slot_match, axis=1)
    outgoing = jnp.where(
        slot_live[:, None], jnp.take(ffn_in, slot_token, axis=0), jnp.zeros((), bf16)
    )
    received = lax.all_to_all(
        outgoing.reshape(expert_count, capacity, model_width),
        "expert",
        split_axis=0,
        concat_axis=0,
        tiled=True,
    )
    expert_rows = received.reshape(expert_count * capacity, model_width)
    expert_pair = jnp.einsum("rd,dcf->rcf", expert_rows, expert_pair_w, preferred_element_type=f32)
    expert_hidden = swish_gate(expert_pair).astype(bf16)
    expert_result = jnp.dot(expert_hidden, expert_down_w, preferred_element_type=f32).astype(bf16)
    returned = lax.all_to_all(
        expert_result.reshape(expert_count, capacity, model_width),
        "expert",
        split_axis=0,
        concat_axis=0,
        tiled=True,
    )
    picked = jnp.take(returned.reshape(expert_count * capacity, model_width), destination, axis=0)
    picked = picked.reshape(row_count, TOP, model_width).astype(f32)
    routed_sum = jnp.sum(picked * gates[:, :, None], axis=1)
    output = (resid + shared_term + routed_sum).astype(bf16)
    dense_back = (
        lax.all_gather(attn_gain, ("dp", "expert"), axis=0, tiled=True),
        lax.all_gather(kv_gain, ("dp", "expert"), axis=0, tiled=True),
        lax.all_gather(ffn_gain, ("dp", "expert"), axis=0, tiled=True),
        lax.all_gather(q_weight, ("dp", "expert"), axis=0, tiled=True),
        lax.all_gather(kv_down_weight, ("dp", "expert"), axis=0, tiled=True),
        lax.all_gather(kv_up_weight, ("dp", "expert"), axis=0, tiled=True),
        lax.all_gather(out_weight, ("dp", "expert"), axis=0, tiled=True),
        lax.all_gather(shared_gate_up, ("dp", "expert"), axis=0, tiled=True),
        lax.all_gather(shared_down, ("dp", "expert"), axis=0, tiled=True),
    )
    pair_again, down_again = (
        lax.all_gather(expert_gate_up, "dp", axis=1, tiled=True),
        lax.all_gather(expert_down, "dp", axis=1, tiled=True),
    )
    expert_pair_b = pair_again[0]
    expert_down_b = down_again[0]
    (
        attn_scale_b,
        kv_scale_b,
        ffn_scale_b,
        q_back,
        kv_down_b,
        kv_up_b,
        out_back,
        shared_pair_b,
        shared_out_b,
    ) = dense_back
    upstream = out_grad.astype(f32)
    slot_grad = (jnp.take(upstream, slot_token, axis=0) * slot_gate[:, None]).astype(bf16)
    slot_recv = lax.all_to_all(
        slot_grad.reshape(expert_count, capacity, model_width),
        "expert",
        split_axis=0,
        concat_axis=0,
        tiled=True,
    )
    slot_recv = slot_recv.reshape(expert_count * capacity, model_width)
    d_expert_hidden = jnp.dot(slot_recv, expert_down_b.T, preferred_element_type=f32)
    grad_edown = jnp.dot(expert_hidden.T, slot_recv, preferred_element_type=f32)
    d_expert_pair = swish_back(expert_pair, d_expert_hidden).astype(bf16)
    grad_epair = jnp.einsum("rd,rcf->dcf", expert_rows, d_expert_pair, preferred_element_type=f32)
    d_rows = jnp.einsum(
        "rcf,dcf->rd", d_expert_pair, expert_pair_b, preferred_element_type=f32
    ).astype(bf16)
    rows_back = lax.all_to_all(
        d_rows.reshape(expert_count, capacity, model_width),
        "expert",
        split_axis=0,
        concat_axis=0,
        tiled=True,
    )
    routed_back = jnp.take(
        rows_back.reshape(expert_count * capacity, model_width), destination, axis=0
    )
    routed_back = jnp.sum(routed_back.reshape(row_count, TOP, model_width).astype(f32), axis=1)
    expert_sums = (
        lax.psum_scatter(
            grad_epair[None].astype(jnp.bfloat16), "dp", scatter_dimension=1, tiled=True
        ).astype(jnp.float32),
        lax.psum_scatter(
            grad_edown[None].astype(jnp.bfloat16), "dp", scatter_dimension=1, tiled=True
        ).astype(jnp.float32),
    )
    d_shared_hidden = jnp.dot(out_grad, shared_out_b.T, preferred_element_type=f32)
    grad_sdown = jnp.dot(shared_hidden.T, out_grad, preferred_element_type=f32)
    d_shared_pair = swish_back(shared_pair, d_shared_hidden).astype(bf16)
    grad_spair = jnp.einsum("td,tcf->dcf", ffn_in, d_shared_pair, preferred_element_type=f32)
    d_ffn_in = (
        jnp.einsum("tcf,dcf->td", d_shared_pair, shared_pair_b, preferred_element_type=f32)
        + routed_back
    )
    d_norm_resid, grad_ffn_scale = norm_back(resid, ffn_scale_b, d_ffn_in)
    ffn_sums = (
        lax.psum_scatter(grad_ffn_scale, ("dp", "expert"), scatter_dimension=0, tiled=True),
        lax.psum_scatter(grad_spair, ("dp", "expert"), scatter_dimension=0, tiled=True),
        lax.psum_scatter(grad_sdown, ("dp", "expert"), scatter_dimension=0, tiled=True),
    )
    d_resid = upstream + d_norm_resid
    d_branch = d_resid.astype(bf16)
    grad_outw = jnp.dot(attended.T, d_branch, preferred_element_type=f32)
    d_attended = (
        jnp.dot(d_branch, out_back.T, preferred_element_type=f32)
        .astype(bf16)
        .reshape(row_count, H, DV)
    )
    probs_again = jnp.exp(scores - log_total)
    probs_low = probs_again.astype(bf16)
    grad_values = jnp.einsum("hts,thd->shd", probs_low, d_attended, preferred_element_type=f32)
    d_probs = jnp.einsum("thd,shd->hts", d_attended, values, preferred_element_type=f32)
    d_scores = (
        probs_again * (d_probs - jnp.sum(d_probs * probs_again, axis=-1, keepdims=True))
    ).astype(bf16)
    d_queries = (
        jnp.einsum("hts,shd->thd", d_scores, key_heads, preferred_element_type=f32) * scale_factor
    )
    d_keys = (
        jnp.einsum("hts,thd->shd", d_scores, queries, preferred_element_type=f32) * scale_factor
    )
    d_q_heads = jnp.concatenate(
        [
            d_queries[..., :DH],
            rotate(d_queries[..., DH:], cosine_table[:, None], -sine_table[:, None]),
        ],
        axis=-1,
    )
    d_q_heads = d_q_heads.astype(bf16).reshape(row_count, H * (DH + DR))
    grad_qw = jnp.dot(normed.T, d_q_heads, preferred_element_type=f32)
    d_rope_key = rotate(jnp.sum(d_keys[..., DH:], axis=1), cosine_table, -sine_table)
    d_kv_heads = (
        jnp.concatenate([d_keys[..., :DH], grad_values], axis=-1)
        .astype(bf16)
        .reshape(row_count, H * (DH + DV))
    )
    grad_kvup = jnp.dot(kv_normed.T, d_kv_heads, preferred_element_type=f32)
    d_kv_normed = jnp.dot(d_kv_heads, kv_up_b.T, preferred_element_type=f32)
    d_latent, grad_kv_scale = norm_back(latent, kv_scale_b, d_kv_normed)
    d_kv_joint = jnp.concatenate([d_latent, d_rope_key], axis=-1).astype(bf16)
    grad_kvdown = jnp.dot(normed.T, d_kv_joint, preferred_element_type=f32)
    d_normed = jnp.dot(d_q_heads, q_back.T, preferred_element_type=f32) + jnp.dot(
        d_kv_joint, kv_down_b.T, preferred_element_type=f32
    )
    d_norm_in, grad_attn_scale = norm_back(resid_in, attn_scale_b, d_normed)
    grad_in = (d_resid + d_norm_in).astype(bf16)
    attn_sums = (
        lax.psum_scatter(grad_attn_scale, ("dp", "expert"), scatter_dimension=0, tiled=True),
        lax.psum_scatter(grad_kv_scale, ("dp", "expert"), scatter_dimension=0, tiled=True),
        lax.psum_scatter(grad_qw, ("dp", "expert"), scatter_dimension=0, tiled=True),
        lax.psum_scatter(grad_kvdown, ("dp", "expert"), scatter_dimension=0, tiled=True),
        lax.psum_scatter(grad_kvup, ("dp", "expert"), scatter_dimension=0, tiled=True),
        lax.psum_scatter(grad_outw, ("dp", "expert"), scatter_dimension=0, tiled=True),
    )
    return (
        output,
        grad_in,
        attn_sums[0],
        attn_sums[1],
        ffn_sums[0],
        attn_sums[2],
        attn_sums[3],
        attn_sums[4],
        attn_sums[5],
        ffn_sums[1],
        ffn_sums[2],
        expert_sums[0],
        expert_sums[1],
    )


def solution(mesh):
    return jax.shard_map(
        shards,
        mesh=mesh,
        in_specs=(
            P(("dp", "expert"), None),
            P(("dp", "expert")),
            P(("dp", "expert")),
            P(("dp", "expert")),
            P(("dp", "expert"), None),
            P(("dp", "expert"), None),
            P(("dp", "expert"), None),
            P(("dp", "expert"), None),
            P(("dp", "expert"), None, None),
            P(("dp", "expert"), None),
            P("expert", "dp", None, None),
            P("expert", "dp", None),
            P(("dp", "expert"), None),
            P(("dp", "expert"), None),
            P(("dp", "expert"), None),
            P(("dp", "expert"), None),
        ),
        out_specs=(
            P(("dp", "expert"), None),
            P(("dp", "expert"), None),
            P(("dp", "expert")),
            P(("dp", "expert")),
            P(("dp", "expert")),
            P(("dp", "expert"), None),
            P(("dp", "expert"), None),
            P(("dp", "expert"), None),
            P(("dp", "expert"), None),
            P(("dp", "expert"), None, None),
            P(("dp", "expert"), None),
            P("expert", "dp", None, None),
            P("expert", "dp", None),
        ),
        check_vma=False,
    )
```

profile of v0, /device:TPU:1, one launch (start us, length us, event | category | flops | bytes accessed | tf_op | source)
XLA Modules:
  0.0 3318.6 jit_solution(14717770014082292909)
XLA Ops:
  10.0 5.9 copy.101
  23.6 42.3 %all-reduce.11 = (bf16[2048]{0:T(1024)(128)(2,1)S(1)}, bf16[512]{0:T(512)(128)(2,1)S(1)}, bf16[2048]{0:T(1024)(128)(2,1)S(1)}) all-reduce(bf16[2048]{0:T(1024)(128)(2,1)S(1)} %dynamic-update-slice, bf16[512]{0:T(512)(128)(2,1)S(1)} %dynamic-update-slice.1, ...), channel_id=1, replica_groups=mesh['dp'=2,'expert'=16] {'dp','expert'}, use_global_device_ids=true, to_apply=%add.4 | all-reduce | flops 4608 | bytes 18432
  75.1 60.3 %all-gather.11.cloned.1.call-done = bf16[512,4096]{1,0:T(8,128)(2,1)} async-done(((bf16[16,4096]{1,0:T(8,128)(2,1)}), bf16[512,4096]{1,0:T(8,128)(2,1)}) %all-gather.11.cloned.1.call-update) | async-done | bytes 4194320 | tf_op jit(solution)/shard_map/all_gather | solution.py:95
  139.2 93.7 %all-gather.13.cloned.1.call-done = bf16[2048,3072]{1,0:T(8,128)(2,1)} async-done(((bf16[64,3072]{1,0:T(8,128)(2,1)}), bf16[2048,3072]{1,0:T(8,128)(2,1)}) %all-gather.13.cloned.1.call-update) | async-done | bytes 12582928 | tf_op jit(solution)/shard_map/all_gather | solution.py:93
  232.9 8.1 fusion.95
  243.1 68.3 %all-gather.15.cloned.1.call-done = bf16[2048,2048]{1,0:T(8,128)(2,1)} async-done(((bf16[64,2048]{1,0:T(8,128)(2,1)}), bf16[2048,2048]{1,0:T(8,128)(2,1)}) %all-gather.15.cloned.1.call-update) | async-done | bytes 8388624 | tf_op jit(solution)/shard_map/all_gather | solution.py:96
  317.3 5.9 gather_fusion
  333.7 6.7 gather_fusion.1
  341.2 7.6 multiply_convert_fusion
  348.8 108.6 %all-to-all-done = bf16[16,72,2048]{2,1,0:T(8,128)(2,1)} async-done(((bf16[16,72,2048]{2,1,0:T(8,128)(2,1)}), bf16[16,72,2048]{2,1,0:T(8,128)(2,1)}, u32[]{:S(2)}, u32[]{:S(2)}) %all-to-all-start) | async-done | bytes 4718624 | tf_op jit(solution)/shard_map/all_to_all | solution.py:175
  457.4 34.2 %all-to-all-start.2 = ((bf16[16,72,2048]{2,1,0:T(8,128)(2,1)}), bf16[16,72,2048]{2,1,0:T(8,128)(2,1)}, u32[]{:S(2)}, u32[]{:S(2)}) async-start(bf16[16,72,2048]{2,1,0:T(8,128)(2,1)} %multiply_convert_fusion), calls=%async_computation.2 | async-start | bytes 9437184 | tf_op jit(solution)/shard_map/all_to_all | solution.py:227
  491.7 19.5 fusion.2
  519.0 119.9 %all-to-all-done.2 = bf16[16,72,2048]{2,1,0:T(8,128)(2,1)} async-done(((bf16[16,72,2048]{2,1,0:T(8,128)(2,1)}), bf16[16,72,2048]{2,1,0:T(8,128)(2,1)}, u32[]{:S(2)}, u32[]{:S(2)}) %all-to-all-start.2) | async-done | bytes 4718624 | tf_op jit(solution)/shard_map/all_to_all | solution.py:227
  639.0 12.1 fusion.6
  651.4 18.2 fusion.14
  669.6 23.5 convert_bitcast_fusion
  693.6 10.9 fusion.44
  704.5 29.1 all-gather.19.cloned.1.call-done
  733.6 9.6 multiply_bitcast_fusion.2
  744.9 21.7 fusion.42
  766.7 22.7 bitcast_convert_fusion
  794.3 11.7 convolution_convert_fusion.1
  806.0 122.8 %all-to-all-done.3 = bf16[16,72,2048]{2,1,0:T(8,128)(2,1)} async-done(((bf16[16,72,2048]{2,1,0:T(8,128)(2,1)}), bf16[16,72,2048]{2,1,0:T(8,128)(2,1)}, u32[]{:S(2)}, u32[]{:S(2)}) %all-to-all-start.3) | async-done | bytes 4718624 | tf_op jit(solution)/shard_map/all_to_all | solution.py:242
  928.8 40.8 %all-to-all-start.1 = ((bf16[16,72,2048]{2,1,0:T(8,128)(2,1)}), bf16[16,72,2048]{2,1,0:T(8,128)(2,1)}, u32[]{:S(2)}, u32[]{:S(2)}) async-start(bf16[16,72,2048]{2,1,0:T(8,128)(2,1)} %bitcast.164), calls=%async_computation.1 | async-start | bytes 9437184 | tf_op jit(solution)/shard_map/all_to_all | solution.py:186
  969.8 9.3 gather_fusion.3
  979.1 115.5 %all-to-all-done.1 = bf16[16,72,2048]{2,1,0:T(8,128)(2,1)} async-done(((bf16[16,72,2048]{2,1,0:T(8,128)(2,1)}), bf16[16,72,2048]{2,1,0:T(8,128)(2,1)}, u32[]{:S(2)}, u32[]{:S(2)}) %all-to-all-start.1) | async-done | bytes 4718624 | tf_op jit(solution)/shard_map/all_to_all | solution.py:186
  1094.6 10.0 gather_fusion.2
  1104.7 7.3 select_convert_fusion
  1112.0 7.9 reshape.396
  1119.9 7.2 reduce_sum.195
  1127.1 13.8 multiply_reduce_fusion.1
  1143.5 6.4 convolution_convert_fusion.3
  1166.3 10.4 fusion.93
  1177.9 9.2 fusion.53
  1187.6 12.2 fusion.103
  1199.8 7.9 reshape.395
  1207.7 7.5 multiply_reduce_fusion
  1215.3 9.0 fusion.102
  1226.4 99.8 %all-reduce.10 = (f32[2048]{0:T(1024)S(1)}, f32[512]{0:T(512)S(1)}, f32[2048]{0:T(1024)S(1)}) all-reduce(f32[2048]{0:T(1024)S(1)} %get-tuple-element.68, f32[512]{0:T(512)S(1)} %get-tuple-element.70, f32[2048]{0:T(1024)S(1)} %get-tuple-element.66), channel_id=2, replica_groups=mesh['dp'=2,'expert'=16] {'dp','expert'}, use_global_device_ids=true, to_apply=%region_22.24.clone | all-reduce | flops 4608 | bytes 36864
  1330.4 7.0 fusion.23
  1337.4 5.2 convert_element_type.185
  1342.6 12.6 copy.114
  1355.3 504.5 %reduce-scatter.17.cloned.1.call-done = f32[64,2,2816]{2,0,1:T(8,128)} async-done(((f32[2048,2,2816]{2,0,1:T(8,128)}), f32[64,2,2816]{2,0,1:T(8,128)}) %reduce-scatter.17.cloned.1.call-update) | async-done | bytes 1441808 | tf_op jit(solution)/shard_map/reduce_scatter | solution.py:272
  1863.3 157.6 %reduce-scatter.11.cloned.1.call-done = f32[64,576]{1,0:T(8,128)} async-done(((f32[2048,576]{1,0:T(8,128)}), f32[64,576]{1,0:T(8,128)}) %reduce-scatter.11.cloned.1.call-update) | async-done | bytes 147472 | tf_op jit(solution)/shard_map/reduce_scatter | solution.py:325
  2020.9 184.9 %reduce-scatter.13.cloned.1.call-done = f32[16,4096]{1,0:T(8,128)} async-done(((f32[512,4096]{1,0:T(8,128)}), f32[16,4096]{1,0:T(8,128)}) %reduce-scatter.13.cloned.1.call-update) | async-done | bytes 262160 | tf_op jit(solution)/shard_map/reduce_scatter | solution.py:326
  2205.8 252.9 %reduce-scatter.9.cloned.1.call-done = f32[64,3072]{1,0:T(8,128)} async-done(((f32[2048,3072]{1,0:T(8,128)}), f32[64,3072]{1,0:T(8,128)}) %reduce-scatter.9.cloned.1.call-update) | async-done | bytes 786448 | tf_op jit(solution)/shard_map/reduce_scatter | solution.py:324
  2458.7 360.1 %reduce-scatter.15.cloned.1.call-done = f32[64,2048]{1,0:T(8,128)} async-done(((f32[2048,2048]{1,0:T(8,128)}), f32[64,2048]{1,0:T(8,128)}) %reduce-scatter.15.cloned.1.call-update) | async-done | bytes 524304 | tf_op jit(solution)/shard_map/reduce_scatter | solution.py:327
  2818.8 493.1 %reduce-scatter.19.cloned.1.call-done = f32[88,2048]{1,0:T(8,128)} async-done(((f32[2816,2048]{1,0:T(8,128)}), f32[88,2048]{1,0:T(8,128)}) %reduce-scatter.19.cloned.1.call-update) | async-done | bytes 720912 | tf_op jit(solution)/shard_map/reduce_scatter | solution.py:273
  (277 shorter events, 87.7 us)
Async XLA Ops:
  7.2 64.4 %all-gather.9.cloned.1.call-start = ((), (), s32[]{:S(2)}) async-start(), calls=%async_computation.12 | async-start | bytes 2703360 | tf_op jit(solution)/shard_map/all_gather | solution.py:94
  7.9 127.5 %all-gather.11.cloned.1.call-start = ((), (), s32[]{:S(2)}) async-start(), calls=%async_computation.13 | async-start | bytes 4325376 | tf_op jit(solution)/shard_map/all_gather | solution.py:95
  8.7 224.2 %all-gather.13.cloned.1.call-start = ((), (), s32[]{:S(2)}) async-start(), calls=%async_computation.14 | async-start | bytes 12976128 | tf_op jit(solution)/shard_map/all_gather | solution.py:93
  9.4 302.0 %all-gather.15.cloned.1.call-start = ((), (), s32[]{:S(2)}) async-start(), calls=%async_computation.15 | async-start | bytes 8650752 | tf_op jit(solution)/shard_map/all_gather | solution.py:96
  10.0 481.7 %all-gather.21.cloned.1.call-start = ((), (), s32[]{:S(2)}) async-start(), calls=%async_computation.18 | async-start | bytes 17301504 | tf_op jit(solution)/shard_map/all_gather | solution.py:112
  15.9 50.0 %copy-start = (bf16[128,2048]{1,0:T(8,128)(2,1)S(1)}, bf16[128,2048]{1,0:T(8,128)(2,1)}, u32[]{:S(2)}) copy-start(bf16[128,2048]{1,0:T(8,128)(2,1)} %param.18) | copy-start | bytes 1572868
  16.0 50.7 %copy-start.70 = (s32[1,2]{1,0:T(1,128)S(1)}, s32[1,2]{1,0:T(1,128)}, u32[]{:S(2)}) copy-start(s32[1,2]{1,0:T(1,128)} %param.32) | copy-start | bytes 28
  16.0 635.4 %all-gather.23.cloned.1.call-start = ((), (), s32[]{:S(2)}) async-start(), calls=%async_computation.19 | async-start | bytes 8650752 | tf_op jit(solution)/shard_map/all_gather | solution.py:113
  16.5 677.0 %all-gather.17.cloned.1.call-start = ((), (), s32[]{:S(2)}) async-start(), calls=%async_computation.16 | async-start | bytes 23789568 | tf_op jit(solution)/shard_map/all_gather | solution.py:97
  18.0 715.6 %all-gather.19.cloned.1.call-start = ((), (), s32[]{:S(2)}) async-start(), calls=%async_computation.17 | async-start | bytes 11894784 | tf_op jit(solution)/shard_map/all_gather | solution.py:98
  18.7 56.0 %copy-start.55 = (f32[32]{0:T(128)}, f32[32]{0:T(128)S(1)}, u32[]{:S(2)}) copy-start(f32[32]{0:T(128)S(1)} %multiply_power_fusion) | copy-start | bytes 388
  21.9 318.8 %copy-start.45 = (s32[768]{0:T(1024)}, s32[768]{0:T(1024)S(1)}, u32[]{:S(2)}) copy-start(s32[768]{0:T(1024)S(1)} %get-tuple-element.81) | copy-start | bytes 9220
  65.9 167.0 %copy-start.29 = (f32[2048]{0:T(1024)}, f32[2048]{0:T(1024)S(1)}, u32[]{:S(2)}) copy-start(f32[2048]{0:T(1024)S(1)} %convert_element_type.145) | copy-start | bytes 24580
  66.6 166.3 %copy-start.47 = (f32[128]{0:T(128)}, f32[128]{0:T(128)S(1)}, u32[]{:S(2)}) copy-start(f32[128]{0:T(128)S(1)} %fusion.79) | copy-start | bytes 1540
  66.6 72.5 %copy-start.43 = (f32[512]{0:T(512)}, f32[512]{0:T(512)S(1)}, u32[]{:S(2)}) copy-start(f32[512]{0:T(512)S(1)} %convert_element_type.147) | copy-start | bytes 6148
  67.0 249.2 %copy-start.37 = (f32[2048]{0:T(1024)}, f32[2048]{0:T(1024)S(1)}, u32[]{:S(2)}) copy-start(f32[2048]{0:T(1024)S(1)} %convert_element_type.155) | copy-start | bytes 24580
  67.3 173.8 %copy-start.35 = (f32[128,32]{0,1:T(8,128)}, f32[128,32]{0,1:T(8,128)S(1)}, u32[]{:S(2)}) copy-start(f32[128,32]{0,1:T(8,128)S(1)} %get-tuple-element.98) | copy-start | bytes 49156
  74.4 166.5 %copy-start.10 = (f32[128,576]{0,1:T(8,128)}, f32[128,576]{0,1:T(8,128)S(1)}, u32[]{:S(2)}) copy-start(f32[128,576]{0,1:T(8,128)S(1)} %fusion.97) | copy-start | bytes 884740
  74.7 166.3 %copy-start.53 = (f32[128]{0:T(128)}, f32[128]{0:T(128)S(1)}, u32[]{:S(2)}) copy-start(f32[128]{0:T(128)S(1)} %fusion.80) | copy-start | bytes 1540
  139.1 103.1 %copy-start.20 = (bf16[128,4096]{0,1:T(8,128)(2,1)}, bf16[128,4096]{0,1:T(8,128)(2,1)S(1)}, u32[]{:S(2)}) copy-start(bf16[128,4096]{0,1:T(8,128)(2,1)S(1)} %copy.124) | copy-start | bytes 3145732
  139.2 102.1 %copy-start.22 = (bf16[128,16,128]{0,2,1:T(8,128)(2,1)}, bf16[128,16,128]{0,2,1:T(8,128)(2,1)S(1)}, u32[]{:S(2)}) copy-start(bf16[128,16,128]{0,2,1:T(8,128)(2,1)S(1)} %slice.115) | copy-start | bytes 1572868
  241.8 74.4 %copy-start.49 = (f32[16,128]{1,0:T(8,128)}, f32[16,128]{1,0:T(8,128)S(1)}, u32[]{:S(2)}) copy-start(f32[16,128]{1,0:T(8,128)S(1)} %get-tuple-element.100) | copy-start | bytes 24580
  242.8 73.4 %copy-start.51 = (f32[16,128]{1,0:T(8,128)}, f32[16,128]{1,0:T(8,128)S(1)}, u32[]{:S(2)}) copy-start(f32[16,128]{1,0:T(8,128)S(1)} %fusion.39) | copy-start | bytes 24580
  243.1 73.1 %copy-start.18 = (bf16[16,128,128]{2,1,0:T(8,128)(2,1)}, bf16[16,128,128]{2,1,0:T(8,128)(2,1)S(1)}, u32[]{:S(2)}) copy-start(bf16[16,128,128]{2,1,0:T(8,128)(2,1)S(1)} %convolution_convert_fusion.5) | copy-start | bytes 1572868
  328.3 129.1 %all-to-all-start = ((bf16[16,72,2048]{2,1,0:T(8,128)(2,1)}), bf16[16,72,2048]{2,1,0:T(8,128)(2,1)}, u32[]{:S(2)}, u32[]{:S(2)}) async-start(bf16[16,72,2048]{2,1,0:T(8,128)(2,1)} %select_select_fusion), calls=%async_computation | async-start | bytes 9437184 | tf_op jit(solution)/shard_map/all_to_all | solution.py:175
  340.5 8.3 copy-start.31
  457.4 181.6 %all-to-all-start.2 = ((bf16[16,72,2048]{2,1,0:T(8,128)(2,1)}), bf16[16,72,2048]{2,1,0:T(8,128)(2,1)}, u32[]{:S(2)}, u32[]{:S(2)}) async-start(bf16[16,72,2048]{2,1,0:T(8,128)(2,1)} %multiply_convert_fusion), calls=%async_computation.2 | async-start | bytes 9437184 | tf_op jit(solution)/shard_map/all_to_all | solution.py:227
  491.6 845.8 %reduce-scatter.23.cloned.1.call-start = ((), (), s32[]{:S(2)}) async-start(), calls=%async_computation.27 | async-start | bytes 8650752 | tf_op jit(solution)/shard_map/reduce_scatter | solution.py:257
  651.1 691.5 %reduce-scatter.21.cloned.1.call-start = ((), (), s32[]{:S(2)}) async-start(), calls=%async_computation.26 | async-start | bytes 17301504 | tf_op jit(solution)/shard_map/reduce_scatter | solution.py:254
  693.1 1166.6 %reduce-scatter.17.cloned.1.call-start = ((), (), s32[]{:S(2)}) async-start(), calls=%async_computation.24 | async-start | bytes 47579136 | tf_op jit(solution)/shard_map/reduce_scatter | solution.py:272
  789.3 139.5 %all-to-all-start.3 = ((bf16[16,72,2048]{2,1,0:T(8,128)(2,1)}), bf16[16,72,2048]{2,1,0:T(8,128)(2,1)}, u32[]{:S(2)}, u32[]{:S(2)}) async-start(bf16[16,72,2048]{2,1,0:T(8,128)(2,1)} %bitcast.165), calls=%async_computation.3 | async-start | bytes 9437184 | tf_op jit(solution)/shard_map/all_to_all | solution.py:242
  928.8 40.9 %copy-start.46 = (s32[768]{0:T(1024)S(1)}, s32[768]{0:T(1024)}, u32[]{:S(2)}) copy-start(s32[768]{0:T(1024)} %copy-done.45) | copy-start | bytes 9220
  928.8 40.9 %copy-start.50 = (f32[16,128]{1,0:T(8,128)S(1)}, f32[16,128]{1,0:T(8,128)}, u32[]{:S(2)}) copy-start(f32[16,128]{1,0:T(8,128)} %copy-done.49) | copy-start | bytes 24580
  928.8 40.9 %copy-start.52 = (f32[16,128]{1,0:T(8,128)S(1)}, f32[16,128]{1,0:T(8,128)}, u32[]{:S(2)}) copy-start(f32[16,128]{1,0:T(8,128)} %copy-done.51) | copy-start | bytes 24580
  928.8 165.8 %all-to-all-start.1 = ((bf16[16,72,2048]{2,1,0:T(8,128)(2,1)}), bf16[16,72,2048]{2,1,0:T(8,128)(2,1)}, u32[]{:S(2)}, u32[]{:S(2)}) async-start(bf16[16,72,2048]{2,1,0:T(8,128)(2,1)} %bitcast.164), calls=%async_computation.1 | async-start | bytes 9437184 | tf_op jit(solution)/shard_map/all_to_all | solution.py:186
  969.6 1051.3 %reduce-scatter.11.cloned.1.call-start = ((), (), s32[]{:S(2)}) async-start(), calls=%async_computation.21 | async-start | bytes 5406720 | tf_op jit(solution)/shard_map/reduce_scatter | solution.py:325
  1094.6 10.0 copy-start.61
  1127.1 13.8 copy-start.65
  1127.1 13.8 copy-start.16
  1159.9 1045.9 %reduce-scatter.13.cloned.1.call-start = ((), (), s32[]{:S(2)}) async-start(), calls=%async_computation.22 | async-start | bytes 8650752 | tf_op jit(solution)/shard_map/reduce_scatter | solution.py:326
  1164.6 1294.1 %reduce-scatter.9.cloned.1.call-start = ((), (), s32[]{:S(2)}) async-start(), calls=%async_computation.20 | async-start | bytes 25952256 | tf_op jit(solution)/shard_map/reduce_scatter | solution.py:324
  1176.7 1642.0 %reduce-scatter.15.cloned.1.call-start = ((), (), s32[]{:S(2)}) async-start(), calls=%async_computation.23 | async-start | bytes 17301504 | tf_op jit(solution)/shard_map/reduce_scatter | solution.py:327
  1187.1 2124.7 %reduce-scatter.19.cloned.1.call-start = ((), (), s32[]{:S(2)}) async-start(), calls=%async_computation.25 | async-start | bytes 23789568 | tf_op jit(solution)/shard_map/reduce_scatter | solution.py:273
  1199.8 7.9 copy-start.32
  1215.3 9.1 copy-start.9
  1215.3 9.1 copy-start.25
  1224.3 103.7 %copy-start.67 = (f32[128]{0:T(128)S(1)}, f32[128]{0:T(128)}, u32[]{:S(2)}) copy-start(f32[128]{0:T(128)} %copy-done.66) | copy-start | bytes 1540
  1224.3 106.1 %copy-start.17 = (bf16[128,2816]{1,0:T(8,128)(2,1)S(1)}, bf16[128,2816]{1,0:T(8,128)(2,1)}, u32[]{:S(2)}) copy-start(bf16[128,2816]{1,0:T(8,128)(2,1)} %get-tuple-element.86) | copy-start | bytes 2162692
  (46 other events, 154.9 us)
Sparse Core Ops, SparseCore 0:
  10.9 60.6 all-gather.8
  74.5 60.8 all-gather.10
  138.3 94.5 all-gather.12
  235.6 75.7 all-gather.14
  313.4 21.5 all-gather.20
  336.4 17.1 all-gather.22
  357.0 281.8 all-gather.16
  641.8 91.7 all-gather.18
  736.5 12.2 reduce-scatter.22
  751.5 21.4 reduce-scatter.20
  775.4 1084.2 reduce-scatter.16
  1862.6 158.2 reduce-scatter.10
  2023.9 181.8 reduce-scatter.12
  2213.8 244.8 reduce-scatter.8
  2461.4 357.3 reduce-scatter.14
  2821.5 490.3 reduce-scatter.18
where the time goes:
time: 3330 us; the launch traced here: 3320 us
  waiting for transfers between devices  2680 us (80%)
  matrix products  251 us (8%)
  blocking collectives  142 us (4%)
  local copies, waits for them, and re-layouts  90.2 us (3%)
  starting transfers between devices  86.9 us (3%)
  other arithmetic  53 us (2%)
    reduce_scatter x1, waiting for transfers between devices, shards(): lax.psum_scatter(grad_spair, ('dp', 'expert'), scatter_dimension=0, tiled...  504 us
    reduce_scatter x1, waiting for transfers between devices, shards(): lax.psum_scatter(grad_sdown, ('dp', 'expert'), scatter_dimension=0, tiled...  493 us
    reduce_scatter x1, waiting for transfers between devices, shards(): lax.psum_scatter(grad_outw, ('dp', 'expert'), scatter_dimension=0, tiled=...  360 us
    reduce_scatter x1, waiting for transfers between devices, shards(): lax.psum_scatter(grad_qw, ('dp', 'expert'), scatter_dimension=0, tiled=True)  253 us
    reduce_scatter x1, waiting for transfers between devices, shards(): lax.psum_scatter(grad_kvup, ('dp', 'expert'), scatter_dimension=0, tiled=...  185 us
    reduce_scatter x1, waiting for transfers between devices, shards(): lax.psum_scatter(grad_kvdown, ('dp', 'expert'), scatter_dimension=0, tile...  158 us
    unnamed x2, blocking collectives  142 us
    all_to_all x1, waiting for transfers between devices, shards(): lax.all_to_all(d_rows.reshape(expert_count, capacity, model_width), 'expe...  123 us
  transfers between devices with their start and end apart: 20, of which 15 were waited for; matrix products, arithmetic and copies ran while one was open for 11% of the time, Pallas kernels for 0%

commit v1 on v0

v1 whole, which is shorter than its diff:
```python
import jax
import jax.numpy as jnp
from jax import lax
from jax.sharding import PartitionSpec as P

H = 16
DH = 128
DR = 64
DV = 128
KVR = 512
TOP = 6
SPLIT = ("dp", "expert")

f32 = jnp.float32
bf16 = jnp.bfloat16

norm_eps = 1e-06
rope_base = 50000.0
masked_score = -1e30


def norm_apply(values, scales):
    return values * lax.rsqrt(jnp.mean(values * values, axis=-1, keepdims=True) + norm_eps) * scales


def norm_back(values, scales, upstream):
    unused, pullback = jax.vjp(norm_apply, values, scales.astype(f32))
    return pullback(upstream)


def rotate(values, cosine_table, sine_table):
    half_width = values.shape[-1] // 2
    front_half = values[..., :half_width]
    back_half = values[..., half_width:]
    return jnp.concatenate(
        [
            front_half * cosine_table - back_half * sine_table,
            front_half * sine_table + back_half * cosine_table,
        ],
        axis=-1,
    )


def swish_gate(gate_part, up_part):
    return gate_part * jax.nn.sigmoid(gate_part) * up_part


def swish_back(gate_part, up_part, upstream):
    unused, pullback = jax.vjp(swish_gate, gate_part, up_part)
    return jnp.concatenate(pullback(upstream), axis=-1)


def layout(lengths_row, row_count):
    doc_ends = jnp.cumsum(lengths_row)
    places = jnp.arange(row_count, dtype=jnp.int32)
    passed_end = (places[:, None] >= doc_ends[None, :]).astype(jnp.int32)
    doc_ids = jnp.sum(passed_end, axis=1)
    starts = jnp.sum(passed_end * lengths_row[None, :], axis=1)
    return (doc_ids, places - starts)


def angles(offsets, rope_width):
    frequency = rope_base ** (-2.0 * jnp.arange(rope_width // 2, dtype=f32) / rope_width)
    turned = offsets.astype(f32)[..., None] * frequency
    return (jnp.cos(turned), jnp.sin(turned))


def dot(left, right):
    return jnp.dot(left, right, preferred_element_type=f32)


def pick(values, place, axis):
    return lax.dynamic_index_in_dim(values, place, axis, keepdims=False)


def dp_gather(values):
    if lax.axis_size("dp") != 2:
        return lax.all_gather(values, "dp")
    other = lax.ppermute(values, "dp", [(0, 1), (1, 0)])
    first = lax.axis_index("dp") == 0
    return jnp.stack([jnp.where(first, values, other), jnp.where(first, other, values)])


def dp_swap(values):
    if lax.axis_size("dp") != 2:
        return lax.all_to_all(values, "dp", split_axis=0, concat_axis=0)
    core = lax.axis_index("dp")
    own = pick(values, core, 0)
    other = lax.ppermute(pick(values, 1 - core, 0), "dp", [(0, 1), (1, 0)])
    first = core == 0
    return jnp.stack([jnp.where(first, own, other), jnp.where(first, other, own)])


def dp_scatter(values, sent=f32):
    if lax.axis_size("dp") != 2:
        return lax.psum_scatter(values.astype(sent), "dp", scatter_dimension=0).astype(f32)
    core = lax.axis_index("dp")
    other = lax.ppermute(pick(values, 1 - core, 0).astype(sent), "dp", [(0, 1), (1, 0)])
    return pick(values, core, 0).astype(f32) + other.astype(f32)


def dp_sum(values):
    if lax.axis_size("dp") != 2:
        return lax.psum(values, "dp")
    return values + lax.ppermute(values, "dp", [(0, 1), (1, 0)])


def bits_of(count):
    return [1 << place for place in reversed(range(count.bit_length() - 1))]


def partner(values, bit):
    count = lax.axis_size("expert")
    return lax.ppermute(values, "expert", [(i, i ^ bit) for i in range(count)])


def gather(values, order):
    me = lax.axis_index("expert")
    held = []
    for bit in order:
        other = partner(values, bit)
        low = (me & bit) == 0
        values = jnp.stack(
            [jnp.where(low, values, other), jnp.where(low, other, values)],
            axis=sum(1 for known in held if known > bit),
        )
        held.append(bit)
    return values.reshape((-1,) + values.shape[len(held) :])


def scatter(values, order, kept=f32):
    me = lax.axis_index("expert")
    bits = bits_of(lax.axis_size("expert"))
    values = values.reshape((2,) * len(bits) + values.shape[1:])
    for step, bit in enumerate(order):
        axis = bits.index(bit)
        bits = [known for known in bits if known != bit]
        place = ((me & bit) != 0).astype(jnp.int32)
        other = partner(pick(values, 1 - place, axis), bit)
        values = pick(values, place, axis).astype(f32) + other.astype(f32)
        values = values.astype(bf16 if bits else kept)
    return values


def gather_near(values, order):
    held = []
    for bit in order:
        other = partner(values, bit)
        values = jnp.stack([values, other], axis=sum(1 for known in held if known > bit))
        held.append(bit)
    return values.reshape((-1,) + values.shape[len(held) :])


def scatter_near(values, order, kept=f32):
    bits = bits_of(lax.axis_size("expert"))
    values = values.reshape((2,) * len(bits) + values.shape[1:])
    for step, bit in enumerate(order):
        axis = bits.index(bit)
        bits = [known for known in bits if known != bit]
        other = partner(lax.index_in_dim(values, 1, axis, keepdims=False), bit)
        values = lax.index_in_dim(values, 0, axis, keepdims=False).astype(f32) + other.astype(f32)
        values = values.astype(bf16 if bits else kept)
    return values


def orders():
    bits = bits_of(lax.axis_size("expert"))
    return bits, bits[:-2] + bits[-1:] + bits[-2:-1]


def gather_both(values, how):
    first, second = orders()
    middle = values.shape[-1] // 2
    return how(values[..., :middle], first), how(values[..., middle:], second)


def scatter_both(left, right, how):
    first, second = orders()
    return jnp.concatenate([how(left, first[::-1]), how(right, second[::-1])], axis=-1)


def shards(
    tokens,
    attn_gain,
    kv_gain,
    ffn_gain,
    q_weight,
    kv_down_weight,
    kv_up_weight,
    out_weight,
    shared_gate_up,
    shared_down,
    expert_gate_up,
    expert_down,
    routes,
    gates,
    lengths,
    out_grad,
):
    row_count, width = tokens.shape
    dp_count = lax.axis_size("dp")
    expert_count = lax.axis_size("expert")
    core = lax.axis_index("dp")
    me = lax.axis_index("expert")
    heads = H // dp_count
    scale_factor = (DH + DR) ** (-0.5)
    first_order, second_order = orders()
    chip_rows = dp_count * row_count
    slice_rows = kv_down_weight.shape[0]
    joint_width = KVR + DR

    combined = jnp.sum(
        jnp.where(
            routes[:, :, None] == jnp.arange(expert_count, dtype=jnp.int32),
            gates[:, :, None],
            0.0,
        ),
        axis=1,
    )
    gates_high = lax.reduce_precision(combined, 8, 7)
    gates_low = (combined - gates_high).astype(bf16)
    gates_flat = jnp.stack([gates_high.astype(bf16), gates_low]).reshape(-1)
    gate_rows = -(-gates_flat.shape[0] // joint_width)
    gates_flat = jnp.pad(gates_flat, (0, gate_rows * joint_width - gates_flat.shape[0]))
    gains = jnp.concatenate([attn_gain, ffn_gain, kv_gain])
    n_gain, n_kv_gain = attn_gain.shape[0], kv_gain.shape[0]
    gains = jnp.pad(gains, (0, joint_width - gains.shape[0]))
    small = jnp.concatenate(
        [kv_down_weight, gains[None], gates_flat.reshape(gate_rows, joint_width)], axis=0
    )
    small_all = gather(small, second_order)
    gates_all = small_all[:, slice_rows + 1 :].reshape(expert_count, -1)
    gates_all = gates_all[:, : 2 * row_count * expert_count]
    gates_all = gates_all.reshape(expert_count, 2, row_count, expert_count)
    near = me ^ jnp.arange(expert_count, dtype=jnp.int32)
    own_gate = jnp.take(pick(gates_all, me, 3).astype(f32).sum(axis=1), near, axis=0)

    joint_all = dp_gather(small_all[:, : slice_rows + 1])
    kv_down = joint_all[:, :, :slice_rows].reshape(width, joint_width)
    gains_all = joint_all[:, :, slice_rows]
    attn_scale = gains_all[..., :n_gain].reshape(-1)
    ffn_scale = gains_all[..., n_gain : 2 * n_gain].reshape(-1)
    kv_scale = gains_all[..., 2 * n_gain : 2 * n_gain + n_kv_gain].reshape(-1)

    q_own = dp_swap(q_weight.reshape(slice_rows, dp_count, -1).transpose(1, 0, 2))
    q_left, q_right = gather_both(q_own, gather)
    q_full = jnp.concatenate([q_left, q_right], axis=-1).transpose(1, 0, 2, 3)
    q_full = q_full.reshape(width, heads * (DH + DR))
    up_own = dp_swap(kv_up_weight.reshape(n_kv_gain, dp_count, -1).transpose(1, 0, 2))
    kv_up = gather(up_own, first_order).transpose(1, 0, 2, 3).reshape(KVR, heads * (DH + DV))
    out_left, out_right = gather_both(out_weight, gather)
    out_full = jnp.concatenate([out_left, out_right], axis=-1).reshape(heads * DV, width)

    pair_w = dp_gather(expert_gate_up[0].reshape(width // dp_count, -1)).reshape(width, -1)
    down_w = dp_gather(expert_down[0]).reshape(-1, width)
    hidden = down_w.shape[0]

    share = shared_down.shape[0]
    units = dp_count * share
    padded = -(-units // 128) * 128
    shared_w = shared_gate_up.reshape(slice_rows, 2, dp_count, expert_count, share)
    shared_w = shared_w.transpose(3, 0, 1, 2, 4).reshape(expert_count, slice_rows, 2 * units)
    shared_w = lax.all_to_all(shared_w, "expert", split_axis=0, concat_axis=0, tiled=True)
    shared_w = dp_gather(shared_w).reshape(width, 2, units)
    shared_w = jnp.pad(shared_w, ((0, 0), (0, 0), (0, padded - units))).reshape(width, 2 * padded)
    shared_out = dp_gather(shared_down).reshape(units, width)
    shared_out = jnp.pad(shared_out, ((0, padded - units), (0, 0)))

    resid_in = tokens.astype(f32)
    chip_in = dp_gather(tokens).reshape(chip_rows, width).astype(f32)
    normed = norm_apply(chip_in, attn_scale).astype(bf16)
    kv_joint = dot(normed, kv_down)
    latent = kv_joint[:, :KVR]
    kv_normed = norm_apply(latent, kv_scale).astype(bf16)
    q_heads = dot(normed, q_full).reshape(dp_count, row_count, heads, DH + DR)
    kv_heads = dot(kv_normed, kv_up).reshape(dp_count, row_count, heads, DH + DV)
    doc_ids, offsets = jax.vmap(lambda row: layout(row, row_count))(
        dp_gather(lengths).reshape(dp_count, -1)
    )
    cosine_table, sine_table = angles(offsets, DR)
    cosine_heads, sine_heads = cosine_table[:, :, None], sine_table[:, :, None]
    queries = jnp.concatenate(
        [q_heads[..., :DH], rotate(q_heads[..., DH:], cosine_heads, sine_heads)], axis=-1
    ).astype(bf16)
    rope_key = rotate(
        kv_joint[:, KVR:].reshape(dp_count, row_count, DR), cosine_table, sine_table
    )
    key_heads = jnp.concatenate(
        [
            kv_heads[..., :DH],
            jnp.broadcast_to(rope_key[:, :, None, :], (dp_count, row_count, heads, DR)),
        ],
        axis=-1,
    ).astype(bf16)
    values = kv_heads[..., DH:].astype(bf16)
    places = jnp.arange(row_count, dtype=jnp.int32)
    allowed = (doc_ids[:, :, None] == doc_ids[:, None, :]) & (places[:, None] >= places[None, :])
    scores = (
        jnp.einsum("bthd,bshd->bhts", queries, key_heads, preferred_element_type=f32)
        * scale_factor
    )
    scores = jnp.where(allowed[:, None], scores, masked_score)
    highest = jnp.max(scores, axis=-1, keepdims=True)
    weights = jnp.exp(scores - highest)
    probs = weights / jnp.sum(weights, axis=-1, keepdims=True)
    probs_low = probs.astype(bf16)
    attended = (
        jnp.einsum("bhts,bshd->bthd", probs_low, values, preferred_element_type=f32)
        .reshape(chip_rows, heads * DV)
        .astype(bf16)
    )
    resid = resid_in + dp_scatter(dot(attended, out_full).reshape(dp_count, row_count, width))
    ffn_in = norm_apply(resid, ffn_scale).astype(bf16)

    capacity = min(row_count, 3 * row_count * TOP // (2 * expert_count))
    slots = expert_count * capacity
    group_rows = expert_count * row_count
    live = own_gate > 0.0
    place = jnp.cumsum(live.astype(jnp.int32), axis=1) - 1
    chosen = (jnp.arange(capacity, dtype=jnp.int32)[None, :, None] == place[:, None, :]) & live[
        :, None, :
    ]
    slot_gate = jnp.sum(jnp.where(chosen, own_gate[:, None, :], 0.0), axis=2).reshape(slots, 1)
    chosen = chosen.astype(bf16)

    upstream = out_grad.astype(f32)
    grad_all = jnp.concatenate(gather_both(out_grad, gather_near), axis=-1)
    slot_grad = (
        jnp.einsum("rst,rtd->rsd", chosen, grad_all, preferred_element_type=f32).reshape(slots, width)
        * slot_gate
    ).astype(bf16)
    grad_rows = grad_all.reshape(group_rows, width)
    d_hidden = dot(slot_grad, down_w.T)
    d_shared_hidden = dot(grad_rows, shared_out.T)

    ffn_all = jnp.concatenate(gather_both(ffn_in, gather_near), axis=-1)
    ffn_rows = ffn_all.reshape(group_rows, width)
    rows = jnp.einsum("rst,rtd->rsd", chosen, ffn_all, preferred_element_type=f32)
    rows = rows.reshape(slots, width).astype(bf16)
    pair = dot(rows, pair_w)
    gate_part, up_part = pair[:, :hidden], pair[:, hidden:]
    expert_hidden = swish_gate(gate_part, up_part).astype(bf16)
    d_pair = swish_back(gate_part, up_part, d_hidden).astype(bf16)
    shared_pair = dot(ffn_rows, shared_w)
    shared_gate, shared_up = shared_pair[:, :padded], shared_pair[:, padded:]
    shared_hidden = swish_gate(shared_gate, shared_up).astype(bf16)
    d_shared_pair = swish_back(shared_gate, shared_up, d_shared_hidden).astype(bf16)

    middle = width // 2

    def to_tokens(slot_rows, shared_rows, shared_matrix):
        back = jnp.einsum(
            "rst,rsd->rtd",
            chosen,
            slot_rows.reshape(expert_count, capacity, -1),
            preferred_element_type=f32,
        )
        back = back.reshape(group_rows, -1) + dot(shared_rows, shared_matrix)
        return back.astype(bf16).reshape(expert_count, row_count, -1)

    d_parts = [
        to_tokens(dot(d_pair, part.T).astype(bf16), d_shared_pair, shared_part.T)
        for part, shared_part in (
            (pair_w[:middle], shared_w[:middle]),
            (pair_w[middle:], shared_w[middle:]),
        )
    ]
    d_ffn_in = scatter_both(d_parts[0], d_parts[1], scatter_near)

    out_parts = [
        to_tokens(
            (dot(expert_hidden, part) * slot_gate).astype(bf16), shared_hidden, shared_part
        )
        for part, shared_part in (
            (down_w[:, :middle], shared_out[:, :middle]),
            (down_w[:, middle:], shared_out[:, middle:]),
        )
    ]
    output = (resid + scatter_both(out_parts[0], out_parts[1], scatter_near)).astype(bf16)

    grad_pair = dp_scatter(dot(rows.T, d_pair).reshape(dp_count, width // dp_count, -1), bf16)
    grad_down = dp_scatter(
        dot(expert_hidden.T, slot_grad).reshape(dp_count, hidden // dp_count, width), bf16
    )
    grad_shared_out = dp_scatter(
        dot(shared_hidden.T, grad_rows)[:units].reshape(dp_count, share, width), bf16
    )
    grad_shared = dot(ffn_rows.T, d_shared_pair).reshape(width, 2, padded)[:, :, :units]
    grad_shared = grad_shared.reshape(dp_count, expert_count, slice_rows, 2 * units)
    grad_shared = dp_scatter(grad_shared, bf16).astype(bf16)
    grad_shared = lax.all_to_all(grad_shared, "expert", split_axis=0, concat_axis=0, tiled=True)
    grad_shared = grad_shared.reshape(expert_count, slice_rows, 2, dp_count, share)
    grad_shared = grad_shared.transpose(1, 2, 3, 0, 4).reshape(shared_gate_up.shape).astype(f32)

    d_norm_resid, grad_ffn_scale = norm_back(resid, ffn_scale, d_ffn_in)
    d_resid = upstream + d_norm_resid
    d_branch = dp_gather(d_resid.astype(bf16)).reshape(chip_rows, width)
    d_attended = (
        dot(d_branch, out_full.T).astype(bf16).reshape(dp_count, row_count, heads, DV)
    )
    out_blocks = (expert_count, slice_rows, middle)
    grad_out = scatter_both(
        dot(attended.T, d_branch[:, :middle]).astype(bf16).reshape(out_blocks),
        dot(attended.T, d_branch[:, middle:]).astype(bf16).reshape(out_blocks),
        scatter,
    )
    grad_values = jnp.einsum("bhts,bthd->bshd", probs_low, d_attended, preferred_element_type=f32)
    d_probs = jnp.einsum("bthd,bshd->bhts", d_attended, values, preferred_element_type=f32)
    d_scores = (probs * (d_probs - jnp.sum(d_probs * probs, axis=-1, keepdims=True))).astype(bf16)
    d_queries = (
        jnp.einsum("bhts,bshd->bthd", d_scores, key_heads, preferred_element_type=f32)
        * scale_factor
    )
    d_keys = (
        jnp.einsum("bhts,bthd->bshd", d_scores, queries, preferred_element_type=f32)
        * scale_factor
    )
    d_q_heads = jnp.concatenate(
        [d_queries[..., :DH], rotate(d_queries[..., DH:], cosine_heads, -sine_heads)], axis=-1
    )
    d_q_heads = d_q_heads.astype(bf16).reshape(chip_rows, heads * (DH + DR))
    d_rope_key = rotate(jnp.sum(d_keys[..., DH:], axis=2), cosine_table, -sine_table)
    d_kv_heads = (
        jnp.concatenate([d_keys[..., :DH], grad_values], axis=-1)
        .astype(bf16)
        .reshape(chip_rows, heads * (DH + DV))
    )
    d_joint = dp_sum(
        jnp.concatenate([dot(d_kv_heads, kv_up.T), d_rope_key.reshape(chip_rows, DR)], axis=-1)
    )
    d_latent, grad_kv_scale = norm_back(latent, kv_scale, d_joint[:, :KVR])
    d_kv_joint = jnp.concatenate([d_latent, d_joint[:, KVR:]], axis=-1).astype(bf16)

    q_cols = heads * (DH + DR) // 2
    by_rows = (dp_count, expert_count, slice_rows)

    def q_part(part):
        found = dot(normed.T, part).astype(bf16).reshape(by_rows + (part.shape[-1],))
        return found.transpose(1, 0, 2, 3)

    grad_q = scatter_both(q_part(d_q_heads[:, :q_cols]), q_part(d_q_heads[:, q_cols:]), scatter)
    grad_q = dp_swap(grad_q.astype(bf16)).transpose(1, 0, 2).reshape(q_weight.shape).astype(f32)
    grad_up = dot(kv_normed.T, d_kv_heads).astype(bf16)
    grad_up = grad_up.reshape(dp_count, expert_count, n_kv_gain, -1).transpose(1, 0, 2, 3)
    grad_up = scatter(grad_up, first_order[::-1])
    grad_up = dp_swap(grad_up.astype(bf16)).transpose(1, 0, 2)
    grad_up = grad_up.reshape(kv_up_weight.shape).astype(f32)

    d_normed = dp_scatter(dot(d_q_heads, q_full.T).reshape(dp_count, row_count, width))
    own_joint = pick(d_kv_joint.reshape(dp_count, row_count, joint_width), core, 0)
    d_normed = d_normed + dot(own_joint, kv_down.T)
    d_norm_in, grad_attn_scale = norm_back(resid_in, attn_scale, d_normed)
    grad_in = (d_resid + d_norm_in).astype(bf16)

    own_normed = pick(normed.reshape(chip_rows, dp_count, width // dp_count), core, 1)
    grad_kvdown = dot(own_normed.T, d_kv_joint).reshape(expert_count, slice_rows, joint_width)
    scale_sums = dp_scatter(
        jnp.concatenate(
            [
                grad_attn_scale.reshape(dp_count, expert_count, n_gain),
                grad_ffn_scale.reshape(dp_count, expert_count, n_gain),
            ],
            axis=-1,
        )
    )
    kv_sums = pick(grad_kv_scale.reshape(dp_count, expert_count, n_kv_gain), core, 0)
    scale_sums = jnp.concatenate([scale_sums, kv_sums], axis=-1)
    scale_sums = jnp.pad(scale_sums, ((0, 0), (0, joint_width - scale_sums.shape[-1])))
    small_sums = scatter(
        jnp.concatenate([grad_kvdown, scale_sums[:, None]], axis=1).astype(bf16),
        second_order[::-1],
    )
    grad_kvdown = small_sums[:slice_rows]
    scale_sums = small_sums[slice_rows]

    return (
        output,
        grad_in,
        scale_sums[:n_gain],
        scale_sums[2 * n_gain : 2 * n_gain + n_kv_gain],
        scale_sums[n_gain : 2 * n_gain],
        grad_q,
        grad_kvdown,
        grad_up,
        grad_out,
        grad_shared,
        grad_shared_out,
        grad_pair.reshape(expert_gate_up.shape),
        grad_down.reshape(expert_down.shape),
    )


def solution(mesh):
    rows = P(SPLIT, None)
    each = P(SPLIT)
    cube = P(SPLIT, None, None)
    pair = P("expert", "dp", None, None)
    down = P("expert", "dp", None)
    dense = (rows, rows, rows, rows, cube, rows)
    return jax.shard_map(
        shards,
        mesh=mesh,
        in_specs=(rows, each, each, each) + dense + (pair, down, rows, rows, rows, rows),
        out_specs=(rows, rows, each, each, each) + dense + (pair, down),
        check_vma=False,
    )
```

time: 3330 us -> 1090 us (0.33)
  waiting for transfers between devices: 2680 us -> 424 us
  blocking collectives: 142 us -> 0 us
  local copies, waits for them, and re-layouts: 90.2 us -> 207 us
  other arithmetic: 53 us -> 161 us
  matrix products: 251 us -> 177 us
    reduce_scatter x8 -> x0, waiting for transfers between devices: 1950 us -> none  [the longest x1 504 us: shards(): lax.psum_scatter(grad_spair, ('dp', 'expert'), scatter_dimension=0, tiled...]
    all_to_all x4 -> x2, waiting for transfers between devices: 467 us -> 32.4 us  [the longest x1 32.4 us: shards(): lax.all_to_all(grad_shared, 'expert', split_axis=0, concat_axis=0, tiled=...]
    ppermute x0 -> x100, waiting for transfers between devices: none -> 392 us  [the longest x80 391 us: partner(): return lax.ppermute(values, 'expert', [(i, i ^ bit) for i in range(count)])]
    all_gather x8 -> x0, waiting for transfers between devices: 256 us -> none  [the longest x1 93.7 us: shards(): lax.all_gather(q_weight, ('dp', 'expert'), axis=0, tiled=True)]
    unnamed x2 -> x0, blocking collectives: 142 us -> none
    ppermute x0 -> x100, starting transfers between devices: none -> 96.5 us  [the longest x80 61.9 us: partner(): return lax.ppermute(values, 'expert', [(i, i ^ bit) for i in range(count)])]
    another operation x8 -> x93, other arithmetic: 2.36 us -> 89.3 us  [the longest x16 30.4 us: gather_near(): jnp.stack([values, other], axis=sum((1 for known in held if known > bit)))]
    dot_general x30 -> x41, matrix products: 251 us -> 175 us  [the longest x30 154 us: dot(): return jnp.dot(left, right, preferred_element_type=f32)]
  transfers between devices with their start and end apart: 20 -> 102, of which waited for: 15 -> 45; matrix products, arithmetic and copies ran while one was open for 11% -> 41% of each run, Pallas kernels for 0% -> 0%
where the time goes in v1:
time: 1090 us; the launch traced here: 1080 us
  waiting for transfers between devices  424 us (39%)
  local copies, waits for them, and re-layouts  207 us (19%)
  matrix products  177 us (16%)
  other arithmetic  161 us (15%)
  starting transfers between devices  107 us (10%)
    ppermute x80, waiting for transfers between devices, partner(): return lax.ppermute(values, 'expert', [(i, i ^ bit) for i in range(count)])  391 us
    dot_general x30, matrix products, dot(): return jnp.dot(left, right, preferred_element_type=f32)  154 us
    ppermute x80, starting transfers between devices, partner(): return lax.ppermute(values, 'expert', [(i, i ^ bit) for i in range(count)])  61.9 us
    unnamed x393, local copies, waits for them, and re-layouts  40.3 us
    all_to_all x1, waiting for transfers between devices, shards(): lax.all_to_all(grad_shared, 'expert', split_axis=0, concat_axis=0, tiled=...  32.4 us
    another operation x16, other arithmetic, gather_near(): jnp.stack([values, other], axis=sum((1 for known in held if known > bit)))  30.4 us
    another operation x15, other arithmetic, dp_gather(): jnp.stack([jnp.where(first, values, other), jnp.where(first, other, value...  28.6 us
    another operation x47, other arithmetic, gather(): jnp.stack([jnp.where(low, values, other), jnp.where(low, other, values)],...  27.2 us
  transfers between devices with their start and end apart: 102, of which 45 were waited for; matrix products, arithmetic and copies ran while one was open for 41% of the time, Pallas kernels for 0%

profile of v1, /device:TPU:1, one launch (start us, length us, event | category | flops | bytes accessed | tf_op | source)
XLA Modules:
  0.0 1081.1 jit_solution(14685054404952593300)
XLA Ops:
  18.2 6.8 all-to-all-start
  28.3 6.3 copy.669
  40.5 21.2 %collective-permute-done.7 = bf16[2,16,2048]{2,1,0:T(8,128)(2,1)S(1)} collective-permute-done((bf16[2,16,2048]{2,1,0:T(8,128)(2,1)S(1)}, bf16[2,16,2048]{2,1,0:T(8,128)(2,1)S(1)}, u32[]{:S(2)}, u32[]{:S(2)}) %collective-permute-start.7) | collective-permute-done | bytes 131104 | tf_op jit(solution)/shard_map/ppermute | solution.py:114
  63.5 7.7 collective-permute-done.2
  89.0 5.7 collective-permute-done.22
  99.4 10.1 collective-permute-done.17
  124.9 14.8 %collective-permute-done.51 = bf16[2,128,1024]{2,1,0:T(8,128)(2,1)} collective-permute-done((bf16[2,128,1024]{2,1,0:T(8,128)(2,1)}, bf16[2,128,1024]{2,1,0:T(8,128)(2,1)}, u32[]{:S(2)}, u32[]{:S(2)}) %collective-permute-start.51) | collective-permute-done | bytes 524320 | tf_op jit(solution)/shard_map/ppermute | solution.py:114
  149.2 7.2 collective-permute-done.18
  167.2 11.0 %collective-permute-done.4 = bf16[2,2,2,73,576]{4,2,3,1,0:T(2,128)(2,1)S(1)} collective-permute-done((bf16[2,2,2,73,576]{4,2,3,1,0:T(2,128)(2,1)S(1)}, bf16[2,2,2,73,576]{4,2,3,1,0:T(2,128)(2,1)S(1)}, u32[]{:S(2)}, u32[]{:S(2)}) %collective-permute-start.4) | collective-permute-done | bytes 672800 | tf_op jit(solution)/shard_map/ppermute | solution.py:114
  198.6 18.9 %collective-permute-done.15 = bf16[2,2,2,64,768]{4,3,2,0,1:T(8,128)(2,1)} collective-permute-done((bf16[2,2,2,64,768]{4,3,2,0,1:T(8,128)(2,1)}, bf16[2,2,2,64,768]{4,3,2,0,1:T(8,128)(2,1)}, u32[]{:S(2)}, u32[]{:S(2)}) %collective-permute-start.15) | collective-permute-done | bytes 786464 | tf_op jit(solution)/shard_map/ppermute | solution.py:114
  239.3 7.7 collective-permute-start.5
  248.9 12.9 %collective-permute-done.10 = bf16[2,2,2,2,16,2048]{5,4,3,0,1,2:T(8,128)(2,1)} collective-permute-done((bf16[2,2,2,2,16,2048]{5,4,3,0,1,2:T(8,128)(2,1)}, bf16[2,2,2,2,16,2048]{5,4,3,0,1,2:T(8,128)(2,1)}, u32[]{:S(2)}, u32[]{:S(2)}) %collective-permute-start.10) | collective-permute-done | bytes 1048608 | tf_op jit(solution)/shard_map/ppermute | solution.py:114
  310.3 9.7 collective-permute-done.20
  326.2 8.7 copy.563
  366.8 14.2 %collective-permute-done.34 = bf16[128,1024]{1,0:T(8,128)(2,1)S(1)} collective-permute-done((bf16[128,1024]{1,0:T(8,128)(2,1)S(1)}, bf16[128,1024]{1,0:T(8,128)(2,1)S(1)}, u32[]{:S(2)}, u32[]{:S(2)}) %collective-permute-start.34) | collective-permute-done | bytes 262176 | tf_op jit(solution)/shard_map/ppermute | solution.py:114
  400.4 9.6 collective-permute-done.31
  418.4 5.8 collective-permute-done.36
  427.0 8.4 collective-permute-done.32
  437.9 9.4 fusion.45
  447.4 5.9 pad_maximum_fusion
  453.3 27.1 %collective-permute-done.37 = bf16[2,2,2,128,1024]{4,3,0,1,2:T(8,128)(2,1)} collective-permute-done((bf16[2,2,2,128,1024]{4,3,0,1,2:T(8,128)(2,1)}, bf16[2,2,2,128,1024]{4,3,0,1,2:T(8,128)(2,1)}, u32[]{:S(2)}, u32[]{:S(2)}) %collective-permute-start.37) | collective-permute-done | bytes 2097184 | tf_op jit(solution)/shard_map/ppermute | solution.py:114
  489.3 7.2 fusion.32
  496.5 18.2 %fusion.247 = f32[1152,2816]{1,0:T(8,128)} fusion(bf16[1152,2048]{1,0:T(8,128)(2,1)} %bitcast.843, bf16[2048,2816]{1,0:T(8,128)(2,1)S(1)} %bitcast.818), kind=kOutput, calls=%fused_computation.638 | convolution fusion | flops 13287555072 | bytes 29229056 | tf_op jit(solution)/shard_map/dot_general | solution.py:69
  514.7 16.4 %fusion.17 = (bf16[1152,1408]{1,0:T(8,128)(2,1)}, bf16[1152,1408]{1,0:T(8,128)(2,1)}, bf16[1152,1408]{1,0:T(8,128)(2,1)}) fusion(f32[1152,2816]{1,0:T(8,128)} %fusion.247, bf16[1152,2048]{1,0:T(8,128)(2,1)} %bitcast.909, bf16[1408,2048]{1,0:T(8,128)(2,1)S(1)} %bitcast.837), kind=kOutput, calls=%fused_computation.29 | convolution fusion | flops 6669729792 | bytes 33193984 | tf_op jit(solution)/shard_map/dot_general | solution.py:69
  531.0 7.2 fusion.38
  543.6 10.3 fusion.23
  579.9 6.7 copy.626
  592.2 10.6 fusion.250
  623.0 9.2 convolution_convert_fusion
  639.8 10.4 convolution_convert_fusion.1
  651.6 20.1 %fusion.18 = f32[2,1024,2816]{2,1,0:T(8,128)} fusion(bf16[2,1024,1152]{2,1,0:T(8,128)(2,1)S(1)} %bitcast.842, bf16[1152,1408]{1,0:T(8,128)(2,1)} %get-tuple-element.29, bf16[1152,1408]{1,0:T(8,128)(2,1)S(1)} %copy-done.179), kind=kOutput, calls=%fused_computation.31 | convolution fusion | flops 13300531200 | bytes 34275328 | tf_op jit(solution)/shard_map/dot_general | solution.py:69
  688.9 7.4 fusion.21
  699.4 32.4 %all-to-all-done.1 = bf16[16,64,352]{2,1,0:T(8,128)(2,1)S(1)} async-done(((bf16[16,64,352]{2,1,0:T(8,128)(2,1)}), bf16[16,64,352]{2,1,0:T(8,128)(2,1)S(1)}, u32[]{:S(2)}, u32[]{:S(2)}) %all-to-all-start.1) | async-done | bytes 720928 | tf_op jit(solution)/shard_map/all_to_all | solution.py:391
  758.9 12.4 %collective-permute-done.47 = bf16[2,2,128,1024]{3,2,0,1:T(8,128)(2,1)S(1)} collective-permute-done((bf16[2,2,128,1024]{3,2,0,1:T(8,128)(2,1)S(1)}, bf16[2,2,128,1024]{3,2,0,1:T(8,128)(2,1)S(1)}, u32[]{:S(2)}, u32[]{:S(2)}) %collective-permute-start.47) | collective-permute-done | bytes 1048608 | tf_op jit(solution)/shard_map/ppermute | solution.py:114
  776.0 17.8 %collective-permute-done.63 = bf16[2,2,128,1024]{3,2,0,1:T(8,128)(2,1)S(1)} collective-permute-done((bf16[2,2,128,1024]{3,2,0,1:T(8,128)(2,1)S(1)}, bf16[2,2,128,1024]{3,2,0,1:T(8,128)(2,1)S(1)}, u32[]{:S(2)}, u32[]{:S(2)}) %collective-permute-start.63) | collective-permute-done | bytes 1048608 | tf_op jit(solution)/shard_map/ppermute | solution.py:114
  800.2 17.5 %collective-permute-done.64 = bf16[2,128,1024]{2,1,0:T(8,128)(2,1)S(1)} collective-permute-done((bf16[2,128,1024]{2,1,0:T(8,128)(2,1)S(1)}, bf16[2,128,1024]{2,1,0:T(8,128)(2,1)S(1)}, u32[]{:S(2)}, u32[]{:S(2)}) %collective-permute-start.64) | collective-permute-done | bytes 524320 | tf_op jit(solution)/shard_map/ppermute | solution.py:114
  818.3 16.2 %collective-permute-done.60 = bf16[2,128,1024]{2,1,0:T(8,128)(2,1)S(1)} collective-permute-done((bf16[2,128,1024]{2,1,0:T(8,128)(2,1)S(1)}, bf16[2,128,1024]{2,1,0:T(8,128)(2,1)S(1)}, u32[]{:S(2)}, u32[]{:S(2)}) %collective-permute-start.60) | collective-permute-done | bytes 524320 | tf_op jit(solution)/shard_map/ppermute | solution.py:114
  837.5 16.4 %collective-permute-done.65 = bf16[128,1024]{1,0:T(8,128)(2,1)S(1)} collective-permute-done((bf16[128,1024]{1,0:T(8,128)(2,1)S(1)}, bf16[128,1024]{1,0:T(8,128)(2,1)S(1)}, u32[]{:S(2)}, u32[]{:S(2)}) %collective-permute-start.65) | collective-permute-done | bytes 262176 | tf_op jit(solution)/shard_map/ppermute | solution.py:114
  854.0 11.2 %collective-permute-done.61 = bf16[128,1024]{1,0:T(8,128)(2,1)S(1)} collective-permute-done((bf16[128,1024]{1,0:T(8,128)(2,1)S(1)}, bf16[128,1024]{1,0:T(8,128)(2,1)S(1)}, u32[]{:S(2)}, u32[]{:S(2)}) %collective-permute-start.61) | collective-permute-done | bytes 262176 | tf_op jit(solution)/shard_map/ppermute | solution.py:114
  873.0 5.6 fusion.22
  944.0 8.8 collective-permute-done.88
  959.8 11.3 %bitcast_add_fusion = f32[1024,2816]{1,0:T(8,128)} fusion(bf16[1024,2816]{1,0:T(8,128)(2,1)} %collective-permute-done.98, f32[2,1024,2816]{2,1,0:T(8,128)} %fusion.18, s32[]{:T(128)S(6)} %select_n.589), kind=kLoop, calls=%fused_computation.3 | loop fusion | flops 5767168 | bytes 28835844 | tf_op jit(solution)/shard_map/add | solution.py:99
  971.1 14.3 %reshape.754 = f32[1,1024,2,1408]{3,2,1,0:T(2,128)} reshape(f32[1024,2816]{1,0:T(8,128)} %bitcast_add_fusion) | data formatting | bytes 23068672 | tf_op jit(solution)/shard_map/reshape | solution.py:488
  987.8 10.0 collective-permute-done.93
  1011.6 5.9 collective-permute-done.90
  1017.6 12.1 %collective-permute-done.71 = bf16[2,2,65,576]{3,2,1,0:T(8,128)(2,1)S(1)} collective-permute-done((bf16[2,2,65,576]{3,2,1,0:T(8,128)(2,1)S(1)}, bf16[2,2,65,576]{3,2,1,0:T(8,128)(2,1)S(1)}, u32[]{:S(2)}, u32[]{:S(2)}) %collective-permute-start.71) | collective-permute-done | bytes 299552 | tf_op jit(solution)/shard_map/ppermute | solution.py:114
  1051.5 10.3 collective-permute-done.76
  1062.1 13.5 %collective-permute-done.77 = bf16[2,64,768]{2,1,0:T(8,128)(2,1)S(1)} collective-permute-done((bf16[2,64,768]{2,1,0:T(8,128)(2,1)S(1)}, bf16[2,64,768]{2,1,0:T(8,128)(2,1)S(1)}, u32[]{:S(2)}, u32[]{:S(2)}) %collective-permute-start.77) | collective-permute-done | bytes 196640 | tf_op jit(solution)/shard_map/ppermute | solution.py:114
  (925 shorter events, 507.6 us)
Async XLA Ops:
  0.6 33.9 %collective-permute-start.11 = (s32[1,2]{1,0:T(1,128)}, s32[1,2]{1,0:T(1,128)S(1)}, u32[]{:S(2)}, u32[]{:S(2)}) collective-permute-start(s32[1,2]{1,0:T(1,128)} %param.30), channel_id=1, source_target_pairs={{0,16},{16,0},{1,17},{17,1},{2,18},{18,2},{3,19},{19,3},{4,20},{20... | collective-permute-start | bytes 32 | tf_op jit(solution)/shard_map/ppermute | solution.py:79
  4.2 33.6 %collective-permute-start.1 = (bf16[73,576]{1,0:T(8,128)(2,1)}, bf16[73,576]{1,0:T(8,128)(2,1)S(1)}, u32[]{:S(2)}, u32[]{:S(2)}) collective-permute-start(bf16[73,576]{1,0:T(8,128)(2,1)} %pad_maximum_fusion.75), channel_id=1, source_target_pairs={{0,8},{1,9},{2,10},{3,11},{4,12},{5,13},{6,14},{7,15},{8,0},{9,1},... | collective-permute-start | bytes 252296 | tf_op jit(solution)/shard_map/ppermute | solution.py:114
  11.1 29.2 %collective-permute-start.21 = (bf16[64,1024]{1,0:T(8,128)(2,1)S(1)}, bf16[64,1024]{1,0:T(8,128)(2,1)S(1)}, u32[]{:S(2)}, u32[]{:S(2)}) collective-permute-start(bf16[64,1024]{1,0:T(8,128)(2,1)S(1)} %slice.306), channel_id=1, source_target_pairs={{0,8},{1,9},{2,10},{3,11},{4,12},{5,13},{6,14},{7,15},{8,0},{9,1},... | collective-permute-start | bytes 393224 | tf_op jit(solution)/shard_map/ppermute | solution.py:114
  11.2 75.0 %collective-permute-start.41 = (bf16[88,2048]{1,0:T(8,128)(2,1)}, bf16[88,2048]{1,0:T(8,128)(2,1)}, u32[]{:S(2)}, u32[]{:S(2)}) collective-permute-start(bf16[88,2048]{1,0:T(8,128)(2,1)} %param.25), channel_id=1, source_target_pairs={{0,16},{16,0},{1,17},{17,1},{2,18},{18,2},{3,19},{19,3},{4,20},{20... | collective-permute-start | bytes 1081352 | tf_op jit(solution)/shard_map/ppermute | solution.py:79
  18.2 230.7 %all-to-all-start = ((bf16[16,64,352]{2,1,0:T(8,128)(2,1)}), bf16[16,64,352]{2,1,0:T(8,128)(2,1)}, u32[]{:S(2)}, u32[]{:S(2)}) async-start(bf16[16,64,352]{2,1,0:T(8,128)(2,1)} %reshape.728), calls=%async_computation | async-start | bytes 1572864 | tf_op jit(solution)/shard_map/all_to_all | solution.py:263
  36.7 77.1 %collective-permute-start = (bf16[128,2048]{1,0:T(8,128)(2,1)S(1)}, bf16[128,2048]{1,0:T(8,128)(2,1)S(1)}, u32[]{:S(2)}, u32[]{:S(2)}) collective-permute-start(bf16[128,2048]{1,0:T(8,128)(2,1)S(1)} %copy-done.23), channel_id=1, source_target_pairs={{0,16},{16,0},{1,17},{17,1},{2,18},{18,2},{3,19},{19,3},{4,20},{20... | collective-permute-start | bytes 1572872 | tf_op jit(solution)/shard_map/ppermute | solution.py:79
  37.8 45.8 %collective-permute-start.54 = (bf16[128,1024]{1,0:T(8,128)(2,1)}, bf16[128,1024]{1,0:T(8,128)(2,1)S(1)}, u32[]{:S(2)}, u32[]{:S(2)}) collective-permute-start(bf16[128,1024]{1,0:T(8,128)(2,1)} %get-tuple-element.126), channel_id=1, source_target_pairs={{0,8},{1,9},{2,10},{3,11},{4,12},{5,13},{6,14},{7,15},{8,0},{9,1},... | collective-permute-start | bytes 786440 | tf_op jit(solution)/shard_map/ppermute | solution.py:114
  78.7 283.5 %collective-permute-start.39 = (bf16[704,2048]{1,0:T(8,128)(2,1)}, bf16[704,2048]{1,0:T(8,128)(2,1)}, u32[]{:S(2)}, u32[]{:S(2)}) collective-permute-start(bf16[704,2048]{1,0:T(8,128)(2,1)} %bitcast.111), channel_id=1, source_target_pairs={{0,16},{16,0},{1,17},{17,1},{2,18},{18,2},{3,19},{19,3},{4,20},{20... | collective-permute-start | bytes 8650760 | tf_op jit(solution)/shard_map/ppermute | solution.py:79
  111.3 32.3 %collective-permute-start.55 = (bf16[2,128,1024]{2,1,0:T(8,128)(2,1)}, bf16[2,128,1024]{2,1,0:T(8,128)(2,1)}, u32[]{:S(2)}, u32[]{:S(2)}) collective-permute-start(bf16[2,128,1024]{2,1,0:T(8,128)(2,1)} %get-tuple-element.129), channel_id=1, source_target_pairs={{0,4},{1,5},{2,6},{3,7},{4,0},{5,1},{6,2},{7,3},{8,12},{9,13},{10,... | collective-permute-start | bytes 1572872 | tf_op jit(solution)/shard_map/ppermute | solution.py:114
  117.5 30.6 %collective-permute-start.14 = (bf16[2,2,64,768]{3,2,1,0:T(8,128)(2,1)}, bf16[2,2,64,768]{3,2,1,0:T(8,128)(2,1)S(1)}, u32[]{:S(2)}, u32[]{:S(2)}) collective-permute-start(bf16[2,2,64,768]{3,2,1,0:T(8,128)(2,1)} %pad_maximum_fusion.65), channel_id=1, source_target_pairs={{0,4},{1,5},{2,6},{3,7},{4,0},{5,1},{6,2},{7,3},{8,12},{9,13},{10,... | collective-permute-start | bytes 1179656 | tf_op jit(solution)/shard_map/ppermute | solution.py:114
  122.6 33.9 %collective-permute-start.18 = (bf16[2,2,64,768]{3,2,1,0:T(8,128)(2,1)S(1)}, bf16[2,2,64,768]{3,2,1,0:T(8,128)(2,1)S(1)}, u32[]{:S(2)}, u32[]{:S(2)}) collective-permute-start(bf16[2,2,64,768]{3,2,1,0:T(8,128)(2,1)S(1)} %copy-done.131), channel_id=1, source_target_pairs={{0,4},{1,5},{2,6},{3,7},{4,0},{5,1},{6,2},{7,3},{8,12},{9,13},{10,... | collective-permute-start | bytes 1179656 | tf_op jit(solution)/shard_map/ppermute | solution.py:114
  159.8 72.2 %collective-permute-start.56 = (bf16[2,2,128,1024]{3,2,1,0:T(8,128)(2,1)}, bf16[2,2,128,1024]{3,2,1,0:T(8,128)(2,1)}, u32[]{:S(2)}, u32[]{:S(2)}) collective-permute-start(bf16[2,2,128,1024]{3,2,1,0:T(8,128)(2,1)} %get-tuple-element.96), channel_id=1, source_target_pairs={{0,1},{1,0},{2,3},{3,2},{4,5},{5,4},{6,7},{7,6},{8,9},{9,8},{10,11... | collective-permute-start | bytes 3145736 | tf_op jit(solution)/shard_map/ppermute | solution.py:114
  162.3 62.4 %collective-permute-start.52 = (bf16[2,2,128,1024]{3,2,1,0:T(8,128)(2,1)}, bf16[2,2,128,1024]{3,2,1,0:T(8,128)(2,1)}, u32[]{:S(2)}, u32[]{:S(2)}) collective-permute-start(bf16[2,2,128,1024]{3,2,1,0:T(8,128)(2,1)} %get-tuple-element.94), channel_id=1, source_target_pairs={{0,2},{1,3},{2,0},{3,1},{4,6},{5,7},{6,4},{7,5},{8,10},{9,11},{10,... | collective-permute-start | bytes 3145736 | tf_op jit(solution)/shard_map/ppermute | solution.py:114
  164.6 52.9 %collective-permute-start.15 = (bf16[2,2,2,64,768]{4,3,2,0,1:T(8,128)(2,1)}, bf16[2,2,2,64,768]{4,3,2,0,1:T(8,128)(2,1)}, u32[]{:S(2)}, u32[]{:S(2)}) collective-permute-start(bf16[2,2,2,64,768]{4,3,2,0,1:T(8,128)(2,1)} %pad_maximum_fusion.51), channel_id=1, source_target_pairs={{0,2},{1,3},{2,0},{3,1},{4,6},{5,7},{6,4},{7,5},{8,10},{9,11},{10,... | collective-permute-start | bytes 2359304 | tf_op jit(solution)/shard_map/ppermute | solution.py:114
  178.2 42.0 %collective-permute-start.19 = (bf16[2,2,2,64,768]{4,3,2,0,1:T(8,128)(2,1)}, bf16[2,2,2,64,768]{4,3,2,0,1:T(8,128)(2,1)}, u32[]{:S(2)}, u32[]{:S(2)}) collective-permute-start(bf16[2,2,2,64,768]{4,3,2,0,1:T(8,128)(2,1)} %pad_maximum_fusion.52), channel_id=1, source_target_pairs={{0,1},{1,0},{2,3},{3,2},{4,5},{5,4},{6,7},{7,6},{8,9},{9,8},{10,11... | collective-permute-start | bytes 2359304 | tf_op jit(solution)/shard_map/ppermute | solution.py:114
  220.2 41.5 %collective-permute-start.10 = (bf16[2,2,2,2,16,2048]{5,4,3,0,1,2:T(8,128)(2,1)}, bf16[2,2,2,2,16,2048]{5,4,3,0,1,2:T(8,128)(2,1)}, u32[]{:S(2)}, u32[]{:S(2)}) collective-permute-start(bf16[2,2,2,2,16,2048]{5,4,3,0,1,2:T(8,128)(2,1)} %pad_maximum_fusion.38), channel_id=1, source_target_pairs={{0,1},{1,0},{2,3},{3,2},{4,5},{5,4},{6,7},{7,6},{8,9},{9,8},{10,11... | collective-permute-start | bytes 3145736 | tf_op jit(solution)/shard_map/ppermute | solution.py:114
  224.7 213.2 %collective-permute-start.38 = (bf16[1024,2816]{1,0:T(8,128)(2,1)}, bf16[1024,2816]{1,0:T(8,128)(2,1)}, u32[]{:S(2)}, u32[]{:S(2)}) collective-permute-start(bf16[1024,2816]{1,0:T(8,128)(2,1)} %bitcast.392), channel_id=1, source_target_pairs={{0,16},{16,0},{1,17},{17,1},{2,18},{18,2},{3,19},{19,3},{4,20},{20... | collective-permute-start | bytes 17301512 | tf_op jit(solution)/shard_map/ppermute | solution.py:79
  231.9 52.0 %collective-permute-start.28 = (bf16[2,2,2,64,1024]{4,3,0,1,2:T(8,128)(2,1)}, bf16[2,2,2,64,1024]{4,3,0,1,2:T(8,128)(2,1)}, u32[]{:S(2)}, u32[]{:S(2)}) collective-permute-start(bf16[2,2,2,64,1024]{4,3,0,1,2:T(8,128)(2,1)} %pad_maximum_fusion.41), channel_id=1, source_target_pairs={{0,2},{1,3},{2,0},{3,1},{4,6},{5,7},{6,4},{7,5},{8,10},{9,11},{10,... | collective-permute-start | bytes 3145736 | tf_op jit(solution)/shard_map/ppermute | solution.py:114
  239.3 49.0 %collective-permute-start.5 = (bf16[16,65,576]{2,0,1:T(8,128)(2,1)}, bf16[16,65,576]{2,0,1:T(8,128)(2,1)}, u32[]{:S(2)}, u32[]{:S(2)}) collective-permute-start(bf16[16,65,576]{2,0,1:T(8,128)(2,1)} %slice.385), channel_id=1, source_target_pairs={{0,16},{16,0},{1,17},{17,1},{2,18},{18,2},{3,19},{19,3},{4,20},{20... | collective-permute-start | bytes 3594248 | tf_op jit(solution)/shard_map/ppermute | solution.py:79
  270.5 36.3 %collective-permute-start.16 = (bf16[2,2,2,2,64,768]{5,4,3,0,1,2:T(8,128)(2,1)}, bf16[2,2,2,2,64,768]{5,4,3,0,1,2:T(8,128)(2,1)}, u32[]{:S(2)}, u32[]{:S(2)}) collective-permute-start(bf16[2,2,2,2,64,768]{5,4,3,0,1,2:T(8,128)(2,1)} %pad_maximum_fusion.31), channel_id=1, source_target_pairs={{0,1},{1,0},{2,3},{3,2},{4,5},{5,4},{6,7},{7,6},{8,9},{9,8},{10,11... | collective-permute-start | bytes 4718600 | tf_op jit(solution)/shard_map/ppermute | solution.py:114
  284.0 36.0 %collective-permute-start.20 = (bf16[2,2,2,2,64,768]{5,4,3,0,1,2:T(8,128)(2,1)}, bf16[2,2,2,2,64,768]{5,4,3,0,1,2:T(8,128)(2,1)}, u32[]{:S(2)}, u32[]{:S(2)}) collective-permute-start(bf16[2,2,2,2,64,768]{5,4,3,0,1,2:T(8,128)(2,1)} %pad_maximum_fusion.32), channel_id=1, source_target_pairs={{0,2},{1,3},{2,0},{3,1},{4,6},{5,7},{6,4},{7,5},{8,10},{9,11},{10,... | collective-permute-start | bytes 4718600 | tf_op jit(solution)/shard_map/ppermute | solution.py:114
  288.2 104.4 %collective-permute-start.57 = (bf16[2,2,2,128,1024]{4,3,2,1,0:T(8,128)(2,1)}, bf16[2,2,2,128,1024]{4,3,2,1,0:T(8,128)(2,1)}, u32[]{:S(2)}, u32[]{:S(2)}) collective-permute-start(bf16[2,2,2,128,1024]{4,3,2,1,0:T(8,128)(2,1)} %get-tuple-element.67), channel_id=1, source_target_pairs={{0,2},{1,3},{2,0},{3,1},{4,6},{5,7},{6,4},{7,5},{8,10},{9,11},{10,... | collective-permute-start | bytes 6291464 | tf_op jit(solution)/shard_map/ppermute | solution.py:114
  306.8 105.5 %collective-permute-start.53 = (bf16[2,2,2,128,1024]{4,3,2,1,0:T(8,128)(2,1)}, bf16[2,2,2,128,1024]{4,3,2,1,0:T(8,128)(2,1)}, u32[]{:S(2)}, u32[]{:S(2)}) collective-permute-start(bf16[2,2,2,128,1024]{4,3,2,1,0:T(8,128)(2,1)} %get-tuple-element.65), channel_id=1, source_target_pairs={{0,1},{1,0},{2,3},{3,2},{4,5},{5,4},{6,7},{7,6},{8,9},{9,8},{10,11... | collective-permute-start | bytes 6291464 | tf_op jit(solution)/shard_map/ppermute | solution.py:114
  425.8 54.7 %collective-permute-start.37 = (bf16[2,2,2,128,1024]{4,3,0,1,2:T(8,128)(2,1)}, bf16[2,2,2,128,1024]{4,3,0,1,2:T(8,128)(2,1)}, u32[]{:S(2)}, u32[]{:S(2)}) collective-permute-start(bf16[2,2,2,128,1024]{4,3,0,1,2:T(8,128)(2,1)} %get-tuple-element.71), channel_id=1, source_target_pairs={{0,2},{1,3},{2,0},{3,1},{4,6},{5,7},{6,4},{7,5},{8,10},{9,11},{10,... | collective-permute-start | bytes 6291464 | tf_op jit(solution)/shard_map/ppermute | solution.py:114
  437.6 47.2 %collective-permute-start.33 = (bf16[2,2,2,128,1024]{4,3,0,1,2:T(8,128)(2,1)}, bf16[2,2,2,128,1024]{4,3,0,1,2:T(8,128)(2,1)}, u32[]{:S(2)}, u32[]{:S(2)}) collective-permute-start(bf16[2,2,2,128,1024]{4,3,0,1,2:T(8,128)(2,1)} %get-tuple-element.69), channel_id=1, source_target_pairs={{0,1},{1,0},{2,3},{3,2},{4,5},{5,4},{6,7},{7,6},{8,9},{9,8},{10,11... | collective-permute-start | bytes 6291464 | tf_op jit(solution)/shard_map/ppermute | solution.py:114
  561.0 135.2 %collective-permute-start.97 = (bf16[88,2048]{1,0:T(8,128)(2,1)S(1)}, bf16[88,2048]{1,0:T(8,128)(2,1)}, u32[]{:S(2)}, u32[]{:S(2)}) collective-permute-start(bf16[88,2048]{1,0:T(8,128)(2,1)S(1)} %fusion.129), channel_id=1, source_target_pairs={{0,16},{16,0},{1,17},{17,1},{2,18},{18,2},{3,19},{19,3},{4,20},{20... | collective-permute-start | bytes 1081352 | tf_op jit(solution)/shard_map/ppermute | solution.py:98
  578.6 97.6 %collective-permute-start.96 = (bf16[16,64,352]{2,1,0:T(8,128)(2,1)}, bf16[16,64,352]{2,1,0:T(8,128)(2,1)}, u32[]{:S(2)}, u32[]{:S(2)}) collective-permute-start(bf16[16,64,352]{2,1,0:T(8,128)(2,1)} %fusion.91), channel_id=1, source_target_pairs={{0,16},{16,0},{1,17},{17,1},{2,18},{18,2},{3,19},{19,3},{4,20},{20... | collective-permute-start | bytes 2162696 | tf_op jit(solution)/shard_map/ppermute | solution.py:98
  604.8 268.2 %collective-permute-start.99 = (bf16[704,2048]{1,0:T(8,128)(2,1)}, bf16[704,2048]{1,0:T(8,128)(2,1)}, u32[]{:S(2)}, u32[]{:S(2)}) collective-permute-start(bf16[704,2048]{1,0:T(8,128)(2,1)} %fusion.41), channel_id=1, source_target_pairs={{0,16},{16,0},{1,17},{17,1},{2,18},{18,2},{3,19},{19,3},{4,20},{20... | collective-permute-start | bytes 8650760 | tf_op jit(solution)/shard_map/ppermute | solution.py:98
  614.4 127.7 %collective-permute-start.46 = (bf16[2,2,2,128,1024]{4,3,0,1,2:T(8,128)(2,1)}, bf16[2,2,2,128,1024]{4,3,0,1,2:T(8,128)(2,1)}, u32[]{:S(2)}, u32[]{:S(2)}) collective-permute-start(bf16[2,2,2,128,1024]{4,3,0,1,2:T(8,128)(2,1)} %bitcast.794), channel_id=1, source_target_pairs={{0,2},{1,3},{2,0},{3,1},{4,6},{5,7},{6,4},{7,5},{8,10},{9,11},{10,... | collective-permute-start | bytes 6291464 | tf_op jit(solution)/shard_map/ppermute | solution.py:114
  621.7 124.8 %collective-permute-start.42 = (bf16[2,2,2,128,1024]{4,3,0,1,2:T(8,128)(2,1)}, bf16[2,2,2,128,1024]{4,3,0,1,2:T(8,128)(2,1)}, u32[]{:S(2)}, u32[]{:S(2)}) collective-permute-start(bf16[2,2,2,128,1024]{4,3,0,1,2:T(8,128)(2,1)} %bitcast.795), channel_id=1, source_target_pairs={{0,1},{1,0},{2,3},{3,2},{4,5},{5,4},{6,7},{7,6},{8,9},{9,8},{10,11... | collective-permute-start | bytes 6291464 | tf_op jit(solution)/shard_map/ppermute | solution.py:114
  676.2 74.4 %collective-permute-start.62 = (bf16[2,2,2,128,1024]{4,3,0,1,2:T(8,128)(2,1)}, bf16[2,2,2,128,1024]{4,3,0,1,2:T(8,128)(2,1)}, u32[]{:S(2)}, u32[]{:S(2)}) collective-permute-start(bf16[2,2,2,128,1024]{4,3,0,1,2:T(8,128)(2,1)} %bitcast.792), channel_id=1, source_target_pairs={{0,2},{1,3},{2,0},{3,1},{4,6},{5,7},{6,4},{7,5},{8,10},{9,11},{10,... | collective-permute-start | bytes 6291464 | tf_op jit(solution)/shard_map/ppermute | solution.py:114
  679.3 52.5 %all-to-all-start.1 = ((bf16[16,64,352]{2,1,0:T(8,128)(2,1)}), bf16[16,64,352]{2,1,0:T(8,128)(2,1)S(1)}, u32[]{:S(2)}, u32[]{:S(2)}) async-start(bf16[16,64,352]{2,1,0:T(8,128)(2,1)} %fusion.62), calls=%async_computation.1 | async-start | bytes 1572864 | tf_op jit(solution)/shard_map/all_to_all | solution.py:391
  696.3 58.5 %collective-permute-start.58 = (bf16[2,2,2,128,1024]{4,3,0,1,2:T(8,128)(2,1)}, bf16[2,2,2,128,1024]{4,3,0,1,2:T(8,128)(2,1)}, u32[]{:S(2)}, u32[]{:S(2)}) collective-permute-start(bf16[2,2,2,128,1024]{4,3,0,1,2:T(8,128)(2,1)} %bitcast.793), channel_id=1, source_target_pairs={{0,1},{1,0},{2,3},{3,2},{4,5},{5,4},{6,7},{7,6},{8,9},{9,8},{10,11... | collective-permute-start | bytes 6291464 | tf_op jit(solution)/shard_map/ppermute | solution.py:114
  742.1 217.2 %collective-permute-start.98 = (bf16[1024,2816]{1,0:T(8,128)(2,1)}, bf16[1024,2816]{1,0:T(8,128)(2,1)}, u32[]{:S(2)}, u32[]{:S(2)}) collective-permute-start(bf16[1024,2816]{1,0:T(8,128)(2,1)} %fusion.21), channel_id=1, source_target_pairs={{0,16},{16,0},{1,17},{17,1},{2,18},{18,2},{3,19},{19,3},{4,20},{20... | collective-permute-start | bytes 17301512 | tf_op jit(solution)/shard_map/ppermute | solution.py:98
  754.8 39.0 %collective-permute-start.63 = (bf16[2,2,128,1024]{3,2,0,1:T(8,128)(2,1)S(1)}, bf16[2,2,128,1024]{3,2,0,1:T(8,128)(2,1)S(1)}, u32[]{:S(2)}, u32[]{:S(2)}) collective-permute-start(bf16[2,2,128,1024]{3,2,0,1:T(8,128)(2,1)S(1)} %slice_bitcast_fusion), channel_id=1, source_target_pairs={{0,1},{1,0},{2,3},{3,2},{4,5},{5,4},{6,7},{7,6},{8,9},{9,8},{10,11... | collective-permute-start | bytes 3145736 | tf_op jit(solution)/shard_map/ppermute | solution.py:114
  793.8 41.0 %collective-permute-start.44 = (bf16[2,128,1024]{2,1,0:T(8,128)(2,1)S(1)}, bf16[2,128,1024]{2,1,0:T(8,128)(2,1)S(1)}, u32[]{:S(2)}, u32[]{:S(2)}) collective-permute-start(bf16[2,128,1024]{2,1,0:T(8,128)(2,1)S(1)} %slice_bitcast_fusion.14), channel_id=1, source_target_pairs={{0,4},{1,5},{2,6},{3,7},{4,0},{5,1},{6,2},{7,3},{8,12},{9,13},{10,... | collective-permute-start | bytes 1572872 | tf_op jit(solution)/shard_map/ppermute | solution.py:114
  798.4 36.1 %collective-permute-start.60 = (bf16[2,128,1024]{2,1,0:T(8,128)(2,1)S(1)}, bf16[2,128,1024]{2,1,0:T(8,128)(2,1)S(1)}, u32[]{:S(2)}, u32[]{:S(2)}) collective-permute-start(bf16[2,128,1024]{2,1,0:T(8,128)(2,1)S(1)} %slice_bitcast_fusion.10), channel_id=1, source_target_pairs={{0,4},{1,5},{2,6},{3,7},{4,0},{5,1},{6,2},{7,3},{8,12},{9,13},{10,... | collective-permute-start | bytes 1572872 | tf_op jit(solution)/shard_map/ppermute | solution.py:114
  817.7 47.9 %collective-permute-start.49 = (bf16[128,1024]{1,0:T(8,128)(2,1)S(1)}, bf16[128,1024]{1,0:T(8,128)(2,1)S(1)}, u32[]{:S(2)}, u32[]{:S(2)}) collective-permute-start(bf16[128,1024]{1,0:T(8,128)(2,1)S(1)} %slice_bitcast_fusion.20), channel_id=1, source_target_pairs={{0,8},{1,9},{2,10},{3,11},{4,12},{5,13},{6,14},{7,15},{8,0},{9,1},... | collective-permute-start | bytes 786440 | tf_op jit(solution)/shard_map/ppermute | solution.py:114
  834.8 30.3 %collective-permute-start.61 = (bf16[128,1024]{1,0:T(8,128)(2,1)S(1)}, bf16[128,1024]{1,0:T(8,128)(2,1)S(1)}, u32[]{:S(2)}, u32[]{:S(2)}) collective-permute-start(bf16[128,1024]{1,0:T(8,128)(2,1)S(1)} %slice_bitcast_fusion.18), channel_id=1, source_target_pairs={{0,8},{1,9},{2,10},{3,11},{4,12},{5,13},{6,14},{7,15},{8,0},{9,1},... | collective-permute-start | bytes 786440 | tf_op jit(solution)/shard_map/ppermute | solution.py:114
  905.3 33.5 %collective-permute-start.83 = (bf16[2,2,2,2,16,2048]{5,4,3,0,1,2:T(8,128)(2,1)}, bf16[2,2,2,2,16,2048]{5,4,3,0,1,2:T(8,128)(2,1)}, u32[]{:S(2)}, u32[]{:S(2)}) collective-permute-start(bf16[2,2,2,2,16,2048]{5,4,3,0,1,2:T(8,128)(2,1)} %bitcast.800), channel_id=1, source_target_pairs={{0,1},{1,0},{2,3},{3,2},{4,5},{5,4},{6,7},{7,6},{8,9},{9,8},{10,11... | collective-permute-start | bytes 3145736 | tf_op jit(solution)/shard_map/ppermute | solution.py:114
  919.4 33.5 %collective-permute-start.88 = (bf16[2,2,2,64,1024]{4,3,0,1,2:T(8,128)(2,1)}, bf16[2,2,2,64,1024]{4,3,0,1,2:T(8,128)(2,1)}, u32[]{:S(2)}, u32[]{:S(2)}) collective-permute-start(bf16[2,2,2,64,1024]{4,3,0,1,2:T(8,128)(2,1)} %bitcast.799), channel_id=1, source_target_pairs={{0,1},{1,0},{2,3},{3,2},{4,5},{5,4},{6,7},{7,6},{8,9},{9,8},{10,11... | collective-permute-start | bytes 3145736 | tf_op jit(solution)/shard_map/ppermute | solution.py:114
  926.0 75.9 %collective-permute-start.78 = (bf16[2,2,2,2,64,768]{5,4,3,0,1,2:T(8,128)(2,1)}, bf16[2,2,2,2,64,768]{5,4,3,0,1,2:T(8,128)(2,1)}, u32[]{:S(2)}, u32[]{:S(2)}) collective-permute-start(bf16[2,2,2,2,64,768]{5,4,3,0,1,2:T(8,128)(2,1)} %bitcast.796), channel_id=1, source_target_pairs={{0,2},{1,3},{2,0},{3,1},{4,6},{5,7},{6,4},{7,5},{8,10},{9,11},{10,... | collective-permute-start | bytes 4718600 | tf_op jit(solution)/shard_map/ppermute | solution.py:114
  935.4 68.6 %collective-permute-start.74 = (bf16[2,2,2,2,64,768]{5,4,3,0,1,2:T(8,128)(2,1)}, bf16[2,2,2,2,64,768]{5,4,3,0,1,2:T(8,128)(2,1)}, u32[]{:S(2)}, u32[]{:S(2)}) collective-permute-start(bf16[2,2,2,2,64,768]{5,4,3,0,1,2:T(8,128)(2,1)} %bitcast.889), channel_id=1, source_target_pairs={{0,1},{1,0},{2,3},{3,2},{4,5},{5,4},{6,7},{7,6},{8,9},{9,8},{10,11... | collective-permute-start | bytes 4718600 | tf_op jit(solution)/shard_map/ppermute | solution.py:114
  952.8 32.6 %collective-permute-start.84 = (bf16[2,2,2,16,2048]{4,3,2,0,1:T(8,128)(2,1)}, bf16[2,2,2,16,2048]{4,3,2,0,1:T(8,128)(2,1)}, u32[]{:S(2)}, u32[]{:S(2)}) collective-permute-start(bf16[2,2,2,16,2048]{4,3,2,0,1:T(8,128)(2,1)} %dynamic-slice_bitcast_fusion.6), channel_id=1, source_target_pairs={{0,2},{1,3},{2,0},{3,1},{4,6},{5,7},{6,4},{7,5},{8,10},{9,11},{10,... | collective-permute-start | bytes 1572872 | tf_op jit(solution)/shard_map/ppermute | solution.py:114
  957.4 40.4 %collective-permute-start.93 = (bf16[2,2,64,1024]{3,2,0,1:T(8,128)(2,1)}, bf16[2,2,64,1024]{3,2,0,1:T(8,128)(2,1)}, u32[]{:S(2)}, u32[]{:S(2)}) collective-permute-start(bf16[2,2,64,1024]{3,2,0,1:T(8,128)(2,1)} %dynamic-slice_bitcast_fusion.4), channel_id=1, source_target_pairs={{0,1},{1,0},{2,3},{3,2},{4,5},{5,4},{6,7},{7,6},{8,9},{9,8},{10,11... | collective-permute-start | bytes 1572872 | tf_op jit(solution)/shard_map/ppermute | solution.py:114
  959.3 39.8 %collective-permute-start.89 = (bf16[2,2,64,1024]{3,2,0,1:T(8,128)(2,1)}, bf16[2,2,64,1024]{3,2,0,1:T(8,128)(2,1)}, u32[]{:S(2)}, u32[]{:S(2)}) collective-permute-start(bf16[2,2,64,1024]{3,2,0,1:T(8,128)(2,1)} %dynamic-slice_bitcast_fusion.5), channel_id=1, source_target_pairs={{0,2},{1,3},{2,0},{3,1},{4,6},{5,7},{6,4},{7,5},{8,10},{9,11},{10,... | collective-permute-start | bytes 1572872 | tf_op jit(solution)/shard_map/ppermute | solution.py:114
  1004.1 39.5 %collective-permute-start.79 = (bf16[2,2,2,64,768]{4,3,2,0,1:T(8,128)(2,1)S(1)}, bf16[2,2,2,64,768]{4,3,2,0,1:T(8,128)(2,1)S(1)}, u32[]{:S(2)}, u32[]{:S(2)}) collective-permute-start(bf16[2,2,2,64,768]{4,3,2,0,1:T(8,128)(2,1)S(1)} %dynamic-slice_bitcast_fusion.2), channel_id=1, source_target_pairs={{0,1},{1,0},{2,3},{3,2},{4,5},{5,4},{6,7},{7,6},{8,9},{9,8},{10,11... | collective-permute-start | bytes 2359304 | tf_op jit(solution)/shard_map/ppermute | solution.py:114
  1006.4 37.5 %collective-permute-start.75 = (bf16[2,2,2,64,768]{4,3,2,0,1:T(8,128)(2,1)S(1)}, bf16[2,2,2,64,768]{4,3,2,0,1:T(8,128)(2,1)S(1)}, u32[]{:S(2)}, u32[]{:S(2)}) collective-permute-start(bf16[2,2,2,64,768]{4,3,2,0,1:T(8,128)(2,1)S(1)} %dynamic-slice_bitcast_fusion.3), channel_id=1, source_target_pairs={{0,2},{1,3},{2,0},{3,1},{4,6},{5,7},{6,4},{7,5},{8,10},{9,11},{10,... | collective-permute-start | bytes 2359304 | tf_op jit(solution)/shard_map/ppermute | solution.py:114
  (244 other events, 2541.1 us)

commit v2 on v1

v2 whole, which is shorter than its diff:
```python
import functools

import jax
import jax.numpy as jnp
from jax import lax
from jax.experimental import pallas as pl
from jax.experimental.pallas import tpu as pltpu
from jax.sharding import PartitionSpec as P

H = 16
DH = 128
DR = 64
DV = 128
KVR = 512
TOP = 6
SPLIT = ("dp", "expert")
ROPE_LANES = 128

f32 = jnp.float32
bf16 = jnp.bfloat16

norm_eps = 1e-06
rope_base = 50000.0
masked_score = -1e30


def norm_apply(values, scales):
    return values * lax.rsqrt(jnp.mean(values * values, axis=-1, keepdims=True) + norm_eps) * scales


def norm_back(values, scales, upstream):
    unused, pullback = jax.vjp(norm_apply, values, scales.astype(f32))
    return pullback(upstream)


def rotate(values, cosine_table, sine_table):
    half_width = values.shape[-1] // 2
    front_half = values[..., :half_width]
    back_half = values[..., half_width:]
    return jnp.concatenate(
        [
            front_half * cosine_table - back_half * sine_table,
            front_half * sine_table + back_half * cosine_table,
        ],
        axis=-1,
    )


def swish_gate(gate_part, up_part):
    return gate_part * jax.nn.sigmoid(gate_part) * up_part


def swish_back(gate_part, up_part, upstream):
    unused, pullback = jax.vjp(swish_gate, gate_part, up_part)
    return jnp.concatenate(pullback(upstream), axis=-1)


def layout(lengths_row, row_count):
    doc_ends = jnp.cumsum(lengths_row)
    places = jnp.arange(row_count, dtype=jnp.int32)
    passed_end = (places[:, None] >= doc_ends[None, :]).astype(jnp.int32)
    doc_ids = jnp.sum(passed_end, axis=1)
    starts = jnp.sum(passed_end * lengths_row[None, :], axis=1)
    return (doc_ids, places - starts)


def angles(offsets, rope_width):
    frequency = rope_base ** (-2.0 * jnp.arange(rope_width // 2, dtype=f32) / rope_width)
    turned = offsets.astype(f32)[..., None] * frequency
    return (jnp.cos(turned), jnp.sin(turned))


def dot(left, right):
    return jnp.dot(left, right, preferred_element_type=f32)


def pick(values, place, axis):
    return lax.dynamic_index_in_dim(values, place, axis, keepdims=False)


def dp_gather(values):
    if lax.axis_size("dp") != 2:
        return lax.all_gather(values, "dp")
    other = lax.ppermute(values, "dp", [(0, 1), (1, 0)])
    first = lax.axis_index("dp") == 0
    return jnp.stack([jnp.where(first, values, other), jnp.where(first, other, values)])


def dp_swap(values):
    if lax.axis_size("dp") != 2:
        return lax.all_to_all(values, "dp", split_axis=0, concat_axis=0)
    core = lax.axis_index("dp")
    own = pick(values, core, 0)
    other = lax.ppermute(pick(values, 1 - core, 0), "dp", [(0, 1), (1, 0)])
    first = core == 0
    return jnp.stack([jnp.where(first, own, other), jnp.where(first, other, own)])


def dp_scatter(values, sent=f32):
    if lax.axis_size("dp") != 2:
        return lax.psum_scatter(values.astype(sent), "dp", scatter_dimension=0).astype(f32)
    core = lax.axis_index("dp")
    other = lax.ppermute(pick(values, 1 - core, 0).astype(sent), "dp", [(0, 1), (1, 0)])
    return pick(values, core, 0).astype(f32) + other.astype(f32)


def dp_sum(values):
    if lax.axis_size("dp") != 2:
        return lax.psum(values, "dp")
    return values + lax.ppermute(values, "dp", [(0, 1), (1, 0)])


def bits_of(count):
    return [1 << place for place in reversed(range(count.bit_length() - 1))]


def partner(values, bit):
    count = lax.axis_size("expert")
    return lax.ppermute(values, "expert", [(i, i ^ bit) for i in range(count)])


def gathering(values, order, held=(), lead=0):
    me = lax.axis_index("expert")
    held = list(held)
    for bit in order:
        other = yield partner(values, bit)
        low = (me & bit) == 0
        values = jnp.stack(
            [jnp.where(low, values, other), jnp.where(low, other, values)],
            axis=lead + sum(1 for known in held if known > bit),
        )
        held.append(bit)
    return values.reshape(values.shape[:lead] + (-1,) + values.shape[lead + len(held) :])


def scattering(values, order, bits, kept=f32, lead=0):
    me = lax.axis_index("expert")
    bits = list(bits)
    values = values.reshape(values.shape[:lead] + (2,) * len(bits) + values.shape[lead + 1 :])
    for step, bit in enumerate(order):
        axis = lead + bits.index(bit)
        bits.remove(bit)
        place = ((me & bit) != 0).astype(jnp.int32)
        other = yield partner(pick(values, 1 - place, axis), bit)
        values = pick(values, place, axis).astype(f32) + other.astype(f32)
        values = values.astype(kept if step + 1 == len(order) else bf16)
    if bits:
        values = values.reshape(values.shape[:lead] + (-1,) + values.shape[lead + len(bits) :])
    return values


def later(steps, values, chain):
    for _ in range(steps):
        values = yield values
    return (yield from chain(values))


def begun(chain, values):
    while True:
        try:
            values = chain.send(values)
        except StopIteration as stop:
            return stop.value
        values = yield values


def last_of(chain, values):
    try:
        chain.send(values)
    except StopIteration as stop:
        return stop.value


def pair_swapping(values, bit, axis):
    place = ((lax.axis_index("expert") & bit) != 0).astype(jnp.int32)
    own = pick(values, place, axis)
    other = yield partner(pick(values, 1 - place, axis), bit)
    low = place == 0
    return jnp.stack([jnp.where(low, own, other), jnp.where(low, other, own)])


def march(*chains, jobs=()):
    results, found = [None] * len(chains), []
    live = {i: next(chain) for i, chain in enumerate(chains)}
    waiting = [operands for _, *operands in jobs]
    while live or len(found) < len(jobs):
        step = len(found)
        job = jobs[step][0](results, found, *waiting[step]) if step < len(jobs) else ()
        live, job, waiting = lax.optimization_barrier((live, job, waiting[step + 1 :]))
        waiting = [()] * (step + 1) + waiting
        found.append(job)
        following = {}
        for i, values in live.items():
            try:
                following[i] = chains[i].send(values)
            except StopIteration as stop:
                results[i] = stop.value
        live = following
    return results, found


def skip(results, found):
    return ()


def alone(chain, *markers):
    values = next(chain)
    step = 0
    while True:
        if step < len(markers):
            values = after(values, markers[step])
        step += 1
        try:
            values = chain.send(values)
        except StopIteration as stop:
            return stop.value


def after(values, *others):
    return lax.optimization_barrier((values, others))[0]


def thirds(width):
    side = width // 128 // 3 * 128
    return (0, side), (side, width - side), (width - side, width)


def whole_orders(bits, pair_bit):
    far, second, first = [bit for bit in bits if bit != pair_bit]
    return (
        (second, far, first, pair_bit),
        (far, first, pair_bit, second),
        (far, pair_bit, second, first),
    )


def lanes_dot(left, right):
    return lax.dot_general(left, right, (((1,), (1,)), ((), ())), preferred_element_type=f32)


def rows_dot(left, right):
    return lax.dot_general(left, right, (((0,), (0,)), ((), ())), preferred_element_type=f32)


def head_lanes(heads):
    lane = lax.broadcasted_iota(jnp.int32, (1, ROPE_LANES), 1) // (DR // 2)
    return [(lane == head).astype(f32) for head in range(heads)]


def attend_kernel(
    heads,
    x_ref,
    gain_ref,
    kv_gain_ref,
    down_ref,
    q_ref,
    up_ref,
    out_ref,
    cos_ref,
    sin_ref,
    column_ref,
    row_ref,
    normed_ref,
    joint_ref,
    kv_normed_ref,
    heads_ref,
    keys_ref,
    values_ref,
    probs_ref,
    attended_ref,
    sum_ref,
):
    nope = heads * DH
    rows = x_ref.shape[0]
    x = x_ref[...].astype(f32)
    scale = lax.rsqrt(jnp.mean(x * x, axis=-1, keepdims=True) + norm_eps)
    normed_ref[...] = (x * scale * gain_ref[...]).astype(bf16)
    joint_ref[...] = dot(normed_ref[...], down_ref[...])
    latent = joint_ref[:, :KVR]
    scale = lax.rsqrt(jnp.mean(latent * latent, axis=-1, keepdims=True) + norm_eps)
    kv_normed_ref[...] = (latent * scale * kv_gain_ref[...]).astype(bf16)
    cos, sin = cos_ref[...], sin_ref[...]
    front = joint_ref[:, KVR : KVR + ROPE_LANES]
    back = joint_ref[:, KVR + ROPE_LANES :]
    keys_ref[:, nope : nope + ROPE_LANES] = (front * cos - back * sin).astype(bf16)
    keys_ref[:, nope + ROPE_LANES :] = (front * sin + back * cos).astype(bf16)
    q = dot(normed_ref[...], q_ref[:, : nope + 2 * ROPE_LANES])
    front = q[:, nope : nope + ROPE_LANES]
    back = q[:, nope + ROPE_LANES :]
    heads_ref[:, :nope] = q[:, :nope].astype(bf16)
    heads_ref[:, nope : nope + ROPE_LANES] = (front * cos - back * sin).astype(bf16)
    heads_ref[:, nope + ROPE_LANES :] = (front * sin + back * cos).astype(bf16)
    kv = dot(kv_normed_ref[...], up_ref[...])
    for head in range(heads):
        start = head * (DH + DV)
        keys_ref[:, head * DH : (head + 1) * DH] = kv[:, start : start + DH].astype(bf16)
        values_ref[:, head * DV : (head + 1) * DV] = kv[:, start + DH : start + DH + DV].astype(bf16)
    tile = probs_ref.shape[-1]
    causal = lax.broadcasted_iota(jnp.int32, (tile, tile), 0) >= lax.broadcasted_iota(
        jnp.int32, (tile, tile), 1
    )
    own = head_lanes(heads)
    for block in range(rows // tile):
        part = pl.ds(block * tile, tile)
        allowed = (column_ref[part, :] == row_ref[block]) & causal
        rotary = heads_ref[part, nope:].astype(f32)
        for head in range(heads):
            both = jnp.concatenate([own[head], own[head]], axis=-1)
            scores = lanes_dot(
                heads_ref[part, head * DH : (head + 1) * DH],
                keys_ref[part, head * DH : (head + 1) * DH],
            ) + lanes_dot((rotary * both).astype(bf16), keys_ref[part, nope:])
            scores = jnp.where(allowed, scores * (DH + DR) ** (-0.5), masked_score)
            weights = jnp.exp(scores - jnp.max(scores, axis=-1, keepdims=True))
            probs = weights / jnp.sum(weights, axis=-1, keepdims=True)
            probs_ref[block * heads + head] = probs
            attended_ref[part, head * DV : (head + 1) * DV] = dot(
                probs.astype(bf16), values_ref[part, head * DV : (head + 1) * DV]
            ).astype(bf16)
    sum_ref[...] = dot(attended_ref[...], out_ref[...]).astype(sum_ref.dtype)


def attend_back_kernel(
    heads,
    branch_ref,
    out_ref,
    probs_ref,
    heads_ref,
    keys_ref,
    values_ref,
    joint_ref,
    kv_gain_ref,
    up_ref,
    q_ref,
    down_ref,
    cos_ref,
    sin_ref,
    d_q_ref,
    d_kv_ref,
    d_joint_ref,
    d_gain_ref,
    sum_ref,
    d_key_ref,
):
    nope = heads * DH
    rows = branch_ref.shape[0]
    tile = probs_ref.shape[-1]
    factor = (DH + DR) ** (-0.5)
    d_attended = lanes_dot(branch_ref[...], out_ref[...]).astype(bf16)
    own = head_lanes(heads)
    for block in range(rows // tile):
        part = slice(block * tile, (block + 1) * tile)
        rotary = heads_ref[part, nope:].astype(f32)
        d_rotary = jnp.zeros((tile, 2 * ROPE_LANES), f32)
        d_key = jnp.zeros((tile, 2 * ROPE_LANES), f32)
        for head in range(heads):
            both = jnp.concatenate([own[head], own[head]], axis=-1)
            columns = slice(head * DH, (head + 1) * DH)
            start = head * (DH + DV)
            upstream = d_attended[part, head * DV : (head + 1) * DV]
            probs = probs_ref[block * heads + head]
            d_kv_ref[part, start + DH : start + DH + DV] = rows_dot(
                probs.astype(bf16), upstream
            ).astype(bf16)
            d_probs = lanes_dot(upstream, values_ref[part, head * DV : (head + 1) * DV])
            d_scores = probs * (d_probs - jnp.sum(d_probs * probs, axis=-1, keepdims=True))
            d_scores = d_scores.astype(bf16)
            d_q_ref[part, columns] = (dot(d_scores, keys_ref[part, columns]) * factor).astype(bf16)
            d_rotary = d_rotary + dot(d_scores, keys_ref[part, nope:]) * (factor * both)
            d_kv_ref[part, start : start + DH] = (
                rows_dot(d_scores, heads_ref[part, columns]) * factor
            ).astype(bf16)
            d_key = d_key + rows_dot(d_scores, (rotary * both).astype(bf16)) * factor
        cos, sin = cos_ref[part, :], sin_ref[part, :]
        front, back = d_rotary[:, :ROPE_LANES], d_rotary[:, ROPE_LANES:]
        d_q_ref[part, nope : nope + ROPE_LANES] = (front * cos + back * sin).astype(bf16)
        d_q_ref[part, nope + ROPE_LANES :] = (back * cos - front * sin).astype(bf16)
        front, back = d_key[:, :ROPE_LANES], d_key[:, ROPE_LANES:]
        d_key_ref[part, :ROPE_LANES] = front * cos + back * sin
        d_key_ref[part, ROPE_LANES:] = back * cos - front * sin
    d_kv_normed = lanes_dot(d_kv_ref[...], up_ref[...])
    latent = joint_ref[:, :KVR]
    scale = lax.rsqrt(jnp.mean(latent * latent, axis=-1, keepdims=True) + norm_eps)
    d_gain_ref[0] = jnp.sum(d_kv_normed * latent * scale, axis=0, keepdims=True)
    d_kv_normed = d_kv_normed * kv_gain_ref[...]
    fall = jnp.mean(d_kv_normed * latent, axis=-1, keepdims=True) * scale * scale * scale
    d_joint_ref[:, :KVR] = (d_kv_normed * scale - latent * fall).astype(bf16)
    d_joint_ref[:, KVR:] = d_key_ref[...].astype(bf16)
    sum_ref[...] = (
        lanes_dot(d_q_ref[...], q_ref[:, : nope + 2 * ROPE_LANES])
        + lanes_dot(d_joint_ref[...], down_ref[...])
    ).astype(sum_ref.dtype)


def by_rows_call(kernel, rows, chunk, streamed, fixed_, outs, scratch=(), order=None):
    steps = rows // chunk
    operands, specs = [], []
    for name in order:
        if name in streamed:
            value = streamed[name]
            block = (value.shape[0] // steps,) + value.shape[1:]
            index = lambda i, ndim=value.ndim: (i,) + (0,) * (ndim - 1)
        else:
            value = fixed_[name]
            block = value.shape
            index = lambda i, ndim=value.ndim: (0,) * ndim
        operands.append(value)
        specs.append(pl.BlockSpec(block, index))
    out_specs = [
        pl.BlockSpec((shape[0] // steps,) + shape[1:], lambda i, ndim=len(shape): (i,) + (0,) * (ndim - 1))
        for shape, dtype in outs
    ]
    return pl.pallas_call(
        kernel,
        grid=(steps,),
        in_specs=specs,
        out_specs=out_specs,
        out_shape=[jax.ShapeDtypeStruct(shape, dtype) for shape, dtype in outs],
        scratch_shapes=scratch,
        compiler_params=pltpu.CompilerParams(vmem_limit_bytes=56 * 2**20),
    )(*operands)


def shards(
    tokens,
    attn_gain,
    kv_gain,
    ffn_gain,
    q_weight,
    kv_down_weight,
    kv_up_weight,
    out_weight,
    shared_gate_up,
    shared_down,
    expert_gate_up,
    expert_down,
    routes,
    gates,
    lengths,
    out_grad,
):
    row_count, width = tokens.shape
    dp_count = lax.axis_size("dp")
    expert_count = lax.axis_size("expert")
    core = lax.axis_index("dp")
    me = lax.axis_index("expert")
    scale_factor = (DH + DR) ** (-0.5)
    slice_rows = kv_down_weight.shape[0]
    joint_width = KVR + DR
    n_gain, n_kv_gain = attn_gain.shape[0], kv_gain.shape[0]

    bits = bits_of(expert_count)
    head_step = expert_count * dp_count // H
    pair_bit = max(4, head_step)
    rest = [bit for bit in bits if bit != pair_bit]
    head_low = pair_bit // head_step
    head_high = H // (dp_count * 2 * head_low)
    heads = head_high * head_low
    blocks = 2 * dp_count
    pair_rows = blocks * row_count

    far, second, first = rest
    orders = whole_orders(bits, pair_bit)
    parts = thirds(width)

    def column_parts(values):
        return [values[..., low:high] for low, high in parts]

    combined = jnp.sum(
        jnp.where(
            routes[:, :, None] == jnp.arange(expert_count, dtype=jnp.int32),
            gates[:, :, None],
            0.0,
        ),
        axis=1,
    ).T
    gates_high = lax.reduce_precision(combined, 8, 7)
    gates_low = (combined - gates_high).astype(bf16)
    gates_both = jnp.stack([gates_high.astype(bf16), gates_low], axis=1)
    gate_cols = 4 * row_count
    gates_both = gates_both.reshape(-1, gate_cols)
    gate_rows = gates_both.shape[0]
    gates_both = jnp.pad(gates_both, ((0, 0), (0, joint_width - gate_cols)))
    gains = jnp.concatenate([attn_gain, ffn_gain, kv_gain, lengths[0].astype(bf16)])
    gains = jnp.pad(gains, (0, joint_width - gains.shape[0]))[None]
    gain_row = slice_rows + gate_rows
    spare = -(gain_row + 1) % 16
    small = jnp.concatenate(
        [kv_down_weight, gates_both, jnp.pad(gains, ((0, spare), (0, 0)))], axis=0
    )

    def turned(values):
        split = values.reshape(values.shape[0], dp_count, expert_count, slice_rows)
        return split.transpose(0, 2, 1, 3).reshape(values.shape)

    def turned_back(values):
        split = values.reshape(values.shape[0], expert_count, dp_count, slice_rows)
        return split.transpose(0, 2, 1, 3).reshape(values.shape)

    q_cols = heads * (DH + DR)
    up_cols = heads * (DH + DV) * n_kv_gain // slice_rows
    head_cols = q_cols + up_cols
    head_rows = dp_count * slice_rows

    def by_pair(weight, head_width, *cuts):
        split = weight.reshape(-1, dp_count, head_high, 2, head_low, head_width)
        split = split.transpose(1, 3, 0, 2, 4, 5)
        lead = (dp_count, 2, slice_rows, -1)
        return [part.reshape(lead) for part in jnp.split(split, cuts, axis=-1)]

    by_head = dp_swap(
        jnp.concatenate(
            by_pair(q_weight, DH + DR, DH, DH + DR // 2) + by_pair(kv_up_weight, DH + DV), axis=-1
        )
    )
    nope_cols = heads * DH
    rope_cols = heads * DR // 2

    def spread(columns):
        if rope_cols == ROPE_LANES:
            return columns
        parts = jnp.split(columns[:, :q_cols], (nope_cols, nope_cols + rope_cols), axis=-1)
        room = ((0, 0), (0, ROPE_LANES - rope_cols))
        return jnp.concatenate([parts[0], jnp.pad(parts[1], room), jnp.pad(parts[2], room)], axis=-1)

    def unspread(columns):
        if rope_cols == ROPE_LANES:
            return columns
        parts = jnp.split(columns, (nope_cols, nope_cols + ROPE_LANES), axis=-1)
        return jnp.concatenate([parts[0], parts[1][:, :rope_cols], parts[2][:, :rope_cols]], axis=-1)

    out_cut = out_weight.reshape(slice_rows, -1, 2, head_cols).transpose(2, 1, 0, 3)
    out_cut = out_cut.reshape(2, -1, head_cols)
    head_cut = head_rows * 3 // 8
    out_mid = out_cut.shape[1] // 2

    share = shared_down.shape[0]
    units = dp_count * share
    padded = -(-units // 128) * 128

    def shared_by_unit(results, found, weight):
        split = weight.reshape(slice_rows, 2, dp_count, expert_count, share)
        split = split.transpose(3, 0, 1, 2, 4).reshape(expert_count, slice_rows, 2, units)
        split = jnp.pad(split, ((0, 0), (0, 0), (0, 0), (0, padded - units)))
        return split.reshape(expert_count, slice_rows, 2 * padded)

    pair_w = lax.all_gather(expert_gate_up[0].reshape(width // dp_count, -1), "dp", tiled=True)
    down_w = lax.all_gather(expert_down[0], "dp", tiled=True)
    def shared_weights(split, shared_down):
        split = lax.all_to_all(split, "expert", split_axis=0, concat_axis=0, tiled=True)
        down = dp_gather(shared_down).reshape(units, width)
        down = jnp.pad(down, ((0, padded - units), (0, 0)))
        return dp_gather(split).reshape(width, 2 * padded), down

    def attend(all_rows, small_all, by_head, out_parts):
        joint_all = dp_gather(small_all[:, :slice_rows])
        kv_down = joint_all.transpose(1, 0, 2, 3).reshape(width, joint_width)
        front, back = kv_down[:, KVR : KVR + DR // 2], kv_down[:, KVR + DR // 2 :]
        copies = 2 * ROPE_LANES // DR
        kv_down = jnp.concatenate([kv_down[:, :KVR]] + [front] * copies + [back] * copies, axis=-1)
        gains_all = dp_gather(small_all[:, gain_row])
        attn_scale = gains_all[..., :n_gain].transpose(1, 0, 2).reshape(-1)
        ffn_scale = gains_all[..., n_gain : 2 * n_gain].reshape(-1)
        n_gains = 2 * n_gain + n_kv_gain
        kv_scale = gains_all[..., 2 * n_gain : n_gains].reshape(-1)
        all_lengths = gains_all[..., n_gains : n_gains + lengths.shape[1]].astype(jnp.int32)
        low = me & ~pair_bit
        all_lengths = jnp.stack([pick(all_lengths, low, 1), pick(all_lengths, low | pair_bit, 1)])
        all_lengths = all_lengths.reshape(blocks, -1)
        doc_ids, offsets = jax.vmap(lambda row: layout(row, row_count))(all_lengths)
        cos, sin = [
            jnp.tile(table.reshape(pair_rows, DR // 2), (1, copies))
            for table in angles(offsets, DR)
        ]
        all_rows = dp_gather(all_rows).transpose(1, 0, 2, 3).reshape(pair_rows, width)
        by_head = jnp.concatenate(by_head, axis=1)
        q_full = spread(by_head.reshape(width, head_cols))
        kv_up = by_head[..., q_cols:].reshape(expert_count, dp_count, n_kv_gain, -1)
        kv_up = kv_up.transpose(1, 0, 2, 3).reshape(KVR, heads * (DH + DV))
        out_full = jnp.concatenate(out_parts, axis=1)
        at = bits.index(pair_bit)
        out_full = out_full.reshape((2,) * len(bits) + (-1, slice_rows, head_cols))
        out_full = jnp.moveaxis(out_full, (len(bits), at), (-3, -2)).reshape(heads * DV, width)
        wide = nope_cols + 2 * ROPE_LANES
        outs = by_rows_call(
            functools.partial(attend_kernel, heads),
            pair_rows,
            4 * row_count,
            dict(
                x=all_rows,
                cos=cos,
                sin=sin,
                column=doc_ids.reshape(pair_rows, 1),
                row=doc_ids.reshape(blocks, 1, row_count),
            ),
            dict(
                gain=attn_scale.astype(f32)[None],
                kv_gain=kv_scale.astype(f32)[None],
                down=kv_down,
                q=q_full,
                up=kv_up,
                out=out_full,
            ),
            (
                ((pair_rows, width), bf16),
                ((pair_rows, KVR + 2 * ROPE_LANES), f32),
                ((pair_rows, KVR), bf16),
                ((pair_rows, wide), bf16),
                ((pair_rows, wide), bf16),
                ((pair_rows, heads * DV), bf16),
                ((blocks * heads, row_count, row_count), f32),
                ((pair_rows, heads * DV), bf16),
                ((pair_rows, width), bf16),
            ),
            order=("x", "gain", "kv_gain", "down", "q", "up", "out", "cos", "sin", "column", "row"),
        )
        return outs, (q_full, kv_up, out_full, kv_down), (attn_scale, kv_scale, ffn_scale), (cos, sin)

    def cut_out(found):
        at = bits.index(pair_bit)
        found = found.reshape((2,) * len(rest) + (slice_rows, -1, 2, head_cols))
        found = jnp.moveaxis(found, (-3, -2), (len(bits), at))
        return found.reshape(expert_count, -1, head_cols)

    def by_owner(found):
        found = found.reshape(2, dp_count, row_count, -1).transpose(1, 0, 2, 3)
        return dp_scatter(found, bf16).astype(bf16)

    (all_rows, by_head), (shared_split,) = march(
        gathering(turned(tokens), [pair_bit]),
        pair_swapping(by_head, pair_bit, 1),
        jobs=((shared_by_unit, shared_gate_up),),
    )
    by_head = by_head.reshape(2, head_rows, head_cols)
    held_grad = []
    results, found = march(
        *(
            gathering(part, order, [pair_bit])
            for part, order in (
                (by_head[:, :head_cut], (second, far, first)),
                (by_head[:, head_cut:], (far, first, second)),
                (out_cut[:, :out_mid], (second, first, far)),
                (out_cut[:, out_mid:], (far, second, first)),
            )
        ),
        gathering(small, (far, first, second, pair_bit)),
        jobs=((skip,), (skip,), (lambda results, found, part: held_grad.append(part), out_grad)),
    )

    grad_all = lax.all_gather(held_grad[0], "expert")
    outs, weights, scales, tables = attend(all_rows, results[4], results[:2], results[2:4])
    normed, joint, kv_normed, query_parts, key_parts, values, probs, attended, attended_sum = outs
    q_full, kv_up, out_full, kv_down = weights
    attn_scale, kv_scale, ffn_scale = scales
    attended_sum = by_owner(attended_sum)
    shared_w, shared_out = shared_weights(shared_split, shared_down)
    hidden = down_w.shape[0]
    gates_all = results[4][:, slice_rows:gain_row, :gate_cols]
    gates_all = gates_all.reshape(expert_count, expert_count, 2, row_count)
    own_gate = pick(gates_all, me, 1).astype(f32).sum(axis=1)

    capacity = min(row_count, 3 * row_count * TOP // (2 * expert_count))
    slots = expert_count * capacity
    group_rows = expert_count * row_count
    grad_rows = grad_all.reshape(group_rows, width)

    def choose(results, found, own_gate, grad_all):
        live = own_gate > 0.0
        place = jnp.cumsum(live.astype(jnp.int32), axis=1) - 1
        chosen = jnp.arange(capacity, dtype=jnp.int32)[None, :, None] == place[:, None, :]
        chosen = chosen & live[:, None, :]
        slot_gate = jnp.sum(jnp.where(chosen, own_gate[:, None, :], 0.0), axis=2)
        slot_gate = slot_gate.reshape(slots, 1)
        chosen = chosen.astype(bf16)
        slot_grad = jnp.einsum("rst,rtd->rsd", chosen, grad_all, preferred_element_type=f32)
        return chosen, slot_gate, (slot_grad.reshape(slots, width) * slot_gate).astype(bf16)

    (attended_sum,), ((chosen, slot_gate, slot_grad),) = march(
        scattering(attended_sum, [pair_bit], [pair_bit]), jobs=((choose, own_gate, grad_all),)
    )
    resid_in = tokens.astype(f32)
    upstream = out_grad.astype(f32)
    resid = resid_in + attended_sum
    ffn_in = norm_apply(resid, ffn_scale).astype(bf16)

    def back_hidden(results, found, slot_grad, matrix):
        return dot(slot_grad, matrix.T)

    ffn_parts, (d_hidden, d_shared_hidden, *unused) = march(
        *(gathering(part, order) for part, order in zip(column_parts(ffn_in), orders)),
        jobs=((back_hidden, slot_grad, down_w), (back_hidden, grad_rows, shared_out)),
    )
    ffn_all = jnp.concatenate(ffn_parts, axis=-1)
    ffn_rows = ffn_all.reshape(group_rows, width)
    rows = jnp.einsum("rst,rtd->rsd", chosen, ffn_all, preferred_element_type=f32)
    rows = rows.reshape(slots, width).astype(bf16)
    pair = dot(rows, pair_w)
    gate_part, up_part = pair[:, :hidden], pair[:, hidden:]
    expert_hidden = swish_gate(gate_part, up_part).astype(bf16)
    d_pair = swish_back(gate_part, up_part, d_hidden).astype(bf16)
    shared_pair = dot(ffn_rows, shared_w)
    shared_gate, shared_up = shared_pair[:, :padded], shared_pair[:, padded:]
    shared_hidden = swish_gate(shared_gate, shared_up).astype(bf16)
    d_shared_pair = swish_back(shared_gate, shared_up, d_shared_hidden).astype(bf16)

    def to_tokens(slot_rows, shared_rows, shared_matrix):
        back = jnp.einsum(
            "rst,rsd->rtd",
            chosen,
            slot_rows.reshape(expert_count, capacity, -1),
            preferred_element_type=f32,
        )
        back = back.reshape(group_rows, -1) + dot(shared_rows, shared_matrix)
        return back.astype(bf16).reshape(expert_count, row_count, -1)

    d_rows = dot(d_pair, pair_w.T).astype(bf16)
    d_parts = [
        to_tokens(d_rows[:, low:high], d_shared_pair, shared_w[low:high].T) for low, high in parts
    ]

    kept_rows = (expert_hidden, d_pair, rows, shared_hidden, d_shared_pair, slot_grad)
    (expert_hidden, d_pair, rows, shared_hidden, d_shared_pair, slot_grad) = after(
        kept_rows, d_parts
    )

    def output_part(results, found, expert_hidden, shared_hidden):
        down = (dot(expert_hidden, down_w) * slot_gate).astype(bf16)
        return to_tokens(down, shared_hidden, shared_out)

    def halves(found):
        if dp_count != 2:
            return lax.psum_scatter(found.astype(bf16), "dp", scatter_dimension=0), ()
        return pick(found, core, 0), pick(found, 1 - core, 0).astype(bf16)

    def exchanged(kept, sent):
        if dp_count != 2:
            return kept.astype(f32)
        return kept + lax.ppermute(sent, "dp", [(0, 1), (1, 0)]).astype(f32)

    def pair_gradient(place, rows, d_pair):
        rows = pick(rows.reshape(slots, dp_count, -1), place, 1)
        return dot(rows.T, d_pair)

    def pair_kept(results, found, rows, d_pair):
        if dp_count != 2:
            found = dot(rows.T, d_pair).astype(bf16).reshape(dp_count, width // dp_count, -1)
            return lax.psum_scatter(found, "dp", scatter_dimension=0)
        return pair_gradient(core, rows, d_pair)

    def pair_sent(results, found, rows, d_pair):
        if dp_count != 2:
            return ()
        return pair_gradient(1 - core, rows, d_pair).astype(bf16)

    def down_gradient(results, found, expert_hidden, slot_grad):
        return halves(
            dot(expert_hidden.T, slot_grad).reshape(dp_count, hidden // dp_count, width)
        )

    def shared_gradient(results, found, shared_hidden, d_shared_pair):
        down = dot(shared_hidden.T, grad_rows)[:units].reshape(dp_count, share, width)
        both = dot(ffn_rows.T, d_shared_pair)
        both = both.reshape(dp_count, expert_count, slice_rows, 2 * padded)
        return dp_scatter(down, bf16), dp_scatter(both, bf16).astype(bf16)

    d_sums, found = march(
        *(scattering(part, order[::-1], bits) for part, order in zip(d_parts, orders)),
        jobs=(
            (pair_sent, rows, d_pair),
            (down_gradient, expert_hidden, slot_grad),
            (shared_gradient, shared_hidden, d_shared_pair),
            (output_part, expert_hidden, shared_hidden),
        ),
    )
    sent, down_halves, (grad_shared_out, grad_shared), out_part = found
    rows, d_pair = after((rows, d_pair), d_sums)
    d_ffn_in = jnp.concatenate(d_sums, axis=-1)

    d_norm_resid, grad_ffn_scale = norm_back(resid, ffn_scale, d_ffn_in)
    d_resid = upstream + d_norm_resid
    (d_branch,), (kept,) = march(
        gathering(d_resid.astype(bf16), [pair_bit]), jobs=((pair_kept, rows, d_pair),)
    )
    pair_halves = (kept, sent)

    def attend_back(results, found, d_branch):
        d_branch = dp_gather(d_branch).transpose(1, 0, 2, 3).reshape(pair_rows, width)
        steps = pair_rows // (4 * row_count)
        wide = nope_cols + 2 * ROPE_LANES
        outs = by_rows_call(
            functools.partial(attend_back_kernel, heads),
            pair_rows,
            4 * row_count,
            dict(
                branch=d_branch,
                probs=probs,
                heads=query_parts,
                keys=key_parts,
                values=values,
                joint=joint,
                cos=tables[0],
                sin=tables[1],
            ),
            dict(
                out=out_full,
                kv_gain=kv_scale.astype(f32)[None],
                up=kv_up,
                q=q_full,
                down=kv_down,
            ),
            (
                ((pair_rows, wide), bf16),
                ((pair_rows, heads * (DH + DV)), bf16),
                ((pair_rows, KVR + 2 * ROPE_LANES), bf16),
                ((steps, 1, KVR), f32),
                ((pair_rows, width), bf16),
            ),
            scratch=[pltpu.VMEM((4 * row_count, 2 * ROPE_LANES), f32)],
            order=(
                "branch", "out", "probs", "heads", "keys", "values", "joint", "kv_gain", "up", "q",
                "down", "cos", "sin",
            ),
        )
        return d_branch, outs

    def back_sum(results, found):
        return by_owner(found[0][1][4])

    def weight_gradients(results, found):
        d_branch, (d_q_heads, d_kv_heads, d_joint, unused, unused) = found[0]
        grad_q = unspread(dot(normed.T, d_q_heads)).astype(bf16)
        grad_q = grad_q.reshape(expert_count, head_rows, q_cols)
        grad_up = dot(kv_normed.T, d_kv_heads).astype(bf16)
        grad_up = grad_up.reshape(dp_count, expert_count, n_kv_gain, -1).transpose(1, 0, 2, 3)
        grad_up = grad_up.reshape(expert_count, head_rows, up_cols)
        by_head = jnp.concatenate([grad_q, grad_up], axis=-1)
        grad_out = cut_out(dot(attended.T, d_branch).astype(bf16))
        grad_kvdown = dot(normed.T, d_joint)
        rotary = grad_kvdown[:, KVR:].reshape(width, 2, -1, DR // 2).sum(axis=2)
        grad_kvdown = jnp.concatenate([grad_kvdown[:, :KVR], rotary.reshape(width, DR)], axis=-1)
        grad_kvdown = grad_kvdown.reshape(expert_count, dp_count, slice_rows, joint_width)
        return by_head, grad_out, dp_scatter(grad_kvdown.transpose(1, 0, 2, 3), bf16)

    results, found = march(
        *(
            scattering(part, order[::-1], bits)
            for part, order in zip(column_parts(out_part), orders)
        ),
        jobs=((attend_back, d_branch), (back_sum,), (weight_gradients,)),
    )
    output = (resid + jnp.concatenate(results, axis=-1)).astype(bf16)
    grad_heads, grad_out, grad_kvdown = found[2]
    d_normed = found[1]
    grad_kv_scale = found[0][1][3].sum(axis=0)
    d_normed = alone(scattering(d_normed, [pair_bit], [pair_bit]))
    pair_halves, down_halves, grad_shared = after((pair_halves, down_halves, grad_shared), results)
    d_norm_in, grad_attn_scale = norm_back(turned(resid_in), attn_scale, d_normed)
    grad_in = (d_resid + turned_back(d_norm_in)).astype(bf16)
    scale_sums = jnp.concatenate(
        [
            grad_attn_scale.reshape(expert_count, dp_count, n_gain).transpose(1, 0, 2),
            grad_ffn_scale.reshape(dp_count, expert_count, n_gain),
            grad_kv_scale.reshape(dp_count, expert_count, n_kv_gain),
        ],
        axis=-1,
    )
    scale_sums = jnp.pad(scale_sums, ((0, 0), (0, 0), (0, joint_width - scale_sums.shape[-1])))
    scale_sums = dp_scatter(scale_sums)[:, None]
    small_sums = jnp.concatenate([grad_kvdown, scale_sums], axis=1).astype(bf16)

    def finish_pair(results, found, kept, sent):
        return exchanged(kept, sent).reshape(expert_gate_up.shape)

    def finish_down(results, found, kept, sent, shared):
        shared = lax.all_to_all(shared, "expert", split_axis=0, concat_axis=0, tiled=True)
        return exchanged(kept, sent).reshape(expert_down.shape), shared

    def finish_shared(results, found):
        both = found[1][1].reshape(expert_count, slice_rows, 2, padded)[..., :units]
        both = both.reshape(expert_count, slice_rows, 2, dp_count, share)
        return both.transpose(1, 2, 3, 0, 4).reshape(shared_gate_up.shape).astype(f32)

    def whole_heads(found, rows, *widths):
        cuts = [heads * sum(widths[: i + 1]) for i in range(len(widths) - 1)]
        lead = (dp_count, 2, rows, head_high, head_low, -1)
        found = jnp.concatenate(
            [part.reshape(lead) for part in jnp.split(found, cuts, axis=-1)], axis=-1
        )
        return found.transpose(2, 0, 3, 1, 4, 5).reshape(rows, -1).astype(f32)

    summed, found = march(
        scattering(small_sums, (pair_bit, second, first, far), bits),
        *(
            scattering(part, order, bits, bf16)
            for part, order in (
                (grad_heads[:, :head_cut], (first, far, second)),
                (grad_heads[:, head_cut:], (second, first, far)),
                (grad_out[:, :out_mid], (far, first, second)),
                (grad_out[:, out_mid:], (first, second, far)),
            )
        ),
        jobs=(
            (finish_pair, *pair_halves),
            (finish_down, *down_halves, grad_shared),
            (finish_shared,),
        ),
    )
    grad_pair, (grad_down, unused), grad_shared = found[:3]
    by_head = jnp.concatenate(summed[1:3], axis=1)
    by_head = alone(pair_swapping(by_head, pair_bit, 0)).reshape(2, dp_count, slice_rows, head_cols)
    by_head = dp_swap(by_head.transpose(1, 0, 2, 3))
    grad_q = whole_heads(by_head[..., :q_cols], slice_rows, DH, DR // 2, DR // 2)
    grad_up = by_head[..., q_cols:].reshape(dp_count, 2, n_kv_gain, -1)
    grad_up = whole_heads(grad_up, n_kv_gain, DH + DV)
    grad_out = jnp.concatenate(summed[3:5], axis=1).reshape(2, -1, slice_rows, head_cols)
    grad_out = grad_out.transpose(2, 1, 0, 3).reshape(out_weight.shape).astype(f32)
    small_sums = summed[0]
    grad_kvdown = small_sums[:slice_rows]
    scale_sums = small_sums[slice_rows]

    return (
        output,
        grad_in,
        scale_sums[:n_gain],
        scale_sums[2 * n_gain : 2 * n_gain + n_kv_gain],
        scale_sums[n_gain : 2 * n_gain],
        grad_q,
        grad_kvdown,
        grad_up,
        grad_out,
        grad_shared,
        grad_shared_out,
        grad_pair,
        grad_down,
    )


def solution(mesh):
    rows = P(SPLIT, None)
    each = P(SPLIT)
    cube = P(SPLIT, None, None)
    pair = P("expert", "dp", None, None)
    down = P("expert", "dp", None)
    dense = (rows, rows, rows, rows, cube, rows)
    return jax.shard_map(
        shards,
        mesh=mesh,
        in_specs=(rows, each, each, each) + dense + (pair, down, rows, rows, rows, rows),
        out_specs=(rows, rows, each, each, each) + dense + (pair, down),
        check_vma=False,
    )
```

time: 1090 us -> 971 us (0.89)
  waiting for transfers between devices: 424 us -> 221 us
  local copies, waits for them, and re-layouts: 207 us -> 247 us
  Pallas kernels: 0 us -> 34.9 us
  between operations: 4.66 us -> 17.1 us
    ppermute x80 -> x74, waiting for transfers between devices: 391 us -> 218 us  [partner(): return lax.ppermute(values, 'expert', [(i, i ^ bit) for i in range(count)])]
    pallas_call x0 -> x2, Pallas kernels: none -> 34.9 us  [by_rows_call(): pl.pallas_call(kernel, grid=(steps,), in_specs=specs, out_specs=out_specs...]
    all_to_all x2, waiting for transfers between devices: 32.4 us -> 0.71 us  [the longest x1 0.71 us: finish_down(): lax.all_to_all(shared, 'expert', split_axis=0, concat_axis=0, tiled=True)]
    another operation x15 -> x8, other arithmetic: 28.6 us -> 7.98 us  [dp_gather(): jnp.stack([jnp.where(first, values, other), jnp.where(first, other, value...]
    dynamic_slice x13 -> x21, local copies, waits for them, and re-layouts: 15.4 us -> 35.6 us  [pick(): return lax.dynamic_index_in_dim(values, place, axis, keepdims=False)]
    ppermute x80 -> x74, starting transfers between devices: 61.9 us -> 77.8 us  [partner(): return lax.ppermute(values, 'expert', [(i, i ^ bit) for i in range(count)])]
    optimization_barrier x0 -> x3, local copies, waits for them, and re-layouts: none -> 14.1 us  [the longest x2 13.5 us: after(): return lax.optimization_barrier((values, others))[0]]
    add x8 -> x7, other arithmetic: 0.4 us -> 13.7 us  [the longest x1 11.2 us: exchanged(): return kept + lax.ppermute(sent, 'dp', [(0, 1), (1, 0)]).astype(f32)]
  transfers between devices with their start and end apart: 102 -> 95, of which waited for: 45 -> 28; matrix products, arithmetic and copies ran while one was open for 41% -> 48% of each run, Pallas kernels for 0% -> 4%
where the time goes in v2:
time: 971 us; the launch traced here: 958 us
  local copies, waits for them, and re-layouts  247 us (25%)
  waiting for transfers between devices  221 us (23%)
  matrix products  168 us (17%)
  other arithmetic  162 us (17%)
  starting transfers between devices  109 us (11%)
  Pallas kernels  34.9 us (4%)
  between operations  17.1 us (2%)
    ppermute x74, waiting for transfers between devices, partner(): return lax.ppermute(values, 'expert', [(i, i ^ bit) for i in range(count)])  218 us
    dot_general x19, matrix products, dot(): return jnp.dot(left, right, preferred_element_type=f32)  142 us
    ppermute x74, starting transfers between devices, partner(): return lax.ppermute(values, 'expert', [(i, i ^ bit) for i in range(count)])  77.8 us
    unnamed x348, local copies, waits for them, and re-layouts  47.5 us
    another operation x56, other arithmetic, gathering(): jnp.stack([jnp.where(low, values, other), jnp.where(low, other, values)],...  44.4 us
    dynamic_slice x21, local copies, waits for them, and re-layouts, pick(): return lax.dynamic_index_in_dim(values, place, axis, keepdims=False)  35.6 us
    pallas_call x2, Pallas kernels, by_rows_call(): pl.pallas_call(kernel, grid=(steps,), in_specs=specs, out_specs=out_specs...  34.9 us
    convert_element_type x33, other arithmetic, scattering(): values = values.astype(kept if step + 1 == len(order) else bf16)  34.2 us
  transfers between devices with their start and end apart: 95, of which 28 were waited for; matrix products, arithmetic and copies ran while one was open for 48% of the time, Pallas kernels for 4%

profile of v2, /device:TPU:1, one launch (start us, length us, event | category | flops | bytes accessed | tf_op | source)
XLA Modules:
  0.0 958.3 jit_solution(6838175264668968331)
XLA Ops:
  35.8 17.3 %collective-permute-done.8 = bf16[80,576]{1,0:T(8,128)(2,1)S(1)} collective-permute-done((bf16[80,576]{1,0:T(8,128)(2,1)S(1)}, bf16[80,576]{1,0:T(8,128)(2,1)S(1)}, u32[]{:S(2)}, u32[]{:S(2)}) %collective-permute-start.8) | collective-permute-done | bytes 92192 | tf_op jit(solution)/shard_map/ppermute | solution.py:119
  59.9 18.8 %collective-permute-done.13 = bf16[2,80,576]{2,1,0:T(8,128)(2,1)S(1)} collective-permute-done((bf16[2,80,576]{2,1,0:T(8,128)(2,1)S(1)}, bf16[2,80,576]{2,1,0:T(8,128)(2,1)S(1)}, u32[]{:S(2)}, u32[]{:S(2)}) %collective-permute-start.13) | collective-permute-done | bytes 184352 | tf_op jit(solution)/shard_map/ppermute | solution.py:119
  83.9 6.2 copy.722
  111.4 33.6 %collective-permute-done.18 = bf16[2,2,80,576]{3,2,1,0:T(8,128)(2,1)} collective-permute-done((bf16[2,2,80,576]{3,2,1,0:T(8,128)(2,1)}, bf16[2,2,80,576]{3,2,1,0:T(8,128)(2,1)}, u32[]{:S(2)}, u32[]{:S(2)}) %collective-permute-start.18) | collective-permute-done | bytes 368672 | tf_op jit(solution)/shard_map/ppermute | solution.py:119
  146.4 4.4 collective-permute-start.19
  166.7 23.4 %collective-permute-done.19 = bf16[2,2,2,80,576]{4,3,2,1,0:T(8,128)(2,1)S(1)} collective-permute-done((bf16[2,2,2,80,576]{4,3,2,1,0:T(8,128)(2,1)S(1)}, bf16[2,2,2,80,576]{4,3,2,1,0:T(8,128)(2,1)S(1)}, u32[]{:S(2)}, u32[]{:S(2)}) %collective-permute-start.19) | collective-permute-done | bytes 737312 | tf_op jit(solution)/shard_map/ppermute | solution.py:119
  206.8 7.2 concatenate.86.down_ref
  214.0 16.8 %shard_map.255 = (bf16[512,2048]{1,0:T(8,128)(2,1)}, f32[512,768]{1,0:T(8,128)}, bf16[512,512]{1,0:T(8,128)(2,1)}, bf16[512,768]{1,0:T(8,128)(2,1)}, bf16[512,76...) custom-call(bf16[512,2048]{1,0:T(8,128)(2,1)} %bitcast.770, ...), custom_call_target="tpu_custom_call" | custom-call | tf_op jit(solution)/shard_map/pallas_call | solution.py:413
  237.0 3.9 all-to-all-start
  248.4 6.8 fusion.100
  258.3 13.0 %collective-permute-done.23 = bf16[128,2048]{0,1:T(8,128)(2,1)S(1)} collective-permute-done((bf16[128,2048]{0,1:T(8,128)(2,1)}, bf16[128,2048]{0,1:T(8,128)(2,1)S(1)}, u32[]{:S(2)}, u32[]{:S(2)}) %collective-permute-start.23) | collective-permute-done | bytes 524320 | tf_op jit(solution)/shard_map/ppermute | solution.py:119
  277.9 13.1 %fusion.15 = f32[1152,1408]{1,0:T(8,128)} fusion(bf16[1152,2048]{1,0:T(8,128)(2,1)} %fusion.1, bf16[1,1408,2048]{2,1,0:T(8,128)(2,1)} %all-gather.10.cloned.1.call-done), kind=kOutput, calls=%fused_computation.29 | convolution fusion | flops 6643777536 | bytes 16973824 | tf_op jit(solution)/shard_map/dot_general | solution.py:74
  295.7 7.1 fusion.180
  302.8 7.0 collective-permute-done.28
  316.7 8.4 collective-permute-done.31
  343.5 15.6 %collective-permute-done.34 = bf16[2,2,2,128,640]{3,4,1,0,2:T(8,128)(2,1)} collective-permute-done((bf16[2,2,2,128,640]{3,4,1,0,2:T(8,128)(2,1)}, bf16[2,2,2,128,640]{3,4,1,0,2:T(8,128)(2,1)}, u32[]{:S(2)}, u32[]{:S(2)}) %collective-permute-start.34) | collective-permute-done | bytes 1310752 | tf_op jit(solution)/shard_map/ppermute | solution.py:119
  359.1 7.5 collective-permute-done.36
  384.4 4.4 copy.641
  388.8 4.8 fusion.19
  393.6 19.2 %fusion.181 = f32[1152,2816]{1,0:T(8,128)S(1)} fusion(bf16[1152,2048]{1,0:T(8,128)(2,1)} %bitcast.724, bf16[2048,2816]{1,0:T(8,128)(2,1)} %all-gather.6.cloned.1.call-done), kind=kOutput, calls=%fused_computation.518 | convolution fusion | flops 13287555072 | bytes 29229056 | tf_op jit(solution)/shard_map/dot_general | solution.py:74
  412.8 7.3 fusion.11
  420.1 18.2 %convolution_convert_fusion = bf16[1152,2048]{1,0:T(8,128)(2,1)} fusion(bf16[2048,2816]{1,0:T(8,128)(2,1)} %all-gather.6.cloned.1.call-done, bf16[1152,1408]{1,0:T(8,128)(2,1)S(1)} %get-tuple-element.403, bf16[1152,1408]{1,0:T(8,128)(2,1)S(1)} %get-tuple-element.402), kind=kOutput, calls=%fused_computation.15 | convolution fusion | flops 13302890496 | bytes 22740992 | tf_op jit(solution)/shard_map/dot_general | solution.py:74
  450.2 3.9 fusion.22
  454.1 4.5 fusion.23
  489.2 6.8 copy.653
  501.9 12.3 %copy.657 = bf16[2048,2048]{1,0:T(8,128)(2,1)} copy(bf16[2048,2048]{0,1:T(8,128)(2,1)} %fusion.22) | data formatting | bytes 16777216 | tf_op jit(solution)/shard_map/dot_general | solution.py:74
  514.2 13.1 %convolution_convert_fusion.1 = bf16[1024,2816]{1,0:T(8,128)(2,1)} fusion(bf16[1152,2816]{1,0:T(8,128)(2,1)} %pad_maximum_fusion.1, bf16[1152,2,1024]{0,2,1:T(8,128)(2,1)} %bitcast.793, s32[]{:T(128)S(6)} %select_n.639), kind=kOutput, calls=%fused_computation.34 | convolution fusion | flops 6646661120 | bytes 14614532 | tf_op jit(solution)/shard_map/dot_general | solution.py:74
  536.9 7.8 fusion.185
  555.9 4.7 fusion.46
  560.8 6.3 collective-permute-start.48
  573.0 5.1 collective-permute-done.46
  581.1 7.9 fusion.8
  589.0 8.3 fusion.186
  597.4 11.4 %fusion = bf16[2048,2048]{1,0:T(8,128)(2,1)} fusion(f32[16,128,2048]{2,1,0:T(8,128)} %fusion.186, bf16[2048,256]{1,0:T(8,128)(2,1)S(1)} %get-tuple-element.223, bf16[176,2048]{1,0:T(8,128)(2,1)S(1)} %bitcast.785), kind=kOutput, calls=%fused_computation.1 | convolution fusion | flops 2155872256 | bytes 26935296 | tf_op jit(solution)/shard_map/dot_general | solution.py:74
  613.0 6.7 copy.663
  619.8 13.5 %fusion.37 = f32[1024,2816]{1,0:T(8,128)} fusion(bf16[1152,2816]{1,0:T(8,128)(2,1)} %pad_maximum_fusion.1, bf16[1152,2,1024]{0,2,1:T(8,128)(2,1)} %bitcast.794, s32[]{:T(128)S(6)} %select_n.638), kind=kOutput, calls=%fused_computation.76 | convolution fusion | flops 6643777536 | bytes 20381700 | tf_op jit(solution)/shard_map/dot_general | solution.py:74
  635.4 5.7 fusion.173
  674.5 18.0 %shard_map.256 = (bf16[512,768]{1,0:T(8,128)(2,1)}, bf16[512,1024]{1,0:T(8,128)(2,1)}, bf16[512,768]{1,0:T(8,128)(2,1)}, f32[1,1,512]{2,1,0:T(1,128)}, bf16[512,2048]{1,0:T(8,128)(2,1)}) custom-call(bf16[512,2048]{1,0:T(8,128)(2,1)} %bitcast.760, bf16[512,2048]{1,0:T(8,128)(2,1)} %bitcast.728, f32[16,128,128]{2,1,0:T(8,128)} %get-tuple-element.231.probs_ref, ...), custom_call_target="tpu_custom_call" | custom-call | tf_op jit(solution)/shard_map/pallas_call | solution.py:413
  721.2 4.8 convolution_convert_fusion.3
  754.5 11.7 %collective-permute-done.61 = bf16[2,128,640]{1,2,0:T(8,128)(2,1)S(1)} collective-permute-done((bf16[2,128,640]{1,2,0:T(8,128)(2,1)S(1)}, bf16[2,128,640]{1,2,0:T(8,128)(2,1)S(1)}, u32[]{:S(2)}, u32[]{:S(2)}) %collective-permute-start.61) | collective-permute-done | bytes 327712 | tf_op jit(solution)/shard_map/ppermute | solution.py:119
  773.4 14.6 %collective-permute-done.67 = bf16[128,640]{0,1:T(8,128)(2,1)S(1)} collective-permute-done((bf16[128,640]{0,1:T(8,128)(2,1)S(1)}, bf16[128,640]{0,1:T(8,128)(2,1)S(1)}, u32[]{:S(2)}, u32[]{:S(2)}) %collective-permute-start.67) | collective-permute-done | bytes 163872 | tf_op jit(solution)/shard_map/ppermute | solution.py:119
  816.9 11.2 %convert_add_fusion = f32[1024,2816]{1,0:T(8,128)} fusion(f32[1024,2816]{1,0:T(8,128)} %fusion.37, bf16[1024,2816]{1,0:T(8,128)(2,1)} %collective-permute-done.75), kind=kLoop, calls=%fused_computation.2 | loop fusion | flops 5767168 | bytes 28835840 | tf_op jit(solution)/shard_map/add | solution.py:738
  828.1 14.3 %reshape.657 = f32[1,1024,2,1408]{3,2,1,0:T(2,128)} reshape(f32[1024,2816]{1,0:T(8,128)} %convert_add_fusion) | data formatting | bytes 23068672 | tf_op jit(solution)/shard_map/reshape | solution.py:872
  859.0 4.7 all-to-all-start.1
  871.8 5.2 add_bitcast_fusion
  877.0 16.9 %collective-permute-done.79 = bf16[2,2,32,1024]{3,2,1,0:T(8,128)(2,1)S(1)} collective-permute-done((bf16[2,2,32,1024]{3,2,1,0:T(8,128)(2,1)S(1)}, bf16[2,2,32,1024]{3,2,1,0:T(8,128)(2,1)S(1)}, u32[]{:S(2)}, u32[]{:S(2)}) %collective-permute-start.79) | collective-permute-done | bytes 262176 | tf_op jit(solution)/shard_map/ppermute | solution.py:119
  913.5 4.7 reshape.715
  931.7 4.4 collective-permute-start.88
  (871 shorter events, 448.8 us)
Async XLA Ops:
  7.2 241.3 %all-gather.8.cloned.1.call-start = ((), (), s32[]{:S(2)}) async-start(), calls=%async_computation.3 | async-start | bytes 8912896 | tf_op jit(solution)/shard_map/all_gather | solution.py:650
  16.0 37.1 %collective-permute-start.6 = (bf16[2,32,1024]{2,0,1:T(2,128)(2,1)}, bf16[2,32,1024]{2,0,1:T(2,128)(2,1)}, u32[]{:S(2)}, u32[]{:S(2)}) collective-permute-start(bf16[2,32,1024]{2,0,1:T(2,128)(2,1)} %get-tuple-element.527), channel_id=1, source_target_pairs={{0,2},{1,3},{2,0},{3,1},{4,6},{5,7},{6,4},{7,5},{8,10},{9,11},{10,... | collective-permute-start | bytes 393224 | tf_op jit(solution)/shard_map/ppermute | solution.py:119
  17.3 35.8 %collective-permute-start.7 = (bf16[2,32,1024]{2,0,1:T(2,128)(2,1)}, bf16[2,32,1024]{2,0,1:T(2,128)(2,1)}, u32[]{:S(2)}, u32[]{:S(2)}) collective-permute-start(bf16[2,32,1024]{2,0,1:T(2,128)(2,1)} %get-tuple-element.526), channel_id=1, source_target_pairs={{0,8},{1,9},{2,10},{3,11},{4,12},{5,13},{6,14},{7,15},{8,0},{9,1},... | collective-permute-start | bytes 393224 | tf_op jit(solution)/shard_map/ppermute | solution.py:119
  53.2 25.5 %collective-permute-start.9 = (bf16[2,2,48,1024]{3,2,0,1:T(8,128)(2,1)S(1)}, bf16[2,2,48,1024]{3,2,0,1:T(8,128)(2,1)S(1)}, u32[]{:S(2)}, u32[]{:S(2)}) collective-permute-start(bf16[2,2,48,1024]{3,2,0,1:T(8,128)(2,1)S(1)} %pad_maximum_fusion.32), channel_id=1, source_target_pairs={{0,8},{1,9},{2,10},{3,11},{4,12},{5,13},{6,14},{7,15},{8,0},{9,1},... | collective-permute-start | bytes 1179656 | tf_op jit(solution)/shard_map/ppermute | solution.py:119
  53.8 26.5 %collective-permute-start.10 = (bf16[2,2,80,1024]{3,2,1,0:T(8,128)(2,1)S(1)}, bf16[2,2,80,1024]{3,2,1,0:T(8,128)(2,1)}, u32[]{:S(2)}, u32[]{:S(2)}) collective-permute-start(bf16[2,2,80,1024]{3,2,1,0:T(8,128)(2,1)S(1)} %pad_maximum_fusion.25), channel_id=1, source_target_pairs={{0,1},{1,0},{2,3},{3,2},{4,5},{5,4},{6,7},{7,6},{8,9},{9,8},{10,11... | collective-permute-start | bytes 1966088 | tf_op jit(solution)/shard_map/ppermute | solution.py:119
  80.3 197.6 %all-gather.10.cloned.1.call-start = ((), (), s32[]{:S(2)}) async-start(), calls=%async_computation.4 | async-start | bytes 8650752 | tf_op jit(solution)/shard_map/all_gather | solution.py:548
  81.1 312.6 %all-gather.6.cloned.1.call-start = ((), (), s32[]{:S(2)}) async-start(), calls=%async_computation.2 | async-start | bytes 17301504 | tf_op jit(solution)/shard_map/all_gather | solution.py:547
  95.5 49.5 %collective-permute-start.14 = (bf16[2,2,2,48,1024]{4,3,1,2,0:T(8,128)(2,1)}, bf16[2,2,2,48,1024]{4,3,1,2,0:T(8,128)(2,1)}, u32[]{:S(2)}, u32[]{:S(2)}) collective-permute-start(bf16[2,2,2,48,1024]{4,3,1,2,0:T(8,128)(2,1)} %pad_maximum_fusion.22), channel_id=1, source_target_pairs={{0,1},{1,0},{2,3},{3,2},{4,5},{5,4},{6,7},{7,6},{8,9},{9,8},{10,11... | collective-permute-start | bytes 2359304 | tf_op jit(solution)/shard_map/ppermute | solution.py:119
  98.8 46.2 %collective-permute-start.15 = (bf16[2,2,2,80,1024]{4,3,1,0,2:T(8,128)(2,1)}, bf16[2,2,2,80,1024]{4,3,1,0,2:T(8,128)(2,1)}, u32[]{:S(2)}, u32[]{:S(2)}) collective-permute-start(bf16[2,2,2,80,1024]{4,3,1,0,2:T(8,128)(2,1)} %pad_maximum_fusion.15), channel_id=1, source_target_pairs={{0,2},{1,3},{2,0},{3,1},{4,6},{5,7},{6,4},{7,5},{8,10},{9,11},{10,... | collective-permute-start | bytes 3932168 | tf_op jit(solution)/shard_map/ppermute | solution.py:119
  102.2 42.7 %collective-permute-start.16 = (bf16[2,2,2,32,1024]{4,0,3,1,2:T(2,128)(2,1)}, bf16[2,2,2,32,1024]{4,0,3,1,2:T(2,128)(2,1)}, u32[]{:S(2)}, u32[]{:S(2)}) collective-permute-start(bf16[2,2,2,32,1024]{4,0,3,1,2:T(2,128)(2,1)} %pad_maximum_fusion.29), channel_id=1, source_target_pairs={{0,8},{1,9},{2,10},{3,11},{4,12},{5,13},{6,14},{7,15},{8,0},{9,1},... | collective-permute-start | bytes 1572872 | tf_op jit(solution)/shard_map/ppermute | solution.py:119
  106.6 38.4 %collective-permute-start.17 = (bf16[2,2,2,32,1024]{4,1,3,2,0:T(2,128)(2,1)}, bf16[2,2,2,32,1024]{4,1,3,2,0:T(2,128)(2,1)}, u32[]{:S(2)}, u32[]{:S(2)}) collective-permute-start(bf16[2,2,2,32,1024]{4,1,3,2,0:T(2,128)(2,1)} %pad_maximum_fusion.30), channel_id=1, source_target_pairs={{0,1},{1,0},{2,3},{3,2},{4,5},{5,4},{6,7},{7,6},{8,9},{9,8},{10,11... | collective-permute-start | bytes 1572872 | tf_op jit(solution)/shard_map/ppermute | solution.py:119
  107.8 37.1 %collective-permute-start.18 = (bf16[2,2,80,576]{3,2,1,0:T(8,128)(2,1)}, bf16[2,2,80,576]{3,2,1,0:T(8,128)(2,1)}, u32[]{:S(2)}, u32[]{:S(2)}) collective-permute-start(bf16[2,2,80,576]{3,2,1,0:T(8,128)(2,1)} %pad_maximum_fusion.31), channel_id=1, source_target_pairs={{0,2},{1,3},{2,0},{3,1},{4,6},{5,7},{6,4},{7,5},{8,10},{9,11},{10,... | collective-permute-start | bytes 1105928 | tf_op jit(solution)/shard_map/ppermute | solution.py:119
  146.4 43.8 %collective-permute-start.19 = (bf16[2,2,2,80,576]{4,3,2,1,0:T(8,128)(2,1)S(1)}, bf16[2,2,2,80,576]{4,3,2,1,0:T(8,128)(2,1)S(1)}, u32[]{:S(2)}, u32[]{:S(2)}) collective-permute-start(bf16[2,2,2,80,576]{4,3,2,1,0:T(8,128)(2,1)S(1)} %pad_maximum_fusion.21), channel_id=1, source_target_pairs={{0,4},{1,5},{2,6},{3,7},{4,0},{5,1},{6,2},{7,3},{8,12},{9,13},{10,... | collective-permute-start | bytes 2211848 | tf_op jit(solution)/shard_map/ppermute | solution.py:119
  237.0 77.5 %all-to-all-start = ((bf16[16,64,512]{2,1,0:T(8,128)(2,1)}), bf16[16,64,512]{2,1,0:T(8,128)(2,1)S(1)}, u32[]{:S(2)}, u32[]{:S(2)}) async-start(bf16[16,64,512]{2,1,0:T(8,128)(2,1)} %reshape.597), calls=%async_computation | async-start | bytes 2097152 | tf_op jit(solution)/shard_map/all_to_all | solution.py:550
  247.1 24.2 %collective-permute-start.23 = (bf16[128,2048]{0,1:T(8,128)(2,1)}, bf16[128,2048]{0,1:T(8,128)(2,1)S(1)}, u32[]{:S(2)}, u32[]{:S(2)}) collective-permute-start(bf16[128,2048]{0,1:T(8,128)(2,1)} %dynamic-slice_bitcast_fusion.10), channel_id=1, source_target_pairs={{0,4},{1,5},{2,6},{3,7},{4,0},{5,1},{6,2},{7,3},{8,12},{9,13},{10,... | collective-permute-start | bytes 1572872 | tf_op jit(solution)/shard_map/ppermute | solution.py:119
  314.6 25.5 %collective-permute-start.37 = (bf16[16,64,512]{2,1,0:T(8,128)(2,1)S(1)}, bf16[16,64,512]{2,1,0:T(8,128)(2,1)}, u32[]{:S(2)}, u32[]{:S(2)}) collective-permute-start(bf16[16,64,512]{2,1,0:T(8,128)(2,1)S(1)} %all-to-all-done), channel_id=1, source_target_pairs={{0,16},{16,0},{1,17},{17,1},{2,18},{18,2},{3,19},{19,3},{4,20},{20... | collective-permute-start | bytes 3145736 | tf_op jit(solution)/shard_map/ppermute | solution.py:84
  331.9 27.2 %collective-permute-start.34 = (bf16[2,2,2,128,640]{3,4,1,0,2:T(8,128)(2,1)}, bf16[2,2,2,128,640]{3,4,1,0,2:T(8,128)(2,1)}, u32[]{:S(2)}, u32[]{:S(2)}) collective-permute-start(bf16[2,2,2,128,640]{3,4,1,0,2:T(8,128)(2,1)} %pad_maximum_fusion.16), channel_id=1, source_target_pairs={{0,4},{1,5},{2,6},{3,7},{4,0},{5,1},{6,2},{7,3},{8,12},{9,13},{10,... | collective-permute-start | bytes 3932168 | tf_op jit(solution)/shard_map/ppermute | solution.py:119
  334.9 33.2 %collective-permute-start.35 = (bf16[2,2,2,128,768]{3,4,0,2,1:T(8,128)(2,1)}, bf16[2,2,2,128,768]{3,4,0,2,1:T(8,128)(2,1)}, u32[]{:S(2)}, u32[]{:S(2)}) collective-permute-start(bf16[2,2,2,128,768]{3,4,0,2,1:T(8,128)(2,1)} %pad_maximum_fusion.14), channel_id=1, source_target_pairs={{0,2},{1,3},{2,0},{3,1},{4,6},{5,7},{6,4},{7,5},{8,10},{9,11},{10,... | collective-permute-start | bytes 4718600 | tf_op jit(solution)/shard_map/ppermute | solution.py:119
  339.0 27.5 %collective-permute-start.36 = (bf16[2,2,2,128,640]{3,4,0,1,2:T(8,128)(2,1)}, bf16[2,2,2,128,640]{3,4,0,1,2:T(8,128)(2,1)}, u32[]{:S(2)}, u32[]{:S(2)}) collective-permute-start(bf16[2,2,2,128,640]{3,4,0,1,2:T(8,128)(2,1)} %pad_maximum_fusion.17), channel_id=1, source_target_pairs={{0,1},{1,0},{2,3},{3,2},{4,5},{5,4},{6,7},{7,6},{8,9},{9,8},{10,11... | collective-permute-start | bytes 3932168 | tf_op jit(solution)/shard_map/ppermute | solution.py:119
  468.3 58.9 %collective-permute-start.38 = (bf16[2,2,2,128,640]{3,4,1,0,2:T(8,128)(2,1)}, bf16[2,2,2,128,640]{3,4,1,0,2:T(8,128)(2,1)}, u32[]{:S(2)}, u32[]{:S(2)}) collective-permute-start(bf16[2,2,2,128,640]{3,4,1,0,2:T(8,128)(2,1)} %bitcast.820), channel_id=1, source_target_pairs={{0,4},{1,5},{2,6},{3,7},{4,0},{5,1},{6,2},{7,3},{8,12},{9,13},{10,... | collective-permute-start | bytes 3932168 | tf_op jit(solution)/shard_map/ppermute | solution.py:119
  479.3 48.0 %collective-permute-start.39 = (bf16[2,2,2,128,768]{3,4,0,2,1:T(8,128)(2,1)}, bf16[2,2,2,128,768]{3,4,0,2,1:T(8,128)(2,1)}, u32[]{:S(2)}, u32[]{:S(2)}) collective-permute-start(bf16[2,2,2,128,768]{3,4,0,2,1:T(8,128)(2,1)} %bitcast.818), channel_id=1, source_target_pairs={{0,2},{1,3},{2,0},{3,1},{4,6},{5,7},{6,4},{7,5},{8,10},{9,11},{10,... | collective-permute-start | bytes 4718600 | tf_op jit(solution)/shard_map/ppermute | solution.py:119
  489.2 38.1 %collective-permute-start.40 = (bf16[2,2,2,128,640]{3,4,0,1,2:T(8,128)(2,1)}, bf16[2,2,2,128,640]{3,4,0,1,2:T(8,128)(2,1)}, u32[]{:S(2)}, u32[]{:S(2)}) collective-permute-start(bf16[2,2,2,128,640]{3,4,0,1,2:T(8,128)(2,1)} %bitcast.822), channel_id=1, source_target_pairs={{0,1},{1,0},{2,3},{3,2},{4,5},{5,4},{6,7},{7,6},{8,9},{9,8},{10,11... | collective-permute-start | bytes 3932168 | tf_op jit(solution)/shard_map/ppermute | solution.py:119
  578.2 30.5 %collective-permute-start.49 = (bf16[128,640]{0,1:T(8,128)(2,1)S(1)}, bf16[128,640]{0,1:T(8,128)(2,1)S(1)}, u32[]{:S(2)}, u32[]{:S(2)}) collective-permute-start(bf16[128,640]{0,1:T(8,128)(2,1)S(1)} %dynamic-slice_bitcast_fusion.30), channel_id=1, source_target_pairs={{0,2},{1,3},{2,0},{3,1},{4,6},{5,7},{6,4},{7,5},{8,10},{9,11},{10,... | collective-permute-start | bytes 491528 | tf_op jit(solution)/shard_map/ppermute | solution.py:119
  578.5 30.3 %collective-permute-start.50 = (bf16[128,768]{0,1:T(8,128)(2,1)S(1)}, bf16[128,768]{0,1:T(8,128)(2,1)S(1)}, u32[]{:S(2)}, u32[]{:S(2)}) collective-permute-start(bf16[128,768]{0,1:T(8,128)(2,1)S(1)} %dynamic-slice_bitcast_fusion.25), channel_id=1, source_target_pairs={{0,8},{1,9},{2,10},{3,11},{4,12},{5,13},{6,14},{7,15},{8,0},{9,1},... | collective-permute-start | bytes 589832 | tf_op jit(solution)/shard_map/ppermute | solution.py:119
  579.0 29.8 %collective-permute-start.51 = (bf16[128,640]{0,1:T(8,128)(2,1)S(1)}, bf16[128,640]{0,1:T(8,128)(2,1)S(1)}, u32[]{:S(2)}, u32[]{:S(2)}) collective-permute-start(bf16[128,640]{0,1:T(8,128)(2,1)S(1)} %dynamic-slice_bitcast_fusion.29), channel_id=1, source_target_pairs={{0,8},{1,9},{2,10},{3,11},{4,12},{5,13},{6,14},{7,15},{8,0},{9,1},... | collective-permute-start | bytes 491528 | tf_op jit(solution)/shard_map/ppermute | solution.py:119
  612.4 28.7 %collective-permute-start.55 = (bf16[128,2048]{0,1:T(8,128)(2,1)S(1)}, bf16[128,2048]{0,1:T(8,128)(2,1)S(1)}, u32[]{:S(2)}, u32[]{:S(2)}) collective-permute-start(bf16[128,2048]{0,1:T(8,128)(2,1)S(1)} %fusion.170), channel_id=1, source_target_pairs={{0,4},{1,5},{2,6},{3,7},{4,0},{5,1},{6,2},{7,3},{8,12},{9,13},{10,... | collective-permute-start | bytes 1572872 | tf_op jit(solution)/shard_map/ppermute | solution.py:119
  642.3 27.8 %collective-permute-start.56 = (bf16[2,128,2048]{1,2,0:T(8,128)(2,1)}, bf16[2,128,2048]{1,2,0:T(8,128)(2,1)}, u32[]{:S(2)}, u32[]{:S(2)}) collective-permute-start(bf16[2,128,2048]{1,2,0:T(8,128)(2,1)} %pad_maximum_fusion.20), channel_id=1, source_target_pairs={{0,16},{16,0},{1,17},{17,1},{2,18},{18,2},{3,19},{19,3},{4,20},{20... | collective-permute-start | bytes 3145736 | tf_op jit(solution)/shard_map/ppermute | solution.py:84
  648.8 44.4 %collective-permute-start.53 = (bf16[2,2,2,128,768]{3,4,0,2,1:T(8,128)(2,1)}, bf16[2,2,2,128,768]{3,4,0,2,1:T(8,128)(2,1)}, u32[]{:S(2)}, u32[]{:S(2)}) collective-permute-start(bf16[2,2,2,128,768]{3,4,0,2,1:T(8,128)(2,1)} %bitcast.817), channel_id=1, source_target_pairs={{0,2},{1,3},{2,0},{3,1},{4,6},{5,7},{6,4},{7,5},{8,10},{9,11},{10,... | collective-permute-start | bytes 4718600 | tf_op jit(solution)/shard_map/ppermute | solution.py:119
  656.1 36.3 %collective-permute-start.52 = (bf16[2,2,2,128,640]{3,4,1,0,2:T(8,128)(2,1)}, bf16[2,2,2,128,640]{3,4,1,0,2:T(8,128)(2,1)}, u32[]{:S(2)}, u32[]{:S(2)}) collective-permute-start(bf16[2,2,2,128,640]{3,4,1,0,2:T(8,128)(2,1)} %bitcast.819), channel_id=1, source_target_pairs={{0,4},{1,5},{2,6},{3,7},{4,0},{5,1},{6,2},{7,3},{8,12},{9,13},{10,... | collective-permute-start | bytes 3932168 | tf_op jit(solution)/shard_map/ppermute | solution.py:119
  663.0 30.1 %collective-permute-start.54 = (bf16[2,2,2,128,640]{3,4,0,1,2:T(8,128)(2,1)}, bf16[2,2,2,128,640]{3,4,0,1,2:T(8,128)(2,1)}, u32[]{:S(2)}, u32[]{:S(2)}) collective-permute-start(bf16[2,2,2,128,640]{3,4,0,1,2:T(8,128)(2,1)} %bitcast.821), channel_id=1, source_target_pairs={{0,1},{1,0},{2,3},{3,2},{4,5},{5,4},{6,7},{7,6},{8,9},{9,8},{10,11... | collective-permute-start | bytes 3932168 | tf_op jit(solution)/shard_map/ppermute | solution.py:119
  702.8 44.6 %collective-permute-start.57 = (bf16[2,2,128,640]{2,3,1,0:T(8,128)(2,1)}, bf16[2,2,128,640]{2,3,1,0:T(8,128)(2,1)}, u32[]{:S(2)}, u32[]{:S(2)}) collective-permute-start(bf16[2,2,128,640]{2,3,1,0:T(8,128)(2,1)} %dynamic-slice_bitcast_fusion.5), channel_id=1, source_target_pairs={{0,1},{1,0},{2,3},{3,2},{4,5},{5,4},{6,7},{7,6},{8,9},{9,8},{10,11... | collective-permute-start | bytes 1966088 | tf_op jit(solution)/shard_map/ppermute | solution.py:119
  706.4 41.0 %collective-permute-start.58 = (bf16[2,2,128,768]{2,3,0,1:T(8,128)(2,1)}, bf16[2,2,128,768]{2,3,0,1:T(8,128)(2,1)}, u32[]{:S(2)}, u32[]{:S(2)}) collective-permute-start(bf16[2,2,128,768]{2,3,0,1:T(8,128)(2,1)} %dynamic-slice_bitcast_fusion.1), channel_id=1, source_target_pairs={{0,4},{1,5},{2,6},{3,7},{4,0},{5,1},{6,2},{7,3},{8,12},{9,13},{10,... | collective-permute-start | bytes 2359304 | tf_op jit(solution)/shard_map/ppermute | solution.py:119
  709.7 37.7 %collective-permute-start.59 = (bf16[2,2,128,640]{2,3,0,1:T(8,128)(2,1)}, bf16[2,2,128,640]{2,3,0,1:T(8,128)(2,1)}, u32[]{:S(2)}, u32[]{:S(2)}) collective-permute-start(bf16[2,2,128,640]{2,3,0,1:T(8,128)(2,1)} %dynamic-slice_bitcast_fusion.4), channel_id=1, source_target_pairs={{0,2},{1,3},{2,0},{3,1},{4,6},{5,7},{6,4},{7,5},{8,10},{9,11},{10,... | collective-permute-start | bytes 1966088 | tf_op jit(solution)/shard_map/ppermute | solution.py:119
  713.9 30.8 %collective-permute-start.60 = (bf16[2,128,2048]{1,2,0:T(8,128)(2,1)}, bf16[2,128,2048]{1,2,0:T(8,128)(2,1)}, u32[]{:S(2)}, u32[]{:S(2)}) collective-permute-start(bf16[2,128,2048]{1,2,0:T(8,128)(2,1)} %bitcast.826), channel_id=1, source_target_pairs={{0,16},{16,0},{1,17},{17,1},{2,18},{18,2},{3,19},{19,3},{4,20},{20... | collective-permute-start | bytes 3145736 | tf_op jit(solution)/shard_map/ppermute | solution.py:103
  790.4 26.5 %collective-permute-start.75 = (bf16[1024,2816]{1,0:T(8,128)(2,1)}, bf16[1024,2816]{1,0:T(8,128)(2,1)}, u32[]{:S(2)}, u32[]{:S(2)}) collective-permute-start(bf16[1024,2816]{1,0:T(8,128)(2,1)} %convolution_convert_fusion.1), channel_id=1, source_target_pairs={{0,16},{16,0},{1,17},{17,1},{2,18},{18,2},{3,19},{19,3},{4,20},{20... | collective-permute-start | bytes 17301512 | tf_op jit(solution)/shard_map/ppermute | solution.py:738
  800.1 43.2 %collective-permute-start.71 = (bf16[2,2,2,48,1024]{4,3,1,2,0:T(8,128)(2,1)}, bf16[2,2,2,48,1024]{4,3,1,2,0:T(8,128)(2,1)}, u32[]{:S(2)}, u32[]{:S(2)}) collective-permute-start(bf16[2,2,2,48,1024]{4,3,1,2,0:T(8,128)(2,1)} %bitcast.704), channel_id=1, source_target_pairs={{0,1},{1,0},{2,3},{3,2},{4,5},{5,4},{6,7},{7,6},{8,9},{9,8},{10,11... | collective-permute-start | bytes 2359304 | tf_op jit(solution)/shard_map/ppermute | solution.py:119
  803.4 39.8 %collective-permute-start.72 = (bf16[2,2,2,80,1024]{4,3,1,0,2:T(8,128)(2,1)}, bf16[2,2,2,80,1024]{4,3,1,0,2:T(8,128)(2,1)}, u32[]{:S(2)}, u32[]{:S(2)}) collective-permute-start(bf16[2,2,2,80,1024]{4,3,1,0,2:T(8,128)(2,1)} %bitcast.702), channel_id=1, source_target_pairs={{0,2},{1,3},{2,0},{3,1},{4,6},{5,7},{6,4},{7,5},{8,10},{9,11},{10,... | collective-permute-start | bytes 3932168 | tf_op jit(solution)/shard_map/ppermute | solution.py:119
  805.6 36.9 %collective-permute-start.73 = (bf16[2,2,2,32,1024]{4,3,2,1,0:T(8,128)(2,1)}, bf16[2,2,2,32,1024]{4,3,2,1,0:T(8,128)(2,1)}, u32[]{:S(2)}, u32[]{:S(2)}) collective-permute-start(bf16[2,2,2,32,1024]{4,3,2,1,0:T(8,128)(2,1)} %dynamic-slice_bitcast_fusion.8), channel_id=1, source_target_pairs={{0,8},{1,9},{2,10},{3,11},{4,12},{5,13},{6,14},{7,15},{8,0},{9,1},... | collective-permute-start | bytes 1572872 | tf_op jit(solution)/shard_map/ppermute | solution.py:119
  814.2 28.3 %collective-permute-start.74 = (bf16[2,2,2,32,1024]{4,3,1,0,2:T(8,128)(2,1)}, bf16[2,2,2,32,1024]{4,3,1,0,2:T(8,128)(2,1)}, u32[]{:S(2)}, u32[]{:S(2)}) collective-permute-start(bf16[2,2,2,32,1024]{4,3,1,0,2:T(8,128)(2,1)} %bitcast.832), channel_id=1, source_target_pairs={{0,1},{1,0},{2,3},{3,2},{4,5},{5,4},{6,7},{7,6},{8,9},{9,8},{10,11... | collective-permute-start | bytes 1572872 | tf_op jit(solution)/shard_map/ppermute | solution.py:119
  816.9 26.3 %collective-permute-start.70 = (bf16[2,2,2,65,576]{4,2,3,1,0:T(2,128)(2,1)}, bf16[2,2,2,65,576]{4,2,3,1,0:T(2,128)(2,1)}, u32[]{:S(2)}, u32[]{:S(2)}) collective-permute-start(bf16[2,2,2,65,576]{4,2,3,1,0:T(2,128)(2,1)} %bitcast.705), channel_id=1, source_target_pairs={{0,4},{1,5},{2,6},{3,7},{4,0},{5,1},{6,2},{7,3},{8,12},{9,13},{10,... | collective-permute-start | bytes 1797128 | tf_op jit(solution)/shard_map/ppermute | solution.py:119
  843.2 27.2 %collective-permute-start.81 = (bf16[704,2048]{1,0:T(8,128)(2,1)}, bf16[704,2048]{1,0:T(8,128)(2,1)}, u32[]{:S(2)}, u32[]{:S(2)}) collective-permute-start(bf16[704,2048]{1,0:T(8,128)(2,1)} %fusion.26), channel_id=1, source_target_pairs={{0,16},{16,0},{1,17},{17,1},{2,18},{18,2},{3,19},{19,3},{4,20},{20... | collective-permute-start | bytes 8650760 | tf_op jit(solution)/shard_map/ppermute | solution.py:738
  854.3 40.3 %collective-permute-start.76 = (bf16[2,2,65,576]{3,2,1,0:T(8,128)(2,1)}, bf16[2,2,65,576]{3,2,1,0:T(8,128)(2,1)}, u32[]{:S(2)}, u32[]{:S(2)}) collective-permute-start(bf16[2,2,65,576]{3,2,1,0:T(8,128)(2,1)} %dynamic-slice_bitcast_fusion.14), channel_id=1, source_target_pairs={{0,2},{1,3},{2,0},{3,1},{4,6},{5,7},{6,4},{7,5},{8,10},{9,11},{10,... | collective-permute-start | bytes 898568 | tf_op jit(solution)/shard_map/ppermute | solution.py:119
  858.2 37.1 %collective-permute-start.77 = (bf16[2,2,48,1024]{3,2,0,1:T(8,128)(2,1)}, bf16[2,2,48,1024]{3,2,0,1:T(8,128)(2,1)}, u32[]{:S(2)}, u32[]{:S(2)}) collective-permute-start(bf16[2,2,48,1024]{3,2,0,1:T(8,128)(2,1)} %dynamic-slice_bitcast_fusion.11), channel_id=1, source_target_pairs={{0,8},{1,9},{2,10},{3,11},{4,12},{5,13},{6,14},{7,15},{8,0},{9,1},... | collective-permute-start | bytes 1179656 | tf_op jit(solution)/shard_map/ppermute | solution.py:119
  859.0 37.0 %all-to-all-start.1 = ((bf16[16,64,512]{2,1,0:T(8,128)(2,1)}), bf16[16,64,512]{2,1,0:T(8,128)(2,1)}, u32[]{:S(2)}, u32[]{:S(2)}) async-start(bf16[16,64,512]{2,1,0:T(8,128)(2,1)} %fusion.49), calls=%async_computation.1 | async-start | bytes 2097152 | tf_op jit(solution)/shard_map/all_to_all | solution.py:875
  866.2 29.1 %collective-permute-start.78 = (bf16[2,2,80,1024]{3,2,1,0:T(8,128)(2,1)S(1)}, bf16[2,2,80,1024]{3,2,1,0:T(8,128)(2,1)}, u32[]{:S(2)}, u32[]{:S(2)}) collective-permute-start(bf16[2,2,80,1024]{3,2,1,0:T(8,128)(2,1)S(1)} %dynamic-slice_bitcast_fusion.3), channel_id=1, source_target_pairs={{0,1},{1,0},{2,3},{3,2},{4,5},{5,4},{6,7},{7,6},{8,9},{9,8},{10,11... | collective-permute-start | bytes 1966088 | tf_op jit(solution)/shard_map/ppermute | solution.py:119
  868.9 25.0 %collective-permute-start.79 = (bf16[2,2,32,1024]{3,2,1,0:T(8,128)(2,1)S(1)}, bf16[2,2,32,1024]{3,2,1,0:T(8,128)(2,1)S(1)}, u32[]{:S(2)}, u32[]{:S(2)}) collective-permute-start(bf16[2,2,32,1024]{3,2,1,0:T(8,128)(2,1)S(1)} %dynamic-slice_bitcast_fusion.21), channel_id=1, source_target_pairs={{0,1},{1,0},{2,3},{3,2},{4,5},{5,4},{6,7},{7,6},{8,9},{9,8},{10,11... | collective-permute-start | bytes 786440 | tf_op jit(solution)/shard_map/ppermute | solution.py:119
  898.1 30.4 %collective-permute-start.82 = (bf16[2,65,576]{2,1,0:T(8,128)(2,1)}, bf16[2,65,576]{2,1,0:T(8,128)(2,1)}, u32[]{:S(2)}, u32[]{:S(2)}) collective-permute-start(bf16[2,65,576]{2,1,0:T(8,128)(2,1)} %dynamic-slice_bitcast_fusion.26), channel_id=1, source_target_pairs={{0,1},{1,0},{2,3},{3,2},{4,5},{5,4},{6,7},{7,6},{8,9},{9,8},{10,11... | collective-permute-start | bytes 449288 | tf_op jit(solution)/shard_map/ppermute | solution.py:119
  902.2 26.2 %collective-permute-start.83 = (bf16[2,48,1024]{2,1,0:T(8,128)(2,1)}, bf16[2,48,1024]{2,1,0:T(8,128)(2,1)}, u32[]{:S(2)}, u32[]{:S(2)}) collective-permute-start(bf16[2,48,1024]{2,1,0:T(8,128)(2,1)} %dynamic-slice_bitcast_fusion.23), channel_id=1, source_target_pairs={{0,2},{1,3},{2,0},{3,1},{4,6},{5,7},{6,4},{7,5},{8,10},{9,11},{10,... | collective-permute-start | bytes 589832 | tf_op jit(solution)/shard_map/ppermute | solution.py:119
  (215 other events, 1854.2 us)
Sparse Core Ops, SparseCore 0:
  80.4 138.1 all-gather.7
  220.1 15.4 all-gather.9
  237.8 25.6 all-gather.5

commit v3 on v2

--- a/solution.py
+++ b/solution.py
@@ -119,10 +119,13 @@
     return lax.ppermute(values, "expert", [(i, i ^ bit) for i in range(count)])
 
 
-def gathering(values, order, held=(), lead=0):
+def gathering(values, order, held=(), lead=0, whole=True):
     me = lax.axis_index("expert")
     held = list(held)
-    for bit in order:
+    for step, bit in enumerate(order):
+        if not whole and step + 1 == len(order):
+            values = values.reshape(-1, values.shape[-1])
+            return values, (yield partner(values, bit))
         other = yield partner(values, bit)
         low = (me & bit) == 0
         values = jnp.stack(
@@ -136,14 +139,24 @@
 def scattering(values, order, bits, kept=f32, lead=0):
     me = lax.axis_index("expert")
     bits = list(bits)
-    values = values.reshape(values.shape[:lead] + (2,) * len(bits) + values.shape[lead + 1 :])
+    split = isinstance(values, tuple)
+    if not split:
+        values = values.reshape(values.shape[:lead] + (2,) * len(bits) + values.shape[lead + 1 :])
     for step, bit in enumerate(order):
         axis = lead + bits.index(bit)
         bits.remove(bit)
         place = ((me & bit) != 0).astype(jnp.int32)
-        other = yield partner(pick(values, 1 - place, axis), bit)
-        values = pick(values, place, axis).astype(f32) + other.astype(f32)
-        values = values.astype(kept if step + 1 == len(order) else bf16)
+        if split and step == 0:
+            own, sent = values
+        else:
+            own, sent = pick(values, place, axis), pick(values, 1 - place, axis)
+        other = yield partner(sent, bit)
+        if step + 1 < len(order):
+            values = own + other
+        else:
+            values = (own.astype(f32) + other.astype(f32)).astype(kept)
+        if split and step == 0:
+            values = values.reshape((2,) * len(bits) + (-1,) + values.shape[-1:])
     if bits:
         values = values.reshape(values.shape[:lead] + (-1,) + values.shape[lead + len(bits) :])
     return values
@@ -169,6 +182,12 @@
         chain.send(values)
     except StopIteration as stop:
         return stop.value
+
+
+def deferred(steps, make):
+    for _ in range(steps):
+        yield ()
+    return (yield from make())
 
 
 def pair_swapping(values, bit, axis):
@@ -280,8 +299,9 @@
     scale = lax.rsqrt(jnp.mean(latent * latent, axis=-1, keepdims=True) + norm_eps)
     kv_normed_ref[...] = (latent * scale * kv_gain_ref[...]).astype(bf16)
     cos, sin = cos_ref[...], sin_ref[...]
-    front = joint_ref[:, KVR : KVR + ROPE_LANES]
-    back = joint_ref[:, KVR + ROPE_LANES :]
+    copies = 2 * ROPE_LANES // DR
+    front = jnp.concatenate([joint_ref[:, KVR : KVR + DR // 2]] * copies, axis=-1)
+    back = jnp.concatenate([joint_ref[:, KVR + DR // 2 :]] * copies, axis=-1)
     keys_ref[:, nope : nope + ROPE_LANES] = (front * cos - back * sin).astype(bf16)
     keys_ref[:, nope + ROPE_LANES :] = (front * sin + back * cos).astype(bf16)
     q = dot(normed_ref[...], q_ref[:, : nope + 2 * ROPE_LANES])
@@ -375,9 +395,13 @@
         front, back = d_rotary[:, :ROPE_LANES], d_rotary[:, ROPE_LANES:]
         d_q_ref[part, nope : nope + ROPE_LANES] = (front * cos + back * sin).astype(bf16)
         d_q_ref[part, nope + ROPE_LANES :] = (back * cos - front * sin).astype(bf16)
-        front, back = d_key[:, :ROPE_LANES], d_key[:, ROPE_LANES:]
-        d_key_ref[part, :ROPE_LANES] = front * cos + back * sin
-        d_key_ref[part, ROPE_LANES:] = back * cos - front * sin
+        front, back = [
+            sum(half[:, at : at + DR // 2] for at in range(0, ROPE_LANES, DR // 2))
+            for half in (d_key[:, :ROPE_LANES], d_key[:, ROPE_LANES:])
+        ]
+        cos, sin = cos[:, : DR // 2], sin[:, : DR // 2]
+        d_key_ref[part, : DR // 2] = front * cos + back * sin
+        d_key_ref[part, DR // 2 :] = back * cos - front * sin
     d_kv_normed = lanes_dot(d_kv_ref[...], up_ref[...])
     latent = joint_ref[:, :KVR]
     scale = lax.rsqrt(jnp.mean(latent * latent, axis=-1, keepdims=True) + norm_eps)
@@ -392,33 +416,262 @@
     ).astype(sum_ref.dtype)
 
 
-def by_rows_call(kernel, rows, chunk, streamed, fixed_, outs, scratch=(), order=None):
-    steps = rows // chunk
+def by_rows_call(
+    kernel, steps, order, streamed, fixed, outs, scratch=(), group=lambda i: i, scalars=(), half=None
+):
+    half = half or ()
+
+    def spec(name, shape):
+        rest = (0,) * (len(shape) - 1)
+        if name in half:
+            block = (shape[0] * 2 // steps,) + shape[1:]
+            return pl.BlockSpec(block, lambda i, *unused: (i // 2,) + rest)
+        block = (shape[0] // steps,) + shape[1:]
+        return pl.BlockSpec(block, lambda i, *unused: (group(i),) + rest)
+
     operands, specs = [], []
     for name in order:
         if name in streamed:
-            value = streamed[name]
-            block = (value.shape[0] // steps,) + value.shape[1:]
-            index = lambda i, ndim=value.ndim: (i,) + (0,) * (ndim - 1)
+            operands.append(streamed[name])
+            specs.append(spec(name, streamed[name].shape))
         else:
-            value = fixed_[name]
-            block = value.shape
-            index = lambda i, ndim=value.ndim: (0,) * ndim
-        operands.append(value)
-        specs.append(pl.BlockSpec(block, index))
-    out_specs = [
-        pl.BlockSpec((shape[0] // steps,) + shape[1:], lambda i, ndim=len(shape): (i,) + (0,) * (ndim - 1))
-        for shape, dtype in outs
-    ]
+            value = fixed[name]
+            operands.append(value)
+            specs.append(
+                pl.BlockSpec(
+                    value.shape,
+                    lambda i, *unused, ndim=value.ndim: (0,) * ndim,
+                    pipeline_mode=pl.Buffered(1),
+                )
+            )
     return pl.pallas_call(
         kernel,
-        grid=(steps,),
-        in_specs=specs,
-        out_specs=out_specs,
-        out_shape=[jax.ShapeDtypeStruct(shape, dtype) for shape, dtype in outs],
-        scratch_shapes=scratch,
+        grid_spec=pltpu.PrefetchScalarGridSpec(
+            num_scalar_prefetch=len(scalars),
+            grid=(steps,),
+            in_specs=specs,
+            out_specs=[spec(name, shape) for name, shape, dtype in outs],
+            scratch_shapes=scratch,
+        ),
+        out_shape=[jax.ShapeDtypeStruct(shape, dtype) for name, shape, dtype in outs],
+        compiler_params=pltpu.CompilerParams(vmem_limit_bytes=60 * 2**20),
+    )(*scalars, *operands)
+
+
+def one_hot(slot_ref, place, count):
+    slots = slot_ref[place]
+    return lax.broadcasted_iota(jnp.int32, (count, slots.shape[1]), 0) == slots
+
+
+def swiglu_back(gate_part, up_part, upstream):
+    sigmoid = jax.nn.sigmoid(gate_part)
+    silu = gate_part * sigmoid
+    slope = sigmoid + silu * (1.0 - sigmoid)
+    return silu * up_part, upstream * up_part * slope, upstream * silu
+
+
+def gradient_kernel(
+    count, grad_ref, slot_ref, gate_ref, down_ref, shared_ref, picked_ref, d_hidden_ref, d_shared_ref
+):
+    span = slot_ref.shape[-1]
+    for place in range(slot_ref.shape[0]):
+        chosen = one_hot(slot_ref, place, count)
+        gate = jnp.sum(jnp.where(chosen, gate_ref[place], 0.0), axis=1, keepdims=True)
+        found = dot(chosen.astype(bf16), grad_ref[place * span : (place + 1) * span])
+        picked_ref[place * count : (place + 1) * count] = (found * gate).astype(bf16)
+    d_hidden_ref[...] = lanes_dot(picked_ref[...], down_ref[...])
+    d_shared_ref[...] = lanes_dot(grad_ref[...], shared_ref[...])
+
+
+def halves_in(me_ref, refs, x_ref, parts, span):
+    for (start, stop), (held_ref, came_ref), mine in zip(parts, refs, my_places(me_ref)):
+        if start == 0:
+            here = lax.rem(pl.program_id(0), 2) == mine
+
+            @pl.when(here)
+            def _():
+                x_ref[:, start:stop] = held_ref[...]
+
+            @pl.when(jnp.logical_not(here))
+            def _():
+                x_ref[:, start:stop] = came_ref[...]
+
+            continue
+        size = span if start == parts[1][0] else span // 2
+        for at in range(2 * span // size):
+            turn, place = (at // 2, at % 2) if size < span else (0, at)
+            source = slice(turn * size, (turn + 1) * size)
+            x_ref[at * size : (at + 1) * size, start:stop] = jnp.where(
+                mine == place, held_ref[source].astype(f32), came_ref[source].astype(f32)
+            ).astype(bf16)
+
+
+def halves_out(me_ref, refs, values, which, span):
+    (kept_ref, sent_ref), mine = refs[which], my_places(me_ref)[which]
+    if which == 0:
+        here = lax.rem(pl.program_id(0), 2) == mine
+
+        @pl.when(here)
+        def _():
+            kept_ref[...] = values.astype(bf16)
+
+        @pl.when(jnp.logical_not(here))
+        def _():
+            sent_ref[...] = values.astype(bf16)
+
+        return
+    size = span if which == 1 else span // 2
+    for turn in range(span // size):
+        low = values[2 * turn * size : (2 * turn + 1) * size]
+        high = values[(2 * turn + 1) * size : (2 * turn + 2) * size]
+        target = slice(turn * size, (turn + 1) * size)
+        kept_ref[target] = jnp.where(mine == 0, low, high).astype(bf16)
+        sent_ref[target] = jnp.where(mine == 0, high, low).astype(bf16)
+
+
+def my_places(me_ref):
+    return me_ref[0], me_ref[1], me_ref[2]
+
+
+def expert_kernel(
+    count,
+    me_ref,
+    slot_ref,
+    d_hidden_ref,
+    d_shared_ref,
+    pair_ref,
+    shared_ref,
+    left_ref,
+    left_came_ref,
+    middle_ref,
+    middle_came_ref,
+    right_ref,
+    right_came_ref,
+    x_ref,
+    rows_ref,
+    hidden_ref,
+    d_pair_ref,
+    shared_hidden_ref,
+    d_shared_pair_ref,
+    left_kept_ref,
+    left_sent_ref,
+    middle_kept_ref,
+    middle_sent_ref,
+    right_kept_ref,
+    right_sent_ref,
+):
+    span = slot_ref.shape[-1]
+    parts = thirds(x_ref.shape[-1])
+    halves_in(
+        me_ref,
+        ((left_ref, left_came_ref), (middle_ref, middle_came_ref), (right_ref, right_came_ref)),
+        x_ref,
+        parts,
+        span,
+    )
+    places = range(slot_ref.shape[0])
+    chosen = [one_hot(slot_ref, place, count).astype(bf16) for place in places]
+    for place in places:
+        rows_ref[place * count : (place + 1) * count] = dot(
+            chosen[place], x_ref[place * span : (place + 1) * span]
+        ).astype(bf16)
+    hidden = hidden_ref.shape[-1]
+    units, d_gate, d_up = swiglu_back(
+        dot(rows_ref[...], pair_ref[:, :hidden]),
+        dot(rows_ref[...], pair_ref[:, hidden:]),
+        d_hidden_ref[...],
+    )
+    hidden_ref[...] = units.astype(bf16)
+    d_pair_ref[:, :hidden] = d_gate.astype(bf16)
+    d_pair_ref[:, hidden:] = d_up.astype(bf16)
+    padded = shared_hidden_ref.shape[-1]
+    units, d_gate, d_up = swiglu_back(
+        dot(x_ref[...], shared_ref[:, :padded]),
+        dot(x_ref[...], shared_ref[:, padded:]),
+        d_shared_ref[...],
+    )
+    shared_hidden_ref[...] = units.astype(bf16)
+    d_shared_pair_ref[:, :padded] = d_gate.astype(bf16)
+    d_shared_pair_ref[:, padded:] = d_up.astype(bf16)
+    refs = (
+        (left_kept_ref, left_sent_ref),
+        (middle_kept_ref, middle_sent_ref),
+        (right_kept_ref, right_sent_ref),
+    )
+    for which, (start, stop) in enumerate(parts):
+        back = lanes_dot(d_pair_ref[...], pair_ref[start:stop]).astype(bf16)
+        found = [
+            rows_dot(chosen[place], back[place * count : (place + 1) * count])
+            + lanes_dot(d_shared_pair_ref[place * span : (place + 1) * span], shared_ref[start:stop])
+            for place in places
+        ]
+        halves_out(me_ref, refs, jnp.concatenate(found, axis=0), which, span)
+
+
+def output_kernel(
+    count,
+    me_ref,
+    hidden_ref,
+    shared_hidden_ref,
+    slot_ref,
+    gate_ref,
+    down_ref,
+    shared_ref,
+    left_kept_ref,
+    left_sent_ref,
+    middle_kept_ref,
+    middle_sent_ref,
+    right_kept_ref,
+    right_sent_ref,
+    rows_ref,
+):
+    span = slot_ref.shape[-1]
+    places = range(slot_ref.shape[0])
+    chosen = [one_hot(slot_ref, place, count) for place in places]
+    found = dot(hidden_ref[...], down_ref[...])
+    for place in places:
+        at = slice(place * count, (place + 1) * count)
+        gate = jnp.sum(jnp.where(chosen[place], gate_ref[place], 0.0), axis=1, keepdims=True)
+        rows_ref[at] = (found[at] * gate).astype(bf16)
+    refs = (
+        (left_kept_ref, left_sent_ref),
+        (middle_kept_ref, middle_sent_ref),
+        (right_kept_ref, right_sent_ref),
+    )
+    for which, (start, stop) in enumerate(thirds(down_ref.shape[-1])):
+        found = [
+            rows_dot(
+                chosen[place].astype(bf16),
+                rows_ref[place * count : (place + 1) * count, start:stop],
+            )
+            + dot(shared_hidden_ref[place * span : (place + 1) * span], shared_ref[:, start:stop])
+            for place in places
+        ]
+        halves_out(me_ref, refs, jnp.concatenate(found, axis=0), which, span)
+
+
+def columns_kernel(place_ref, left_ref, right_ref, out_ref):
+    out_ref[...] = rows_dot(left_ref[...], right_ref[...]).astype(out_ref.dtype)
+
+
+def columns_product(left, right, place, parts, dtype):
+    width = left.shape[1] // parts
+    block = 256 if width % 256 == 0 else 128
+    steps = width // block
+    return pl.pallas_call(
+        columns_kernel,
+        grid_spec=pltpu.PrefetchScalarGridSpec(
+            num_scalar_prefetch=1,
+            grid=(steps,),
+            in_specs=[
+                pl.BlockSpec((left.shape[0], block), lambda i, place: (0, place[0] * steps + i)),
+                pl.BlockSpec(right.shape, lambda i, place: (0, 0), pipeline_mode=pl.Buffered(1)),
+            ],
+            out_specs=pl.BlockSpec((block, right.shape[1]), lambda i, place: (i, 0)),
+        ),
+        out_shape=jax.ShapeDtypeStruct((width, right.shape[1]), dtype),
         compiler_params=pltpu.CompilerParams(vmem_limit_bytes=56 * 2**20),
-    )(*operands)
+    )(jnp.reshape(place, (1,)).astype(jnp.int32), left, right)
 
 
 def shards(
@@ -555,9 +808,7 @@
     def attend(all_rows, small_all, by_head, out_parts):
         joint_all = dp_gather(small_all[:, :slice_rows])
         kv_down = joint_all.transpose(1, 0, 2, 3).reshape(width, joint_width)
-        front, back = kv_down[:, KVR : KVR + DR // 2], kv_down[:, KVR + DR // 2 :]
         copies = 2 * ROPE_LANES // DR
-        kv_down = jnp.concatenate([kv_down[:, :KVR]] + [front] * copies + [back] * copies, axis=-1)
         gains_all = dp_gather(small_all[:, gain_row])
         attn_scale = gains_all[..., :n_gain].transpose(1, 0, 2).reshape(-1)
         ffn_scale = gains_all[..., n_gain : 2 * n_gain].reshape(-1)
@@ -584,8 +835,8 @@
         wide = nope_cols + 2 * ROPE_LANES
         outs = by_rows_call(
             functools.partial(attend_kernel, heads),
-            pair_rows,
-            4 * row_count,
+            pair_rows // (4 * row_count),
+            ("x", "gain", "kv_gain", "down", "q", "up", "out", "cos", "sin", "column", "row"),
             dict(
                 x=all_rows,
                 cos=cos,
@@ -602,17 +853,16 @@
                 out=out_full,
             ),
             (
-                ((pair_rows, width), bf16),
-                ((pair_rows, KVR + 2 * ROPE_LANES), f32),
-                ((pair_rows, KVR), bf16),
-                ((pair_rows, wide), bf16),
-                ((pair_rows, wide), bf16),
-                ((pair_rows, heads * DV), bf16),
-                ((blocks * heads, row_count, row_count), f32),
-                ((pair_rows, heads * DV), bf16),
-                ((pair_rows, width), bf16),
+                ("normed", (pair_rows, width), bf16),
+                ("joint", (pair_rows, joint_width), f32),
+                ("kv_normed", (pair_rows, KVR), bf16),
+                ("heads", (pair_rows, wide), bf16),
+                ("keys", (pair_rows, wide), bf16),
+                ("values", (pair_rows, heads * DV), bf16),
+                ("probs", (blocks * heads, row_count, row_count), f32),
+                ("attended", (pair_rows, heads * DV), bf16),
+                ("sum", (pair_rows, width), bf16),
             ),
-            order=("x", "gain", "kv_gain", "down", "q", "up", "out", "cos", "sin", "column", "row"),
         )
         return outs, (q_full, kv_up, out_full, kv_down), (attn_scale, kv_scale, ffn_scale), (cos, sin)
 
@@ -663,69 +913,87 @@
     slots = expert_count * capacity
     group_rows = expert_count * row_count
     grad_rows = grad_all.reshape(group_rows, width)
-
-    def choose(results, found, own_gate, grad_all):
-        live = own_gate > 0.0
-        place = jnp.cumsum(live.astype(jnp.int32), axis=1) - 1
-        chosen = jnp.arange(capacity, dtype=jnp.int32)[None, :, None] == place[:, None, :]
-        chosen = chosen & live[:, None, :]
-        slot_gate = jnp.sum(jnp.where(chosen, own_gate[:, None, :], 0.0), axis=2)
-        slot_gate = slot_gate.reshape(slots, 1)
-        chosen = chosen.astype(bf16)
-        slot_grad = jnp.einsum("rst,rtd->rsd", chosen, grad_all, preferred_element_type=f32)
-        return chosen, slot_gate, (slot_grad.reshape(slots, width) * slot_gate).astype(bf16)
-
-    (attended_sum,), ((chosen, slot_gate, slot_grad),) = march(
-        scattering(attended_sum, [pair_bit], [pair_bit]), jobs=((choose, own_gate, grad_all),)
-    )
+    live = own_gate > 0.0
+    slot = jnp.cumsum(live.astype(jnp.int32), axis=1) - 1
+    slot = slot + capacity * (jnp.arange(expert_count, dtype=jnp.int32) % 2)[:, None]
+    slot = jnp.where(live, slot, -1).reshape(expert_count // 2, 1, 2 * row_count)
+    gate = own_gate.reshape(expert_count // 2, 1, 2 * row_count)
+    chunk = 4 * row_count
+
+    steps = group_rows // chunk
+    my_place = [((me & bit) != 0).astype(jnp.int32) for bit in (pair_bit, second, first)]
+    my_place = jnp.stack(my_place)
+
+    def group(i):
+        return i if pair_bit == 4 else (i % 2) * (steps // 2) + i // 2
+
+    def halves_of(name):
+        return [
+            (f"{name}{i}{kind}", (group_rows // 2, high - low), bf16)
+            for i, (low, high) in enumerate(parts)
+            for kind in ("kept", "sent")
+        ]
+
+    def from_gradient(results, found, grad_rows):
+        return by_rows_call(
+            functools.partial(gradient_kernel, 2 * capacity),
+            steps,
+            ("grad", "slot", "gate", "down", "shared"),
+            dict(grad=grad_rows, slot=slot, gate=gate),
+            dict(down=down_w, shared=shared_out),
+            (
+                ("picked", (slots, width), bf16),
+                ("d_hidden", (slots, hidden), f32),
+                ("d_shared", (group_rows, padded), f32),
+            ),
+        )
+
+    attended_sum = alone(scattering(attended_sum, [pair_bit], [pair_bit]))
     resid_in = tokens.astype(f32)
     upstream = out_grad.astype(f32)
     resid = resid_in + attended_sum
     ffn_in = norm_apply(resid, ffn_scale).astype(bf16)
 
-    def back_hidden(results, found, slot_grad, matrix):
-        return dot(slot_grad, matrix.T)
-
-    ffn_parts, (d_hidden, d_shared_hidden, *unused) = march(
-        *(gathering(part, order) for part, order in zip(column_parts(ffn_in), orders)),
-        jobs=((back_hidden, slot_grad, down_w), (back_hidden, grad_rows, shared_out)),
-    )
-    ffn_all = jnp.concatenate(ffn_parts, axis=-1)
-    ffn_rows = ffn_all.reshape(group_rows, width)
-    rows = jnp.einsum("rst,rtd->rsd", chosen, ffn_all, preferred_element_type=f32)
-    rows = rows.reshape(slots, width).astype(bf16)
-    pair = dot(rows, pair_w)
-    gate_part, up_part = pair[:, :hidden], pair[:, hidden:]
-    expert_hidden = swish_gate(gate_part, up_part).astype(bf16)
-    d_pair = swish_back(gate_part, up_part, d_hidden).astype(bf16)
-    shared_pair = dot(ffn_rows, shared_w)
-    shared_gate, shared_up = shared_pair[:, :padded], shared_pair[:, padded:]
-    shared_hidden = swish_gate(shared_gate, shared_up).astype(bf16)
-    d_shared_pair = swish_back(shared_gate, shared_up, d_shared_hidden).astype(bf16)
-
-    def to_tokens(slot_rows, shared_rows, shared_matrix):
-        back = jnp.einsum(
-            "rst,rsd->rtd",
-            chosen,
-            slot_rows.reshape(expert_count, capacity, -1),
-            preferred_element_type=f32,
+    ffn_parts, ((slot_grad, d_hidden, d_shared_hidden), *unused) = march(
+        *(gathering(part, order, whole=False) for part, order in zip(column_parts(ffn_in), orders)),
+        jobs=((from_gradient, grad_rows),),
+    )
+    names = [f"in{i}{kind}" for i in range(3) for kind in ("held", "came")]
+    ffn_parts = [part.reshape(group_rows // 2, -1) for both in ffn_parts for part in both]
+    ffn_rows, rows, expert_hidden, d_pair, shared_hidden, d_shared_pair, *d_parts = by_rows_call(
+        functools.partial(expert_kernel, 2 * capacity),
+        steps,
+        ["slot", "d_hidden", "d_shared", "pair", "shared"] + names,
+        dict(zip(names, ffn_parts), slot=slot, d_hidden=d_hidden, d_shared=d_shared_hidden),
+        dict(pair=pair_w, shared=shared_w),
+        [
+            ("x", (group_rows, width), bf16),
+            ("rows", (slots, width), bf16),
+            ("hidden", (slots, hidden), bf16),
+            ("d_pair", (slots, 2 * hidden), bf16),
+            ("shared_hidden", (group_rows, padded), bf16),
+            ("d_shared_pair", (group_rows, 2 * padded), bf16),
+        ]
+        + halves_of("out"),
+        group=group,
+        scalars=(my_place,),
+        half=("in0held", "in0came", "out0kept", "out0sent"),
+    )
+    d_parts = [(d_parts[2 * i], d_parts[2 * i + 1]) for i in range(3)]
+
+    def output_part(results, found, expert_hidden, shared_hidden):
+        return by_rows_call(
+            functools.partial(output_kernel, 2 * capacity),
+            steps,
+            ("hidden", "shared_hidden", "slot", "gate", "down", "shared"),
+            dict(hidden=expert_hidden, shared_hidden=shared_hidden, slot=slot, gate=gate),
+            dict(down=down_w, shared=shared_out),
+            halves_of("out"),
+            scratch=[pltpu.VMEM((slots // steps, width), bf16)],
+            group=group,
+            scalars=(my_place,),
+            half=("out0kept", "out0sent"),
         )
-        back = back.reshape(group_rows, -1) + dot(shared_rows, shared_matrix)
-        return back.astype(bf16).reshape(expert_count, row_count, -1)
-
-    d_rows = dot(d_pair, pair_w.T).astype(bf16)
-    d_parts = [
-        to_tokens(d_rows[:, low:high], d_shared_pair, shared_w[low:high].T) for low, high in parts
-    ]
-
-    kept_rows = (expert_hidden, d_pair, rows, shared_hidden, d_shared_pair, slot_grad)
-    (expert_hidden, d_pair, rows, shared_hidden, d_shared_pair, slot_grad) = after(
-        kept_rows, d_parts
-    )
-
-    def output_part(results, found, expert_hidden, shared_hidden):
-        down = (dot(expert_hidden, down_w) * slot_gate).astype(bf16)
-        return to_tokens(down, shared_hidden, shared_out)
 
     def halves(found):
         if dp_count != 2:
@@ -737,20 +1005,16 @@
             return kept.astype(f32)
         return kept + lax.ppermute(sent, "dp", [(0, 1), (1, 0)]).astype(f32)
 
-    def pair_gradient(place, rows, d_pair):
-        rows = pick(rows.reshape(slots, dp_count, -1), place, 1)
-        return dot(rows.T, d_pair)
-
     def pair_kept(results, found, rows, d_pair):
         if dp_count != 2:
             found = dot(rows.T, d_pair).astype(bf16).reshape(dp_count, width // dp_count, -1)
             return lax.psum_scatter(found, "dp", scatter_dimension=0)
-        return pair_gradient(core, rows, d_pair)
+        return columns_product(rows, d_pair, core, dp_count, f32)
 
     def pair_sent(results, found, rows, d_pair):
         if dp_count != 2:
             return ()
-        return pair_gradient(1 - core, rows, d_pair).astype(bf16)
+        return columns_product(rows, d_pair, 1 - core, dp_count, bf16)
 
     def down_gradient(results, found, expert_hidden, slot_grad):
         return halves(
@@ -758,8 +1022,9 @@
         )
 
     def shared_gradient(results, found, shared_hidden, d_shared_pair):
-        down = dot(shared_hidden.T, grad_rows)[:units].reshape(dp_count, share, width)
-        both = dot(ffn_rows.T, d_shared_pair)
+        down = columns_product(shared_hidden, grad_rows, jnp.int32(0), 1, f32)
+        down = down[:units].reshape(dp_count, share, width)
+        both = columns_product(ffn_rows, d_shared_pair, jnp.int32(0), 1, bf16)
         both = both.reshape(dp_count, expert_count, slice_rows, 2 * padded)
         return dp_scatter(down, bf16), dp_scatter(both, bf16).astype(bf16)
 
@@ -778,10 +1043,7 @@
 
     d_norm_resid, grad_ffn_scale = norm_back(resid, ffn_scale, d_ffn_in)
     d_resid = upstream + d_norm_resid
-    (d_branch,), (kept,) = march(
-        gathering(d_resid.astype(bf16), [pair_bit]), jobs=((pair_kept, rows, d_pair),)
-    )
-    pair_halves = (kept, sent)
+    out_part = [(out_part[2 * i], out_part[2 * i + 1]) for i in range(3)]
 
     def attend_back(results, found, d_branch):
         d_branch = dp_gather(d_branch).transpose(1, 0, 2, 3).reshape(pair_rows, width)
@@ -789,8 +1051,11 @@
         wide = nope_cols + 2 * ROPE_LANES
         outs = by_rows_call(
             functools.partial(attend_back_kernel, heads),
-            pair_rows,
-            4 * row_count,
+            steps,
+            (
+                "branch", "out", "probs", "heads", "keys", "values", "joint", "kv_gain", "up", "q",
+                "down", "cos", "sin",
+            ),
             dict(
                 branch=d_branch,
                 probs=probs,
@@ -809,22 +1074,15 @@
                 down=kv_down,
             ),
             (
-                ((pair_rows, wide), bf16),
-                ((pair_rows, heads * (DH + DV)), bf16),
-                ((pair_rows, KVR + 2 * ROPE_LANES), bf16),
-                ((steps, 1, KVR), f32),
-                ((pair_rows, width), bf16),
+                ("d_q", (pair_rows, wide), bf16),
+                ("d_kv", (pair_rows, heads * (DH + DV)), bf16),
+                ("d_joint", (pair_rows, joint_width), bf16),
+                ("d_gain", (steps, 1, KVR), f32),
+                ("sum", (pair_rows, width), bf16),
             ),
-            scratch=[pltpu.VMEM((4 * row_count, 2 * ROPE_LANES), f32)],
-            order=(
-                "branch", "out", "probs", "heads", "keys", "values", "joint", "kv_gain", "up", "q",
-                "down", "cos", "sin",
-            ),
+            scratch=[pltpu.VMEM((4 * row_count, DR), f32)],
         )
         return d_branch, outs
-
-    def back_sum(results, found):
-        return by_owner(found[0][1][4])
 
     def weight_gradients(results, found):
         d_branch, (d_q_heads, d_kv_heads, d_joint, unused, unused) = found[0]
@@ -836,23 +1094,31 @@
         by_head = jnp.concatenate([grad_q, grad_up], axis=-1)
         grad_out = cut_out(dot(attended.T, d_branch).astype(bf16))
         grad_kvdown = dot(normed.T, d_joint)
-        rotary = grad_kvdown[:, KVR:].reshape(width, 2, -1, DR // 2).sum(axis=2)
-        grad_kvdown = jnp.concatenate([grad_kvdown[:, :KVR], rotary.reshape(width, DR)], axis=-1)
         grad_kvdown = grad_kvdown.reshape(expert_count, dp_count, slice_rows, joint_width)
         return by_head, grad_out, dp_scatter(grad_kvdown.transpose(1, 0, 2, 3), bf16)
 
-    results, found = march(
+    sums = []
+
+    def back_of(results, found):
+        return attend_back(results, found, results[0])
+
+    def sum_and_gradients(results, found):
+        sums.append(by_owner(found[1][1][4]))
+        return weight_gradients(results, found[1:])
+
+    (unused, d_normed, *results), found = march(
+        gathering(d_resid.astype(bf16), [pair_bit]),
+        deferred(3, lambda: scattering(sums[0], [pair_bit], [pair_bit])),
         *(
-            scattering(part, order[::-1], bits)
-            for part, order in zip(column_parts(out_part), orders)
+            scattering(after(part, d_resid), order[::-1], bits)
+            for part, order in zip(out_part, orders)
         ),
-        jobs=((attend_back, d_branch), (back_sum,), (weight_gradients,)),
-    )
+        jobs=((pair_kept, rows, d_pair), (back_of,), (sum_and_gradients,)),
+    )
+    pair_halves = (found[0], sent)
     output = (resid + jnp.concatenate(results, axis=-1)).astype(bf16)
     grad_heads, grad_out, grad_kvdown = found[2]
-    d_normed = found[1]
-    grad_kv_scale = found[0][1][3].sum(axis=0)
-    d_normed = alone(scattering(d_normed, [pair_bit], [pair_bit]))
+    grad_kv_scale = found[1][1][3].sum(axis=0)
     pair_halves, down_halves, grad_shared = after((pair_halves, down_halves, grad_shared), results)
     d_norm_in, grad_attn_scale = norm_back(turned(resid_in), attn_scale, d_normed)
     grad_in = (d_resid + turned_back(d_norm_in)).astype(bf16)

time: 971 us -> 890 us (0.917)
  matrix products: 168 us -> 21.3 us
  Pallas kernels: 34.9 us -> 177 us
  local copies, waits for them, and re-layouts: 247 us -> 172 us
  other arithmetic: 162 us -> 144 us
  starting transfers between devices: 109 us -> 123 us
    pallas_call x2 -> x9, Pallas kernels: 34.9 us -> 177 us  [the longest x5 133 us: by_rows_call(): pl.pallas_call(kernel, grid_spec=pltpu.PrefetchScalarGridSpec(num_scalar_...]
    dot_general x19 -> x5, matrix products: 142 us -> 21.3 us  [dot(): return jnp.dot(left, right, preferred_element_type=f32)]
    convert_element_type x37 -> x6, other arithmetic: 38.7 us -> 5.44 us  [the longest x4 4.26 us: scattering(): values = (own.astype(f32) + other.astype(f32)).astype(kept)]
    add x6 -> x35, other arithmetic: 2.47 us -> 33.5 us  [the longest x28 29.9 us: scattering(): values = own + other]
    dot_general x6 -> x0, matrix products: 25.5 us -> none  [the longest x4 14 us: to_tokens(): jnp.einsum('rst,rsd->rtd', chosen, slot_rows.reshape(expert_count, capaci...]
    unnamed x348 -> x247, local copies, waits for them, and re-layouts: 47.5 us -> 31.9 us
    dynamic_slice x21 -> x22, local copies, waits for them, and re-layouts: 35.6 us -> 20.3 us  [pick(): return lax.dynamic_index_in_dim(values, place, axis, keepdims=False)]
    optimization_barrier x2 -> x0, local copies, waits for them, and re-layouts: 13.5 us -> none  [after(): return lax.optimization_barrier((values, others))[0]]
  transfers between devices with their start and end apart: 95 -> 95, of which waited for: 28 -> 28; matrix products, arithmetic and copies ran while one was open for 48% -> 34% of each run, Pallas kernels for 4% -> 12%
where the time goes in v3:
time: 890 us; the launch traced here: 879 us
  waiting for transfers between devices  226 us (25%)
  Pallas kernels  177 us (20%)
  local copies, waits for them, and re-layouts  172 us (19%)
  other arithmetic  144 us (16%)
  starting transfers between devices  123 us (14%)
  matrix products  21.3 us (2%)
  between operations  16.5 us (2%)
    ppermute x74, waiting for transfers between devices, partner(): return lax.ppermute(values, 'expert', [(i, i ^ bit) for i in range(count)])  214 us
    pallas_call x5, Pallas kernels, by_rows_call(): pl.pallas_call(kernel, grid_spec=pltpu.PrefetchScalarGridSpec(num_scalar_...  133 us
    ppermute x74, starting transfers between devices, partner(): return lax.ppermute(values, 'expert', [(i, i ^ bit) for i in range(count)])  74.7 us
    pallas_call x4, Pallas kernels, columns_product(): pl.pallas_call(columns_kernel, grid_spec=pltpu.PrefetchScalarGridSpec(num...  43.7 us
    another operation x50, other arithmetic, gathering(): jnp.stack([jnp.where(low, values, other), jnp.where(low, other, values)],...  36.1 us
    unnamed x247, local copies, waits for them, and re-layouts  31.9 us
    add x28, other arithmetic, scattering(): values = own + other  29.9 us
    squeeze x31, local copies, waits for them, and re-layouts, pick(): return lax.dynamic_index_in_dim(values, place, axis, keepdims=False)  21.7 us
  transfers between devices with their start and end apart: 95, of which 28 were waited for; matrix products, arithmetic and copies ran while one was open for 34% of the time, Pallas kernels for 12%

profile of v3, /device:TPU:1, one launch (start us, length us, event | category | flops | bytes accessed | tf_op | source)
XLA Modules:
  0.0 878.6 jit_solution(6710767668666688419)
XLA Ops:
  28.1 7.1 collective-permute-done.2
  40.2 17.1 %collective-permute-done.8 = bf16[80,576]{1,0:T(8,128)(2,1)S(1)} collective-permute-done((bf16[80,576]{1,0:T(8,128)(2,1)S(1)}, bf16[80,576]{1,0:T(8,128)(2,1)S(1)}, u32[]{:S(2)}, u32[]{:S(2)}) %collective-permute-start.8) | collective-permute-done | bytes 92192 | tf_op jit(solution)/shard_map/ppermute | solution.py:119
  64.1 20.9 %collective-permute-done.13 = bf16[2,80,576]{2,1,0:T(8,128)(2,1)S(1)} collective-permute-done((bf16[2,80,576]{2,1,0:T(8,128)(2,1)S(1)}, bf16[2,80,576]{2,1,0:T(8,128)(2,1)S(1)}, u32[]{:S(2)}, u32[]{:S(2)}) %collective-permute-start.13) | collective-permute-done | bytes 184352 | tf_op jit(solution)/shard_map/ppermute | solution.py:119
  87.0 6.2 copy.696
  95.1 2.8 collective-permute-start.3
  111.2 4.0 copy.594
  116.5 28.3 %collective-permute-done.16 = bf16[2,2,2,32,1024]{4,0,3,1,2:T(2,128)(2,1)} collective-permute-done((bf16[2,2,2,32,1024]{4,0,3,1,2:T(2,128)(2,1)}, bf16[2,2,2,32,1024]{4,0,3,1,2:T(2,128)(2,1)}, u32[]{:S(2)}, u32[]{:S(2)}) %collective-permute-start.16) | collective-permute-done | bytes 524320 | tf_op jit(solution)/shard_map/ppermute | solution.py:119
  144.7 3.8 collective-permute-done.15
  165.5 16.0 %collective-permute-done.19 = bf16[2,2,2,80,576]{4,3,2,1,0:T(8,128)(2,1)S(1)} collective-permute-done((bf16[2,2,2,80,576]{4,3,2,1,0:T(8,128)(2,1)S(1)}, bf16[2,2,2,80,576]{4,3,2,1,0:T(8,128)(2,1)S(1)}, u32[]{:S(2)}, u32[]{:S(2)}) %collective-permute-start.19) | collective-permute-done | bytes 737312 | tf_op jit(solution)/shard_map/ppermute | solution.py:119
  204.1 16.8 %shard_map.255 = (bf16[512,2048]{1,0:T(8,128)(2,1)}, f32[512,576]{1,0:T(8,128)}, bf16[512,512]{1,0:T(8,128)(2,1)}, bf16[512,768]{1,0:T(8,128)(2,1)}, bf16[512,76...) custom-call(bf16[512,2048]{1,0:T(8,128)(2,1)} %bitcast.617, ...), custom_call_target="tpu_custom_call" | custom-call | tf_op jit(solution)/shard_map/pallas_call | solution.py:447
  237.4 11.6 %collective-permute-done.23 = bf16[128,2048]{0,1:T(8,128)(2,1)} collective-permute-done((bf16[128,2048]{0,1:T(8,128)(2,1)}, bf16[128,2048]{0,1:T(8,128)(2,1)}, u32[]{:S(2)}, u32[]{:S(2)}) %collective-permute-start.23) | collective-permute-done | bytes 524320 | tf_op jit(solution)/shard_map/ppermute | solution.py:119
  254.0 16.5 %shard_map.256 = (bf16[1152,2048]{1,0:T(8,128)(2,1)}, f32[1152,1408]{1,0:T(8,128)}, f32[2048,256]{1,0:T(8,128)}) custom-call(bf16[2048,2048]{1,0:T(8,128)(2,1)} %all-gather.8.cloned.1.call-done.grad_ref.right_ref, s32[8,1,256]{2,1,0:T(1,128)} %compare_select_fusion.slot_ref, f32[8,1,256]{2,1,0:T(1,128)} %bitcast.696, bf16[1408,2048]{1,0:T(8,128)(2,1)} %bitcast.598, ...), custom_call_target="tpu_custom_call" | custom-call | tf_op jit(solution)/shard_map/pallas_call | solution.py:447
  273.8 5.7 all-to-all-start
  279.5 4.3 collective-permute-done.31
  293.5 5.8 collective-permute-start.32
  299.3 8.8 %all-to-all-done = bf16[16,64,512]{2,1,0:T(8,128)(2,1)} async-done(((bf16[16,64,512]{2,1,0:T(8,128)(2,1)}), bf16[16,64,512]{2,1,0:T(8,128)(2,1)}, u32[]{:S(2)}, u32[]{:S(2)}) %all-to-all-start) | async-done | bytes 1048608 | tf_op jit(solution)/shard_map/all_to_all | solution.py:803
  308.1 5.7 collective-permute-start.28
  323.4 3.2 collective-permute-start.36
  335.4 6.7 collective-permute-done.37.right_came_ref
  342.1 10.7 %collective-permute-done.35.left_came_ref = bf16[1024,640]{1,0:T(8,128)(2,1)} collective-permute-done((bf16[1024,640]{1,0:T(8,128)(2,1)}, bf16[1024,640]{1,0:T(8,128)(2,1)}, u32[]{:S(2)}, u32[]{:S(2)}) %collective-permute-start.35) | collective-permute-done | bytes 1310752 | tf_op jit(solution)/shard_map/ppermute | solution.py:119
  353.4 62.2 %shard_map.257 = (bf16[2048,2048]{1,0:T(8,128)(2,1)}, bf16[1152,2048]{1,0:T(8,128)(2,1)}, bf16[1152,1408]{1,0:T(8,128)(2,1)}, bf16[1152,2816]{1,0:T(8,128)(2,1)}...) custom-call(s32[3]{0:T(128)} %pad_add_fusion.1.me_ref, ...), custom_call_target="tpu_custom_call" | custom-call | tf_op jit(solution)/shard_map/pallas_call | solution.py:447
  418.1 12.7 %shard_map.258 = bf16[1024,2816]{1,0:T(8,128)(2,1)} custom-call(s32[1]{0:T(128)} %bitcast.131.place_ref, bf16[1152,2048]{1,0:T(8,128)(2,1)} %get-tuple-element.268.left_ref, bf16[1152,2816]{1,0:T(8,128)(2,1)} %get-tuple-element.269.right_ref), custom_call_target="tpu_custom_call" | custom-call | tf_op jit(solution)/shard_map/pallas_call | solution.py:661
  430.9 9.3 %collective-permute-done.38 = bf16[1024,640]{1,0:T(8,128)(2,1)} collective-permute-done((bf16[1024,640]{1,0:T(8,128)(2,1)}, bf16[1024,640]{1,0:T(8,128)(2,1)}, u32[]{:S(2)}, u32[]{:S(2)}) %collective-permute-start.38) | collective-permute-done | bytes 1310752 | tf_op jit(solution)/shard_map/ppermute | solution.py:119
  440.2 3.7 collective-permute-done.39
  453.0 9.7 %fusion.79 = f32[1408,2048]{1,0:T(8,128)S(1)} fusion(bf16[1152,1408]{1,0:T(8,128)(2,1)S(1)} %copy-done.27, bf16[1152,2048]{1,0:T(8,128)(2,1)} %get-tuple-element.231), kind=kOutput, calls=%fused_computation.378 | convolution fusion | flops 6643777536 | bytes 19496960 | tf_op jit(solution)/shard_map/dot_general | solution.py:74
  468.6 10.6 %shard_map.260 = bf16[2048,512]{1,0:T(8,128)(2,1)} custom-call(s32[1]{0:T(128)} %constant.339.clone.1.place_ref, bf16[2048,2048]{1,0:T(8,128)(2,1)} %get-tuple-element.240.left_ref, bf16[2048,512]{1,0:T(8,128)(2,1)} %get-tuple-element.241.right_ref), custom_call_target="tpu_custom_call" | custom-call | tf_op jit(solution)/shard_map/pallas_call | solution.py:661
  481.5 11.4 %collective-permute-start.48 = (bf16[16,64,512]{2,1,0:T(8,128)(2,1)}, bf16[16,64,512]{2,1,0:T(8,128)(2,1)}, u32[]{:S(2)}, u32[]{:S(2)}) collective-permute-start(bf16[16,64,512]{2,1,0:T(8,128)(2,1)} %dynamic-slice_bitcast_fusion.2), channel_id=1, source_target_pairs={{0,16},{16,0},{1,17},{17,1},{2,18},{18,2},{3,19},{19,3},{4,20},{20... | collective-permute-start | bytes 3145736 | tf_op jit(solution)/shard_map/ppermute | solution.py:103
  492.9 7.4 shard_map.259
  520.3 7.7 collective-permute-done.44
  535.2 19.7 %shard_map.261 = (bf16[1024,640]{1,0:T(8,128)(2,1)}, bf16[1024,640]{1,0:T(8,128)(2,1)}, bf16[1024,768]{1,0:T(8,128)(2,1)}, bf16[1024,768]{1,0:T(8,128)(2,1)}, bf...) custom-call(s32[3]{0:T(128)} %pad_add_fusion.1.me_ref, bf16[1152,1408]{1,0:T(8,128)(2,1)} %get-tuple-element.247.hidden_ref, ...), custom_call_target="tpu_custom_call" | custom-call | tf_op jit(solution)/shard_map/pallas_call | solution.py:447
  562.7 13.0 %shard_map.262 = f32[1024,2816]{1,0:T(8,128)} custom-call(s32[1]{0:T(128)} %bitcast.162.place_ref, bf16[1152,2048]{1,0:T(8,128)(2,1)} %get-tuple-element.268.left_ref, bf16[1152,2816]{1,0:T(8,128)(2,1)} %get-tuple-element.269.right_ref), custom_call_target="tpu_custom_call" | custom-call | tf_op jit(solution)/shard_map/pallas_call | solution.py:661
  575.7 20.6 %collective-permute-done.52 = bf16[128,2048]{0,1:T(8,128)(2,1)S(1)} collective-permute-done((bf16[128,2048]{0,1:T(8,128)(2,1)S(1)}, bf16[128,2048]{0,1:T(8,128)(2,1)S(1)}, u32[]{:S(2)}, u32[]{:S(2)}) %collective-permute-start.52) | collective-permute-done | bytes 524320 | tf_op jit(solution)/shard_map/ppermute | solution.py:119
  596.5 7.7 collective-permute-start.59
  610.6 3.1 copy.633
  613.7 18.0 %shard_map.263 = (bf16[512,768]{1,0:T(8,128)(2,1)}, bf16[512,1024]{1,0:T(8,128)(2,1)}, bf16[512,576]{1,0:T(8,128)(2,1)}, f32[1,1,512]{2,1,0:T(1,128)}, bf16[512,2048]{1,0:T(8,128)(2,1)}) custom-call(bf16[512,2048]{1,0:T(8,128)(2,1)} %bitcast.620, bf16[512,2048]{1,0:T(8,128)(2,1)} %bitcast.602, f32[16,128,128]{2,1,0:T(8,128)} %get-tuple-element.276.probs_ref, ...), custom_call_target="tpu_custom_call" | custom-call | tf_op jit(solution)/shard_map/pallas_call | solution.py:447
  631.8 2.9 fusion.80
  642.0 3.3 reshape.578
  660.4 5.4 convolution_convert_fusion
  674.0 4.7 pad_maximum_fusion.1
  683.2 3.3 collective-permute-done.60
  696.8 8.9 %collective-permute-done.67 = bf16[128,768]{0,1:T(8,128)(2,1)S(1)} collective-permute-done((bf16[128,768]{0,1:T(8,128)(2,1)S(1)}, bf16[128,768]{0,1:T(8,128)(2,1)S(1)}, u32[]{:S(2)}, u32[]{:S(2)}) %collective-permute-start.67) | collective-permute-done | bytes 196640 | tf_op jit(solution)/shard_map/ppermute | solution.py:119
  739.4 11.2 %convert_add_fusion = f32[1024,2816]{1,0:T(8,128)} fusion(f32[1024,2816]{1,0:T(8,128)} %shard_map.262, bf16[1024,2816]{1,0:T(8,128)(2,1)} %collective-permute-done.75), kind=kLoop, calls=%fused_computation | loop fusion | flops 5767168 | bytes 28835840 | tf_op jit(solution)/shard_map/add | solution.py:1006
  750.6 14.4 %reshape.593 = f32[1,1024,2,1408]{3,2,1,0:T(2,128)} reshape(f32[1024,2816]{1,0:T(8,128)} %convert_add_fusion) | data formatting | bytes 23068672 | tf_op jit(solution)/shard_map/reshape | solution.py:1138
  777.5 4.9 all-to-all-start.1
  794.5 5.2 add_bitcast_fusion
  799.6 4.7 collective-permute-done.76
  804.4 20.0 %collective-permute-done.77 = bf16[2,2,48,1024]{3,2,1,0:T(8,128)(2,1)S(1)} collective-permute-done((bf16[2,2,48,1024]{3,2,1,0:T(8,128)(2,1)S(1)}, bf16[2,2,48,1024]{3,2,1,0:T(8,128)(2,1)S(1)}, u32[]{:S(2)}, u32[]{:S(2)}) %collective-permute-start.77) | collective-permute-done | bytes 393248 | tf_op jit(solution)/shard_map/ppermute | solution.py:119
  860.6 3.8 collective-permute-start.89
  (722 shorter events, 350.7 us)
Async XLA Ops:
  7.2 246.8 %all-gather.10.cloned.1.call-start = ((), (), s32[]{:S(2)}) async-start(), calls=%async_computation.4 | async-start | bytes 8650752 | tf_op jit(solution)/shard_map/all_gather | solution.py:801
  7.9 246.0 %all-gather.8.cloned.1.call-start = ((), (), s32[]{:S(2)}) async-start(), calls=%async_computation.3 | async-start | bytes 8912896 | tf_op jit(solution)/shard_map/all_gather | solution.py:900
  11.8 23.5 %collective-permute-start = (bf16[128,2048]{0,1:T(8,128)(2,1)}, bf16[128,2048]{0,1:T(8,128)(2,1)}, u32[]{:S(2)}, u32[]{:S(2)}) collective-permute-start(bf16[128,2048]{0,1:T(8,128)(2,1)} %bitcast.2), channel_id=1, source_target_pairs={{0,4},{1,5},{2,6},{3,7},{4,0},{5,1},{6,2},{7,3},{8,12},{9,13},{10,... | collective-permute-start | bytes 1572872 | tf_op jit(solution)/shard_map/ppermute | solution.py:119
  15.5 41.9 %collective-permute-start.6 = (bf16[2,32,1024]{2,0,1:T(2,128)(2,1)}, bf16[2,32,1024]{2,0,1:T(2,128)(2,1)}, u32[]{:S(2)}, u32[]{:S(2)}) collective-permute-start(bf16[2,32,1024]{2,0,1:T(2,128)(2,1)} %get-tuple-element.545), channel_id=1, source_target_pairs={{0,2},{1,3},{2,0},{3,1},{4,6},{5,7},{6,4},{7,5},{8,10},{9,11},{10,... | collective-permute-start | bytes 393224 | tf_op jit(solution)/shard_map/ppermute | solution.py:119
  16.7 40.6 %collective-permute-start.7 = (bf16[2,32,1024]{2,0,1:T(2,128)(2,1)}, bf16[2,32,1024]{2,0,1:T(2,128)(2,1)}, u32[]{:S(2)}, u32[]{:S(2)}) collective-permute-start(bf16[2,32,1024]{2,0,1:T(2,128)(2,1)} %get-tuple-element.544), channel_id=1, source_target_pairs={{0,8},{1,9},{2,10},{3,11},{4,12},{5,13},{6,14},{7,15},{8,0},{9,1},... | collective-permute-start | bytes 393224 | tf_op jit(solution)/shard_map/ppermute | solution.py:119
  59.1 25.8 %collective-permute-start.12 = (bf16[2,2,32,1024]{3,1,2,0:T(2,128)(2,1)S(1)}, bf16[2,2,32,1024]{3,1,2,0:T(2,128)(2,1)S(1)}, u32[]{:S(2)}, u32[]{:S(2)}) collective-permute-start(bf16[2,2,32,1024]{3,1,2,0:T(2,128)(2,1)S(1)} %pad_maximum_fusion.31), channel_id=1, source_target_pairs={{0,2},{1,3},{2,0},{3,1},{4,6},{5,7},{6,4},{7,5},{8,10},{9,11},{10,... | collective-permute-start | bytes 786440 | tf_op jit(solution)/shard_map/ppermute | solution.py:119
  60.5 26.0 %collective-permute-start.10 = (bf16[2,2,80,1024]{3,2,1,0:T(8,128)(2,1)S(1)}, bf16[2,2,80,1024]{3,2,1,0:T(8,128)(2,1)}, u32[]{:S(2)}, u32[]{:S(2)}) collective-permute-start(bf16[2,2,80,1024]{3,2,1,0:T(8,128)(2,1)S(1)} %pad_maximum_fusion.18), channel_id=1, source_target_pairs={{0,1},{1,0},{2,3},{3,2},{4,5},{5,4},{6,7},{7,6},{8,9},{9,8},{10,11... | collective-permute-start | bytes 1966088 | tf_op jit(solution)/shard_map/ppermute | solution.py:119
  62.0 23.1 %collective-permute-start.9 = (bf16[2,2,48,1024]{3,2,0,1:T(8,128)(2,1)S(1)}, bf16[2,2,48,1024]{3,2,0,1:T(8,128)(2,1)S(1)}, u32[]{:S(2)}, u32[]{:S(2)}) collective-permute-start(bf16[2,2,48,1024]{3,2,0,1:T(8,128)(2,1)S(1)} %pad_maximum_fusion.25), channel_id=1, source_target_pairs={{0,8},{1,9},{2,10},{3,11},{4,12},{5,13},{6,14},{7,15},{8,0},{9,1},... | collective-permute-start | bytes 1179656 | tf_op jit(solution)/shard_map/ppermute | solution.py:119
  62.5 22.5 %collective-permute-start.11 = (bf16[2,2,32,1024]{3,0,2,1:T(2,128)(2,1)S(1)}, bf16[2,2,32,1024]{3,0,2,1:T(2,128)(2,1)S(1)}, u32[]{:S(2)}, u32[]{:S(2)}) collective-permute-start(bf16[2,2,32,1024]{3,0,2,1:T(2,128)(2,1)S(1)} %pad_maximum_fusion.30), channel_id=1, source_target_pairs={{0,1},{1,0},{2,3},{3,2},{4,5},{5,4},{6,7},{7,6},{8,9},{9,8},{10,11... | collective-permute-start | bytes 786440 | tf_op jit(solution)/shard_map/ppermute | solution.py:119
  86.6 266.9 %all-gather.6.cloned.1.call-start = ((), (), s32[]{:S(2)}) async-start(), calls=%async_computation.2 | async-start | bytes 17301504 | tf_op jit(solution)/shard_map/all_gather | solution.py:800
  104.9 43.6 %collective-permute-start.15 = (bf16[2,2,2,80,1024]{4,3,1,0,2:T(8,128)(2,1)}, bf16[2,2,2,80,1024]{4,3,1,0,2:T(8,128)(2,1)}, u32[]{:S(2)}, u32[]{:S(2)}) collective-permute-start(bf16[2,2,2,80,1024]{4,3,1,0,2:T(8,128)(2,1)} %pad_maximum_fusion.8), channel_id=1, source_target_pairs={{0,2},{1,3},{2,0},{3,1},{4,6},{5,7},{6,4},{7,5},{8,10},{9,11},{10,... | collective-permute-start | bytes 3932168 | tf_op jit(solution)/shard_map/ppermute | solution.py:119
  108.3 36.4 %collective-permute-start.16 = (bf16[2,2,2,32,1024]{4,0,3,1,2:T(2,128)(2,1)}, bf16[2,2,2,32,1024]{4,0,3,1,2:T(2,128)(2,1)}, u32[]{:S(2)}, u32[]{:S(2)}) collective-permute-start(bf16[2,2,2,32,1024]{4,0,3,1,2:T(2,128)(2,1)} %pad_maximum_fusion.22), channel_id=1, source_target_pairs={{0,8},{1,9},{2,10},{3,11},{4,12},{5,13},{6,14},{7,15},{8,0},{9,1},... | collective-permute-start | bytes 1572872 | tf_op jit(solution)/shard_map/ppermute | solution.py:119
  109.3 35.4 %collective-permute-start.14 = (bf16[2,2,2,48,1024]{4,3,1,2,0:T(8,128)(2,1)}, bf16[2,2,2,48,1024]{4,3,1,2,0:T(8,128)(2,1)}, u32[]{:S(2)}, u32[]{:S(2)}) collective-permute-start(bf16[2,2,2,48,1024]{4,3,1,2,0:T(8,128)(2,1)} %pad_maximum_fusion.15), channel_id=1, source_target_pairs={{0,1},{1,0},{2,3},{3,2},{4,5},{5,4},{6,7},{7,6},{8,9},{9,8},{10,11... | collective-permute-start | bytes 2359304 | tf_op jit(solution)/shard_map/ppermute | solution.py:119
  149.9 31.6 %collective-permute-start.19 = (bf16[2,2,2,80,576]{4,3,2,1,0:T(8,128)(2,1)S(1)}, bf16[2,2,2,80,576]{4,3,2,1,0:T(8,128)(2,1)S(1)}, u32[]{:S(2)}, u32[]{:S(2)}) collective-permute-start(bf16[2,2,2,80,576]{4,3,2,1,0:T(8,128)(2,1)S(1)} %pad_maximum_fusion.14), channel_id=1, source_target_pairs={{0,4},{1,5},{2,6},{3,7},{4,0},{5,1},{6,2},{7,3},{8,12},{9,13},{10,... | collective-permute-start | bytes 2211848 | tf_op jit(solution)/shard_map/ppermute | solution.py:119
  273.8 34.3 %all-to-all-start = ((bf16[16,64,512]{2,1,0:T(8,128)(2,1)}), bf16[16,64,512]{2,1,0:T(8,128)(2,1)}, u32[]{:S(2)}, u32[]{:S(2)}) async-start(bf16[16,64,512]{2,1,0:T(8,128)(2,1)} %reshape.540), calls=%async_computation | async-start | bytes 2097152 | tf_op jit(solution)/shard_map/all_to_all | solution.py:803
  286.6 27.2 %collective-permute-start.34 = (bf16[2,2,128,640]{2,3,0,1:T(8,128)(2,1)}, bf16[2,2,128,640]{2,3,0,1:T(8,128)(2,1)}, u32[]{:S(2)}, u32[]{:S(2)}) collective-permute-start(bf16[2,2,128,640]{2,3,0,1:T(8,128)(2,1)} %pad_maximum_fusion.20), channel_id=1, source_target_pairs={{0,2},{1,3},{2,0},{3,1},{4,6},{5,7},{6,4},{7,5},{8,10},{9,11},{10,... | collective-permute-start | bytes 1966088 | tf_op jit(solution)/shard_map/ppermute | solution.py:119
  289.7 24.3 %collective-permute-start.33 = (bf16[2,2,128,768]{2,3,0,1:T(8,128)(2,1)}, bf16[2,2,128,768]{2,3,0,1:T(8,128)(2,1)}, u32[]{:S(2)}, u32[]{:S(2)}) collective-permute-start(bf16[2,2,128,768]{2,3,0,1:T(8,128)(2,1)} %pad_maximum_fusion.16), channel_id=1, source_target_pairs={{0,4},{1,5},{2,6},{3,7},{4,0},{5,1},{6,2},{7,3},{8,12},{9,13},{10,... | collective-permute-start | bytes 2359304 | tf_op jit(solution)/shard_map/ppermute | solution.py:119
  308.1 24.0 %collective-permute-start.28 = (bf16[16,64,512]{2,1,0:T(8,128)(2,1)}, bf16[16,64,512]{2,1,0:T(8,128)(2,1)}, u32[]{:S(2)}, u32[]{:S(2)}) collective-permute-start(bf16[16,64,512]{2,1,0:T(8,128)(2,1)} %all-to-all-done), channel_id=1, source_target_pairs={{0,16},{16,0},{1,17},{17,1},{2,18},{18,2},{3,19},{19,3},{4,20},{20... | collective-permute-start | bytes 3145736 | tf_op jit(solution)/shard_map/ppermute | solution.py:84
  316.8 25.3 %collective-permute-start.37 = (bf16[1024,640]{1,0:T(8,128)(2,1)}, bf16[1024,640]{1,0:T(8,128)(2,1)}, u32[]{:S(2)}, u32[]{:S(2)}) collective-permute-start(bf16[1024,640]{1,0:T(8,128)(2,1)} %bitcast.130.right_ref), channel_id=1, source_target_pairs={{0,1},{1,0},{2,3},{3,2},{4,5},{5,4},{6,7},{7,6},{8,9},{9,8},{10,11... | collective-permute-start | bytes 3932168 | tf_op jit(solution)/shard_map/ppermute | solution.py:119
  323.4 30.0 %collective-permute-start.36 = (bf16[1024,768]{1,0:T(8,128)(2,1)S(1)}, bf16[1024,768]{1,0:T(8,128)(2,1)}, u32[]{:S(2)}, u32[]{:S(2)}) collective-permute-start(bf16[1024,768]{1,0:T(8,128)(2,1)S(1)} %bitcast.637), channel_id=1, source_target_pairs={{0,2},{1,3},{2,0},{3,1},{4,6},{5,7},{6,4},{7,5},{8,10},{9,11},{10,... | collective-permute-start | bytes 4718600 | tf_op jit(solution)/shard_map/ppermute | solution.py:119
  415.6 28.3 %collective-permute-start.39 = (bf16[1024,768]{1,0:T(8,128)(2,1)}, bf16[1024,768]{1,0:T(8,128)(2,1)S(1)}, u32[]{:S(2)}, u32[]{:S(2)}) collective-permute-start(bf16[1024,768]{1,0:T(8,128)(2,1)} %get-tuple-element.217), channel_id=1, source_target_pairs={{0,2},{1,3},{2,0},{3,1},{4,6},{5,7},{6,4},{7,5},{8,10},{9,11},{10,... | collective-permute-start | bytes 4718600 | tf_op jit(solution)/shard_map/ppermute | solution.py:119
  481.5 36.1 %collective-permute-start.48 = (bf16[16,64,512]{2,1,0:T(8,128)(2,1)}, bf16[16,64,512]{2,1,0:T(8,128)(2,1)}, u32[]{:S(2)}, u32[]{:S(2)}) collective-permute-start(bf16[16,64,512]{2,1,0:T(8,128)(2,1)} %dynamic-slice_bitcast_fusion.2), channel_id=1, source_target_pairs={{0,16},{16,0},{1,17},{17,1},{2,18},{18,2},{3,19},{19,3},{4,20},{20... | collective-permute-start | bytes 3145736 | tf_op jit(solution)/shard_map/ppermute | solution.py:103
  503.9 24.1 %collective-permute-start.45 = (bf16[2,128,768]{1,2,0:T(8,128)(2,1)}, bf16[2,128,768]{1,2,0:T(8,128)(2,1)}, u32[]{:S(2)}, u32[]{:S(2)}) collective-permute-start(bf16[2,128,768]{1,2,0:T(8,128)(2,1)} %bitcast.145), channel_id=1, source_target_pairs={{0,1},{1,0},{2,3},{3,2},{4,5},{5,4},{6,7},{7,6},{8,9},{9,8},{10,11... | collective-permute-start | bytes 1179656 | tf_op jit(solution)/shard_map/ppermute | solution.py:119
  529.7 25.2 %collective-permute-start.51 = (bf16[128,640]{0,1:T(8,128)(2,1)}, bf16[128,640]{0,1:T(8,128)(2,1)}, u32[]{:S(2)}, u32[]{:S(2)}) collective-permute-start(bf16[128,640]{0,1:T(8,128)(2,1)} %dynamic-slice_bitcast_fusion.27), channel_id=1, source_target_pairs={{0,8},{1,9},{2,10},{3,11},{4,12},{5,13},{6,14},{7,15},{8,0},{9,1},... | collective-permute-start | bytes 491528 | tf_op jit(solution)/shard_map/ppermute | solution.py:119
  531.5 23.5 %collective-permute-start.50 = (bf16[128,768]{0,1:T(8,128)(2,1)}, bf16[128,768]{0,1:T(8,128)(2,1)}, u32[]{:S(2)}, u32[]{:S(2)}) collective-permute-start(bf16[128,768]{0,1:T(8,128)(2,1)} %dynamic-slice_bitcast_fusion.24), channel_id=1, source_target_pairs={{0,8},{1,9},{2,10},{3,11},{4,12},{5,13},{6,14},{7,15},{8,0},{9,1},... | collective-permute-start | bytes 589832 | tf_op jit(solution)/shard_map/ppermute | solution.py:119
  559.8 36.5 %collective-permute-start.54 = (bf16[1024,768]{1,0:T(8,128)(2,1)S(1)}, bf16[1024,768]{1,0:T(8,128)(2,1)S(1)}, u32[]{:S(2)}, u32[]{:S(2)}) collective-permute-start(bf16[1024,768]{1,0:T(8,128)(2,1)S(1)} %copy-done.107), channel_id=1, source_target_pairs={{0,2},{1,3},{2,0},{3,1},{4,6},{5,7},{6,4},{7,5},{8,10},{9,11},{10,... | collective-permute-start | bytes 4718600 | tf_op jit(solution)/shard_map/ppermute | solution.py:119
  561.2 35.0 %collective-permute-start.55 = (bf16[1024,640]{1,0:T(8,128)(2,1)}, bf16[1024,640]{1,0:T(8,128)(2,1)S(1)}, u32[]{:S(2)}, u32[]{:S(2)}) collective-permute-start(bf16[1024,640]{1,0:T(8,128)(2,1)} %get-tuple-element.267), channel_id=1, source_target_pairs={{0,1},{1,0},{2,3},{3,2},{4,5},{5,4},{6,7},{7,6},{8,9},{9,8},{10,11... | collective-permute-start | bytes 3932168 | tf_op jit(solution)/shard_map/ppermute | solution.py:119
  561.2 35.0 %collective-permute-start.53 = (bf16[1024,640]{1,0:T(8,128)(2,1)}, bf16[1024,640]{1,0:T(8,128)(2,1)S(1)}, u32[]{:S(2)}, u32[]{:S(2)}) collective-permute-start(bf16[1024,640]{1,0:T(8,128)(2,1)} %get-tuple-element.261), channel_id=1, source_target_pairs={{0,4},{1,5},{2,6},{3,7},{4,0},{5,1},{6,2},{7,3},{8,12},{9,13},{10,... | collective-permute-start | bytes 3932168 | tf_op jit(solution)/shard_map/ppermute | solution.py:119
  561.2 35.0 %collective-permute-start.52 = (bf16[128,2048]{0,1:T(8,128)(2,1)S(1)}, bf16[128,2048]{0,1:T(8,128)(2,1)S(1)}, u32[]{:S(2)}, u32[]{:S(2)}) collective-permute-start(bf16[128,2048]{0,1:T(8,128)(2,1)S(1)} %get-tuple-element.440), channel_id=1, source_target_pairs={{0,4},{1,5},{2,6},{3,7},{4,0},{5,1},{6,2},{7,3},{8,12},{9,13},{10,... | collective-permute-start | bytes 1572872 | tf_op jit(solution)/shard_map/ppermute | solution.py:119
  605.8 25.9 %collective-permute-start.58 = (bf16[2,2,128,640]{3,2,1,0:T(8,128)(2,1)}, bf16[2,2,128,640]{3,2,1,0:T(8,128)(2,1)}, u32[]{:S(2)}, u32[]{:S(2)}) collective-permute-start(bf16[2,2,128,640]{3,2,1,0:T(8,128)(2,1)} %dynamic-slice_bitcast_fusion.8), channel_id=1, source_target_pairs={{0,2},{1,3},{2,0},{3,1},{4,6},{5,7},{6,4},{7,5},{8,10},{9,11},{10,... | collective-permute-start | bytes 1966088 | tf_op jit(solution)/shard_map/ppermute | solution.py:119
  607.4 24.4 %collective-permute-start.57 = (bf16[2,2,128,768]{3,2,1,0:T(8,128)(2,1)}, bf16[2,2,128,768]{3,2,1,0:T(8,128)(2,1)}, u32[]{:S(2)}, u32[]{:S(2)}) collective-permute-start(bf16[2,2,128,768]{3,2,1,0:T(8,128)(2,1)} %dynamic-slice_bitcast_fusion.4), channel_id=1, source_target_pairs={{0,4},{1,5},{2,6},{3,7},{4,0},{5,1},{6,2},{7,3},{8,12},{9,13},{10,... | collective-permute-start | bytes 2359304 | tf_op jit(solution)/shard_map/ppermute | solution.py:119
  608.8 23.0 %collective-permute-start.56 = (bf16[2,2,128,640]{3,2,1,0:T(8,128)(2,1)}, bf16[2,2,128,640]{3,2,1,0:T(8,128)(2,1)}, u32[]{:S(2)}, u32[]{:S(2)}) collective-permute-start(bf16[2,2,128,640]{3,2,1,0:T(8,128)(2,1)} %dynamic-slice_bitcast_fusion.9), channel_id=1, source_target_pairs={{0,1},{1,0},{2,3},{3,2},{4,5},{5,4},{6,7},{7,6},{8,9},{9,8},{10,11... | collective-permute-start | bytes 1966088 | tf_op jit(solution)/shard_map/ppermute | solution.py:119
  638.6 41.9 %collective-permute-start.63 = (bf16[16,64,576]{2,1,0:T(8,128)(2,1)}, bf16[16,64,576]{2,1,0:T(8,128)(2,1)}, u32[]{:S(2)}, u32[]{:S(2)}) collective-permute-start(bf16[16,64,576]{2,1,0:T(8,128)(2,1)} %fusion.4), channel_id=1, source_target_pairs={{0,16},{16,0},{1,17},{17,1},{2,18},{18,2},{3,19},{19,3},{4,20},{20... | collective-permute-start | bytes 3538952 | tf_op jit(solution)/shard_map/ppermute | solution.py:103
  652.3 30.9 %collective-permute-start.62 = (bf16[2,128,640]{1,2,0:T(8,128)(2,1)}, bf16[2,128,640]{1,2,0:T(8,128)(2,1)}, u32[]{:S(2)}, u32[]{:S(2)}) collective-permute-start(bf16[2,128,640]{1,2,0:T(8,128)(2,1)} %bitcast.693), channel_id=1, source_target_pairs={{0,4},{1,5},{2,6},{3,7},{4,0},{5,1},{6,2},{7,3},{8,12},{9,13},{10,... | collective-permute-start | bytes 983048 | tf_op jit(solution)/shard_map/ppermute | solution.py:119
  660.4 26.0 %collective-permute-start.61 = (bf16[2,128,768]{1,2,0:T(8,128)(2,1)}, bf16[2,128,768]{1,2,0:T(8,128)(2,1)}, u32[]{:S(2)}, u32[]{:S(2)}) collective-permute-start(bf16[2,128,768]{1,2,0:T(8,128)(2,1)} %bitcast.180), channel_id=1, source_target_pairs={{0,1},{1,0},{2,3},{3,2},{4,5},{5,4},{6,7},{7,6},{8,9},{9,8},{10,11... | collective-permute-start | bytes 1179656 | tf_op jit(solution)/shard_map/ppermute | solution.py:119
  680.2 25.5 %collective-permute-start.65 = (bf16[128,2048]{0,1:T(8,128)(2,1)S(1)}, bf16[128,2048]{0,1:T(8,128)(2,1)S(1)}, u32[]{:S(2)}, u32[]{:S(2)}) collective-permute-start(bf16[128,2048]{0,1:T(8,128)(2,1)S(1)} %dynamic-slice_bitcast_fusion.14), channel_id=1, source_target_pairs={{0,4},{1,5},{2,6},{3,7},{4,0},{5,1},{6,2},{7,3},{8,12},{9,13},{10,... | collective-permute-start | bytes 1572872 | tf_op jit(solution)/shard_map/ppermute | solution.py:119
  707.3 31.3 %collective-permute-start.75 = (bf16[1024,2816]{1,0:T(8,128)(2,1)}, bf16[1024,2816]{1,0:T(8,128)(2,1)}, u32[]{:S(2)}, u32[]{:S(2)}) collective-permute-start(bf16[1024,2816]{1,0:T(8,128)(2,1)} %shard_map.258), channel_id=1, source_target_pairs={{0,16},{16,0},{1,17},{17,1},{2,18},{18,2},{3,19},{19,3},{4,20},{20... | collective-permute-start | bytes 17301512 | tf_op jit(solution)/shard_map/ppermute | solution.py:1006
  721.6 43.4 %collective-permute-start.72 = (bf16[2,2,2,80,1024]{4,3,2,1,0:T(8,128)(2,1)}, bf16[2,2,2,80,1024]{4,3,2,1,0:T(8,128)(2,1)}, u32[]{:S(2)}, u32[]{:S(2)}) collective-permute-start(bf16[2,2,2,80,1024]{4,3,2,1,0:T(8,128)(2,1)} %dynamic-slice_bitcast_fusion.1), channel_id=1, source_target_pairs={{0,2},{1,3},{2,0},{3,1},{4,6},{5,7},{6,4},{7,5},{8,10},{9,11},{10,... | collective-permute-start | bytes 3932168 | tf_op jit(solution)/shard_map/ppermute | solution.py:119
  724.2 40.9 %collective-permute-start.73 = (bf16[2,2,2,32,1024]{4,3,2,1,0:T(8,128)(2,1)}, bf16[2,2,2,32,1024]{4,3,2,1,0:T(8,128)(2,1)}, u32[]{:S(2)}, u32[]{:S(2)}) collective-permute-start(bf16[2,2,2,32,1024]{4,3,2,1,0:T(8,128)(2,1)} %dynamic-slice_bitcast_fusion.13), channel_id=1, source_target_pairs={{0,8},{1,9},{2,10},{3,11},{4,12},{5,13},{6,14},{7,15},{8,0},{9,1},... | collective-permute-start | bytes 1572872 | tf_op jit(solution)/shard_map/ppermute | solution.py:119
  725.0 40.0 %collective-permute-start.74 = (bf16[2,2,2,32,1024]{4,3,2,1,0:T(8,128)(2,1)}, bf16[2,2,2,32,1024]{4,3,2,1,0:T(8,128)(2,1)}, u32[]{:S(2)}, u32[]{:S(2)}) collective-permute-start(bf16[2,2,2,32,1024]{4,3,2,1,0:T(8,128)(2,1)} %dynamic-slice_bitcast_fusion.12), channel_id=1, source_target_pairs={{0,1},{1,0},{2,3},{3,2},{4,5},{5,4},{6,7},{7,6},{8,9},{9,8},{10,11... | collective-permute-start | bytes 1572872 | tf_op jit(solution)/shard_map/ppermute | solution.py:119
  735.4 29.6 %collective-permute-start.71 = (bf16[2,2,2,48,1024]{4,3,2,1,0:T(8,128)(2,1)}, bf16[2,2,2,48,1024]{4,3,2,1,0:T(8,128)(2,1)}, u32[]{:S(2)}, u32[]{:S(2)}) collective-permute-start(bf16[2,2,2,48,1024]{4,3,2,1,0:T(8,128)(2,1)} %dynamic-slice_bitcast_fusion.3), channel_id=1, source_target_pairs={{0,1},{1,0},{2,3},{3,2},{4,5},{5,4},{6,7},{7,6},{8,9},{9,8},{10,11... | collective-permute-start | bytes 2359304 | tf_op jit(solution)/shard_map/ppermute | solution.py:119
  738.6 26.4 %collective-permute-start.70 = (bf16[2,2,2,65,576]{4,2,3,1,0:T(2,128)(2,1)}, bf16[2,2,2,65,576]{4,2,3,1,0:T(2,128)(2,1)}, u32[]{:S(2)}, u32[]{:S(2)}) collective-permute-start(bf16[2,2,2,65,576]{4,2,3,1,0:T(2,128)(2,1)} %dynamic-slice_bitcast_fusion.6), channel_id=1, source_target_pairs={{0,4},{1,5},{2,6},{3,7},{4,0},{5,1},{6,2},{7,3},{8,12},{9,13},{10,... | collective-permute-start | bytes 1797128 | tf_op jit(solution)/shard_map/ppermute | solution.py:119
  765.0 28.2 %collective-permute-start.81 = (bf16[704,2048]{1,0:T(8,128)(2,1)}, bf16[704,2048]{1,0:T(8,128)(2,1)}, u32[]{:S(2)}, u32[]{:S(2)}) collective-permute-start(bf16[704,2048]{1,0:T(8,128)(2,1)} %fusion), channel_id=1, source_target_pairs={{0,16},{16,0},{1,17},{17,1},{2,18},{18,2},{3,19},{19,3},{4,20},{20... | collective-permute-start | bytes 8650760 | tf_op jit(solution)/shard_map/ppermute | solution.py:1006
  773.0 26.6 %collective-permute-start.80 = (bf16[2,2,32,1024]{3,2,1,0:T(8,128)(2,1)}, bf16[2,2,32,1024]{3,2,1,0:T(8,128)(2,1)}, u32[]{:S(2)}, u32[]{:S(2)}) collective-permute-start(bf16[2,2,32,1024]{3,2,1,0:T(8,128)(2,1)} %dynamic-slice_bitcast_fusion.19), channel_id=1, source_target_pairs={{0,2},{1,3},{2,0},{3,1},{4,6},{5,7},{6,4},{7,5},{8,10},{9,11},{10,... | collective-permute-start | bytes 786440 | tf_op jit(solution)/shard_map/ppermute | solution.py:119
  776.1 23.5 %collective-permute-start.79 = (bf16[2,2,32,1024]{3,2,1,0:T(8,128)(2,1)}, bf16[2,2,32,1024]{3,2,1,0:T(8,128)(2,1)}, u32[]{:S(2)}, u32[]{:S(2)}) collective-permute-start(bf16[2,2,32,1024]{3,2,1,0:T(8,128)(2,1)} %dynamic-slice_bitcast_fusion.20), channel_id=1, source_target_pairs={{0,1},{1,0},{2,3},{3,2},{4,5},{5,4},{6,7},{7,6},{8,9},{9,8},{10,11... | collective-permute-start | bytes 786440 | tf_op jit(solution)/shard_map/ppermute | solution.py:119
  777.5 46.9 %all-to-all-start.1 = ((bf16[16,64,512]{2,1,0:T(8,128)(2,1)}), bf16[16,64,512]{2,1,0:T(8,128)(2,1)}, u32[]{:S(2)}, u32[]{:S(2)}) async-start(bf16[16,64,512]{2,1,0:T(8,128)(2,1)} %fusion.2), calls=%async_computation.1 | async-start | bytes 2097152 | tf_op jit(solution)/shard_map/all_to_all | solution.py:1141
  784.5 39.9 %collective-permute-start.78 = (bf16[2,2,80,1024]{3,2,1,0:T(8,128)(2,1)S(1)}, bf16[2,2,80,1024]{3,2,1,0:T(8,128)(2,1)}, u32[]{:S(2)}, u32[]{:S(2)}) collective-permute-start(bf16[2,2,80,1024]{3,2,1,0:T(8,128)(2,1)S(1)} %dynamic-slice_bitcast_fusion.7), channel_id=1, source_target_pairs={{0,1},{1,0},{2,3},{3,2},{4,5},{5,4},{6,7},{7,6},{8,9},{9,8},{10,11... | collective-permute-start | bytes 1966088 | tf_op jit(solution)/shard_map/ppermute | solution.py:119
  788.2 36.2 %collective-permute-start.77 = (bf16[2,2,48,1024]{3,2,1,0:T(8,128)(2,1)S(1)}, bf16[2,2,48,1024]{3,2,1,0:T(8,128)(2,1)S(1)}, u32[]{:S(2)}, u32[]{:S(2)}) collective-permute-start(bf16[2,2,48,1024]{3,2,1,0:T(8,128)(2,1)S(1)} %dynamic-slice_bitcast_fusion.16), channel_id=1, source_target_pairs={{0,8},{1,9},{2,10},{3,11},{4,12},{5,13},{6,14},{7,15},{8,0},{9,1},... | collective-permute-start | bytes 1179656 | tf_op jit(solution)/shard_map/ppermute | solution.py:119
  (163 other events, 1729.9 us)
Sparse Core Ops, SparseCore 0:
  9.6 18.4 all-gather.9
  86.7 140.1 all-gather.7
  229.0 23.2 all-gather.5

commit v4 on v3

--- a/solution.py
+++ b/solution.py
@@ -124,7 +124,9 @@
     held = list(held)
     for step, bit in enumerate(order):
         if not whole and step + 1 == len(order):
-            values = values.reshape(-1, values.shape[-1])
+            values = values.reshape((-1,) + values.shape[lead + len(held) :])
+            if values.shape[1] % 128 == 0:
+                values = values.reshape(-1, values.shape[-1])
             return values, (yield partner(values, bit))
         other = yield partner(values, bit)
         low = (me & bit) == 0
@@ -298,8 +300,8 @@
     latent = joint_ref[:, :KVR]
     scale = lax.rsqrt(jnp.mean(latent * latent, axis=-1, keepdims=True) + norm_eps)
     kv_normed_ref[...] = (latent * scale * kv_gain_ref[...]).astype(bf16)
-    cos, sin = cos_ref[...], sin_ref[...]
     copies = 2 * ROPE_LANES // DR
+    cos, sin = [jnp.concatenate([ref[...]] * copies, axis=-1) for ref in (cos_ref, sin_ref)]
     front = jnp.concatenate([joint_ref[:, KVR : KVR + DR // 2]] * copies, axis=-1)
     back = jnp.concatenate([joint_ref[:, KVR + DR // 2 :]] * copies, axis=-1)
     keys_ref[:, nope : nope + ROPE_LANES] = (front * cos - back * sin).astype(bf16)
@@ -391,7 +393,8 @@
                 rows_dot(d_scores, heads_ref[part, columns]) * factor
             ).astype(bf16)
             d_key = d_key + rows_dot(d_scores, (rotary * both).astype(bf16)) * factor
-        cos, sin = cos_ref[part, :], sin_ref[part, :]
+        narrow = cos_ref[part, :], sin_ref[part, :]
+        cos, sin = [jnp.concatenate([table] * (2 * ROPE_LANES // DR), axis=-1) for table in narrow]
         front, back = d_rotary[:, :ROPE_LANES], d_rotary[:, ROPE_LANES:]
         d_q_ref[part, nope : nope + ROPE_LANES] = (front * cos + back * sin).astype(bf16)
         d_q_ref[part, nope + ROPE_LANES :] = (back * cos - front * sin).astype(bf16)
@@ -399,7 +402,7 @@
             sum(half[:, at : at + DR // 2] for at in range(0, ROPE_LANES, DR // 2))
             for half in (d_key[:, :ROPE_LANES], d_key[:, ROPE_LANES:])
         ]
-        cos, sin = cos[:, : DR // 2], sin[:, : DR // 2]
+        cos, sin = narrow
         d_key_ref[part, : DR // 2] = front * cos + back * sin
         d_key_ref[part, DR // 2 :] = back * cos - front * sin
     d_kv_normed = lanes_dot(d_kv_ref[...], up_ref[...])
@@ -454,6 +457,121 @@
             scratch_shapes=scratch,
         ),
         out_shape=[jax.ShapeDtypeStruct(shape, dtype) for name, shape, dtype in outs],
+        compiler_params=pltpu.CompilerParams(vmem_limit_bytes=60 * 2**20),
+    )(*scalars, *operands)
+
+
+def without(index, place):
+    return (index >> (place + 1) << place) | (index & ((1 << place) - 1))
+
+
+def assemble_kernel(shape, me_ref, *refs):
+    places, pair_place, slice_rows, pieces = shape
+    sources, (q_ref, up_ref, out_ref) = refs[:8], refs[8:]
+    q_cols, up_cols = q_ref.shape[1], sources[0].shape[-1] - q_ref.shape[1]
+    piece_rows = slice_rows // pieces
+    count = 2 * sources[0].shape[0]
+    start = 0
+    for which, place in enumerate(places):
+        held_ref, came_ref = sources[2 * which : 2 * which + 2]
+        if which == 2:
+            start = 0
+        size = held_ref.shape[1]
+
+        def put(mine, start=start, size=size, which=which, place=place, both=(held_ref, came_ref)):
+            for e in range(count):
+                source = both[(e >> place & 1) ^ mine]
+                at = without(e, place)
+                if which >= 2:
+                    row = without(e, pair_place) * slice_rows + start
+                    half = (e >> pair_place & 1) * source.shape[-1]
+                    out_ref[row : row + size, half : half + source.shape[-1]] = source[at]
+                    continue
+                row = e * 2 * slice_rows + start
+                q_ref[row : row + size, :] = source[at, :, :q_cols]
+                for piece in range(start // piece_rows, (start + size) // piece_rows):
+                    core, column = piece // pieces, piece % pieces
+                    row = (core * count + e) * piece_rows
+                    begin = piece * piece_rows - start
+                    up_ref[row : row + piece_rows, column * up_cols : (column + 1) * up_cols] = (
+                        source[at, begin : begin + piece_rows, q_cols:]
+                    )
+
+        pl.when(me_ref[which] == 0)(functools.partial(put, 0))
+        pl.when(me_ref[which] == 1)(functools.partial(put, 1))
+        start += size
+
+
+def attention_gradients_kernel(
+    shape,
+    normed_ref,
+    d_q_ref,
+    kv_normed_ref,
+    d_kv_ref,
+    attended_ref,
+    branch_ref,
+    d_joint_ref,
+    first_ref,
+    last_ref,
+    out_first_ref,
+    out_last_ref,
+    joint_ref,
+):
+    pair_place, slice_rows, pieces = shape
+    count, cut, _ = first_ref.shape
+    out_cut = out_first_ref.shape[1]
+    q_cols, piece_rows = d_q_ref.shape[1], slice_rows // pieces
+    up_cols = first_ref.shape[-1] - q_cols
+    up = rows_dot(kv_normed_ref[...], d_kv_ref[...]).astype(bf16)
+    for e in range(count):
+        for piece in range(2 * pieces):
+            core, column = piece // pieces, piece % pieces
+            row = (core * count + e) * piece_rows
+            found = up[row : row + piece_rows, column * up_cols : (column + 1) * up_cols]
+            begin = piece * piece_rows
+            if begin < cut:
+                first_ref[e, begin : begin + piece_rows, q_cols:] = found
+            else:
+                last_ref[e, begin - cut : begin - cut + piece_rows, q_cols:] = found
+    width = normed_ref.shape[1]
+    per = 4
+    for at in range(0, count, per):
+        columns = slice(at * 2 * slice_rows, (at + per) * 2 * slice_rows)
+        found = rows_dot(normed_ref[:, columns], d_q_ref[...]).astype(bf16)
+        for e in range(per):
+            row = e * 2 * slice_rows
+            first_ref[at + e, :, :q_cols] = found[row : row + cut]
+            last_ref[at + e, :, :q_cols] = found[row + cut : row + 2 * slice_rows]
+        found = rows_dot(normed_ref[:, columns], d_joint_ref[...]).astype(bf16)
+        for e in range(per):
+            for core in range(2):
+                row = (2 * e + core) * slice_rows
+                joint_ref[core, at + e] = found[row : row + slice_rows]
+    found = rows_dot(attended_ref[...], branch_ref[...]).astype(bf16)
+    half = width // 2
+    for e in range(count):
+        row = without(e, pair_place) * slice_rows
+        side = (e >> pair_place & 1) * half
+        out_first_ref[e] = found[row : row + out_cut, side : side + half]
+        out_last_ref[e] = found[row + out_cut : row + slice_rows, side : side + half]
+
+
+def whole_call(kernel, operands, outs, scalars=()):
+    return pl.pallas_call(
+        kernel,
+        grid_spec=pltpu.PrefetchScalarGridSpec(
+            num_scalar_prefetch=len(scalars),
+            grid=(1,),
+            in_specs=[
+                pl.BlockSpec(value.shape, lambda i, *unused, ndim=value.ndim: (0,) * ndim)
+                for value in operands
+            ],
+            out_specs=[
+                pl.BlockSpec(shape, lambda i, *unused, ndim=len(shape): (0,) * ndim)
+                for shape, dtype in outs
+            ],
+        ),
+        out_shape=[jax.ShapeDtypeStruct(shape, dtype) for shape, dtype in outs],
         compiler_params=pltpu.CompilerParams(vmem_limit_bytes=60 * 2**20),
     )(*scalars, *operands)
 
@@ -654,6 +772,34 @@
     out_ref[...] = rows_dot(left_ref[...], right_ref[...]).astype(out_ref.dtype)
 
 
+def columns_sum_kernel(place_ref, left_ref, right_ref, came_ref, out_ref):
+    found = rows_dot(left_ref[...], right_ref[...]) + came_ref[...].astype(f32)
+    hidden = found.shape[1] // 2
+    out_ref[:, 0, :] = found[:, :hidden]
+    out_ref[:, 1, :] = found[:, hidden:]
+
+
+def columns_sum(left, right, came, place):
+    width, block = left.shape[1] // 2, 256
+    steps = width // block
+    hidden = right.shape[1] // 2
+    return pl.pallas_call(
+        columns_sum_kernel,
+        grid_spec=pltpu.PrefetchScalarGridSpec(
+            num_scalar_prefetch=1,
+            grid=(steps,),
+            in_specs=[
+                pl.BlockSpec((left.shape[0], block), lambda i, place: (0, place[0] * steps + i)),
+                pl.BlockSpec(right.shape, lambda i, place: (0, 0), pipeline_mode=pl.Buffered(1)),
+                pl.BlockSpec((block, right.shape[1]), lambda i, place: (i, 0)),
+            ],
+            out_specs=pl.BlockSpec((block, 2, hidden), lambda i, place: (i, 0, 0)),
+        ),
+        out_shape=jax.ShapeDtypeStruct((width, 2, hidden), f32),
+        compiler_params=pltpu.CompilerParams(vmem_limit_bytes=60 * 2**20),
+    )(jnp.reshape(place, (1,)).astype(jnp.int32), left, right, came)
+
+
 def columns_product(left, right, place, parts, dtype):
     width = left.shape[1] // parts
     block = 256 if width % 256 == 0 else 128
@@ -758,12 +904,24 @@
     def by_pair(weight, head_width, *cuts):
         split = weight.reshape(-1, dp_count, head_high, 2, head_low, head_width)
         split = split.transpose(1, 3, 0, 2, 4, 5)
-        lead = (dp_count, 2, slice_rows, -1)
+        lead = (dp_count, 2, weight.shape[0], -1)
         return [part.reshape(lead) for part in jnp.split(split, cuts, axis=-1)]
+
+    pieces = slice_rows // n_kv_gain
+
+    def in_pieces(found):
+        found = found.reshape(found.shape[:-2] + (n_kv_gain, pieces, -1))
+        return jnp.swapaxes(found, -3, -2).reshape(found.shape[:-3] + (slice_rows, -1))
+
+    def of_pieces(found):
+        found = found.reshape(found.shape[:-2] + (pieces, n_kv_gain, -1))
+        return jnp.swapaxes(found, -3, -2).reshape(found.shape[:-3] + (n_kv_gain, -1))
 
     by_head = dp_swap(
         jnp.concatenate(
-            by_pair(q_weight, DH + DR, DH, DH + DR // 2) + by_pair(kv_up_weight, DH + DV), axis=-1
+            by_pair(q_weight, DH + DR, DH, DH + DR // 2)
+            + [in_pieces(part) for part in by_pair(kv_up_weight, DH + DV)],
+            axis=-1,
         )
     )
     nope_cols = heads * DH
@@ -808,7 +966,6 @@
     def attend(all_rows, small_all, by_head, out_parts):
         joint_all = dp_gather(small_all[:, :slice_rows])
         kv_down = joint_all.transpose(1, 0, 2, 3).reshape(width, joint_width)
-        copies = 2 * ROPE_LANES // DR
         gains_all = dp_gather(small_all[:, gain_row])
         attn_scale = gains_all[..., :n_gain].transpose(1, 0, 2).reshape(-1)
         ffn_scale = gains_all[..., n_gain : 2 * n_gain].reshape(-1)
@@ -819,19 +976,38 @@
         all_lengths = jnp.stack([pick(all_lengths, low, 1), pick(all_lengths, low | pair_bit, 1)])
         all_lengths = all_lengths.reshape(blocks, -1)
         doc_ids, offsets = jax.vmap(lambda row: layout(row, row_count))(all_lengths)
-        cos, sin = [
-            jnp.tile(table.reshape(pair_rows, DR // 2), (1, copies))
-            for table in angles(offsets, DR)
-        ]
+        cos, sin = [table.reshape(pair_rows, DR // 2) for table in angles(offsets, DR)]
         all_rows = dp_gather(all_rows).transpose(1, 0, 2, 3).reshape(pair_rows, width)
-        by_head = jnp.concatenate(by_head, axis=1)
-        q_full = spread(by_head.reshape(width, head_cols))
-        kv_up = by_head[..., q_cols:].reshape(expert_count, dp_count, n_kv_gain, -1)
-        kv_up = kv_up.transpose(1, 0, 2, 3).reshape(KVR, heads * (DH + DV))
-        out_full = jnp.concatenate(out_parts, axis=1)
-        at = bits.index(pair_bit)
-        out_full = out_full.reshape((2,) * len(bits) + (-1, slice_rows, head_cols))
-        out_full = jnp.moveaxis(out_full, (len(bits), at), (-3, -2)).reshape(heads * DV, width)
+        if dp_count == 2:
+            last = (first, second, far, first)
+            places = jnp.stack([((me & bit) != 0).astype(jnp.int32) for bit in last])
+            q_full, kv_up, out_full = whole_call(
+                functools.partial(
+                    assemble_kernel,
+                    (
+                        [bit.bit_length() - 1 for bit in last],
+                        pair_bit.bit_length() - 1,
+                        slice_rows,
+                        pieces,
+                    ),
+                ),
+                [part for both in by_head + out_parts for part in both],
+                (
+                    ((width, q_cols), bf16),
+                    ((KVR, heads * (DH + DV)), bf16),
+                    ((heads * DV, width), bf16),
+                ),
+                scalars=(places,),
+            )
+        else:
+            by_head = jnp.concatenate(by_head, axis=1)
+            q_full = spread(by_head.reshape(width, head_cols))
+            kv_up = by_head[..., q_cols:].reshape(expert_count, dp_count, slice_rows, -1)
+            kv_up = of_pieces(kv_up).transpose(1, 0, 2, 3).reshape(KVR, heads * (DH + DV))
+            out_full = jnp.concatenate(out_parts, axis=1)
+            at = bits.index(pair_bit)
+            out_full = out_full.reshape((2,) * len(bits) + (-1, slice_rows, head_cols))
+            out_full = jnp.moveaxis(out_full, (len(bits), at), (-3, -2)).reshape(heads * DV, width)
         wide = nope_cols + 2 * ROPE_LANES
         outs = by_rows_call(
             functools.partial(attend_kernel, heads),
@@ -876,16 +1052,17 @@
         found = found.reshape(2, dp_count, row_count, -1).transpose(1, 0, 2, 3)
         return dp_scatter(found, bf16).astype(bf16)
 
-    (all_rows, by_head), (shared_split,) = march(
+    (all_rows, by_head, small), (shared_split,) = march(
         gathering(turned(tokens), [pair_bit]),
         pair_swapping(by_head, pair_bit, 1),
+        gathering(small, [far]),
         jobs=((shared_by_unit, shared_gate_up),),
     )
     by_head = by_head.reshape(2, head_rows, head_cols)
     held_grad = []
     results, found = march(
         *(
-            gathering(part, order, [pair_bit])
+            gathering(part, order, [pair_bit], whole=dp_count != 2)
             for part, order in (
                 (by_head[:, :head_cut], (second, far, first)),
                 (by_head[:, head_cut:], (far, first, second)),
@@ -893,7 +1070,7 @@
                 (out_cut[:, out_mid:], (far, second, first)),
             )
         ),
-        gathering(small, (far, first, second, pair_bit)),
+        gathering(small, (first, second, pair_bit), [far]),
         jobs=((skip,), (skip,), (lambda results, found, part: held_grad.append(part), out_grad)),
     )
 
@@ -1005,16 +1182,19 @@
             return kept.astype(f32)
         return kept + lax.ppermute(sent, "dp", [(0, 1), (1, 0)]).astype(f32)
 
+    def pair_sent(results, found, rows, d_pair, expert_hidden, shared_hidden):
+        out_part = output_part(results, found, expert_hidden, shared_hidden)
+        if dp_count != 2:
+            return (), out_part
+        return columns_product(rows, d_pair, 1 - core, dp_count, bf16), out_part
+
     def pair_kept(results, found, rows, d_pair):
         if dp_count != 2:
-            found = dot(rows.T, d_pair).astype(bf16).reshape(dp_count, width // dp_count, -1)
-            return lax.psum_scatter(found, "dp", scatter_dimension=0)
-        return columns_product(rows, d_pair, core, dp_count, f32)
-
-    def pair_sent(results, found, rows, d_pair):
-        if dp_count != 2:
-            return ()
-        return columns_product(rows, d_pair, 1 - core, dp_count, bf16)
+            whole = dot(rows.T, d_pair).astype(bf16).reshape(dp_count, width // dp_count, -1)
+            whole = lax.psum_scatter(whole, "dp", scatter_dimension=0).astype(f32)
+            return whole.reshape(-1, 2, hidden)
+        came = lax.ppermute(found[0][0], "dp", [(0, 1), (1, 0)])
+        return columns_sum(rows, d_pair, came, core)
 
     def down_gradient(results, found, expert_hidden, slot_grad):
         return halves(
@@ -1031,14 +1211,11 @@
     d_sums, found = march(
         *(scattering(part, order[::-1], bits) for part, order in zip(d_parts, orders)),
         jobs=(
-            (pair_sent, rows, d_pair),
-            (down_gradient, expert_hidden, slot_grad),
-            (shared_gradient, shared_hidden, d_shared_pair),
-            (output_part, expert_hidden, shared_hidden),
+            (pair_sent, rows, d_pair, expert_hidden, shared_hidden),
+            (pair_kept, rows, d_pair),
         ),
     )
-    sent, down_halves, (grad_shared_out, grad_shared), out_part = found
-    rows, d_pair = after((rows, d_pair), d_sums)
+    (unused, out_part), grad_pair, *unused = found
     d_ffn_in = jnp.concatenate(d_sums, axis=-1)
 
     d_norm_resid, grad_ffn_scale = norm_back(resid, ffn_scale, d_ffn_in)
@@ -1086,16 +1263,34 @@
 
     def weight_gradients(results, found):
         d_branch, (d_q_heads, d_kv_heads, d_joint, unused, unused) = found[0]
+        if dp_count == 2:
+            *parts, grad_kvdown = whole_call(
+                functools.partial(
+                    attention_gradients_kernel, (pair_bit.bit_length() - 1, slice_rows, pieces)
+                ),
+                (normed, d_q_heads, kv_normed, d_kv_heads, attended, d_branch, d_joint),
+                (
+                    ((expert_count, head_cut, head_cols), bf16),
+                    ((expert_count, head_rows - head_cut, head_cols), bf16),
+                    ((expert_count, out_mid, head_cols), bf16),
+                    ((expert_count, slice_rows - out_mid, head_cols), bf16),
+                    ((dp_count, expert_count, slice_rows, joint_width), bf16),
+                ),
+            )
+            return *parts, dp_scatter(grad_kvdown, bf16)
         grad_q = unspread(dot(normed.T, d_q_heads)).astype(bf16)
         grad_q = grad_q.reshape(expert_count, head_rows, q_cols)
         grad_up = dot(kv_normed.T, d_kv_heads).astype(bf16)
         grad_up = grad_up.reshape(dp_count, expert_count, n_kv_gain, -1).transpose(1, 0, 2, 3)
-        grad_up = grad_up.reshape(expert_count, head_rows, up_cols)
+        grad_up = in_pieces(grad_up).reshape(expert_count, head_rows, up_cols)
         by_head = jnp.concatenate([grad_q, grad_up], axis=-1)
         grad_out = cut_out(dot(attended.T, d_branch).astype(bf16))
         grad_kvdown = dot(normed.T, d_joint)
         grad_kvdown = grad_kvdown.reshape(expert_count, dp_count, slice_rows, joint_width)
-        return by_head, grad_out, dp_scatter(grad_kvdown.transpose(1, 0, 2, 3), bf16)
+        parts = (
+            by_head[:, :head_cut], by_head[:, head_cut:], grad_out[:, :out_mid], grad_out[:, out_mid:]
+        )
+        return *parts, dp_scatter(grad_kvdown.transpose(1, 0, 2, 3), bf16)
 
     sums = []
 
@@ -1113,13 +1308,17 @@
             scattering(after(part, d_resid), order[::-1], bits)
             for part, order in zip(out_part, orders)
         ),
-        jobs=((pair_kept, rows, d_pair), (back_of,), (sum_and_gradients,)),
-    )
-    pair_halves = (found[0], sent)
+        jobs=(
+            (skip,),
+            (back_of,),
+            (sum_and_gradients,),
+            (shared_gradient, shared_hidden, d_shared_pair),
+        ),
+    )
+    *grad_parts, grad_kvdown = found[2]
+    grad_shared_out, grad_shared = found[3]
     output = (resid + jnp.concatenate(results, axis=-1)).astype(bf16)
-    grad_heads, grad_out, grad_kvdown = found[2]
     grad_kv_scale = found[1][1][3].sum(axis=0)
-    pair_halves, down_halves, grad_shared = after((pair_halves, down_halves, grad_shared), results)
     d_norm_in, grad_attn_scale = norm_back(turned(resid_in), attn_scale, d_normed)
     grad_in = (d_resid + turned_back(d_norm_in)).astype(bf16)
     scale_sums = jnp.concatenate(
@@ -1134,15 +1333,15 @@
     scale_sums = dp_scatter(scale_sums)[:, None]
     small_sums = jnp.concatenate([grad_kvdown, scale_sums], axis=1).astype(bf16)
 
-    def finish_pair(results, found, kept, sent):
-        return exchanged(kept, sent).reshape(expert_gate_up.shape)
-
-    def finish_down(results, found, kept, sent, shared):
+    def start_down(results, found, expert_hidden, slot_grad, shared):
         shared = lax.all_to_all(shared, "expert", split_axis=0, concat_axis=0, tiled=True)
-        return exchanged(kept, sent).reshape(expert_down.shape), shared
+        return down_gradient(results, found, expert_hidden, slot_grad), shared
+
+    def finish_down(results, found):
+        return exchanged(*found[0][0]).reshape(expert_down.shape)
 
     def finish_shared(results, found):
-        both = found[1][1].reshape(expert_count, slice_rows, 2, padded)[..., :units]
+        both = found[0][1].reshape(expert_count, slice_rows, 2, padded)[..., :units]
         both = both.reshape(expert_count, slice_rows, 2, dp_count, share)
         return both.transpose(1, 2, 3, 0, 4).reshape(shared_gate_up.shape).astype(f32)
 
@@ -1159,24 +1358,24 @@
         *(
             scattering(part, order, bits, bf16)
             for part, order in (
-                (grad_heads[:, :head_cut], (first, far, second)),
-                (grad_heads[:, head_cut:], (second, first, far)),
-                (grad_out[:, :out_mid], (far, first, second)),
-                (grad_out[:, out_mid:], (first, second, far)),
+                (grad_parts[0], (first, far, second)),
+                (grad_parts[1], (second, first, far)),
+                (grad_parts[2], (far, first, second)),
+                (grad_parts[3], (first, second, far)),
             )
         ),
         jobs=(
-            (finish_pair, *pair_halves),
-            (finish_down, *down_halves, grad_shared),
+            (start_down, *after((expert_hidden, slot_grad, grad_shared), results)),
+            (finish_down,),
             (finish_shared,),
         ),
     )
-    grad_pair, (grad_down, unused), grad_shared = found[:3]
+    unused, grad_down, grad_shared = found[:3]
     by_head = jnp.concatenate(summed[1:3], axis=1)
     by_head = alone(pair_swapping(by_head, pair_bit, 0)).reshape(2, dp_count, slice_rows, head_cols)
     by_head = dp_swap(by_head.transpose(1, 0, 2, 3))
     grad_q = whole_heads(by_head[..., :q_cols], slice_rows, DH, DR // 2, DR // 2)
-    grad_up = by_head[..., q_cols:].reshape(dp_count, 2, n_kv_gain, -1)
+    grad_up = of_pieces(by_head[..., q_cols:])
     grad_up = whole_heads(grad_up, n_kv_gain, DH + DV)
     grad_out = jnp.concatenate(summed[3:5], axis=1).reshape(2, -1, slice_rows, head_cols)
     grad_out = grad_out.transpose(2, 1, 0, 3).reshape(out_weight.shape).astype(f32)
@@ -1196,7 +1395,7 @@
         grad_out,
         grad_shared,
         grad_shared_out,
-        grad_pair,
+        grad_pair.reshape(expert_gate_up.shape),
         grad_down,
     )
 

time: 890 us -> 844 us (0.948)
  local copies, waits for them, and re-layouts: 172 us -> 137 us
  other arithmetic: 144 us -> 118 us
  Pallas kernels: 177 us -> 197 us
    pallas_call x0 -> x3, Pallas kernels: none -> 31.9 us  [the longest x2 16.9 us: whole_call(): pl.pallas_call(kernel, grid_spec=pltpu.PrefetchScalarGridSpec(num_scalar_...]
    reshape x7 -> x1, local copies, waits for them, and re-layouts: 26.6 us -> 1.59 us  [finish_shared(): both = found[0][1].reshape(expert_count, slice_rows, 2, padded)[..., :units]]
    pallas_call x4 -> x3, Pallas kernels: 43.7 us -> 30.5 us  [columns_product(): pl.pallas_call(columns_kernel, grid_spec=pltpu.PrefetchScalarGridSpec(num...]
    another operation x50 -> x44, other arithmetic: 36.1 us -> 24 us  [gathering(): jnp.stack([jnp.where(low, values, other), jnp.where(low, other, values)],...]
    ppermute x74, starting transfers between devices: 74.7 us -> 86.6 us  [partner(): return lax.ppermute(values, 'expert', [(i, i ^ bit) for i in range(count)])]
    add x1 -> x0, other arithmetic: 11.2 us -> none  [exchanged(): return kept + lax.ppermute(sent, 'dp', [(0, 1), (1, 0)]).astype(f32)]
    ppermute x6, starting transfers between devices: 13.6 us -> 2.97 us  [dp_scatter(): lax.ppermute(pick(values, 1 - core, 0).astype(sent), 'dp', [(0, 1), (1, 0)])]
    concatenate x6 -> x2, other arithmetic: 10.9 us -> 1.08 us  [the longest x1 1.02 us: shards(): small_sums = jnp.concatenate([grad_kvdown, scale_sums], axis=1).astype(bf16)]
  transfers between devices with their start and end apart: 95 -> 95, of which waited for: 28 -> 29; matrix products, arithmetic and copies ran while one was open for 34% -> 27% of each run, Pallas kernels for 12% -> 15%
where the time goes in v4:
time: 844 us; the launch traced here: 833 us
  waiting for transfers between devices  227 us (27%)
  Pallas kernels  197 us (23%)
  local copies, waits for them, and re-layouts  137 us (16%)
  starting transfers between devices  126 us (15%)
  other arithmetic  118 us (14%)
  between operations  16.6 us (2%)
  matrix products  13 us (2%)
    ppermute x74, waiting for transfers between devices, partner(): return lax.ppermute(values, 'expert', [(i, i ^ bit) for i in range(count)])  216 us
    pallas_call x5, Pallas kernels, by_rows_call(): pl.pallas_call(kernel, grid_spec=pltpu.PrefetchScalarGridSpec(num_scalar_...  134 us
    ppermute x74, starting transfers between devices, partner(): return lax.ppermute(values, 'expert', [(i, i ^ bit) for i in range(count)])  86.6 us
    add x28, other arithmetic, scattering(): values = own + other  35.4 us
    unnamed x243, local copies, waits for them, and re-layouts  31.1 us
    pallas_call x3, Pallas kernels, columns_product(): pl.pallas_call(columns_kernel, grid_spec=pltpu.PrefetchScalarGridSpec(num...  30.5 us
    squeeze x29, local copies, waits for them, and re-layouts, pick(): return lax.dynamic_index_in_dim(values, place, axis, keepdims=False)  27.4 us
    another operation x44, other arithmetic, gathering(): jnp.stack([jnp.where(low, values, other), jnp.where(low, other, values)],...  24 us
  transfers between devices with their start and end apart: 95, of which 29 were waited for; matrix products, arithmetic and copies ran while one was open for 27% of the time, Pallas kernels for 15%

profile of v4, /device:TPU:1, one launch (start us, length us, event | category | flops | bytes accessed | tf_op | source)
XLA Modules:
  0.0 833.4 jit_solution(3069251151857120426)
XLA Ops:
  27.2 7.0 collective-permute-done.3
  41.4 4.5 collective-permute-done.7
  45.8 11.5 %collective-permute-done.8 = bf16[2,32,1024]{2,1,0:T(8,128)(2,1)S(1)} collective-permute-done((bf16[2,32,1024]{2,1,0:T(8,128)(2,1)S(1)}, bf16[2,32,1024]{2,1,0:T(8,128)(2,1)S(1)}, u32[]{:S(2)}, u32[]{:S(2)}) %collective-permute-start.8) | collective-permute-done | bytes 131104 | tf_op jit(solution)/shard_map/ppermute | solution.py:119
  63.6 10.4 %collective-permute-done.13 = bf16[2,2,32,1024]{3,2,1,0:T(8,128)(2,1)S(1)} collective-permute-done((bf16[2,2,32,1024]{3,2,1,0:T(8,128)(2,1)S(1)}, bf16[2,2,32,1024]{3,2,1,0:T(8,128)(2,1)S(1)}, u32[]{:S(2)}, u32[]{:S(2)}) %collective-permute-start.13) | collective-permute-done | bytes 262176 | tf_op jit(solution)/shard_map/ppermute | solution.py:119
  74.0 6.9 collective-permute-done.12
  82.7 6.2 copy.734
  101.4 3.2 collective-permute-start.17
  104.8 7.4 collective-permute-done.18.refs_7_
  112.2 27.3 %collective-permute-done.17.refs_5_ = bf16[8,32,1024]{2,1,0:T(8,128)(2,1)S(1)} collective-permute-done((bf16[8,32,1024]{2,1,0:T(8,128)(2,1)S(1)}, bf16[8,32,1024]{2,1,0:T(8,128)(2,1)S(1)}, u32[]{:S(2)}, u32[]{:S(2)}) %collective-permute-start.17) | collective-permute-done | bytes 524320 | tf_op jit(solution)/shard_map/ppermute | solution.py:119
  146.2 4.0 copy.640
  150.5 6.5 shard_map.255
  168.1 16.6 %shard_map.256 = (bf16[512,2048]{1,0:T(8,128)(2,1)}, f32[512,576]{1,0:T(8,128)}, bf16[512,512]{1,0:T(8,128)(2,1)}, bf16[512,768]{1,0:T(8,128)(2,1)}, bf16[512,76...) custom-call(bf16[512,2048]{1,0:T(8,128)(2,1)} %bitcast.572, ...), custom_call_target="tpu_custom_call" | custom-call | tf_op jit(solution)/shard_map/pallas_call | solution.py:450
  190.2 3.0 collective-permute-done.27
  202.4 25.2 %collective-permute-done.23 = bf16[128,2048]{0,1:T(8,128)(2,1)} collective-permute-done((bf16[128,2048]{0,1:T(8,128)(2,1)}, bf16[128,2048]{0,1:T(8,128)(2,1)}, u32[]{:S(2)}, u32[]{:S(2)}) %collective-permute-start.23) | collective-permute-done | bytes 524320 | tf_op jit(solution)/shard_map/ppermute | solution.py:119
  233.7 17.9 %shard_map.257 = (bf16[1152,2048]{1,0:T(8,128)(2,1)}, f32[1152,1408]{1,0:T(8,128)}, f32[2048,256]{1,0:T(8,128)}) custom-call(bf16[2048,2048]{1,0:T(8,128)(2,1)} %all-gather.8.cloned.1.call-done.grad_ref.right_ref, s32[8,1,256]{2,1,0:T(1,128)} %compare_select_fusion.slot_ref, f32[8,1,256]{2,1,0:T(1,128)} %bitcast.653, bf16[1408,2048]{1,0:T(8,128)(2,1)} %bitcast.557, ...), custom_call_target="tpu_custom_call" | custom-call | tf_op jit(solution)/shard_map/pallas_call | solution.py:450
  257.5 4.5 all-to-all-start
  262.0 3.2 collective-permute-done.31
  269.7 7.2 collective-permute-start.34
  284.1 6.9 all-to-all-done
  291.0 4.6 collective-permute-start.28
  295.6 3.9 collective-permute-done.33
  318.4 9.4 %collective-permute-done.37.right_came_ref = bf16[1024,640]{1,0:T(8,128)(2,1)} collective-permute-done((bf16[1024,640]{1,0:T(8,128)(2,1)}, bf16[1024,640]{1,0:T(8,128)(2,1)}, u32[]{:S(2)}, u32[]{:S(2)}) %collective-permute-start.37) | collective-permute-done | bytes 1310752 | tf_op jit(solution)/shard_map/ppermute | solution.py:119
  327.8 9.3 %collective-permute-done.35.left_came_ref = bf16[1024,640]{1,0:T(8,128)(2,1)} collective-permute-done((bf16[1024,640]{1,0:T(8,128)(2,1)}, bf16[1024,640]{1,0:T(8,128)(2,1)}, u32[]{:S(2)}, u32[]{:S(2)}) %collective-permute-start.35) | collective-permute-done | bytes 1310752 | tf_op jit(solution)/shard_map/ppermute | solution.py:119
  338.6 62.3 %shard_map.258 = (bf16[2048,2048]{1,0:T(8,128)(2,1)}, bf16[1152,2048]{1,0:T(8,128)(2,1)}, bf16[1152,1408]{1,0:T(8,128)(2,1)}, bf16[1152,2816]{1,0:T(8,128)(2,1)}...) custom-call(s32[3]{0:T(128)} %pad_add_fusion.2.me_ref, ...), custom_call_target="tpu_custom_call" | custom-call | tf_op jit(solution)/shard_map/pallas_call | solution.py:450
  401.5 19.7 %shard_map.260 = (bf16[1024,640]{1,0:T(8,128)(2,1)}, bf16[1024,640]{1,0:T(8,128)(2,1)}, bf16[1024,768]{1,0:T(8,128)(2,1)}, bf16[1024,768]{1,0:T(8,128)(2,1)}, bf...) custom-call(s32[3]{0:T(128)} %pad_add_fusion.2.me_ref, bf16[1152,1408]{1,0:T(8,128)(2,1)} %get-tuple-element.314.hidden_ref, ...), custom_call_target="tpu_custom_call" | custom-call | tf_op jit(solution)/shard_map/pallas_call | solution.py:450
  421.2 12.5 %shard_map.259 = bf16[1024,2816]{1,0:T(8,128)(2,1)} custom-call(s32[1]{0:T(128)} %bitcast.120.place_ref, bf16[1152,2048]{1,0:T(8,128)(2,1)} %get-tuple-element.239.left_ref, bf16[1152,2816]{1,0:T(8,128)(2,1)} %get-tuple-element.240.right_ref), custom_call_target="tpu_custom_call" | custom-call | tf_op jit(solution)/shard_map/pallas_call | solution.py:807
  433.7 8.9 %collective-permute-start.44 = (bf16[1024,2816]{1,0:T(8,128)(2,1)}, bf16[1024,2816]{1,0:T(8,128)(2,1)}, u32[]{:S(2)}, u32[]{:S(2)}) collective-permute-start(bf16[1024,2816]{1,0:T(8,128)(2,1)} %shard_map.259), channel_id=1, source_target_pairs={{0,16},{16,0},{1,17},{17,1},{2,18},{18,2},{3,19},{19,3},{4,20},{20... | collective-permute-start | bytes 17301512 | tf_op jit(solution)/shard_map/ppermute | solution.py:1196
  456.1 15.0 %shard_map.261 = f32[1024,2,1408]{2,1,0:T(2,128)} custom-call(s32[1]{0:T(128)} %bitcast.128.place_ref, bf16[1152,2048]{1,0:T(8,128)(2,1)} %get-tuple-element.239.left_ref, bf16[1152,2816]{1,0:T(8,128)(2,1)} %get-tuple-element.240.right_ref, bf16[1024,2816]{1,0:T(8,128)(2,1)} %collective-permute-done.44.came_ref), custom_call_target="tpu_custom_call" | custom-call | tf_op jit(solution)/shard_map/pallas_call | solution.py:786
  483.9 6.6 collective-permute-done.45
  492.2 3.1 collective-permute-start.50
  500.1 3.2 collective-permute-done.48
  510.7 7.7 collective-permute-start.54
  519.8 35.7 %collective-permute-done.51 = bf16[128,2048]{0,1:T(8,128)(2,1)S(1)} collective-permute-done((bf16[128,2048]{0,1:T(8,128)(2,1)S(1)}, bf16[128,2048]{0,1:T(8,128)(2,1)S(1)}, u32[]{:S(2)}, u32[]{:S(2)}) %collective-permute-start.51) | collective-permute-done | bytes 524320 | tf_op jit(solution)/shard_map/ppermute | solution.py:119
  559.5 5.2 collective-permute-start.58
  577.0 4.3 copy.675
  581.3 17.7 %shard_map.262 = (bf16[512,768]{1,0:T(8,128)(2,1)}, bf16[512,1024]{1,0:T(8,128)(2,1)}, bf16[512,576]{1,0:T(8,128)(2,1)}, f32[1,1,512]{2,1,0:T(1,128)}, bf16[512,2048]{1,0:T(8,128)(2,1)}) custom-call(bf16[512,2048]{1,0:T(8,128)(2,1)} %bitcast.560, bf16[512,2048]{1,0:T(8,128)(2,1)} %get-tuple-element.197.out_ref, ...), custom_call_target="tpu_custom_call" | custom-call | tf_op jit(solution)/shard_map/pallas_call | solution.py:450
  599.1 10.4 %shard_map.263 = (bf16[16,48,1024]{2,1,0:T(8,128)(2,1)}, bf16[16,80,1024]{2,1,0:T(8,128)(2,1)}, bf16[16,32,1024]{2,1,0:T(8,128)(2,1)}, bf16[16,32,1024]{2,1,0:T(8,128)(2,1)}, bf16[2,16,64,576]{3,2,1,0:T(8,128)(2,1)}) custom-call(bf16[512,2048]{1,0:T(8,128)(2,1)} %get-tuple-element.281.normed_ref, bf16[512,768]{1,0:T(8,128)(2,1)} %get-tuple-element.282.d_q_ref, ...), custom_call_target="tpu_custom_call" | custom-call | tf_op jit(solution)/shard_map/pallas_call | solution.py:560
  643.6 10.6 %shard_map.265 = bf16[2048,512]{1,0:T(8,128)(2,1)} custom-call(s32[1]{0:T(128)} %constant.340.clone.1.place_ref, bf16[2048,2048]{1,0:T(8,128)(2,1)} %get-tuple-element.300.left_ref, bf16[2048,512]{1,0:T(8,128)(2,1)} %get-tuple-element.301.right_ref), custom_call_target="tpu_custom_call" | custom-call | tf_op jit(solution)/shard_map/pallas_call | solution.py:807
  656.7 7.4 shard_map.264
  681.9 14.9 %collective-permute-done.66 = bf16[128,768]{0,1:T(8,128)(2,1)S(1)} collective-permute-done((bf16[128,768]{0,1:T(8,128)(2,1)S(1)}, bf16[128,768]{0,1:T(8,128)(2,1)S(1)}, u32[]{:S(2)}, u32[]{:S(2)}) %collective-permute-start.66) | collective-permute-done | bytes 196640 | tf_op jit(solution)/shard_map/ppermute | solution.py:119
  699.0 4.5 all-to-all-start.1
  706.5 13.0 %fusion.66 = f32[1408,2048]{1,0:T(8,128)} fusion(bf16[1152,1408]{1,0:T(8,128)(2,1)} %get-tuple-element.314.hidden_ref, bf16[1152,2048]{1,0:T(8,128)(2,1)} %get-tuple-element.315), kind=kOutput, calls=%fused_computation.351 | convolution fusion | flops 6643777536 | bytes 19496960 | tf_op jit(solution)/shard_map/dot_general | solution.py:74
  724.8 4.6 fusion
  729.5 6.0 dynamic-slice_bitcast_fusion
  735.5 6.9 collective-permute-done.71
  765.7 7.4 add_bitcast_fusion
  773.1 6.2 collective-permute-done.77
  809.8 3.2 collective-permute-start.87
  (690 shorter events, 313.0 us)
Async XLA Ops:
  7.2 226.5 %all-gather.10.cloned.1.call-start = ((), (), s32[]{:S(2)}) async-start(), calls=%async_computation.4 | async-start | bytes 8650752 | tf_op jit(solution)/shard_map/all_gather | solution.py:959
  7.9 225.8 %all-gather.8.cloned.1.call-start = ((), (), s32[]{:S(2)}) async-start(), calls=%async_computation.3 | async-start | bytes 8912896 | tf_op jit(solution)/shard_map/all_gather | solution.py:1077
  12.0 23.0 %collective-permute-start = (bf16[128,2048]{0,1:T(8,128)(2,1)}, bf16[128,2048]{0,1:T(8,128)(2,1)}, u32[]{:S(2)}, u32[]{:S(2)}) collective-permute-start(bf16[128,2048]{0,1:T(8,128)(2,1)} %bitcast.2), channel_id=1, source_target_pairs={{0,4},{1,5},{2,6},{3,7},{4,0},{5,1},{6,2},{7,3},{8,12},{9,13},{10,... | collective-permute-start | bytes 1572872 | tf_op jit(solution)/shard_map/ppermute | solution.py:119
  35.1 23.0 %collective-permute-start.6 = (bf16[2,80,1024]{2,1,0:T(8,128)(2,1)S(1)}, bf16[2,80,1024]{2,1,0:T(8,128)(2,1)S(1)}, u32[]{:S(2)}, u32[]{:S(2)}) collective-permute-start(bf16[2,80,1024]{2,1,0:T(8,128)(2,1)S(1)} %pad_maximum_fusion.22), channel_id=1, source_target_pairs={{0,8},{1,9},{2,10},{3,11},{4,12},{5,13},{6,14},{7,15},{8,0},{9,1},... | collective-permute-start | bytes 983048 | tf_op jit(solution)/shard_map/ppermute | solution.py:119
  58.8 22.1 %collective-permute-start.14 = (bf16[2,2,80,576]{3,2,1,0:T(8,128)(2,1)S(1)}, bf16[2,2,80,576]{3,2,1,0:T(8,128)(2,1)S(1)}, u32[]{:S(2)}, u32[]{:S(2)}) collective-permute-start(bf16[2,2,80,576]{3,2,1,0:T(8,128)(2,1)S(1)} %pad_maximum_fusion.19), channel_id=1, source_target_pairs={{0,2},{1,3},{2,0},{3,1},{4,6},{5,7},{6,4},{7,5},{8,10},{9,11},{10,... | collective-permute-start | bytes 1105928 | tf_op jit(solution)/shard_map/ppermute | solution.py:119
  61.0 21.4 %collective-permute-start.11 = (bf16[2,2,80,1024]{3,2,1,0:T(8,128)(2,1)S(1)}, bf16[2,2,80,1024]{3,2,1,0:T(8,128)(2,1)}, u32[]{:S(2)}, u32[]{:S(2)}) collective-permute-start(bf16[2,2,80,1024]{3,2,1,0:T(8,128)(2,1)S(1)} %pad_maximum_fusion.13), channel_id=1, source_target_pairs={{0,1},{1,0},{2,3},{3,2},{4,5},{5,4},{6,7},{7,6},{8,9},{9,8},{10,11... | collective-permute-start | bytes 1966088 | tf_op jit(solution)/shard_map/ppermute | solution.py:119
  82.5 256.1 %all-gather.6.cloned.1.call-start = ((), (), s32[]{:S(2)}) async-start(), calls=%async_computation.2 | async-start | bytes 17301504 | tf_op jit(solution)/shard_map/all_gather | solution.py:958
  94.7 46.8 %collective-permute-start.19 = (bf16[2,2,2,80,576]{4,3,2,1,0:T(8,128)(2,1)S(1)}, bf16[2,2,2,80,576]{4,3,2,1,0:T(8,128)(2,1)S(1)}, u32[]{:S(2)}, u32[]{:S(2)}) collective-permute-start(bf16[2,2,2,80,576]{4,3,2,1,0:T(8,128)(2,1)S(1)} %pad_maximum_fusion.9), channel_id=1, source_target_pairs={{0,4},{1,5},{2,6},{3,7},{4,0},{5,1},{6,2},{7,3},{8,12},{9,13},{10,... | collective-permute-start | bytes 2211848 | tf_op jit(solution)/shard_map/ppermute | solution.py:119
  97.7 43.8 %collective-permute-start.16 = (bf16[8,80,1024]{2,1,0:T(8,128)(2,1)S(1)}, bf16[8,80,1024]{2,1,0:T(8,128)(2,1)S(1)}, u32[]{:S(2)}, u32[]{:S(2)}) collective-permute-start(bf16[8,80,1024]{2,1,0:T(8,128)(2,1)S(1)} %bitcast.593), channel_id=1, source_target_pairs={{0,2},{1,3},{2,0},{3,1},{4,6},{5,7},{6,4},{7,5},{8,10},{9,11},{10,... | collective-permute-start | bytes 3932168 | tf_op jit(solution)/shard_map/ppermute | solution.py:119
  100.4 41.2 %collective-permute-start.15 = (bf16[8,48,1024]{2,1,0:T(8,128)(2,1)S(1)}, bf16[8,48,1024]{2,1,0:T(8,128)(2,1)S(1)}, u32[]{:S(2)}, u32[]{:S(2)}) collective-permute-start(bf16[8,48,1024]{2,1,0:T(8,128)(2,1)S(1)} %bitcast.609), channel_id=1, source_target_pairs={{0,1},{1,0},{2,3},{3,2},{4,5},{5,4},{6,7},{7,6},{8,9},{9,8},{10,11... | collective-permute-start | bytes 2359304 | tf_op jit(solution)/shard_map/ppermute | solution.py:119
  101.4 38.1 %collective-permute-start.17 = (bf16[8,32,1024]{2,1,0:T(8,128)(2,1)S(1)}, bf16[8,32,1024]{2,1,0:T(8,128)(2,1)S(1)}, u32[]{:S(2)}, u32[]{:S(2)}) collective-permute-start(bf16[8,32,1024]{2,1,0:T(8,128)(2,1)S(1)} %bitcast.626), channel_id=1, source_target_pairs={{0,8},{1,9},{2,10},{3,11},{4,12},{5,13},{6,14},{7,15},{8,0},{9,1},... | collective-permute-start | bytes 1572872 | tf_op jit(solution)/shard_map/ppermute | solution.py:119
  199.2 28.5 %collective-permute-start.23 = (bf16[128,2048]{0,1:T(8,128)(2,1)}, bf16[128,2048]{0,1:T(8,128)(2,1)}, u32[]{:S(2)}, u32[]{:S(2)}) collective-permute-start(bf16[128,2048]{0,1:T(8,128)(2,1)} %dynamic-slice_bitcast_fusion.15), channel_id=1, source_target_pairs={{0,4},{1,5},{2,6},{3,7},{4,0},{5,1},{6,2},{7,3},{8,12},{9,13},{10,... | collective-permute-start | bytes 1572872 | tf_op jit(solution)/shard_map/ppermute | solution.py:119
  229.4 22.1 %collective-permute-start.24 = (bf16[128,640]{0,1:T(8,128)(2,1)S(1)}, bf16[128,640]{0,1:T(8,128)(2,1)S(1)}, u32[]{:S(2)}, u32[]{:S(2)}) collective-permute-start(bf16[128,640]{0,1:T(8,128)(2,1)S(1)} %get-tuple-element.534), channel_id=1, source_target_pairs={{0,2},{1,3},{2,0},{3,1},{4,6},{5,7},{6,4},{7,5},{8,10},{9,11},{10,... | collective-permute-start | bytes 491528 | tf_op jit(solution)/shard_map/ppermute | solution.py:119
  230.6 20.9 %collective-permute-start.26 = (bf16[128,640]{0,1:T(8,128)(2,1)S(1)}, bf16[128,640]{0,1:T(8,128)(2,1)S(1)}, u32[]{:S(2)}, u32[]{:S(2)}) collective-permute-start(bf16[128,640]{0,1:T(8,128)(2,1)S(1)} %get-tuple-element.533), channel_id=1, source_target_pairs={{0,8},{1,9},{2,10},{3,11},{4,12},{5,13},{6,14},{7,15},{8,0},{9,1},... | collective-permute-start | bytes 491528 | tf_op jit(solution)/shard_map/ppermute | solution.py:119
  257.5 33.5 %all-to-all-start = ((bf16[16,64,512]{2,1,0:T(8,128)(2,1)}), bf16[16,64,512]{2,1,0:T(8,128)(2,1)}, u32[]{:S(2)}, u32[]{:S(2)}) async-start(bf16[16,64,512]{2,1,0:T(8,128)(2,1)} %reshape.470), calls=%async_computation | async-start | bytes 2097152 | tf_op jit(solution)/shard_map/all_to_all | solution.py:961
  269.7 25.9 %collective-permute-start.34 = (bf16[2,2,128,640]{2,3,0,1:T(8,128)(2,1)}, bf16[2,2,128,640]{2,3,0,1:T(8,128)(2,1)}, u32[]{:S(2)}, u32[]{:S(2)}) collective-permute-start(bf16[2,2,128,640]{2,3,0,1:T(8,128)(2,1)} %pad_maximum_fusion.15), channel_id=1, source_target_pairs={{0,2},{1,3},{2,0},{3,1},{4,6},{5,7},{6,4},{7,5},{8,10},{9,11},{10,... | collective-permute-start | bytes 1966088 | tf_op jit(solution)/shard_map/ppermute | solution.py:119
  279.0 20.6 %collective-permute-start.33 = (bf16[2,2,128,768]{2,3,0,1:T(8,128)(2,1)}, bf16[2,2,128,768]{2,3,0,1:T(8,128)(2,1)}, u32[]{:S(2)}, u32[]{:S(2)}) collective-permute-start(bf16[2,2,128,768]{2,3,0,1:T(8,128)(2,1)} %pad_maximum_fusion.11), channel_id=1, source_target_pairs={{0,4},{1,5},{2,6},{3,7},{4,0},{5,1},{6,2},{7,3},{8,12},{9,13},{10,... | collective-permute-start | bytes 2359304 | tf_op jit(solution)/shard_map/ppermute | solution.py:119
  291.0 24.1 %collective-permute-start.28 = (bf16[16,64,512]{2,1,0:T(8,128)(2,1)}, bf16[16,64,512]{2,1,0:T(8,128)(2,1)}, u32[]{:S(2)}, u32[]{:S(2)}) collective-permute-start(bf16[16,64,512]{2,1,0:T(8,128)(2,1)} %all-to-all-done), channel_id=1, source_target_pairs={{0,16},{16,0},{1,17},{17,1},{2,18},{18,2},{3,19},{19,3},{4,20},{20... | collective-permute-start | bytes 3145736 | tf_op jit(solution)/shard_map/ppermute | solution.py:84
  302.6 25.2 %collective-permute-start.37 = (bf16[1024,640]{1,0:T(8,128)(2,1)}, bf16[1024,640]{1,0:T(8,128)(2,1)}, u32[]{:S(2)}, u32[]{:S(2)}) collective-permute-start(bf16[1024,640]{1,0:T(8,128)(2,1)} %bitcast.119.right_ref), channel_id=1, source_target_pairs={{0,1},{1,0},{2,3},{3,2},{4,5},{5,4},{6,7},{7,6},{8,9},{9,8},{10,11... | collective-permute-start | bytes 3932168 | tf_op jit(solution)/shard_map/ppermute | solution.py:119
  309.1 29.5 %collective-permute-start.36 = (bf16[1024,768]{1,0:T(8,128)(2,1)S(1)}, bf16[1024,768]{1,0:T(8,128)(2,1)}, u32[]{:S(2)}, u32[]{:S(2)}) collective-permute-start(bf16[1024,768]{1,0:T(8,128)(2,1)S(1)} %bitcast.583), channel_id=1, source_target_pairs={{0,2},{1,3},{2,0},{3,1},{4,6},{5,7},{6,4},{7,5},{8,10},{9,11},{10,... | collective-permute-start | bytes 4718600 | tf_op jit(solution)/shard_map/ppermute | solution.py:119
  314.6 22.5 %collective-permute-start.35 = (bf16[1024,640]{1,0:T(8,128)(2,1)}, bf16[1024,640]{1,0:T(8,128)(2,1)}, u32[]{:S(2)}, u32[]{:S(2)}) collective-permute-start(bf16[1024,640]{1,0:T(8,128)(2,1)} %bitcast.590), channel_id=1, source_target_pairs={{0,4},{1,5},{2,6},{3,7},{4,0},{5,1},{6,2},{7,3},{8,12},{9,13},{10,... | collective-permute-start | bytes 3932168 | tf_op jit(solution)/shard_map/ppermute | solution.py:119
  400.9 32.8 %collective-permute-start.39 = (bf16[1024,768]{1,0:T(8,128)(2,1)}, bf16[1024,768]{1,0:T(8,128)(2,1)S(1)}, u32[]{:S(2)}, u32[]{:S(2)}) collective-permute-start(bf16[1024,768]{1,0:T(8,128)(2,1)} %get-tuple-element.219), channel_id=1, source_target_pairs={{0,2},{1,3},{2,0},{3,1},{4,6},{5,7},{6,4},{7,5},{8,10},{9,11},{10,... | collective-permute-start | bytes 4718600 | tf_op jit(solution)/shard_map/ppermute | solution.py:119
  401.2 32.5 %collective-permute-start.38 = (bf16[1024,640]{1,0:T(8,128)(2,1)}, bf16[1024,640]{1,0:T(8,128)(2,1)}, u32[]{:S(2)}, u32[]{:S(2)}) collective-permute-start(bf16[1024,640]{1,0:T(8,128)(2,1)} %get-tuple-element.218), channel_id=1, source_target_pairs={{0,4},{1,5},{2,6},{3,7},{4,0},{5,1},{6,2},{7,3},{8,12},{9,13},{10,... | collective-permute-start | bytes 3932168 | tf_op jit(solution)/shard_map/ppermute | solution.py:119
  401.2 32.5 %collective-permute-start.40 = (bf16[1024,640]{1,0:T(8,128)(2,1)}, bf16[1024,640]{1,0:T(8,128)(2,1)}, u32[]{:S(2)}, u32[]{:S(2)}) collective-permute-start(bf16[1024,640]{1,0:T(8,128)(2,1)} %get-tuple-element.220), channel_id=1, source_target_pairs={{0,1},{1,0},{2,3},{3,2},{4,5},{5,4},{6,7},{7,6},{8,9},{9,8},{10,11... | collective-permute-start | bytes 3932168 | tf_op jit(solution)/shard_map/ppermute | solution.py:119
  433.7 22.4 %collective-permute-start.44 = (bf16[1024,2816]{1,0:T(8,128)(2,1)}, bf16[1024,2816]{1,0:T(8,128)(2,1)}, u32[]{:S(2)}, u32[]{:S(2)}) collective-permute-start(bf16[1024,2816]{1,0:T(8,128)(2,1)} %shard_map.259), channel_id=1, source_target_pairs={{0,16},{16,0},{1,17},{17,1},{2,18},{18,2},{3,19},{19,3},{4,20},{20... | collective-permute-start | bytes 17301512 | tf_op jit(solution)/shard_map/ppermute | solution.py:1196
  445.8 25.3 %collective-permute-start.42 = (bf16[2,2,128,768]{3,2,1,0:T(8,128)(2,1)}, bf16[2,2,128,768]{3,2,1,0:T(8,128)(2,1)}, u32[]{:S(2)}, u32[]{:S(2)}) collective-permute-start(bf16[2,2,128,768]{3,2,1,0:T(8,128)(2,1)} %dynamic-slice_bitcast_fusion.6), channel_id=1, source_target_pairs={{0,4},{1,5},{2,6},{3,7},{4,0},{5,1},{6,2},{7,3},{8,12},{9,13},{10,... | collective-permute-start | bytes 2359304 | tf_op jit(solution)/shard_map/ppermute | solution.py:119
  449.9 21.2 %collective-permute-start.43 = (bf16[2,2,128,640]{3,2,1,0:T(8,128)(2,1)}, bf16[2,2,128,640]{3,2,1,0:T(8,128)(2,1)}, u32[]{:S(2)}, u32[]{:S(2)}) collective-permute-start(bf16[2,2,128,640]{3,2,1,0:T(8,128)(2,1)} %dynamic-slice_bitcast_fusion.10), channel_id=1, source_target_pairs={{0,2},{1,3},{2,0},{3,1},{4,6},{5,7},{6,4},{7,5},{8,10},{9,11},{10,... | collective-permute-start | bytes 1966088 | tf_op jit(solution)/shard_map/ppermute | solution.py:119
  509.7 45.9 %collective-permute-start.53 = (bf16[1024,768]{1,0:T(8,128)(2,1)S(1)}, bf16[1024,768]{1,0:T(8,128)(2,1)S(1)}, u32[]{:S(2)}, u32[]{:S(2)}) collective-permute-start(bf16[1024,768]{1,0:T(8,128)(2,1)S(1)} %copy-done.111), channel_id=1, source_target_pairs={{0,2},{1,3},{2,0},{3,1},{4,6},{5,7},{6,4},{7,5},{8,10},{9,11},{10,... | collective-permute-start | bytes 4718600 | tf_op jit(solution)/shard_map/ppermute | solution.py:119
  510.7 44.9 %collective-permute-start.54 = (bf16[1024,640]{1,0:T(8,128)(2,1)S(1)}, bf16[1024,640]{1,0:T(8,128)(2,1)S(1)}, u32[]{:S(2)}, u32[]{:S(2)}) collective-permute-start(bf16[1024,640]{1,0:T(8,128)(2,1)S(1)} %copy-done.113), channel_id=1, source_target_pairs={{0,1},{1,0},{2,3},{3,2},{4,5},{5,4},{6,7},{7,6},{8,9},{9,8},{10,11... | collective-permute-start | bytes 3932168 | tf_op jit(solution)/shard_map/ppermute | solution.py:119
  518.4 37.2 %collective-permute-start.52 = (bf16[1024,640]{1,0:T(8,128)(2,1)S(1)}, bf16[1024,640]{1,0:T(8,128)(2,1)S(1)}, u32[]{:S(2)}, u32[]{:S(2)}) collective-permute-start(bf16[1024,640]{1,0:T(8,128)(2,1)S(1)} %copy-done.112), channel_id=1, source_target_pairs={{0,4},{1,5},{2,6},{3,7},{4,0},{5,1},{6,2},{7,3},{8,12},{9,13},{10,... | collective-permute-start | bytes 3932168 | tf_op jit(solution)/shard_map/ppermute | solution.py:119
  518.4 37.2 %collective-permute-start.51 = (bf16[128,2048]{0,1:T(8,128)(2,1)S(1)}, bf16[128,2048]{0,1:T(8,128)(2,1)S(1)}, u32[]{:S(2)}, u32[]{:S(2)}) collective-permute-start(bf16[128,2048]{0,1:T(8,128)(2,1)S(1)} %get-tuple-element.451), channel_id=1, source_target_pairs={{0,4},{1,5},{2,6},{3,7},{4,0},{5,1},{6,2},{7,3},{8,12},{9,13},{10,... | collective-permute-start | bytes 1572872 | tf_op jit(solution)/shard_map/ppermute | solution.py:119
  568.8 30.3 %collective-permute-start.57 = (bf16[2,2,128,640]{3,2,1,0:T(8,128)(2,1)}, bf16[2,2,128,640]{3,2,1,0:T(8,128)(2,1)}, u32[]{:S(2)}, u32[]{:S(2)}) collective-permute-start(bf16[2,2,128,640]{3,2,1,0:T(8,128)(2,1)} %dynamic-slice_bitcast_fusion.8), channel_id=1, source_target_pairs={{0,2},{1,3},{2,0},{3,1},{4,6},{5,7},{6,4},{7,5},{8,10},{9,11},{10,... | collective-permute-start | bytes 1966088 | tf_op jit(solution)/shard_map/ppermute | solution.py:119
  571.0 28.1 %collective-permute-start.56 = (bf16[2,2,128,768]{3,2,1,0:T(8,128)(2,1)}, bf16[2,2,128,768]{3,2,1,0:T(8,128)(2,1)}, u32[]{:S(2)}, u32[]{:S(2)}) collective-permute-start(bf16[2,2,128,768]{3,2,1,0:T(8,128)(2,1)} %dynamic-slice_bitcast_fusion.5), channel_id=1, source_target_pairs={{0,4},{1,5},{2,6},{3,7},{4,0},{5,1},{6,2},{7,3},{8,12},{9,13},{10,... | collective-permute-start | bytes 2359304 | tf_op jit(solution)/shard_map/ppermute | solution.py:119
  573.7 25.4 %collective-permute-start.55 = (bf16[2,2,128,640]{3,2,1,0:T(8,128)(2,1)}, bf16[2,2,128,640]{3,2,1,0:T(8,128)(2,1)}, u32[]{:S(2)}, u32[]{:S(2)}) collective-permute-start(bf16[2,2,128,640]{3,2,1,0:T(8,128)(2,1)} %dynamic-slice_bitcast_fusion.9), channel_id=1, source_target_pairs={{0,1},{1,0},{2,3},{3,2},{4,5},{5,4},{6,7},{7,6},{8,9},{9,8},{10,11... | collective-permute-start | bytes 1966088 | tf_op jit(solution)/shard_map/ppermute | solution.py:119
  612.2 25.8 %collective-permute-start.62 = (bf16[16,64,576]{2,1,0:T(8,128)(2,1)}, bf16[16,64,576]{2,1,0:T(8,128)(2,1)}, u32[]{:S(2)}, u32[]{:S(2)}) collective-permute-start(bf16[16,64,576]{2,1,0:T(8,128)(2,1)} %dynamic-slice_bitcast_fusion.2), channel_id=1, source_target_pairs={{0,16},{16,0},{1,17},{17,1},{2,18},{18,2},{3,19},{19,3},{4,20},{20... | collective-permute-start | bytes 3538952 | tf_op jit(solution)/shard_map/ppermute | solution.py:103
  618.9 21.8 %collective-permute-start.61 = (bf16[2,128,640]{1,2,0:T(8,128)(2,1)}, bf16[2,128,640]{1,2,0:T(8,128)(2,1)}, u32[]{:S(2)}, u32[]{:S(2)}) collective-permute-start(bf16[2,128,640]{1,2,0:T(8,128)(2,1)} %bitcast.161), channel_id=1, source_target_pairs={{0,4},{1,5},{2,6},{3,7},{4,0},{5,1},{6,2},{7,3},{8,12},{9,13},{10,... | collective-permute-start | bytes 983048 | tf_op jit(solution)/shard_map/ppermute | solution.py:119
  621.6 22.0 %collective-permute-start.60 = (bf16[2,128,768]{1,2,0:T(8,128)(2,1)}, bf16[2,128,768]{1,2,0:T(8,128)(2,1)}, u32[]{:S(2)}, u32[]{:S(2)}) collective-permute-start(bf16[2,128,768]{1,2,0:T(8,128)(2,1)} %bitcast.648), channel_id=1, source_target_pairs={{0,1},{1,0},{2,3},{3,2},{4,5},{5,4},{6,7},{7,6},{8,9},{9,8},{10,11... | collective-permute-start | bytes 1179656 | tf_op jit(solution)/shard_map/ppermute | solution.py:119
  637.4 59.9 %collective-permute-start.64 = (bf16[128,2048]{0,1:T(8,128)(2,1)S(1)}, bf16[128,2048]{0,1:T(8,128)(2,1)S(1)}, u32[]{:S(2)}, u32[]{:S(2)}) collective-permute-start(bf16[128,2048]{0,1:T(8,128)(2,1)S(1)} %dynamic-slice_bitcast_fusion.14), channel_id=1, source_target_pairs={{0,4},{1,5},{2,6},{3,7},{4,0},{5,1},{6,2},{7,3},{8,12},{9,13},{10,... | collective-permute-start | bytes 1572872 | tf_op jit(solution)/shard_map/ppermute | solution.py:119
  655.5 21.5 %collective-permute-start.69 = (bf16[16,64,512]{2,1,0:T(8,128)(2,1)S(1)}, bf16[16,64,512]{2,1,0:T(8,128)(2,1)S(1)}, u32[]{:S(2)}, u32[]{:S(2)}) collective-permute-start(bf16[16,64,512]{2,1,0:T(8,128)(2,1)S(1)} %dynamic-slice_bitcast_fusion.3), channel_id=1, source_target_pairs={{0,16},{16,0},{1,17},{17,1},{2,18},{18,2},{3,19},{19,3},{4,20},{20... | collective-permute-start | bytes 3145736 | tf_op jit(solution)/shard_map/ppermute | solution.py:103
  668.1 28.8 %collective-permute-start.66 = (bf16[128,768]{0,1:T(8,128)(2,1)S(1)}, bf16[128,768]{0,1:T(8,128)(2,1)S(1)}, u32[]{:S(2)}, u32[]{:S(2)}) collective-permute-start(bf16[128,768]{0,1:T(8,128)(2,1)S(1)} %dynamic-slice_bitcast_fusion.21), channel_id=1, source_target_pairs={{0,8},{1,9},{2,10},{3,11},{4,12},{5,13},{6,14},{7,15},{8,0},{9,1},... | collective-permute-start | bytes 589832 | tf_op jit(solution)/shard_map/ppermute | solution.py:119
  677.0 58.4 %collective-permute-start.73 = (bf16[2,2,2,80,1024]{4,3,2,1,0:T(8,128)(2,1)}, bf16[2,2,2,80,1024]{4,3,2,1,0:T(8,128)(2,1)}, u32[]{:S(2)}, u32[]{:S(2)}) collective-permute-start(bf16[2,2,2,80,1024]{4,3,2,1,0:T(8,128)(2,1)} %dynamic-slice_bitcast_fusion.1), channel_id=1, source_target_pairs={{0,2},{1,3},{2,0},{3,1},{4,6},{5,7},{6,4},{7,5},{8,10},{9,11},{10,... | collective-permute-start | bytes 3932168 | tf_op jit(solution)/shard_map/ppermute | solution.py:119
  681.4 54.0 %collective-permute-start.72 = (bf16[2,2,2,48,1024]{4,3,2,1,0:T(8,128)(2,1)}, bf16[2,2,2,48,1024]{4,3,2,1,0:T(8,128)(2,1)}, u32[]{:S(2)}, u32[]{:S(2)}) collective-permute-start(bf16[2,2,2,48,1024]{4,3,2,1,0:T(8,128)(2,1)} %dynamic-slice_bitcast_fusion.4), channel_id=1, source_target_pairs={{0,1},{1,0},{2,3},{3,2},{4,5},{5,4},{6,7},{7,6},{8,9},{9,8},{10,11... | collective-permute-start | bytes 2359304 | tf_op jit(solution)/shard_map/ppermute | solution.py:119
  681.9 53.5 %collective-permute-start.74 = (bf16[2,2,2,32,1024]{4,3,2,1,0:T(8,128)(2,1)}, bf16[2,2,2,32,1024]{4,3,2,1,0:T(8,128)(2,1)}, u32[]{:S(2)}, u32[]{:S(2)}) collective-permute-start(bf16[2,2,2,32,1024]{4,3,2,1,0:T(8,128)(2,1)} %dynamic-slice_bitcast_fusion.13), channel_id=1, source_target_pairs={{0,8},{1,9},{2,10},{3,11},{4,12},{5,13},{6,14},{7,15},{8,0},{9,1},... | collective-permute-start | bytes 1572872 | tf_op jit(solution)/shard_map/ppermute | solution.py:119
  696.9 38.6 %collective-permute-start.75 = (bf16[2,2,2,32,1024]{4,3,2,1,0:T(8,128)(2,1)}, bf16[2,2,2,32,1024]{4,3,2,1,0:T(8,128)(2,1)}, u32[]{:S(2)}, u32[]{:S(2)}) collective-permute-start(bf16[2,2,2,32,1024]{4,3,2,1,0:T(8,128)(2,1)} %dynamic-slice_bitcast_fusion.12), channel_id=1, source_target_pairs={{0,1},{1,0},{2,3},{3,2},{4,5},{5,4},{6,7},{7,6},{8,9},{9,8},{10,11... | collective-permute-start | bytes 1572872 | tf_op jit(solution)/shard_map/ppermute | solution.py:119
  699.0 43.5 %all-to-all-start.1 = ((bf16[16,64,512]{2,1,0:T(8,128)(2,1)}), bf16[16,64,512]{2,1,0:T(8,128)(2,1)}, u32[]{:S(2)}, u32[]{:S(2)}) async-start(bf16[16,64,512]{2,1,0:T(8,128)(2,1)} %fusion.1), calls=%async_computation.1 | async-start | bytes 2097152 | tf_op jit(solution)/shard_map/all_to_all | solution.py:1337
  742.4 21.9 %collective-permute-start.81 = (bf16[704,2048]{1,0:T(8,128)(2,1)}, bf16[704,2048]{1,0:T(8,128)(2,1)}, u32[]{:S(2)}, u32[]{:S(2)}) collective-permute-start(bf16[704,2048]{1,0:T(8,128)(2,1)} %fusion), channel_id=1, source_target_pairs={{0,16},{16,0},{1,17},{17,1},{2,18},{18,2},{3,19},{19,3},{4,20},{20... | collective-permute-start | bytes 8650760 | tf_op jit(solution)/shard_map/ppermute | solution.py:1183
  749.7 23.3 %collective-permute-start.80 = (bf16[2,2,32,1024]{3,1,2,0:T(2,128)(2,1)}, bf16[2,2,32,1024]{3,1,2,0:T(2,128)(2,1)}, u32[]{:S(2)}, u32[]{:S(2)}) collective-permute-start(bf16[2,2,32,1024]{3,1,2,0:T(2,128)(2,1)} %bitcast.547), channel_id=1, source_target_pairs={{0,2},{1,3},{2,0},{3,1},{4,6},{5,7},{6,4},{7,5},{8,10},{9,11},{10,... | collective-permute-start | bytes 786440 | tf_op jit(solution)/shard_map/ppermute | solution.py:119
  756.4 22.9 %collective-permute-start.78 = (bf16[2,2,80,1024]{3,2,1,0:T(8,128)(2,1)}, bf16[2,2,80,1024]{3,2,1,0:T(8,128)(2,1)}, u32[]{:S(2)}, u32[]{:S(2)}) collective-permute-start(bf16[2,2,80,1024]{3,2,1,0:T(8,128)(2,1)} %dynamic-slice_bitcast_fusion.7), channel_id=1, source_target_pairs={{0,1},{1,0},{2,3},{3,2},{4,5},{5,4},{6,7},{7,6},{8,9},{9,8},{10,11... | collective-permute-start | bytes 1966088 | tf_op jit(solution)/shard_map/ppermute | solution.py:119
  (162 other events, 1310.0 us)
Sparse Core Ops, SparseCore 0:
  9.6 18.4 all-gather.9
  82.6 142.5 all-gather.7
  227.3 26.2 all-gather.5

commit v5 on v4

--- a/solution.py
+++ b/solution.py
@@ -344,6 +344,7 @@
 
 def attend_back_kernel(
     heads,
+    x_ref,
     branch_ref,
     out_ref,
     probs_ref,
@@ -361,6 +362,7 @@
     d_kv_ref,
     d_joint_ref,
     d_gain_ref,
+    d_first_gain_ref,
     sum_ref,
     d_key_ref,
 ):
@@ -413,10 +415,13 @@
     fall = jnp.mean(d_kv_normed * latent, axis=-1, keepdims=True) * scale * scale * scale
     d_joint_ref[:, :KVR] = (d_kv_normed * scale - latent * fall).astype(bf16)
     d_joint_ref[:, KVR:] = d_key_ref[...].astype(bf16)
-    sum_ref[...] = (
-        lanes_dot(d_q_ref[...], q_ref[:, : nope + 2 * ROPE_LANES])
-        + lanes_dot(d_joint_ref[...], down_ref[...])
-    ).astype(sum_ref.dtype)
+    total = lanes_dot(d_q_ref[...], q_ref[:, : nope + 2 * ROPE_LANES]) + lanes_dot(
+        d_joint_ref[...], down_ref[...]
+    )
+    sum_ref[...] = total.astype(sum_ref.dtype)
+    x = x_ref[...].astype(f32)
+    scale = lax.rsqrt(jnp.mean(x * x, axis=-1, keepdims=True) + norm_eps)
+    d_first_gain_ref[0] = jnp.sum(total * (x * scale), axis=0, keepdims=True)
 
 
 def by_rows_call(
@@ -1040,7 +1045,8 @@
                 ("sum", (pair_rows, width), bf16),
             ),
         )
-        return outs, (q_full, kv_up, out_full, kv_down), (attn_scale, kv_scale, ffn_scale), (cos, sin)
+        weights = (q_full, kv_up, out_full, kv_down)
+        return outs, weights, (attn_scale, kv_scale, ffn_scale), (cos, sin), all_rows
 
     def cut_out(found):
         at = bits.index(pair_bit)
@@ -1075,7 +1081,7 @@
     )
 
     grad_all = lax.all_gather(held_grad[0], "expert")
-    outs, weights, scales, tables = attend(all_rows, results[4], results[:2], results[2:4])
+    outs, weights, scales, tables, all_rows = attend(all_rows, results[4], results[:2], results[2:4])
     normed, joint, kv_normed, query_parts, key_parts, values, probs, attended, attended_sum = outs
     q_full, kv_up, out_full, kv_down = weights
     attn_scale, kv_scale, ffn_scale = scales
@@ -1230,10 +1236,11 @@
             functools.partial(attend_back_kernel, heads),
             steps,
             (
-                "branch", "out", "probs", "heads", "keys", "values", "joint", "kv_gain", "up", "q",
+                "x", "branch", "out", "probs", "heads", "keys", "values", "joint", "kv_gain", "up", "q",
                 "down", "cos", "sin",
             ),
             dict(
+                x=all_rows,
                 branch=d_branch,
                 probs=probs,
                 heads=query_parts,
@@ -1255,6 +1262,7 @@
                 ("d_kv", (pair_rows, heads * (DH + DV)), bf16),
                 ("d_joint", (pair_rows, joint_width), bf16),
                 ("d_gain", (steps, 1, KVR), f32),
+                ("d_first_gain", (steps, 1, width), f32),
                 ("sum", (pair_rows, width), bf16),
             ),
             scratch=[pltpu.VMEM((4 * row_count, DR), f32)],
@@ -1262,7 +1270,7 @@
         return d_branch, outs
 
     def weight_gradients(results, found):
-        d_branch, (d_q_heads, d_kv_heads, d_joint, unused, unused) = found[0]
+        d_branch, (d_q_heads, d_kv_heads, d_joint, *unused) = found[0]
         if dp_count == 2:
             *parts, grad_kvdown = whole_call(
                 functools.partial(
@@ -1292,18 +1300,36 @@
         )
         return *parts, dp_scatter(grad_kvdown.transpose(1, 0, 2, 3), bf16)
 
+    def small_gradients(found, grad_kvdown):
+        unused, (*unused, grad_kv_scale, grad_attn_scale, unused) = found
+        grad_attn_scale = grad_attn_scale.sum(axis=0).reshape(expert_count, dp_count, n_gain)
+        scale_sums = jnp.concatenate(
+            [
+                grad_attn_scale.transpose(1, 0, 2),
+                grad_ffn_scale.reshape(dp_count, expert_count, n_gain),
+                grad_kv_scale.sum(axis=0).reshape(dp_count, expert_count, n_kv_gain),
+            ],
+            axis=-1,
+        )
+        room = joint_width - scale_sums.shape[-1]
+        scale_sums = dp_scatter(jnp.pad(scale_sums, ((0, 0), (0, 0), (0, room))))
+        return jnp.concatenate([grad_kvdown, scale_sums[:, None]], axis=1).astype(bf16)
+
     sums = []
 
     def back_of(results, found):
         return attend_back(results, found, results[0])
 
     def sum_and_gradients(results, found):
-        sums.append(by_owner(found[1][1][4]))
-        return weight_gradients(results, found[1:])
-
-    (unused, d_normed, *results), found = march(
+        sums.append(by_owner(found[1][1][-1]))
+        *parts, grad_kvdown = weight_gradients(results, found[1:])
+        sums.append(small_gradients(found[1], grad_kvdown))
+        return parts, sums[1]
+
+    (unused, d_normed, small_sums, *results), found = march(
         gathering(d_resid.astype(bf16), [pair_bit]),
         deferred(3, lambda: scattering(sums[0], [pair_bit], [pair_bit])),
+        deferred(3, lambda: scattering(sums[1], [pair_bit], bits, bf16)),
         *(
             scattering(after(part, d_resid), order[::-1], bits)
             for part, order in zip(out_part, orders)
@@ -1315,23 +1341,11 @@
             (shared_gradient, shared_hidden, d_shared_pair),
         ),
     )
-    *grad_parts, grad_kvdown = found[2]
+    grad_parts, unused = found[2]
     grad_shared_out, grad_shared = found[3]
     output = (resid + jnp.concatenate(results, axis=-1)).astype(bf16)
-    grad_kv_scale = found[1][1][3].sum(axis=0)
-    d_norm_in, grad_attn_scale = norm_back(turned(resid_in), attn_scale, d_normed)
+    d_norm_in, unused = norm_back(turned(resid_in), attn_scale, d_normed)
     grad_in = (d_resid + turned_back(d_norm_in)).astype(bf16)
-    scale_sums = jnp.concatenate(
-        [
-            grad_attn_scale.reshape(expert_count, dp_count, n_gain).transpose(1, 0, 2),
-            grad_ffn_scale.reshape(dp_count, expert_count, n_gain),
-            grad_kv_scale.reshape(dp_count, expert_count, n_kv_gain),
-        ],
-        axis=-1,
-    )
-    scale_sums = jnp.pad(scale_sums, ((0, 0), (0, 0), (0, joint_width - scale_sums.shape[-1])))
-    scale_sums = dp_scatter(scale_sums)[:, None]
-    small_sums = jnp.concatenate([grad_kvdown, scale_sums], axis=1).astype(bf16)
 
     def start_down(results, found, expert_hidden, slot_grad, shared):
         shared = lax.all_to_all(shared, "expert", split_axis=0, concat_axis=0, tiled=True)
@@ -1354,7 +1368,7 @@
         return found.transpose(2, 0, 3, 1, 4, 5).reshape(rows, -1).astype(f32)
 
     summed, found = march(
-        scattering(small_sums, (pair_bit, second, first, far), bits),
+        scattering(small_sums, (second, first, far), rest),
         *(
             scattering(part, order, bits, bf16)
             for part, order in (

time: 844 us -> 851 us (level)
  waiting for transfers between devices: 227 us -> 248 us
    ppermute x74, waiting for transfers between devices: 216 us -> 236 us  [partner(): return lax.ppermute(values, 'expert', [(i, i ^ bit) for i in range(count)])]
    squeeze x29 -> x31, local copies, waits for them, and re-layouts: 27.4 us -> 24.8 us  [pick(): return lax.dynamic_index_in_dim(values, place, axis, keepdims=False)]
    add x28 -> x27, other arithmetic: 35.4 us -> 33.2 us  [scattering(): values = own + other]
    unnamed x243 -> x237, local copies, waits for them, and re-layouts: 31.1 us -> 31.8 us
  transfers between devices with their start and end apart: 95 -> 95, of which waited for: 29 -> 30; matrix products, arithmetic and copies ran while one was open for 27% -> 26% of each run, Pallas kernels for 15% -> 16%
where the time goes in v5:
time: 851 us; the launch traced here: 841 us
  waiting for transfers between devices  248 us (29%)
  Pallas kernels  198 us (23%)
  local copies, waits for them, and re-layouts  133 us (16%)
  starting transfers between devices  121 us (14%)
  other arithmetic  114 us (13%)
  between operations  16.5 us (2%)
  matrix products  10.7 us (1%)
    ppermute x74, waiting for transfers between devices, partner(): return lax.ppermute(values, 'expert', [(i, i ^ bit) for i in range(count)])  236 us
    pallas_call x5, Pallas kernels, by_rows_call(): pl.pallas_call(kernel, grid_spec=pltpu.PrefetchScalarGridSpec(num_scalar_...  135 us
    ppermute x74, starting transfers between devices, partner(): return lax.ppermute(values, 'expert', [(i, i ^ bit) for i in range(count)])  80.3 us
    add x27, other arithmetic, scattering(): values = own + other  33.2 us
    unnamed x237, local copies, waits for them, and re-layouts  31.8 us
    pallas_call x3, Pallas kernels, columns_product(): pl.pallas_call(columns_kernel, grid_spec=pltpu.PrefetchScalarGridSpec(num...  30.6 us
    squeeze x31, local copies, waits for them, and re-layouts, pick(): return lax.dynamic_index_in_dim(values, place, axis, keepdims=False)  24.8 us
    another operation x44, other arithmetic, gathering(): jnp.stack([jnp.where(low, values, other), jnp.where(low, other, values)],...  21.9 us
  transfers between devices with their start and end apart: 95, of which 30 were waited for; matrix products, arithmetic and copies ran while one was open for 26% of the time, Pallas kernels for 16%

profile of v5, /device:TPU:1, one launch (start us, length us, event | category | flops | bytes accessed | tf_op | source)
XLA Modules:
  0.0 841.2 jit_solution(7274201095808416923)
XLA Ops:
  27.2 7.0 collective-permute-done.3
  42.0 4.0 collective-permute-done.7
  46.0 11.4 %collective-permute-done.8 = bf16[2,32,1024]{2,1,0:T(8,128)(2,1)S(1)} collective-permute-done((bf16[2,32,1024]{2,1,0:T(8,128)(2,1)S(1)}, bf16[2,32,1024]{2,1,0:T(8,128)(2,1)S(1)}, u32[]{:S(2)}, u32[]{:S(2)}) %collective-permute-start.8) | collective-permute-done | bytes 131104 | tf_op jit(solution)/shard_map/ppermute | solution.py:119
  62.5 10.8 %collective-permute-done.13 = bf16[2,2,32,1024]{3,2,1,0:T(8,128)(2,1)S(1)} collective-permute-done((bf16[2,2,32,1024]{3,2,1,0:T(8,128)(2,1)S(1)}, bf16[2,2,32,1024]{3,2,1,0:T(8,128)(2,1)S(1)}, u32[]{:S(2)}, u32[]{:S(2)}) %collective-permute-start.13) | collective-permute-done | bytes 262176 | tf_op jit(solution)/shard_map/ppermute | solution.py:119
  73.4 6.0 collective-permute-done.12
  81.1 6.2 copy.554
  98.4 3.2 collective-permute-start.17
  101.8 9.3 %collective-permute-done.18.refs_7_ = bf16[8,32,1024]{2,1,0:T(8,128)(2,1)S(1)} collective-permute-done((bf16[8,32,1024]{2,1,0:T(8,128)(2,1)S(1)}, bf16[8,32,1024]{2,1,0:T(8,128)(2,1)S(1)}, u32[]{:S(2)}, u32[]{:S(2)}) %collective-permute-start.18) | collective-permute-done | bytes 524320 | tf_op jit(solution)/shard_map/ppermute | solution.py:119
  111.0 26.8 %collective-permute-done.17.refs_5_ = bf16[8,32,1024]{2,1,0:T(8,128)(2,1)S(1)} collective-permute-done((bf16[8,32,1024]{2,1,0:T(8,128)(2,1)S(1)}, bf16[8,32,1024]{2,1,0:T(8,128)(2,1)S(1)}, u32[]{:S(2)}, u32[]{:S(2)}) %collective-permute-start.17) | collective-permute-done | bytes 524320 | tf_op jit(solution)/shard_map/ppermute | solution.py:119
  143.9 4.0 copy.464
  148.2 6.5 shard_map.255
  165.3 17.1 %shard_map.256 = (bf16[512,2048]{1,0:T(8,128)(2,1)}, f32[512,576]{1,0:T(8,128)}, bf16[512,512]{1,0:T(8,128)(2,1)}, bf16[512,768]{1,0:T(8,128)(2,1)}, bf16[512,76...) custom-call(bf16[512,2048]{1,0:T(8,128)(2,1)} %bitcast.555, ...), custom_call_target="tpu_custom_call" | custom-call | tf_op jit(solution)/shard_map/pallas_call | solution.py:455
  188.0 3.1 collective-permute-done.27
  200.8 25.3 %collective-permute-done.23 = bf16[128,2048]{0,1:T(8,128)(2,1)} collective-permute-done((bf16[128,2048]{0,1:T(8,128)(2,1)}, bf16[128,2048]{0,1:T(8,128)(2,1)}, u32[]{:S(2)}, u32[]{:S(2)}) %collective-permute-start.23) | collective-permute-done | bytes 524320 | tf_op jit(solution)/shard_map/ppermute | solution.py:119
  232.0 17.8 %shard_map.257 = (bf16[1152,2048]{1,0:T(8,128)(2,1)}, f32[1152,1408]{1,0:T(8,128)}, f32[2048,256]{1,0:T(8,128)}) custom-call(bf16[2048,2048]{1,0:T(8,128)(2,1)} %all-gather.8.cloned.1.call-done.grad_ref.right_ref, s32[8,1,256]{2,1,0:T(1,128)} %compare_select_fusion.slot_ref, f32[8,1,256]{2,1,0:T(1,128)} %bitcast.647, bf16[1408,2048]{1,0:T(8,128)(2,1)} %bitcast.552, ...), custom_call_target="tpu_custom_call" | custom-call | tf_op jit(solution)/shard_map/pallas_call | solution.py:455
  255.9 4.3 all-to-all-start
  262.9 9.6 %collective-permute-done.29 = bf16[2,128,640]{1,2,0:T(8,128)(2,1)} collective-permute-done((bf16[2,128,640]{1,2,0:T(8,128)(2,1)}, bf16[2,128,640]{1,2,0:T(8,128)(2,1)}, u32[]{:S(2)}, u32[]{:S(2)}) %collective-permute-start.29) | collective-permute-done | bytes 327712 | tf_op jit(solution)/shard_map/ppermute | solution.py:119
  281.9 7.3 all-to-all-done
  289.2 4.7 collective-permute-start.28
  293.9 4.4 collective-permute-done.33
  316.5 9.1 %collective-permute-done.37.right_came_ref = bf16[1024,640]{1,0:T(8,128)(2,1)} collective-permute-done((bf16[1024,640]{1,0:T(8,128)(2,1)}, bf16[1024,640]{1,0:T(8,128)(2,1)}, u32[]{:S(2)}, u32[]{:S(2)}) %collective-permute-start.37) | collective-permute-done | bytes 1310752 | tf_op jit(solution)/shard_map/ppermute | solution.py:119
  325.6 9.3 %collective-permute-done.35.left_came_ref = bf16[1024,640]{1,0:T(8,128)(2,1)} collective-permute-done((bf16[1024,640]{1,0:T(8,128)(2,1)}, bf16[1024,640]{1,0:T(8,128)(2,1)}, u32[]{:S(2)}, u32[]{:S(2)}) %collective-permute-start.35) | collective-permute-done | bytes 1310752 | tf_op jit(solution)/shard_map/ppermute | solution.py:119
  336.7 62.4 %shard_map.258 = (bf16[2048,2048]{1,0:T(8,128)(2,1)}, bf16[1152,2048]{1,0:T(8,128)(2,1)}, bf16[1152,1408]{1,0:T(8,128)(2,1)}, bf16[1152,2816]{1,0:T(8,128)(2,1)}...) custom-call(s32[3]{0:T(128)} %pad_add_fusion.2.me_ref, ...), custom_call_target="tpu_custom_call" | custom-call | tf_op jit(solution)/shard_map/pallas_call | solution.py:455
  400.2 19.7 %shard_map.260 = (bf16[1024,640]{1,0:T(8,128)(2,1)}, bf16[1024,640]{1,0:T(8,128)(2,1)}, bf16[1024,768]{1,0:T(8,128)(2,1)}, bf16[1024,768]{1,0:T(8,128)(2,1)}, bf...) custom-call(s32[3]{0:T(128)} %pad_add_fusion.2.me_ref, bf16[1152,1408]{1,0:T(8,128)(2,1)} %get-tuple-element.318.hidden_ref, ...), custom_call_target="tpu_custom_call" | custom-call | tf_op jit(solution)/shard_map/pallas_call | solution.py:455
  419.9 12.5 %shard_map.259 = bf16[1024,2816]{1,0:T(8,128)(2,1)} custom-call(s32[1]{0:T(128)} %bitcast.120.place_ref, bf16[1152,2048]{1,0:T(8,128)(2,1)} %get-tuple-element.241.left_ref, bf16[1152,2816]{1,0:T(8,128)(2,1)} %get-tuple-element.242.right_ref), custom_call_target="tpu_custom_call" | custom-call | tf_op jit(solution)/shard_map/pallas_call | solution.py:812
  432.4 8.3 collective-permute-start.44
  454.3 15.0 %shard_map.261 = f32[1024,2,1408]{2,1,0:T(2,128)} custom-call(s32[1]{0:T(128)} %bitcast.128.place_ref, bf16[1152,2048]{1,0:T(8,128)(2,1)} %get-tuple-element.241.left_ref, bf16[1152,2816]{1,0:T(8,128)(2,1)} %get-tuple-element.242.right_ref, bf16[1024,2816]{1,0:T(8,128)(2,1)} %collective-permute-done.44.came_ref), custom_call_target="tpu_custom_call" | custom-call | tf_op jit(solution)/shard_map/pallas_call | solution.py:791
  482.1 6.6 collective-permute-done.45
  490.4 3.1 collective-permute-start.50
  498.3 3.3 collective-permute-done.48
  508.9 7.9 collective-permute-start.54
  518.2 36.0 %collective-permute-done.51 = bf16[128,2048]{0,1:T(8,128)(2,1)S(1)} collective-permute-done((bf16[128,2048]{0,1:T(8,128)(2,1)S(1)}, bf16[128,2048]{0,1:T(8,128)(2,1)S(1)}, u32[]{:S(2)}, u32[]{:S(2)}) %collective-permute-start.51) | collective-permute-done | bytes 524320 | tf_op jit(solution)/shard_map/ppermute | solution.py:119
  558.0 5.0 collective-permute-start.58
  575.3 4.4 copy.499
  579.7 18.5 %shard_map.262 = (bf16[512,768]{1,0:T(8,128)(2,1)}, bf16[512,1024]{1,0:T(8,128)(2,1)}, bf16[512,576]{1,0:T(8,128)(2,1)}, f32[1,1,512]{2,1,0:T(1,128)}, f32[1,1,2048]{2,1,0:T(1,128)}, /*index=5*/bf16[512,2048]{1,0:T(8,128)(2,1)}) custom-call(bf16[512,2048]{1,0:T(8,128)(2,1)} %bitcast.556, bf16[512,2048]{1,0:T(8,128)(2,1)} %bitcast.557, ...), custom_call_target="tpu_custom_call" | custom-call | tf_op jit(solution)/shard_map/pallas_call | solution.py:455
  616.3 10.6 %shard_map.263 = (bf16[16,48,1024]{2,1,0:T(8,128)(2,1)}, bf16[16,80,1024]{2,1,0:T(8,128)(2,1)}, bf16[16,32,1024]{2,1,0:T(8,128)(2,1)}, bf16[16,32,1024]{2,1,0:T(8,128)(2,1)}, bf16[2,16,64,576]{3,2,1,0:T(8,128)(2,1)}) custom-call(bf16[512,2048]{1,0:T(8,128)(2,1)} %get-tuple-element.284.normed_ref, bf16[512,768]{1,0:T(8,128)(2,1)} %get-tuple-element.285.d_q_ref, ...), custom_call_target="tpu_custom_call" | custom-call | tf_op jit(solution)/shard_map/pallas_call | solution.py:565
  636.1 10.6 %shard_map.265 = bf16[2048,512]{1,0:T(8,128)(2,1)} custom-call(s32[1]{0:T(128)} %constant.340.clone.1.place_ref, bf16[2048,2048]{1,0:T(8,128)(2,1)} %get-tuple-element.305.left_ref, bf16[2048,512]{1,0:T(8,128)(2,1)} %get-tuple-element.306.right_ref), custom_call_target="tpu_custom_call" | custom-call | tf_op jit(solution)/shard_map/pallas_call | solution.py:812
  648.2 7.4 shard_map.264
  681.2 18.1 %collective-permute-done.63 = bf16[128,2048]{0,1:T(8,128)(2,1)S(1)} collective-permute-done((bf16[128,2048]{0,1:T(8,128)(2,1)S(1)}, bf16[128,2048]{0,1:T(8,128)(2,1)S(1)}, u32[]{:S(2)}, u32[]{:S(2)}) %collective-permute-start.63) | collective-permute-done | bytes 524320 | tf_op jit(solution)/shard_map/ppermute | solution.py:119
  699.5 14.1 %collective-permute-done.66 = bf16[2,2,2,65,576]{4,2,3,0,1:T(2,128)(2,1)S(1)} collective-permute-done((bf16[2,2,2,65,576]{4,2,3,0,1:T(2,128)(2,1)S(1)}, bf16[2,2,2,65,576]{4,2,3,0,1:T(2,128)(2,1)S(1)}, u32[]{:S(2)}, u32[]{:S(2)}) %collective-permute-start.66) | collective-permute-done | bytes 599072 | tf_op jit(solution)/shard_map/ppermute | solution.py:119
  716.0 4.6 all-to-all-start.1
  724.2 10.7 %fusion.64 = f32[1408,2048]{1,0:T(8,128)S(1)} fusion(bf16[1152,1408]{1,0:T(8,128)(2,1)} %get-tuple-element.318.hidden_ref, bf16[1152,2048]{1,0:T(8,128)(2,1)} %get-tuple-element.319), kind=kOutput, calls=%fused_computation.346 | convolution fusion | flops 6643777536 | bytes 19496960 | tf_op jit(solution)/shard_map/dot_general | solution.py:74
  742.7 3.2 collective-permute-start.82
  770.8 7.4 add_bitcast_fusion
  778.2 4.8 collective-permute-done.77
  805.5 5.6 collective-permute-done.83
  817.3 3.4 collective-permute-done.88
  820.9 3.2 collective-permute-start.89
  (683 shorter events, 310.8 us)
Async XLA Ops:
  7.2 224.8 %all-gather.10.cloned.1.call-start = ((), (), s32[]{:S(2)}) async-start(), calls=%async_computation.4 | async-start | bytes 8650752 | tf_op jit(solution)/shard_map/all_gather | solution.py:964
  7.9 224.1 %all-gather.8.cloned.1.call-start = ((), (), s32[]{:S(2)}) async-start(), calls=%async_computation.3 | async-start | bytes 8912896 | tf_op jit(solution)/shard_map/all_gather | solution.py:1083
  12.0 23.0 %collective-permute-start = (bf16[128,2048]{0,1:T(8,128)(2,1)}, bf16[128,2048]{0,1:T(8,128)(2,1)}, u32[]{:S(2)}, u32[]{:S(2)}) collective-permute-start(bf16[128,2048]{0,1:T(8,128)(2,1)} %bitcast.2), channel_id=1, source_target_pairs={{0,4},{1,5},{2,6},{3,7},{4,0},{5,1},{6,2},{7,3},{8,12},{9,13},{10,... | collective-permute-start | bytes 1572872 | tf_op jit(solution)/shard_map/ppermute | solution.py:119
  35.1 22.3 %collective-permute-start.6 = (bf16[2,80,1024]{2,1,0:T(8,128)(2,1)S(1)}, bf16[2,80,1024]{2,1,0:T(8,128)(2,1)S(1)}, u32[]{:S(2)}, u32[]{:S(2)}) collective-permute-start(bf16[2,80,1024]{2,1,0:T(8,128)(2,1)S(1)} %pad_maximum_fusion.22), channel_id=1, source_target_pairs={{0,8},{1,9},{2,10},{3,11},{4,12},{5,13},{6,14},{7,15},{8,0},{9,1},... | collective-permute-start | bytes 983048 | tf_op jit(solution)/shard_map/ppermute | solution.py:119
  59.5 21.4 %collective-permute-start.11 = (bf16[2,2,80,1024]{3,2,1,0:T(8,128)(2,1)S(1)}, bf16[2,2,80,1024]{3,2,1,0:T(8,128)(2,1)S(1)}, u32[]{:S(2)}, u32[]{:S(2)}) collective-permute-start(bf16[2,2,80,1024]{3,2,1,0:T(8,128)(2,1)S(1)} %pad_maximum_fusion.13), channel_id=1, source_target_pairs={{0,1},{1,0},{2,3},{3,2},{4,5},{5,4},{6,7},{7,6},{8,9},{9,8},{10,11... | collective-permute-start | bytes 1966088 | tf_op jit(solution)/shard_map/ppermute | solution.py:119
  80.9 255.9 %all-gather.6.cloned.1.call-start = ((), (), s32[]{:S(2)}) async-start(), calls=%async_computation.2 | async-start | bytes 17301504 | tf_op jit(solution)/shard_map/all_gather | solution.py:963
  93.1 46.6 %collective-permute-start.19 = (bf16[2,2,2,80,576]{4,3,2,1,0:T(8,128)(2,1)S(1)}, bf16[2,2,2,80,576]{4,3,2,1,0:T(8,128)(2,1)S(1)}, u32[]{:S(2)}, u32[]{:S(2)}) collective-permute-start(bf16[2,2,2,80,576]{4,3,2,1,0:T(8,128)(2,1)S(1)} %pad_maximum_fusion.9), channel_id=1, source_target_pairs={{0,4},{1,5},{2,6},{3,7},{4,0},{5,1},{6,2},{7,3},{8,12},{9,13},{10,... | collective-permute-start | bytes 2211848 | tf_op jit(solution)/shard_map/ppermute | solution.py:119
  95.0 44.7 %collective-permute-start.16 = (bf16[8,80,1024]{2,1,0:T(8,128)(2,1)S(1)}, bf16[8,80,1024]{2,1,0:T(8,128)(2,1)S(1)}, u32[]{:S(2)}, u32[]{:S(2)}) collective-permute-start(bf16[8,80,1024]{2,1,0:T(8,128)(2,1)S(1)} %bitcast.589), channel_id=1, source_target_pairs={{0,2},{1,3},{2,0},{3,1},{4,6},{5,7},{6,4},{7,5},{8,10},{9,11},{10,... | collective-permute-start | bytes 3932168 | tf_op jit(solution)/shard_map/ppermute | solution.py:119
  97.4 42.2 %collective-permute-start.15 = (bf16[8,48,1024]{2,1,0:T(8,128)(2,1)S(1)}, bf16[8,48,1024]{2,1,0:T(8,128)(2,1)S(1)}, u32[]{:S(2)}, u32[]{:S(2)}) collective-permute-start(bf16[8,48,1024]{2,1,0:T(8,128)(2,1)S(1)} %bitcast.605), channel_id=1, source_target_pairs={{0,1},{1,0},{2,3},{3,2},{4,5},{5,4},{6,7},{7,6},{8,9},{9,8},{10,11... | collective-permute-start | bytes 2359304 | tf_op jit(solution)/shard_map/ppermute | solution.py:119
  98.4 39.5 %collective-permute-start.17 = (bf16[8,32,1024]{2,1,0:T(8,128)(2,1)S(1)}, bf16[8,32,1024]{2,1,0:T(8,128)(2,1)S(1)}, u32[]{:S(2)}, u32[]{:S(2)}) collective-permute-start(bf16[8,32,1024]{2,1,0:T(8,128)(2,1)S(1)} %bitcast.622), channel_id=1, source_target_pairs={{0,8},{1,9},{2,10},{3,11},{4,12},{5,13},{6,14},{7,15},{8,0},{9,1},... | collective-permute-start | bytes 1572872 | tf_op jit(solution)/shard_map/ppermute | solution.py:119
  197.1 29.0 %collective-permute-start.23 = (bf16[128,2048]{0,1:T(8,128)(2,1)}, bf16[128,2048]{0,1:T(8,128)(2,1)}, u32[]{:S(2)}, u32[]{:S(2)}) collective-permute-start(bf16[128,2048]{0,1:T(8,128)(2,1)} %dynamic-slice_bitcast_fusion.16), channel_id=1, source_target_pairs={{0,4},{1,5},{2,6},{3,7},{4,0},{5,1},{6,2},{7,3},{8,12},{9,13},{10,... | collective-permute-start | bytes 1572872 | tf_op jit(solution)/shard_map/ppermute | solution.py:119
  227.8 21.9 %collective-permute-start.24 = (bf16[128,640]{0,1:T(8,128)(2,1)S(1)}, bf16[128,640]{0,1:T(8,128)(2,1)S(1)}, u32[]{:S(2)}, u32[]{:S(2)}) collective-permute-start(bf16[128,640]{0,1:T(8,128)(2,1)S(1)} %get-tuple-element.508), channel_id=1, source_target_pairs={{0,2},{1,3},{2,0},{3,1},{4,6},{5,7},{6,4},{7,5},{8,10},{9,11},{10,... | collective-permute-start | bytes 491528 | tf_op jit(solution)/shard_map/ppermute | solution.py:119
  255.9 33.3 %all-to-all-start = ((bf16[16,64,512]{2,1,0:T(8,128)(2,1)}), bf16[16,64,512]{2,1,0:T(8,128)(2,1)}, u32[]{:S(2)}, u32[]{:S(2)}) async-start(bf16[16,64,512]{2,1,0:T(8,128)(2,1)} %reshape.470), calls=%async_computation | async-start | bytes 2097152 | tf_op jit(solution)/shard_map/all_to_all | solution.py:966
  289.2 24.1 %collective-permute-start.28 = (bf16[16,64,512]{2,1,0:T(8,128)(2,1)}, bf16[16,64,512]{2,1,0:T(8,128)(2,1)}, u32[]{:S(2)}, u32[]{:S(2)}) collective-permute-start(bf16[16,64,512]{2,1,0:T(8,128)(2,1)} %all-to-all-done), channel_id=1, source_target_pairs={{0,16},{16,0},{1,17},{17,1},{2,18},{18,2},{3,19},{19,3},{4,20},{20... | collective-permute-start | bytes 3145736 | tf_op jit(solution)/shard_map/ppermute | solution.py:84
  301.3 24.3 %collective-permute-start.37 = (bf16[1024,640]{1,0:T(8,128)(2,1)}, bf16[1024,640]{1,0:T(8,128)(2,1)}, u32[]{:S(2)}, u32[]{:S(2)}) collective-permute-start(bf16[1024,640]{1,0:T(8,128)(2,1)} %bitcast.119.right_ref), channel_id=1, source_target_pairs={{0,1},{1,0},{2,3},{3,2},{4,5},{5,4},{6,7},{7,6},{8,9},{9,8},{10,11... | collective-permute-start | bytes 3932168 | tf_op jit(solution)/shard_map/ppermute | solution.py:119
  307.3 29.5 %collective-permute-start.36 = (bf16[1024,768]{1,0:T(8,128)(2,1)S(1)}, bf16[1024,768]{1,0:T(8,128)(2,1)}, u32[]{:S(2)}, u32[]{:S(2)}) collective-permute-start(bf16[1024,768]{1,0:T(8,128)(2,1)S(1)} %bitcast.579), channel_id=1, source_target_pairs={{0,2},{1,3},{2,0},{3,1},{4,6},{5,7},{6,4},{7,5},{8,10},{9,11},{10,... | collective-permute-start | bytes 4718600 | tf_op jit(solution)/shard_map/ppermute | solution.py:119
  312.7 22.2 %collective-permute-start.35 = (bf16[1024,640]{1,0:T(8,128)(2,1)}, bf16[1024,640]{1,0:T(8,128)(2,1)}, u32[]{:S(2)}, u32[]{:S(2)}) collective-permute-start(bf16[1024,640]{1,0:T(8,128)(2,1)} %bitcast.586), channel_id=1, source_target_pairs={{0,4},{1,5},{2,6},{3,7},{4,0},{5,1},{6,2},{7,3},{8,12},{9,13},{10,... | collective-permute-start | bytes 3932168 | tf_op jit(solution)/shard_map/ppermute | solution.py:119
  399.1 33.3 %collective-permute-start.39 = (bf16[1024,768]{1,0:T(8,128)(2,1)}, bf16[1024,768]{1,0:T(8,128)(2,1)S(1)}, u32[]{:S(2)}, u32[]{:S(2)}) collective-permute-start(bf16[1024,768]{1,0:T(8,128)(2,1)} %get-tuple-element.221), channel_id=1, source_target_pairs={{0,2},{1,3},{2,0},{3,1},{4,6},{5,7},{6,4},{7,5},{8,10},{9,11},{10,... | collective-permute-start | bytes 4718600 | tf_op jit(solution)/shard_map/ppermute | solution.py:119
  399.2 33.2 %collective-permute-start.38 = (bf16[1024,640]{1,0:T(8,128)(2,1)}, bf16[1024,640]{1,0:T(8,128)(2,1)}, u32[]{:S(2)}, u32[]{:S(2)}) collective-permute-start(bf16[1024,640]{1,0:T(8,128)(2,1)} %get-tuple-element.220), channel_id=1, source_target_pairs={{0,4},{1,5},{2,6},{3,7},{4,0},{5,1},{6,2},{7,3},{8,12},{9,13},{10,... | collective-permute-start | bytes 3932168 | tf_op jit(solution)/shard_map/ppermute | solution.py:119
  399.3 33.1 %collective-permute-start.40 = (bf16[1024,640]{1,0:T(8,128)(2,1)}, bf16[1024,640]{1,0:T(8,128)(2,1)}, u32[]{:S(2)}, u32[]{:S(2)}) collective-permute-start(bf16[1024,640]{1,0:T(8,128)(2,1)} %get-tuple-element.222), channel_id=1, source_target_pairs={{0,1},{1,0},{2,3},{3,2},{4,5},{5,4},{6,7},{7,6},{8,9},{9,8},{10,11... | collective-permute-start | bytes 3932168 | tf_op jit(solution)/shard_map/ppermute | solution.py:119
  432.4 21.9 %collective-permute-start.44 = (bf16[1024,2816]{1,0:T(8,128)(2,1)}, bf16[1024,2816]{1,0:T(8,128)(2,1)}, u32[]{:S(2)}, u32[]{:S(2)}) collective-permute-start(bf16[1024,2816]{1,0:T(8,128)(2,1)} %shard_map.259), channel_id=1, source_target_pairs={{0,16},{16,0},{1,17},{17,1},{2,18},{18,2},{3,19},{19,3},{4,20},{20... | collective-permute-start | bytes 17301512 | tf_op jit(solution)/shard_map/ppermute | solution.py:1202
  444.0 25.3 %collective-permute-start.42 = (bf16[2,2,128,768]{3,2,1,0:T(8,128)(2,1)}, bf16[2,2,128,768]{3,2,1,0:T(8,128)(2,1)}, u32[]{:S(2)}, u32[]{:S(2)}) collective-permute-start(bf16[2,2,128,768]{3,2,1,0:T(8,128)(2,1)} %dynamic-slice_bitcast_fusion.6), channel_id=1, source_target_pairs={{0,4},{1,5},{2,6},{3,7},{4,0},{5,1},{6,2},{7,3},{8,12},{9,13},{10,... | collective-permute-start | bytes 2359304 | tf_op jit(solution)/shard_map/ppermute | solution.py:119
  508.0 46.2 %collective-permute-start.53 = (bf16[1024,768]{1,0:T(8,128)(2,1)S(1)}, bf16[1024,768]{1,0:T(8,128)(2,1)S(1)}, u32[]{:S(2)}, u32[]{:S(2)}) collective-permute-start(bf16[1024,768]{1,0:T(8,128)(2,1)S(1)} %copy-done.108), channel_id=1, source_target_pairs={{0,2},{1,3},{2,0},{3,1},{4,6},{5,7},{6,4},{7,5},{8,10},{9,11},{10,... | collective-permute-start | bytes 4718600 | tf_op jit(solution)/shard_map/ppermute | solution.py:119
  508.9 45.3 %collective-permute-start.54 = (bf16[1024,640]{1,0:T(8,128)(2,1)S(1)}, bf16[1024,640]{1,0:T(8,128)(2,1)S(1)}, u32[]{:S(2)}, u32[]{:S(2)}) collective-permute-start(bf16[1024,640]{1,0:T(8,128)(2,1)S(1)} %copy-done.110), channel_id=1, source_target_pairs={{0,1},{1,0},{2,3},{3,2},{4,5},{5,4},{6,7},{7,6},{8,9},{9,8},{10,11... | collective-permute-start | bytes 3932168 | tf_op jit(solution)/shard_map/ppermute | solution.py:119
  516.7 37.4 %collective-permute-start.52 = (bf16[1024,640]{1,0:T(8,128)(2,1)S(1)}, bf16[1024,640]{1,0:T(8,128)(2,1)S(1)}, u32[]{:S(2)}, u32[]{:S(2)}) collective-permute-start(bf16[1024,640]{1,0:T(8,128)(2,1)S(1)} %copy-done.109), channel_id=1, source_target_pairs={{0,4},{1,5},{2,6},{3,7},{4,0},{5,1},{6,2},{7,3},{8,12},{9,13},{10,... | collective-permute-start | bytes 3932168 | tf_op jit(solution)/shard_map/ppermute | solution.py:119
  516.9 37.2 %collective-permute-start.51 = (bf16[128,2048]{0,1:T(8,128)(2,1)S(1)}, bf16[128,2048]{0,1:T(8,128)(2,1)S(1)}, u32[]{:S(2)}, u32[]{:S(2)}) collective-permute-start(bf16[128,2048]{0,1:T(8,128)(2,1)S(1)} %get-tuple-element.427), channel_id=1, source_target_pairs={{0,4},{1,5},{2,6},{3,7},{4,0},{5,1},{6,2},{7,3},{8,12},{9,13},{10,... | collective-permute-start | bytes 1572872 | tf_op jit(solution)/shard_map/ppermute | solution.py:119
  567.0 31.2 %collective-permute-start.57 = (bf16[2,2,128,640]{3,2,1,0:T(8,128)(2,1)}, bf16[2,2,128,640]{3,2,1,0:T(8,128)(2,1)}, u32[]{:S(2)}, u32[]{:S(2)}) collective-permute-start(bf16[2,2,128,640]{3,2,1,0:T(8,128)(2,1)} %dynamic-slice_bitcast_fusion.9), channel_id=1, source_target_pairs={{0,2},{1,3},{2,0},{3,1},{4,6},{5,7},{6,4},{7,5},{8,10},{9,11},{10,... | collective-permute-start | bytes 1966088 | tf_op jit(solution)/shard_map/ppermute | solution.py:119
  569.3 28.9 %collective-permute-start.56 = (bf16[2,2,128,768]{3,2,1,0:T(8,128)(2,1)}, bf16[2,2,128,768]{3,2,1,0:T(8,128)(2,1)}, u32[]{:S(2)}, u32[]{:S(2)}) collective-permute-start(bf16[2,2,128,768]{3,2,1,0:T(8,128)(2,1)} %dynamic-slice_bitcast_fusion.5), channel_id=1, source_target_pairs={{0,4},{1,5},{2,6},{3,7},{4,0},{5,1},{6,2},{7,3},{8,12},{9,13},{10,... | collective-permute-start | bytes 2359304 | tf_op jit(solution)/shard_map/ppermute | solution.py:119
  571.9 26.3 %collective-permute-start.55 = (bf16[2,2,128,640]{3,2,1,0:T(8,128)(2,1)}, bf16[2,2,128,640]{3,2,1,0:T(8,128)(2,1)}, u32[]{:S(2)}, u32[]{:S(2)}) collective-permute-start(bf16[2,2,128,640]{3,2,1,0:T(8,128)(2,1)} %dynamic-slice_bitcast_fusion.10), channel_id=1, source_target_pairs={{0,1},{1,0},{2,3},{3,2},{4,5},{5,4},{6,7},{7,6},{8,9},{9,8},{10,11... | collective-permute-start | bytes 1966088 | tf_op jit(solution)/shard_map/ppermute | solution.py:119
  601.3 34.8 %collective-permute-start.61 = (bf16[2,128,640]{1,2,0:T(8,128)(2,1)}, bf16[2,128,640]{1,2,0:T(8,128)(2,1)}, u32[]{:S(2)}, u32[]{:S(2)}) collective-permute-start(bf16[2,128,640]{1,2,0:T(8,128)(2,1)} %bitcast.161), channel_id=1, source_target_pairs={{0,4},{1,5},{2,6},{3,7},{4,0},{5,1},{6,2},{7,3},{8,12},{9,13},{10,... | collective-permute-start | bytes 983048 | tf_op jit(solution)/shard_map/ppermute | solution.py:119
  603.9 32.2 %collective-permute-start.60 = (bf16[2,128,768]{1,2,0:T(8,128)(2,1)}, bf16[2,128,768]{1,2,0:T(8,128)(2,1)}, u32[]{:S(2)}, u32[]{:S(2)}) collective-permute-start(bf16[2,128,768]{1,2,0:T(8,128)(2,1)} %bitcast.159), channel_id=1, source_target_pairs={{0,1},{1,0},{2,3},{3,2},{4,5},{5,4},{6,7},{7,6},{8,9},{9,8},{10,11... | collective-permute-start | bytes 1179656 | tf_op jit(solution)/shard_map/ppermute | solution.py:119
  608.0 28.1 %collective-permute-start.59 = (bf16[2,128,640]{1,2,0:T(8,128)(2,1)}, bf16[2,128,640]{1,2,0:T(8,128)(2,1)}, u32[]{:S(2)}, u32[]{:S(2)}) collective-permute-start(bf16[2,128,640]{1,2,0:T(8,128)(2,1)} %bitcast.644), channel_id=1, source_target_pairs={{0,8},{1,9},{2,10},{3,11},{4,12},{5,13},{6,14},{7,15},{8,0},{9,1},... | collective-permute-start | bytes 983048 | tf_op jit(solution)/shard_map/ppermute | solution.py:119
  629.5 40.3 %collective-permute-start.64 = (bf16[16,64,576]{2,1,0:T(8,128)(2,1)}, bf16[16,64,576]{2,1,0:T(8,128)(2,1)}, u32[]{:S(2)}, u32[]{:S(2)}) collective-permute-start(bf16[16,64,576]{2,1,0:T(8,128)(2,1)} %dynamic-slice_bitcast_fusion.2), channel_id=1, source_target_pairs={{0,16},{16,0},{1,17},{17,1},{2,18},{18,2},{3,19},{19,3},{4,20},{20... | collective-permute-start | bytes 3538952 | tf_op jit(solution)/shard_map/ppermute | solution.py:103
  635.6 29.4 %collective-permute-start.62 = (bf16[2,128,2048]{1,2,0:T(8,128)(2,1)}, bf16[2,128,2048]{1,2,0:T(8,128)(2,1)}, u32[]{:S(2)}, u32[]{:S(2)}) collective-permute-start(bf16[2,128,2048]{1,2,0:T(8,128)(2,1)} %bitcast.628), channel_id=1, source_target_pairs={{0,16},{16,0},{1,17},{17,1},{2,18},{18,2},{3,19},{19,3},{4,20},{20... | collective-permute-start | bytes 3145736 | tf_op jit(solution)/shard_map/ppermute | solution.py:103
  648.1 27.9 %collective-permute-start.71 = (bf16[16,64,512]{2,1,0:T(8,128)(2,1)S(1)}, bf16[16,64,512]{2,1,0:T(8,128)(2,1)S(1)}, u32[]{:S(2)}, u32[]{:S(2)}) collective-permute-start(bf16[16,64,512]{2,1,0:T(8,128)(2,1)S(1)} %dynamic-slice_bitcast_fusion.3), channel_id=1, source_target_pairs={{0,16},{16,0},{1,17},{17,1},{2,18},{18,2},{3,19},{19,3},{4,20},{20... | collective-permute-start | bytes 3145736 | tf_op jit(solution)/shard_map/ppermute | solution.py:103
  669.9 29.5 %collective-permute-start.63 = (bf16[128,2048]{0,1:T(8,128)(2,1)S(1)}, bf16[128,2048]{0,1:T(8,128)(2,1)S(1)}, u32[]{:S(2)}, u32[]{:S(2)}) collective-permute-start(bf16[128,2048]{0,1:T(8,128)(2,1)S(1)} %dynamic-slice_bitcast_fusion.15), channel_id=1, source_target_pairs={{0,4},{1,5},{2,6},{3,7},{4,0},{5,1},{6,2},{7,3},{8,12},{9,13},{10,... | collective-permute-start | bytes 1572872 | tf_op jit(solution)/shard_map/ppermute | solution.py:119
  674.0 39.6 %collective-permute-start.66 = (bf16[2,2,2,65,576]{4,2,3,0,1:T(2,128)(2,1)S(1)}, bf16[2,2,2,65,576]{4,2,3,0,1:T(2,128)(2,1)S(1)}, u32[]{:S(2)}, u32[]{:S(2)}) collective-permute-start(bf16[2,2,2,65,576]{4,2,3,0,1:T(2,128)(2,1)S(1)} %dynamic-slice_bitcast_fusion.7), channel_id=1, source_target_pairs={{0,4},{1,5},{2,6},{3,7},{4,0},{5,1},{6,2},{7,3},{8,12},{9,13},{10,... | collective-permute-start | bytes 1797128 | tf_op jit(solution)/shard_map/ppermute | solution.py:119
  677.9 63.7 %collective-permute-start.74 = (bf16[2,2,2,80,1024]{4,3,2,1,0:T(8,128)(2,1)}, bf16[2,2,2,80,1024]{4,3,2,1,0:T(8,128)(2,1)}, u32[]{:S(2)}, u32[]{:S(2)}) collective-permute-start(bf16[2,2,2,80,1024]{4,3,2,1,0:T(8,128)(2,1)} %dynamic-slice_bitcast_fusion.1), channel_id=1, source_target_pairs={{0,2},{1,3},{2,0},{3,1},{4,6},{5,7},{6,4},{7,5},{8,10},{9,11},{10,... | collective-permute-start | bytes 3932168 | tf_op jit(solution)/shard_map/ppermute | solution.py:119
  680.5 61.2 %collective-permute-start.73 = (bf16[2,2,2,48,1024]{4,3,2,1,0:T(8,128)(2,1)}, bf16[2,2,2,48,1024]{4,3,2,1,0:T(8,128)(2,1)}, u32[]{:S(2)}, u32[]{:S(2)}) collective-permute-start(bf16[2,2,2,48,1024]{4,3,2,1,0:T(8,128)(2,1)} %dynamic-slice_bitcast_fusion.4), channel_id=1, source_target_pairs={{0,1},{1,0},{2,3},{3,2},{4,5},{5,4},{6,7},{7,6},{8,9},{9,8},{10,11... | collective-permute-start | bytes 2359304 | tf_op jit(solution)/shard_map/ppermute | solution.py:119
  680.7 61.0 %collective-permute-start.75 = (bf16[2,2,2,32,1024]{4,3,2,1,0:T(8,128)(2,1)}, bf16[2,2,2,32,1024]{4,3,2,1,0:T(8,128)(2,1)}, u32[]{:S(2)}, u32[]{:S(2)}) collective-permute-start(bf16[2,2,2,32,1024]{4,3,2,1,0:T(8,128)(2,1)} %dynamic-slice_bitcast_fusion.14), channel_id=1, source_target_pairs={{0,8},{1,9},{2,10},{3,11},{4,12},{5,13},{6,14},{7,15},{8,0},{9,1},... | collective-permute-start | bytes 1572872 | tf_op jit(solution)/shard_map/ppermute | solution.py:119
  699.3 42.3 %collective-permute-start.76 = (bf16[2,2,2,32,1024]{4,3,2,1,0:T(8,128)(2,1)}, bf16[2,2,2,32,1024]{4,3,2,1,0:T(8,128)(2,1)}, u32[]{:S(2)}, u32[]{:S(2)}) collective-permute-start(bf16[2,2,2,32,1024]{4,3,2,1,0:T(8,128)(2,1)} %dynamic-slice_bitcast_fusion.13), channel_id=1, source_target_pairs={{0,1},{1,0},{2,3},{3,2},{4,5},{5,4},{6,7},{7,6},{8,9},{9,8},{10,11... | collective-permute-start | bytes 1572872 | tf_op jit(solution)/shard_map/ppermute | solution.py:119
  716.0 26.7 %all-to-all-start.1 = ((bf16[16,64,512]{2,1,0:T(8,128)(2,1)}), bf16[16,64,512]{2,1,0:T(8,128)(2,1)}, u32[]{:S(2)}, u32[]{:S(2)}) async-start(bf16[16,64,512]{2,1,0:T(8,128)(2,1)} %fusion.2), calls=%async_computation.1 | async-start | bytes 2097152 | tf_op jit(solution)/shard_map/all_to_all | solution.py:1351
  742.7 26.8 %collective-permute-start.82 = (bf16[704,2048]{1,0:T(8,128)(2,1)}, bf16[704,2048]{1,0:T(8,128)(2,1)}, u32[]{:S(2)}, u32[]{:S(2)}) collective-permute-start(bf16[704,2048]{1,0:T(8,128)(2,1)} %fusion), channel_id=1, source_target_pairs={{0,16},{16,0},{1,17},{17,1},{2,18},{18,2},{3,19},{19,3},{4,20},{20... | collective-permute-start | bytes 8650760 | tf_op jit(solution)/shard_map/ppermute | solution.py:1189
  752.9 30.1 %collective-permute-start.81 = (bf16[2,2,32,1024]{3,1,2,0:T(2,128)(2,1)}, bf16[2,2,32,1024]{3,1,2,0:T(2,128)(2,1)}, u32[]{:S(2)}, u32[]{:S(2)}) collective-permute-start(bf16[2,2,32,1024]{3,1,2,0:T(2,128)(2,1)} %bitcast.542), channel_id=1, source_target_pairs={{0,2},{1,3},{2,0},{3,1},{4,6},{5,7},{6,4},{7,5},{8,10},{9,11},{10,... | collective-permute-start | bytes 786440 | tf_op jit(solution)/shard_map/ppermute | solution.py:119
  757.4 25.6 %collective-permute-start.80 = (bf16[2,2,32,1024]{3,0,2,1:T(2,128)(2,1)}, bf16[2,2,32,1024]{3,0,2,1:T(2,128)(2,1)}, u32[]{:S(2)}, u32[]{:S(2)}) collective-permute-start(bf16[2,2,32,1024]{3,0,2,1:T(2,128)(2,1)} %bitcast.543), channel_id=1, source_target_pairs={{0,1},{1,0},{2,3},{3,2},{4,5},{5,4},{6,7},{7,6},{8,9},{9,8},{10,11... | collective-permute-start | bytes 786440 | tf_op jit(solution)/shard_map/ppermute | solution.py:119
  760.1 22.9 %collective-permute-start.79 = (bf16[2,2,80,1024]{3,2,1,0:T(8,128)(2,1)}, bf16[2,2,80,1024]{3,2,1,0:T(8,128)(2,1)}, u32[]{:S(2)}, u32[]{:S(2)}) collective-permute-start(bf16[2,2,80,1024]{3,2,1,0:T(8,128)(2,1)} %dynamic-slice_bitcast_fusion.8), channel_id=1, source_target_pairs={{0,1},{1,0},{2,3},{3,2},{4,5},{5,4},{6,7},{7,6},{8,9},{9,8},{10,11... | collective-permute-start | bytes 1966088 | tf_op jit(solution)/shard_map/ppermute | solution.py:119
  785.1 26.1 %collective-permute-start.87 = (bf16[2,32,1024]{2,0,1:T(2,128)(2,1)}, bf16[2,32,1024]{2,0,1:T(2,128)(2,1)}, u32[]{:S(2)}, u32[]{:S(2)}) collective-permute-start(bf16[2,32,1024]{2,0,1:T(2,128)(2,1)} %dynamic-slice_bitcast_fusion.28), channel_id=1, source_target_pairs={{0,8},{1,9},{2,10},{3,11},{4,12},{5,13},{6,14},{7,15},{8,0},{9,1},... | collective-permute-start | bytes 393224 | tf_op jit(solution)/shard_map/ppermute | solution.py:119
  788.2 23.0 %collective-permute-start.86 = (bf16[2,32,1024]{2,0,1:T(2,128)(2,1)}, bf16[2,32,1024]{2,0,1:T(2,128)(2,1)}, u32[]{:S(2)}, u32[]{:S(2)}) collective-permute-start(bf16[2,32,1024]{2,0,1:T(2,128)(2,1)} %dynamic-slice_bitcast_fusion.29), channel_id=1, source_target_pairs={{0,2},{1,3},{2,0},{3,1},{4,6},{5,7},{6,4},{7,5},{8,10},{9,11},{10,... | collective-permute-start | bytes 393224 | tf_op jit(solution)/shard_map/ppermute | solution.py:119
  (159 other events, 1243.2 us)
Sparse Core Ops, SparseCore 0:
  9.6 18.4 all-gather.9
  81.0 142.5 all-gather.7
  225.7 26.2 all-gather.5
